TPU v7x, 128 devices: a whole 4x4x4 slice. The times are simulated.
128 devices in a mesh: child: 2 (over y_lo), row: 8 (over x, core), col: 8 (over z, y_hi).
Axes of the slice: x: 4, y: 4 (y_hi: 2, y_lo: 2; y = y_hi * 2 + y_lo), z: 4, core: 2. Of those that a mesh axis runs over, the one named last changes fastest.
Arguments:
- child_blocks: float32 [2, 8192, 8192], P('child', 'row', 'col'), as said below
- child_panels: bfloat16 [2, 8192, 1024], P('child', 'row'), may hold values from -0.1875 to 0.1875
- child_patterns: int32 [2, 32, 32], replicated, may hold values from 0 to 1, as said below
- child_maps: int32 [2, 32], replicated, may hold values from 0 to 47, as said below
- parent_place: int32 [48], replicated, may hold values from 0 to 47, as said below
- parent_front: float32 [12288, 12288], P(('child', 'row'), 'col'), as said below
Outputs:
- factored: float32 [12288, 12288], P(('child', 'row'), 'col')
Inputs may be any that keep to these rules, and one draw needn't show every extreme that they name: `parent_place`: a permutation. The entries of one child are distinct; within each aligned block of 4 entries of one child, the values parent_place[child_maps[c, i]] // 6 are distinct. `child_patterns`: symmetric in its two tile dimensions, with ones on the diagonal. `child_blocks`: each child's block is symmetric. `parent_front`: symmetric; the diagonal entries inside stored tiles (parent_place[0], parent_place[0]) and (parent_place[1], parent_place[1]) lie between 200 and 400.
All inputs are finite; a program needn't handle non-finite values.
Results may differ from a plain program's by a relative error of at most 0.0003.
Values may be sent and summed in bfloat16 or wider, within the bound.
No kernel may reach another device: no remote copies, remote signals or barrier semaphores. Data moves between devices by JAX's collectives and lax.ppermute only.
A program may use at most 128 MiB of HBM per device.

v0:
```python
import jax
import jax.numpy as jnp
from jax import lax
from jax.sharding import PartitionSpec as P

TILE = 256
PANEL = 512


def spread_2(block, axis, source):
    block = jnp.where(lax.axis_index(axis) == source, block, jnp.zeros_like(block))
    return lax.psum(block, axis)


def filled_up(lines, size):
    spare = -len(lines) % size
    return jnp.pad(lines, [(0, spare)] + [(0, 0)] * (lines.ndim - 1))


def sum_by_parts(shard, axis):
    lines = shard.reshape(-1, *shard.shape[1:][-1:])
    own = lax.psum_scatter(
        filled_up(lines, lax.axis_size(axis)), axis, scatter_dimension=0, tiled=True
    )
    whole = lax.all_gather(own, axis).reshape(-1, *lines.shape[1:])
    return lax.slice_in_dim(whole, 0, len(lines)).reshape(shard.shape)


def lookup(lookup_table, positions):
    matches = positions[:, None] == jnp.arange(lookup_table.shape[0], dtype=jnp.int32)[None, :]
    return jnp.sum(jnp.where(matches, lookup_table[None, :], 0), axis=1)


def find_owner(slot_list, targets):
    matches = targets[:, None] == slot_list[None, :]
    located = jnp.any(matches, axis=1)
    chosen = jnp.sum(
        jnp.where(matches, jnp.arange(slot_list.shape[0], dtype=jnp.int32)[None, :], 0), axis=1
    )
    return (located, chosen)


def select_tiles(source, located, chosen, axis_pos):
    selected = jnp.take(source, chosen, axis=axis_pos)
    dims_shape = [1] * source.ndim
    dims_shape[axis_pos] = located.shape[0]
    return jnp.where(located.reshape(dims_shape), selected, jnp.zeros((), source.dtype))


def body(child_blocks, child_panels, child_patterns, child_maps, parent_place, parent_front):
    child_index = lax.axis_index("child")
    row_index = lax.axis_index("row")
    col_index = lax.axis_index("col")
    row_count = lax.axis_size("row")
    col_count = lax.axis_size("col")
    group_count = lax.axis_size(("child", "row"))
    own_block = child_blocks[0]
    block_width = own_block.shape[0]
    tiles_dev = block_width // TILE
    rows_dev = parent_front.shape[0] // TILE
    cols_dev = parent_front.shape[1] // TILE
    own_panel = child_panels[0]
    partner = spread_2(own_panel, "row", col_index)
    product = lax.dot_general(
        own_panel, partner, (((1,), (1,)), ((), ())), preferred_element_type=jnp.float32
    )
    pattern = lax.dynamic_index_in_dim(child_patterns, child_index, 0, keepdims=False)
    pattern = lax.dynamic_slice(
        pattern, (row_index * tiles_dev, col_index * tiles_dev), (tiles_dev, tiles_dev)
    ).astype(jnp.float32)
    update = (own_block - product).reshape(tiles_dev, TILE, tiles_dev, TILE) * pattern[
        :, None, :, None
    ]
    slot_table = jnp.stack(
        [lookup(parent_place, child_maps[0]), lookup(parent_place, child_maps[1])]
    )
    own_slots = lax.dynamic_index_in_dim(slot_table, child_index, 0, keepdims=False)
    row_slots = lax.dynamic_slice_in_dim(own_slots, row_index * tiles_dev, tiles_dev)
    group_index = child_index * row_count + row_index
    row_targets = group_index * rows_dev + jnp.arange(rows_dev, dtype=jnp.int32)
    col_targets = col_index * cols_dev + jnp.arange(cols_dev, dtype=jnp.int32)
    group_ids = jnp.arange(group_count, dtype=jnp.int32)
    column_ids = jnp.arange(col_count, dtype=jnp.int32)
    located, chosen = find_owner(row_slots // rows_dev, group_ids)
    outgoing = select_tiles(update.reshape(tiles_dev, TILE, block_width), located, chosen, 0)
    incoming = lax.all_to_all(outgoing, ("child", "row"), split_axis=0, concat_axis=0, tiled=True)
    outgoing_cols = []
    for member in range(2):
        located, chosen = find_owner(slot_table[member], row_targets)
        sender = member * row_count + chosen // tiles_dev
        arranged = select_tiles(incoming, located, sender, 0).reshape(
            rows_dev * TILE, tiles_dev, TILE
        )
        member_cols = lax.dynamic_slice_in_dim(slot_table[member], col_index * tiles_dev, tiles_dev)
        located, chosen = find_owner(member_cols // cols_dev, column_ids)
        outgoing_cols.append(select_tiles(arranged, located, chosen, 1))
    incoming_cols = lax.all_to_all(
        jnp.stack(outgoing_cols), "col", split_axis=2, concat_axis=2, tiled=True
    )
    contribution = jnp.zeros((rows_dev * TILE, cols_dev, TILE), jnp.float32)
    for member in range(2):
        located, chosen = find_owner(slot_table[member], col_targets)
        contribution = contribution + select_tiles(
            incoming_cols[member], located, chosen // tiles_dev, 1
        )
    assembled = parent_front + contribution.reshape(parent_front.shape)
    panel_slots = parent_place[0:2]
    col_local = panel_slots // cols_dev == col_index
    col_pos = panel_slots % cols_dev
    row_local = panel_slots // rows_dev == group_index
    row_pos = panel_slots % rows_dev
    front_tiles = assembled.reshape(rows_dev * TILE, cols_dev, TILE)
    column = select_tiles(front_tiles, col_local, col_pos, 1).reshape(rows_dev * TILE, PANEL)
    diagonal_part = select_tiles(
        column.reshape(rows_dev, TILE, PANEL), row_local, row_pos, 0
    ).reshape(PANEL, PANEL)
    panel_column = sum_by_parts(column, "col")
    diagonal_block = lax.psum(diagonal_part, ("child", "row", "col"))
    factor = jnp.linalg.cholesky(diagonal_block)
    panel_rows = lax.linalg.triangular_solve(
        factor, panel_column, left_side=False, lower=True, transpose_a=True
    )
    owned = jnp.logical_and(
        jnp.arange(2, dtype=jnp.int32) == group_index % 2, group_index // 2 == col_index
    )
    spread = jnp.where(owned[:, None, None], panel_rows[None, :, :], 0.0).reshape(
        2 * rows_dev * TILE, PANEL
    )
    panel_cols = sum_by_parts(spread, ("child", "row"))
    result = assembled - lax.dot_general(
        panel_rows,
        panel_cols,
        (((1,), (1,)), ((), ())),
        precision=lax.Precision.HIGHEST,
        preferred_element_type=jnp.float32,
    )
    result_tiles = result.reshape(rows_dev * TILE, cols_dev, TILE)
    tile_positions = jnp.arange(cols_dev, dtype=jnp.int32)
    for member in range(2):
        chosen_cols = jnp.logical_and(tile_positions == col_pos[member], col_local[member])
        result_tiles = jnp.where(
            chosen_cols[None, :, None],
            panel_rows[:, None, member * TILE : (member + 1) * TILE],
            result_tiles,
        )
    return result_tiles.reshape(parent_front.shape)


def solution(mesh):
    return jax.shard_map(
        body,
        mesh=mesh,
        in_specs=(
            P("child", "row", "col"),
            P("child", "row", None),
            P(),
            P(),
            P(),
            P(("child", "row"), "col"),
        ),
        out_specs=P(("child", "row"), "col"),
        check_vma=False,
    )
```

profile of v0, /device:TPU:1, one launch (start us, length us, event | category | flops | bytes accessed | tf_op | source)
XLA Modules:
  0.0 1057.3 jit_solution(6001793039365585537)
XLA Ops:
  6.5 3.2 bitcast_select_fusion.5
  11.2 65.6 %all-reduce.4.cloned.1.call-done = bf16[1024,1024]{1,0:T(8,128)(2,1)} async-done(((bf16[1024,1024]{1,0:T(8,128)(2,1)}), bf16[1024,1024]{1,0:T(8,128)(2,1)}) %all-reduce.4.cloned.1.call-update) | async-done | bytes 2097168 | tf_op jit(solution)/shard_map/psum | solution.py:12
  76.8 5.2 bitcast_subtract_fusion
  82.0 2.5 broadcast_multiply_fusion
  84.5 9.8 gather_fusion
  94.3 12.5 %select_select_fusion = f32[16,256,1024]{2,1,0:T(8,128)} fusion(f32[16,256,1024]{2,1,0:T(8,128)} %gather_fusion, pred[16]{0:T(512)(128)(4,1)S(1)} %compare_and_fusion.9, pred[16]{0:T(512)(128)(4,1)S(1)} %fusion.34), kind=kLoop, calls=%fused_computation.11 | loop fusion | flops 8388608 | bytes 33554464 | tf_op jit(solution)/shard_map/jit(_where)/select_n | solution.py:47
  106.8 7.9 all-to-all-start
  115.6 223.2 %all-to-all-done = f32[16,256,1024]{2,1,0:T(8,128)} async-done(((f32[16,256,1024]{2,1,0:T(8,128)}), f32[16,256,1024]{2,1,0:T(8,128)}, u32[]{:S(2)}, u32[]{:S(2)}) %all-to-all-start) | async-done | bytes 16777248 | tf_op jit(solution)/shard_map/all_to_all | solution.py:86
  338.8 6.5 gather_fusion.3
  345.3 2.1 select_select_fusion.3
  347.4 5.1 reshape.182
  352.6 2.5 copy.83
  355.1 8.2 gather_fusion.5
  363.3 4.3 select_select_fusion.2
  367.6 5.1 reshape.183
  372.7 4.2 copy.84
  376.9 3.6 gather_fusion.4
  380.5 5.5 gather_fusion.6
  386.0 3.8 fusion.1
  390.6 3.3 fusion
  393.9 8.6 pad_maximum_fusion
  402.4 10.2 copy.85
  412.6 6.6 all-to-all-start.1
  420.3 138.8 %all-to-all-done.1 = f32[2,768,8,256]{3,1,0,2:T(8,128)} async-done(((f32[2,768,8,256]{3,1,0,2:T(8,128)}), f32[2,768,8,256]{3,1,0,2:T(8,128)}, u32[]{:S(2)}, u32[]{:S(2)}) %all-to-all-start.1) | async-done | bytes 12582944 | tf_op jit(solution)/shard_map/all_to_all | solution.py:97
  559.1 10.2 slice_bitcast_fusion.1
  569.3 5.8 gather_fusion.7
  575.1 5.8 gather_fusion.8
  580.9 7.0 fusion.2
  587.9 6.0 copy.88
  593.9 6.0 copy.89
  600.0 6.9 add.171
  606.9 6.0 copy.90
  613.0 6.1 copy.91
  619.1 3.0 gather_fusion.1
  622.1 2.4 copy.94
  624.4 2.5 gather.32
  627.0 1.4 select_select_fusion.4
  628.4 2.0 gather_fusion.2
  631.7 2.3 select_select_fusion.7
  637.1 142.6 %all-reduce.6.cloned.1.call-done = f32[512,512]{0,1:T(8,128)} async-done(((f32[512,512]{0,1:T(8,128)}), f32[512,512]{0,1:T(8,128)}) %all-reduce.6.cloned.1.call-update) | async-done | bytes 1048592 | tf_op jit(solution)/shard_map/psum | solution.py:118
  779.7 1.6 copy.96
  781.2 1.4 fusion.9
  782.7 11.7 %cholesky.102 = f32[128,128]{1,0:T(8,128)S(1)} custom-call(f32[128,128]{1,0:T(8,128)S(1)} %cholesky.260), custom_call_target="Cholesky" | custom-call | tf_op jit(solution)/shard_map/jit(cholesky)/cholesky | solution.py:119
  794.6 9.8 custom-call.30
  805.2 11.7 %cholesky.213 = f32[128,128]{1,0:T(8,128)S(1)} custom-call(f32[128,128]{1,0:T(8,128)S(1)} %cholesky.264), custom_call_target="Cholesky" | custom-call | tf_op jit(solution)/shard_map/jit(cholesky)/cholesky | solution.py:119
  817.0 10.0 custom-call.31
  828.1 11.7 %cholesky.234 = f32[128,128]{1,0:T(8,128)S(1)} custom-call(f32[128,128]{1,0:T(8,128)S(1)} %cholesky.269), custom_call_target="Cholesky" | custom-call | tf_op jit(solution)/shard_map/jit(cholesky)/cholesky | solution.py:119
  839.9 9.8 custom-call.32
  850.6 11.9 %cholesky.251 = f32[128,128]{1,0:T(8,128)S(1)} custom-call(f32[128,128]{1,0:T(8,128)S(1)} %convolution_subtract_fusion.5), custom_call_target="Cholesky" | custom-call | tf_op jit(solution)/shard_map/jit(cholesky)/cholesky | solution.py:119
  868.0 8.5 while.1
  876.5 39.3 %custom-call.33 = f32[4,128,128]{1,2,0:T(8,128)S(1)} custom-call(f32[4,128,128]{2,1,0:T(8,128)S(1)} %get-tuple-element.15), custom_call_target="InvertDiagBlocksLowerTriangular" | custom-call | tf_op jit(solution)/shard_map/triangular_solve | solution.py:120
  915.9 1.6 fusion.10
  917.5 1.8 convolution_subtract_fusion.1
  919.9 1.4 convolution_subtract_fusion.2
  921.8 2.1 convolution_subtract_fusion
  924.5 1.6 copy.105
  926.1 3.4 bitcast_select_fusion.4
  929.8 59.7 %reduce-scatter.5.cloned.1.call-done = f32[96,512]{1,0:T(8,128)} async-done(((f32[1536,512]{1,0:T(8,128)}), f32[96,512]{1,0:T(8,128)}) %reduce-scatter.5.cloned.1.call-update) | async-done | bytes 196624 | tf_op jit(solution)/shard_map/reduce_scatter | solution.py:22
  993.6 2.6 broadcast_in_dim.411
  996.2 6.0 copy.106
  1002.2 2.6 broadcast_in_dim.406
  1004.9 6.2 copy.107
  1011.1 18.4 %all-gather.7.cloned.1.call-done = f32[1536,512]{1,0:T(8,128)} async-done(((f32[96,512]{1,0:T(8,128)}), f32[1536,512]{1,0:T(8,128)}) %all-gather.7.cloned.1.call-update) | async-done | bytes 3145744 | tf_op jit(solution)/shard_map/all_gather | solution.py:25
  1029.5 20.8 %select_select_fusion.1 = f32[768,1536]{1,0:T(8,128)} fusion(f32[768,1536]{1,0:T(8,128)} %copy.107, f32[768,1536]{1,0:T(8,128)} %copy.106, f32[768,1536]{1,0:T(8,128)} %add.171, f32[1536,512]{1,0:T(8,128)} %all-gather.7.cloned.1.call-done, pred[1536]{0:T(1024)(128)(4,1)S(1)} %broadcast_in_dim.409, pred[1536]{0:T(1024)(128)(4,1)S(1)} %broadcast_in_dim.355, ...), kind=kOutput, calls=%fused_computation.22 | convolution fusion | flops 7252475904 | bytes 23596032 | tf_op jit(solution)/shard_map/dot_general | solution.py:130
  (143 shorter events, 28.9 us)
Async XLA Ops:
  6.5 70.2 %all-reduce.4.cloned.1.call-start = ((), (), s32[]{:S(2)}) async-start(), calls=%async_computation.4 | async-start | bytes 4194304 | tf_op jit(solution)/shard_map/psum | solution.py:12
  6.5 4.1 copy-start.4
  6.5 4.1 copy-start.3
  6.5 70.2 %copy-start.1 = (bf16[1,1024,1024]{2,1,0:T(8,128)(2,1)S(1)}, bf16[1,1024,1024]{2,1,0:T(8,128)(2,1)}, u32[]{:S(2)}) copy-start(bf16[1,1024,1024]{2,1,0:T(8,128)(2,1)} %param.13) | copy-start | bytes 6291460
  106.8 232.0 %all-to-all-start = ((f32[16,256,1024]{2,1,0:T(8,128)}), f32[16,256,1024]{2,1,0:T(8,128)}, u32[]{:S(2)}, u32[]{:S(2)}) async-start(f32[16,256,1024]{2,1,0:T(8,128)} %select_select_fusion), calls=%async_computation | async-start | bytes 33554432 | tf_op jit(solution)/shard_map/all_to_all | solution.py:86
  386.0 4.6 copy-start
  412.6 146.5 %all-to-all-start.1 = ((f32[2,768,8,256]{3,1,0,2:T(8,128)}), f32[2,768,8,256]{3,1,0,2:T(8,128)}, u32[]{:S(2)}, u32[]{:S(2)}) async-start(f32[2,768,8,256]{3,1,0,2:T(8,128)} %copy.85), calls=%async_computation.1 | async-start | bytes 25165824 | tf_op jit(solution)/shard_map/all_to_all | solution.py:97
  419.2 360.5 %all-reduce.6.cloned.1.call-start = ((), (), s32[]{:S(2)}) async-start(), calls=%async_computation.6 | async-start | bytes 2097152 | tf_op jit(solution)/shard_map/psum | solution.py:118
  634.1 228.5 %reduce-scatter.3.cloned.1.call-start = ((), (), s32[]{:S(2)}) async-start(), calls=%async_computation.5 | async-start | bytes 1769472 | tf_op jit(solution)/shard_map/reduce_scatter | solution.py:22
  636.5 279.4 %all-gather.5.cloned.1.call-start = ((), (), s32[]{:S(2)}) async-start(), calls=%async_computation.8 | async-start | bytes 1769472 | tf_op jit(solution)/shard_map/all_gather | solution.py:25
  862.6 126.9 %reduce-scatter.5.cloned.1.call-start = ((), (), s32[]{:S(2)}) async-start(), calls=%async_computation.7 | async-start | bytes 3342336 | tf_op jit(solution)/shard_map/reduce_scatter | solution.py:22
  915.9 4.0 copy-start.2
  929.5 99.9 %all-gather.7.cloned.1.call-start = ((), (), s32[]{:S(2)}) async-start(), calls=%async_computation.9 | async-start | bytes 3342336 | tf_op jit(solution)/shard_map/all_gather | solution.py:25
Sparse Core Ops, SparseCore 0:
  9.9 66.8 all-reduce.3
  634.2 145.3 all-reduce.5
  783.8 71.5 reduce-scatter.2
  862.7 48.1 all-gather.4
  929.7 59.8 reduce-scatter.4
  991.1 38.3 all-gather.6
where the time goes:
time: 1060 us
  waiting for transfers between devices  648 us (61%)
  other arithmetic  188 us (18%)
  local copies, waits for them, and re-layouts  151 us (14%)
  matrix products  36.7 us (3%)
  between operations  16.8 us (2%)
  starting transfers between devices  15.5 us (1%)
    all_to_all x1, waiting for transfers between devices, body(): lax.all_to_all(outgoing, ('child', 'row'), split_axis=0, concat_axis=0, t...  223 us
    psum x1, waiting for transfers between devices, body(): diagonal_block = lax.psum(diagonal_part, ('child', 'row', 'col'))  143 us
    all_to_all x1, waiting for transfers between devices, body(): lax.all_to_all(jnp.stack(outgoing_cols), 'col', split_axis=2, concat_axis...  139 us
    another operation x15, other arithmetic, body(): factor = jnp.linalg.cholesky(diagonal_block)  79.4 us
    psum x1, waiting for transfers between devices, spread_2(): return lax.psum(block, axis)  65.6 us
    reduce_scatter x2, waiting for transfers between devices, sum_by_parts(): lax.psum_scatter(filled_up(lines, lax.axis_size(axis)), axis, scatter_dim...  59.7 us
    gather x14, local copies, waits for them, and re-layouts, select_tiles(): selected = jnp.take(source, chosen, axis=axis_pos)  57.4 us
    another operation x6, other arithmetic, body(): lax.linalg.triangular_solve(factor, panel_column, left_side=False, lower=...  39.7 us
  transfers between devices with their start and end apart: 8, of which 6 were waited for; matrix products, arithmetic and copies ran while one was open for 15% of the time, Pallas kernels for 0%

commit v1 on v0

v1 whole, which is shorter than its diff:
```python
import functools

import jax
import jax.numpy as jnp
from jax import lax
from jax.experimental import pallas as pl
from jax.experimental.pallas import tpu as pltpu
from jax.sharding import Mesh
from jax.sharding import PartitionSpec as P

TILE = 256
PANEL = 512
CODE = 16
CT = 4
RT = 3
QT = 6
STRIP = 32
SROWS = RT * STRIP + CODE
AXES = ("child", "x", "core", "z", "yh")
SIZES = (2, 4, 2, 4, 2)
MIB = 1 << 20
F32 = jnp.float32
I32 = jnp.int32
I16 = jnp.int16
BF16 = jnp.bfloat16
HIGHEST = lax.Precision.HIGHEST


def flat(c, x, k, z, y):
    return (((c * 4 + x) * 2 + k) * 4 + z) * 2 + y


def everyone():
    return [
        (c, x, k, z, y)
        for c in range(2)
        for x in range(4)
        for k in range(2)
        for z in range(4)
        for y in range(2)
    ]


def shift(v, dc=0, dx=0, dk=0, dz=0, dy=0):
    pairs = [
        (flat(c, x, k, z, y), flat(c ^ dc, (x + dx) % 4, k ^ dk, (z + dz) % 4, y ^ dy))
        for c, x, k, z, y in everyone()
    ]
    return lax.ppermute(v, AXES, pairs)


def encode(u):
    top = jnp.max(jnp.abs(u), axis=0, keepdims=True)
    code = jnp.ceil(jnp.log2(jnp.maximum(top, 1e-30)) * 128.0)
    q = jnp.clip(jnp.floor(u * jnp.exp2(15.0 - code * (1.0 / 128.0)) + 0.5), -32767.0, 32767.0)
    return q.astype(I32).astype(I16), code


def scale_rows(code):
    return jnp.broadcast_to(code, (CODE, code.shape[1])).astype(I32).astype(I16)


def as_float(q):
    return q.astype(I32).astype(F32)


def column_scale(codes):
    return jnp.exp2(as_float(codes)[0:1, :] * (1.0 / 128.0) - 15.0)


def update_kernel(ids, maps, place, pat, blk, pan, par, front, send, diag, tile, sem):
    i = pl.program_id(0)
    ch, r, c, g = ids[0], ids[1], ids[2], ids[3]

    @pl.when(i == 0)
    def _():
        diag[...] = jnp.zeros_like(diag)
        for a in range(2):
            for b in range(2):
                ea, eb = place[a], place[b]

                @pl.when((ea // RT == g) & (eb // QT == c))
                def _():
                    rows = pl.multiple_of((ea % RT) * TILE, TILE)
                    cols = pl.multiple_of((eb % QT) * TILE, TILE)
                    copy = pltpu.make_async_copy(
                        front.at[pl.ds(rows, TILE), pl.ds(cols, TILE)], tile, sem
                    )
                    copy.start()
                    copy.wait()
                    diag[a * TILE : (a + 1) * TILE, b * TILE : (b + 1) * TILE] = tile[...]

    si = place[maps[ch, r * CT + i]]
    for j in range(CT):
        cols = slice(j * TILE, (j + 1) * TILE)
        prod = lax.dot_general(
            pan[...], par[cols, :], (((1,), (1,)), ((), ())), preferred_element_type=F32
        )
        u = (blk[:, cols] - prod) * pat[ch, r * CT + i, c * CT + j].astype(F32)
        q, code = encode(u)
        send[0, 0:TILE, cols] = q
        send[0, TILE:, cols] = scale_rows(code)
        sj = place[maps[ch, c * CT + j]]
        for a in range(2):
            for b in range(2):

                @pl.when((si == place[a]) & (sj == place[b]))
                def _():
                    diag[a * TILE : (a + 1) * TILE, b * TILE : (b + 1) * TILE] += u


def update(ids, maps, place, pat, blk, pan, par, front):
    def slot(i, ids, maps, place, pat):
        return place[maps[ids[0], ids[1] * CT + i]] // QT, 0, 0

    return pl.pallas_call(
        update_kernel,
        grid_spec=pltpu.PrefetchScalarGridSpec(
            num_scalar_prefetch=4,
            grid=(CT,),
            in_specs=[
                pl.BlockSpec((TILE, 1024), lambda i, *s: (i, 0)),
                pl.BlockSpec((TILE, 1024), lambda i, *s: (i, 0)),
                pl.BlockSpec((1024, 1024), lambda i, *s: (0, 0)),
                pl.BlockSpec(memory_space=pl.ANY),
            ],
            out_specs=[
                pl.BlockSpec((1, TILE + CODE, 1024), slot),
                pl.BlockSpec((PANEL, PANEL), lambda i, *s: (0, 0)),
            ],
            scratch_shapes=[pltpu.VMEM((TILE, TILE), F32), pltpu.SemaphoreType.DMA],
        ),
        out_shape=[
            jax.ShapeDtypeStruct((8, TILE + CODE, 1024), I16),
            jax.ShapeDtypeStruct((PANEL, PANEL), F32),
        ],
        compiler_params=pltpu.CompilerParams(vmem_limit_bytes=40 * MIB),
        cost_estimate=pl.CostEstimate(flops=1 << 31, bytes_accessed=14 * MIB, transcendentals=0),
    )(ids, maps, place, pat, blk, pan, par, front)


def find(maps, place, ch, slot):
    def step(i, found):
        return jnp.where(place[maps[ch, i]] == slot, i, found)

    return lax.fori_loop(0, 32, step, jnp.int32(-1))


def route_kernel(ids, maps, place, own, other, send, sems):
    c, g, core = ids[2], ids[3], ids[4]

    def each(act):
        for ch in range(2):
            for p in range(RT):
                i = rows[ch * RT + p]
                src = ch * 4 + i // 8
                for j in range(CT):
                    q = place[maps[ch, c * CT + j]] // QT
                    sem = sems.at[(ch * RT + p) * CT + j]
                    for here, buf in ((True, own), (False, other)):

                        @pl.when((i >= 0) & (((i // 4) % 2 == core) == here))
                        def _():
                            copy = pltpu.make_async_copy(
                                buf.at[src, :, pl.ds(j * TILE, TILE)],
                                send.at[q, ch * RT + p],
                                sem,
                            )
                            act(copy)

    rows = [find(maps, place, ch, g * RT + p) for ch in range(2) for p in range(RT)]
    each(lambda copy: copy.start())
    each(lambda copy: copy.wait())


def route(ids, maps, place, own, other):
    return pl.pallas_call(
        route_kernel,
        grid_spec=pltpu.PrefetchScalarGridSpec(
            num_scalar_prefetch=3,
            grid=(1,),
            in_specs=[pl.BlockSpec(memory_space=pl.ANY)] * 2,
            out_specs=pl.BlockSpec(memory_space=pl.ANY),
            scratch_shapes=[pltpu.SemaphoreType.DMA((24,))],
        ),
        out_shape=jax.ShapeDtypeStruct((8, 2 * RT, TILE + CODE, TILE), I16),
        cost_estimate=pl.CostEstimate(flops=0, bytes_accessed=8 * MIB, transcendentals=0),
    )(ids, maps, place, own, other)


def strips_kernel(ids, maps, place, own, other, front, *rest):
    outs, (acc, tile, wide, sem) = rest[:8], rest[8:]
    c, g, core, z, yh = ids[2], ids[3], ids[4], ids[5], ids[6]
    acc[...] = jnp.zeros_like(acc)
    for a in range(2):
        cols = slice(a * TILE, (a + 1) * TILE)

        @pl.when(place[a] // QT == c)
        def _():
            at = pl.multiple_of((place[a] % QT) * TILE, TILE)
            copy = pltpu.make_async_copy(front.at[:, pl.ds(at, TILE)], wide, sem)
            copy.start()
            copy.wait()
            acc[:, cols] = wide[...]

        for ch in range(2):
            ja = find(maps, place, ch, place[a])

            @pl.when((ja >= 0) & (ja // CT == c))
            def _():
                at = pl.multiple_of((ja % CT) * TILE, TILE)
                for p in range(RT):
                    i = find(maps, place, ch, g * RT + p)
                    for here, buf in ((True, own), (False, other)):

                        @pl.when((i >= 0) & (((i // 4) % 2 == core) == here))
                        def _():
                            copy = pltpu.make_async_copy(
                                buf.at[ch * 4 + i // 8, :, pl.ds(at, TILE)], tile, sem
                            )
                            copy.start()
                            copy.wait()
                            acc[p * TILE : (p + 1) * TILE, cols] += as_float(
                                tile[0:TILE, :]
                            ) * column_scale(tile[TILE:, :])

    for m in range(8):
        s = ((z + m // 2) % 4) * 2 + (yh + m % 2) % 2
        parts = [
            acc[pl.ds(pl.multiple_of(p * TILE + s * STRIP, STRIP), STRIP), :] for p in range(RT)
        ]
        q, code = encode(jnp.concatenate(parts, 0))
        outs[m][0 : RT * STRIP, :] = q
        outs[m][RT * STRIP :, :] = scale_rows(code)


def strips(ids, maps, place, own, other, front):
    return pl.pallas_call(
        strips_kernel,
        grid_spec=pltpu.PrefetchScalarGridSpec(
            num_scalar_prefetch=3,
            grid=(1,),
            in_specs=[pl.BlockSpec(memory_space=pl.ANY)] * 3,
            out_specs=[pl.BlockSpec((SROWS, PANEL), lambda i, *s: (0, 0))] * 8,
            scratch_shapes=[
                pltpu.VMEM((RT * TILE, PANEL), F32),
                pltpu.VMEM((TILE + CODE, TILE), I16),
                pltpu.VMEM((RT * TILE, TILE), F32),
                pltpu.SemaphoreType.DMA,
            ],
        ),
        out_shape=[jax.ShapeDtypeStruct((SROWS, PANEL), I16)] * 8,
        compiler_params=pltpu.CompilerParams(vmem_limit_bytes=24 * MIB),
        cost_estimate=pl.CostEstimate(flops=0, bytes_accessed=4 * MIB, transcendentals=0),
    )(ids, maps, place, own, other, front)


def decode_strip(ref, lead=()):
    q = ref[lead + (slice(0, RT * STRIP), slice(None))]
    codes = ref[lead + (slice(RT * STRIP, SROWS), slice(None))]
    return as_float(q) * column_scale(codes)


def merge_kernel(*refs):
    total = decode_strip(refs[0])
    for ref in refs[1:8]:
        total = total + decode_strip(ref)
    q, code = encode(total)
    refs[8][0 : RT * STRIP, :] = q
    refs[8][RT * STRIP :, :] = scale_rows(code)


def merge(parts):
    return pl.pallas_call(
        merge_kernel,
        out_shape=jax.ShapeDtypeStruct((SROWS, PANEL), I16),
        cost_estimate=pl.CostEstimate(flops=0, bytes_accessed=MIB, transcendentals=0),
    )(*parts)


def nt(a, b):
    return lax.dot_general(
        a, b, (((1,), (1,)), ((), ())), precision=HIGHEST, preferred_element_type=F32
    )


def nn(a, b):
    return lax.dot_general(
        a, b, (((1,), (0,)), ((), ())), precision=HIGHEST, preferred_element_type=F32
    )


NB = 128


def inverse_kernel(a_ref, out, w, f):
    n = PANEL // NB
    out[...] = jnp.zeros_like(out)
    row = lax.broadcasted_iota(I32, (NB, NB), 0)
    col = lax.broadcasted_iota(I32, (NB, NB), 1)
    eye = row == col
    lanes = lax.broadcasted_iota(I32, (1, 2 * NB), 1)
    sub = lax.broadcasted_iota(I32, (NB, 1), 0)

    def blk(i):
        return slice(i * NB, (i + 1) * NB)

    f[...] = a_ref[...]
    for k in range(n):
        w[:, :NB] = f[blk(k), blk(k)]
        w[:, NB:] = jnp.where(eye, 1.0, 0.0).astype(F32)

        def step(j, _):
            line = w[pl.ds(j, 1), :]
            pivot = jnp.sum(jnp.where(lanes == j, line, 0.0), axis=1, keepdims=True)
            column = jnp.sum(jnp.where(col == j, w[:, :NB], 0.0), axis=1, keepdims=True)
            factor = jnp.where(sub > j, column / pivot, 0.0)
            w[...] = w[...] - factor * line
            return 0

        lax.fori_loop(0, NB, step, 0)
        d = jnp.sum(jnp.where(eye, w[:, :NB], 0.0), axis=1, keepdims=True)
        inv = w[:, NB:] * (1.0 / jnp.sqrt(d))
        out[blk(k), blk(k)] = inv
        rest = (k + 1) * NB
        if rest < PANEL:
            below = nt(f[rest:, blk(k)], inv)
            f[rest:, blk(k)] = below
            f[rest:, rest:] = f[rest:, rest:] - nt(below, below)
    for k in range(1, n):
        acc = nn(f[blk(k), : k * NB], out[: k * NB, : k * NB])
        out[blk(k), : k * NB] = -nn(out[blk(k), blk(k)], acc)


def inverse_factor(a):
    return pl.pallas_call(
        inverse_kernel,
        out_shape=jax.ShapeDtypeStruct((PANEL, PANEL), F32),
        scratch_shapes=[pltpu.VMEM((NB, 2 * NB), F32), pltpu.VMEM((PANEL, PANEL), F32)],
        compiler_params=pltpu.CompilerParams(vmem_limit_bytes=24 * MIB),
        cost_estimate=pl.CostEstimate(flops=1 << 34, bytes_accessed=2 * MIB, transcendentals=0),
    )(a)


def split(v):
    hi = v.astype(BF16)
    return hi, (v - hi.astype(F32)).astype(BF16)


def dot3(a, b):
    def one(x, y):
        return lax.dot_general(x, y, (((1,), (1,)), ((), ())), preferred_element_type=F32)

    return one(a[0], b[0]) + (one(a[0], b[1]) + one(a[1], b[0]))


def final_kernel(
    ids, maps, place, diag, inv, gr, gown, goth, recv, front, out,
    gbuf, ph, plo, rows_f, tiles, inv_h, inv_l, tsem,
):
    p = pl.program_id(0)
    c, g, core, k = ids[2], ids[3], ids[4], ids[7]
    e = (place[0], place[1])

    @pl.when(p == 0)
    def _():
        hi, lo = split(inv[...])
        inv_h[...] = hi
        inv_l[...] = lo

        def fill(base, ref, order, first):
            for s in range(8):
                v = decode_strip(ref, (order(s),))
                for t in range(RT):
                    gbuf[base + t * TILE + s * STRIP : base + t * TILE + (s + 1) * STRIP, :] = v[
                        t * STRIP : (t + 1) * STRIP, :
                    ]
            for t in range(RT):
                for a in range(2):

                    @pl.when(first + t == e[a])
                    def _():
                        gbuf[base + t * TILE : base + (t + 1) * TILE, :] = diag[
                            a * TILE : (a + 1) * TILE, :
                        ]

        fill(0, gr, lambda s: s, g * RT)
        for b in range(2):
            base = RT * TILE * (1 + b)

            @pl.when(core == b)
            def _():
                fill(base, gown, lambda s: k ^ s, c * QT + b * RT)

            @pl.when(core != b)
            def _():
                fill(base, goth, lambda s: k ^ s, c * QT + b * RT)

        for t in range(9):
            rows = slice(t * TILE, (t + 1) * TILE)
            v = dot3(split(gbuf[rows, :]), (inv_h[...], inv_l[...]))
            hi, lo = split(v)
            ph[rows, :] = hi
            plo[rows, :] = lo
            if t < RT:
                rows_f[rows, :] = v

    pr = pl.ds(pl.multiple_of(p * TILE, TILE), TILE)
    left = (ph[pr, :], plo[pr, :])
    srow = g * RT + p
    there = [find(maps, place, ch, srow) >= 0 for ch in range(2)]
    js = [[find(maps, place, ch, c * QT + t) for t in range(QT)] for ch in range(2)]

    def each(act):
        for ch in range(2):
            for t in range(QT):

                @pl.when(there[ch] & (js[ch][t] >= 0))
                def _():
                    act(
                        pltpu.make_async_copy(
                            recv.at[js[ch][t] // CT, ch * RT + p],
                            tiles.at[ch * QT + t],
                            tsem.at[ch * QT + t],
                        )
                    )

    each(lambda copy: copy.start())
    for t in range(QT):
        cols = slice(t * TILE, (t + 1) * TILE)
        right = slice((RT + t) * TILE, (RT + t + 1) * TILE)
        out[:, cols] = front[:, cols] - dot3(left, (ph[right, :], plo[right, :]))
    each(lambda copy: copy.wait())
    for t in range(QT):
        cols = slice(t * TILE, (t + 1) * TILE)
        for ch in range(2):

            @pl.when(there[ch] & (js[ch][t] >= 0))
            def _():
                out[:, cols] += as_float(tiles[ch * QT + t, 0:TILE, :]) * column_scale(
                    tiles[ch * QT + t, TILE:, :]
                )

        for a in range(2):

            @pl.when(c * QT + t == e[a])
            def _():
                out[:, cols] = rows_f[pr, a * TILE : (a + 1) * TILE]


def final(ids, maps, place, diag, inv, gr, gown, goth, recv, front):
    def whole(*shape):
        return pl.BlockSpec(shape, lambda i, *s: (0,) * len(shape))

    line = pl.BlockSpec((TILE, QT * TILE), lambda i, *s: (i, 0))
    return pl.pallas_call(
        final_kernel,
        grid_spec=pltpu.PrefetchScalarGridSpec(
            num_scalar_prefetch=3,
            grid=(RT,),
            in_specs=[
                whole(PANEL, PANEL),
                whole(PANEL, PANEL),
                whole(8, SROWS, PANEL),
                whole(8, SROWS, PANEL),
                whole(8, SROWS, PANEL),
                pl.BlockSpec(memory_space=pl.ANY),
                line,
            ],
            out_specs=line,
            scratch_shapes=[
                pltpu.VMEM((9 * TILE, PANEL), F32),
                pltpu.VMEM((9 * TILE, PANEL), BF16),
                pltpu.VMEM((9 * TILE, PANEL), BF16),
                pltpu.VMEM((RT * TILE, PANEL), F32),
                pltpu.VMEM((2 * QT, TILE + CODE, TILE), I16),
                pltpu.VMEM((PANEL, PANEL), BF16),
                pltpu.VMEM((PANEL, PANEL), BF16),
                pltpu.SemaphoreType.DMA((2 * QT,)),
            ],
        ),
        out_shape=jax.ShapeDtypeStruct((RT * TILE, QT * TILE), F32),
        compiler_params=pltpu.CompilerParams(vmem_limit_bytes=52 * MIB),
        cost_estimate=pl.CostEstimate(flops=1 << 33, bytes_accessed=20 * MIB, transcendentals=0),
    )(ids, maps, place, diag, inv, gr, gown, goth, recv, front)


def pick(v, at):
    return lax.dynamic_index_in_dim(v, at, 0, keepdims=False)


def fetch_partner(panel, x, core, z, yh):
    tiles = panel.reshape(4, TILE, 1024)
    piece = pick(tiles, (z - x) % 4)
    halves = []
    for h in range(2):
        came = []
        for dx in (1, 2, 3):
            pairs = [
                (flat(c, xs, y, (xs + 2 * h + b) % 4, y), flat(c, (xs + dx) % 4, b, xs, y))
                for c in range(2)
                for xs in range(4)
                for y in range(2)
                for b in range(2)
            ]
            came.append(lax.ppermute(piece, AXES, pairs))
        halves.append(came)
    two = jnp.stack([pick(tiles, 1 - core), pick(tiles, 3 - core)])
    pairs = [
        (flat(c, x, y, x, y), flat(c, x, 1 - y, x, y))
        for c in range(2)
        for x in range(4)
        for y in range(2)
    ]
    beside = lax.ppermute(two, AXES, pairs)
    owner = (x == z) & (core == yh)
    way = (x - z) % 4
    mine = []
    for h in range(2):
        a, b, d = halves[h]
        got = jnp.where(way == 1, a, jnp.where(way == 2, b, jnp.where(way == 3, d, beside[h])))
        mine.append(jnp.where(owner, pick(tiles, core + 2 * h), got))
    mine = jnp.stack(mine)
    other = shift(mine, dk=1)
    even = jnp.where(core == 0, mine, other)
    odd = jnp.where(core == 0, other, mine)
    return jnp.stack([even[0], odd[0], even[1], odd[1]]).reshape(1024, 1024)


def sum_everywhere(v, x, z):
    v = v.reshape(4, 128, PANEL)
    got = [shift(pick(v, (x + d) % 4), dx=d) for d in (1, 3, 2)]
    v = pick(v, x) + got[0] + got[1] + got[2]
    v = v.reshape(4, 32, PANEL)
    got = [shift(pick(v, (z + d) % 4), dz=d) for d in (1, 3, 2)]
    v = pick(v, z) + got[0] + got[1] + got[2]
    v = v + shift(v, dk=1)
    v = (v + shift(v, dc=1, dy=1)) + (shift(v, dc=1) + shift(v, dy=1))
    full = jnp.zeros((4, 32, PANEL), F32)
    full = lax.dynamic_update_index_in_dim(full, v, z, 0)
    for d in (1, 3, 2):
        full = lax.dynamic_update_index_in_dim(full, shift(v, dz=d), (z - d) % 4, 0)
    v = full.reshape(128, PANEL)
    full = jnp.zeros((4, 128, PANEL), F32)
    full = lax.dynamic_update_index_in_dim(full, v, x, 0)
    for d in (1, 3, 2):
        full = lax.dynamic_update_index_in_dim(full, shift(v, dx=d), (x - d) % 4, 0)
    return full.reshape(PANEL, PANEL)


def cross(v, m):
    pairs = []
    for c, x, k, z, y in everyone():
        kd, qd = (z * 2 + y) ^ m, c * 4 + x
        pairs.append((flat(c, x, k, z, y), flat(kd // 4, kd % 4, k, qd // 2, qd % 2)))
    return lax.ppermute(v, AXES, pairs)


def body(child_blocks, child_panels, child_patterns, child_maps, parent_place, parent_front):
    ch, x, core, z, yh = (lax.axis_index(n).astype(I32) for n in AXES)
    r, c = x * 2 + core, z * 2 + yh
    ids = jnp.stack([ch, r, c, ch * 8 + r, core, z, yh, ch * 4 + x])
    maps, place = child_maps, parent_place
    panel = child_panels[0]
    partner = fetch_partner(panel, x, core, z, yh)
    send, diag = update(
        ids, maps, place, child_patterns, child_blocks[0], panel, partner, parent_front
    )
    own = lax.all_to_all(send, ("child", "x"), split_axis=0, concat_axis=0, tiled=True)
    other = shift(own, dk=1)
    diag = sum_everywhere(diag, x, z)
    inv = inverse_factor(diag)
    send = route(ids, maps, place, own, other)
    recv = lax.all_to_all(send, ("z", "yh"), split_axis=0, concat_axis=0, tiled=True)
    parts = strips(ids, maps, place, own, other, parent_front)
    parts = [parts[0]] + [shift(parts[m], dz=m // 2, dy=m % 2) for m in range(1, 8)]
    strip = merge(parts)
    gr = lax.all_gather(strip, ("z", "yh"))
    gown = jnp.stack([cross(strip, m) for m in range(8)])
    goth = shift(gown, dk=1)
    return final(ids, maps, place, diag, inv, gr, gown, goth, recv, parent_front)


def solution(mesh):
    fine = Mesh(mesh.devices.reshape(SIZES), AXES)
    rows, cols = ("x", "core"), ("z", "yh")
    return jax.shard_map(
        body,
        mesh=fine,
        in_specs=(
            P("child", rows, cols),
            P("child", rows, None),
            P(),
            P(),
            P(),
            P(("child", "x", "core"), cols),
        ),
        out_specs=P(("child", "x", "core"), cols),
        check_vma=False,
    )
```

time: 1060 us -> 525 us (0.50)
  waiting for transfers between devices: 648 us -> 102 us
  Pallas kernels: 0 us -> 192 us
  other arithmetic: 188 us -> 4.38 us
  local copies, waits for them, and re-layouts: 151 us -> 9.1 us
  starting transfers between devices: 15.5 us -> 113 us
  blocking collectives: 0 us -> 94.4 us
  matrix products: 36.7 us -> 0 us
  between operations: 16.8 us -> 0.73 us
    all_to_all x2 -> x1, waiting for transfers between devices: 362 us -> 0.01 us  [body(): lax.all_to_all(send, ('z', 'yh'), split_axis=0, concat_axis=0, tiled=True)]
    psum x2 -> x0, waiting for transfers between devices: 208 us -> none  [the longest x1 143 us: body(): diagonal_block = lax.psum(diagonal_part, ('child', 'row', 'col'))]
    pallas_call x0 -> x6, Pallas kernels: none -> 192 us  [the longest x1 72.3 us: route(): pl.pallas_call(route_kernel, grid_spec=pltpu.PrefetchScalarGridSpec(num_s...]
    another operation x25 -> x4, other arithmetic: 135 us -> 2.88 us  [the longest x2 2.52 us: fetch_partner(): mine = jnp.stack(mine)]
    ppermute x0 -> x41, starting transfers between devices: none -> 107 us  [the longest x26 73.8 us: shift(): return lax.ppermute(v, AXES, pairs)]
    ppermute x0 -> x41, waiting for transfers between devices: none -> 102 us  [the longest x26 89.6 us: shift(): return lax.ppermute(v, AXES, pairs)]
    reduce_scatter x2 -> x0, waiting for transfers between devices: 59.7 us -> none  [sum_by_parts(): lax.psum_scatter(filled_up(lines, lax.axis_size(axis)), axis, scatter_dim...]
    gather x14 -> x0, local copies, waits for them, and re-layouts: 57.4 us -> none  [select_tiles(): selected = jnp.take(source, chosen, axis=axis_pos)]
  transfers between devices with their start and end apart: 8 -> 42, of which waited for: 6 -> 13; matrix products, arithmetic and copies ran while one was open for 15% -> 0% of each run, Pallas kernels for 0% -> 28%
where the time goes in v1:
time: 525 us; the launch traced here: 515 us
  Pallas kernels  192 us (37%)
  starting transfers between devices  113 us (22%)
  waiting for transfers between devices  102 us (19%)
  blocking collectives  94.4 us (18%)
  local copies, waits for them, and re-layouts  9.1 us (2%)
    ppermute x26, waiting for transfers between devices, shift(): return lax.ppermute(v, AXES, pairs)  89.6 us
    ppermute x26, starting transfers between devices, shift(): return lax.ppermute(v, AXES, pairs)  73.8 us
    pallas_call x1, Pallas kernels, route(): pl.pallas_call(route_kernel, grid_spec=pltpu.PrefetchScalarGridSpec(num_s...  72.3 us
    pallas_call x1, Pallas kernels, inverse_factor(): pl.pallas_call(inverse_kernel, out_shape=jax.ShapeDtypeStruct((PANEL, PAN...  60.5 us
    all_to_all x1, blocking collectives, body(): lax.all_to_all(send, ('child', 'x'), split_axis=0, concat_axis=0, tiled=T...  55.3 us
    all_gather x1, blocking collectives, body(): gr = lax.all_gather(strip, ('z', 'yh'))  39.1 us
    pallas_call x1, Pallas kernels, final(): pl.pallas_call(final_kernel, grid_spec=pltpu.PrefetchScalarGridSpec(num_s...  36 us
    ppermute x8, starting transfers between devices, cross(): return lax.ppermute(v, AXES, pairs)  23.5 us
  transfers between devices with their start and end apart: 42, of which 13 were waited for; matrix products, arithmetic and copies ran while one was open for 0% of the time, Pallas kernels for 28%

profile of v1, /device:TPU:1, one launch (start us, length us, event | category | flops | bytes accessed | tf_op | source)
XLA Modules:
  0.0 515.3 jit_solution(13804163205010773773)
XLA Ops:
  0.0 2.4 constant_dynamic-slice_fusion.1
  2.4 1.5 collective-permute-start.6
  3.9 1.5 collective-permute-start.5
  5.5 1.3 collective-permute-start.3
  6.8 1.5 collective-permute-start.4
  8.2 1.5 collective-permute-start.2
  9.7 1.5 collective-permute-start.1
  11.1 1.5 collective-permute-start
  12.7 1.5 fusion.9
  14.1 1.1 pad_maximum_fusion.2
  15.2 25.4 %collective-permute-start.7 = (bf16[2,256,1024]{2,1,0:T(8,128)(2,1)}, bf16[2,256,1024]{2,1,0:T(8,128)(2,1)}, u32[]{:S(2)}, u32[]{:S(2)}) collective-permute-start(bf16[2,256,1024]{2,1,0:T(8,128)(2,1)} %pad_maximum_fusion.2), channel_id=1, source_target_pairs={{0,8},{1,9},{2,10},{3,11},{4,12},{5,13},{6,14},{7,15},{8,0},{9,1},... | collective-permute-start | bytes 3145736 | tf_op jit(solution)/shard_map/ppermute | solution.py:49
  40.7 2.5 collective-permute-done.7
  43.2 1.4 broadcast_select_fusion.1
  45.4 1.7 copy-done.2
  47.0 11.2 %shard_map.64 = (s16[8,272,1024]{2,1,0:T(8,128)(2,1)S(1)}, f32[512,512]{1,0:T(8,128)S(1)}) custom-call(s32[8]{0:T(128)S(1)} %stack.79.ids, s32[2,32]{1,0:T(2,128)S(1)} %copy-done.6, s32[48]{0:T(128)S(1)} %copy-done.10, s32[2,32,32]{2,1,0:T(8,128)S(1)} %copy-done.5, f32[1024,1024]{1,0:T(8,128)S(1)} %bitcast.112, bf16[1024,1024]{1,0:T(8,128)(2,1)S(1)} %bitcast.110, ...), custom_call_target="tpu_custom_call" | custom-call | flops 2147483648 | bytes 14680064 | tf_op jit(solution)/shard_map/pallas_call | solution.py:116
  58.3 55.3 %all_to_all.10.own = s16[8,272,1024]{2,1,0:T(8,128)(2,1)} all-to-all(s16[8,272,1024]{2,1,0:T(8,128)(2,1)S(1)} %get-tuple-element.16), channel_id=1, replica_groups=mesh['child'=2,'x'=4,'core'=2,'z'=4,'yh'=2] {'child','x'}, dimensions={0} | all-to-all | bytes 8912896 | tf_op jit(solution)/shard_map/all_to_all | solution.py:569
  113.6 1.6 collective-permute-start.24
  115.3 0.6 collective-permute-start.8
  115.9 1.4 collective-permute-start.10
  117.3 1.0 collective-permute-start.9
  118.4 11.7 %collective-permute-done.8 = f32[128,512]{1,0:T(8,128)S(1)} collective-permute-done((f32[128,512]{1,0:T(8,128)S(1)}, f32[128,512]{1,0:T(8,128)S(1)}, u32[]{:S(2)}, u32[]{:S(2)}) %collective-permute-start.8) | collective-permute-done | bytes 262176 | tf_op jit(solution)/shard_map/ppermute | solution.py:49
  130.6 2.0 collective-permute-start.13
  132.6 2.0 collective-permute-start.12
  134.6 0.8 collective-permute-done.11
  135.4 0.4 collective-permute-done.13
  135.8 0.7 collective-permute-done.12
  136.5 2.3 collective-permute-start.14
  138.8 0.9 collective-permute-done.14
  139.7 4.0 collective-permute-start.17
  143.7 0.4 collective-permute-start.15
  144.1 72.3 %shard_map.68 = s16[8,6,272,256]{3,2,1,0:T(8,128)(2,1)} custom-call(s32[8]{0:T(128)} %copy-done.8, s32[2,32]{1,0:T(2,128)} %maps.7, s32[48]{0:T(128)} %place.7, s16[8,272,1024]{2,1,0:T(8,128)(2,1)} %all_to_all.10.own, s16[8,272,1024]{2,1,0:T(8,128)(2,1)} %collective-permute-done.24.other), custom_call_target="tpu_custom_call" | custom-call | bytes 8388608 | tf_op jit(solution)/shard_map/pallas_call | solution.py:177
  216.4 5.1 all-to-all-start.1
  221.7 1.5 collective-permute-start.18
  223.2 1.4 collective-permute-start.19
  224.5 1.6 collective-permute-start.20
  226.2 49.4 %collective-permute-done.18 = f32[32,512]{1,0:T(8,128)S(1)} collective-permute-done((f32[32,512]{1,0:T(8,128)S(1)}, f32[32,512]{1,0:T(8,128)S(1)}, u32[]{:S(2)}, u32[]{:S(2)}) %collective-permute-start.18) | collective-permute-done | bytes 65568 | tf_op jit(solution)/shard_map/ppermute | solution.py:49
  275.6 19.9 %collective-permute-done.19 = f32[32,512]{1,0:T(8,128)S(1)} collective-permute-done((f32[32,512]{1,0:T(8,128)S(1)}, f32[32,512]{1,0:T(8,128)S(1)}, u32[]{:S(2)}, u32[]{:S(2)}) %collective-permute-start.19) | collective-permute-done | bytes 65568 | tf_op jit(solution)/shard_map/ppermute | solution.py:49
  295.6 0.7 collective-permute-start.21
  296.3 2.9 collective-permute-start.23
  299.4 2.3 copy-done
  301.7 10.1 %shard_map.66 = (s16[112,512]{1,0:T(8,128)(2,1)S(1)}, s16[112,512]{1,0:T(8,128)(2,1)S(1)}, s16[112,512]{1,0:T(8,128)(2,1)S(1)}, s16[112,512]{1,0:T(8,128)(2,1)S(...) custom-call(s32[8]{0:T(128)S(1)} %copy-done.9, ...), custom_call_target="tpu_custom_call" | custom-call | bytes 4194304 | tf_op jit(solution)/shard_map/pallas_call | solution.py:238
  311.9 0.8 collective-permute-start.26
  312.8 6.7 %collective-permute-start.28 = (s16[112,512]{1,0:T(8,128)(2,1)S(1)}, s16[112,512]{1,0:T(8,128)(2,1)S(1)}, u32[]{:S(2)}, u32[]{:S(2)}) collective-permute-start(s16[112,512]{1,0:T(8,128)(2,1)S(1)} %get-tuple-element.21), channel_id=1, source_target_pairs={{0,4},{1,5},{2,6},{3,7},{4,0},{5,1},{6,2},{7,3},{8,12},{9,13},{10,... | collective-permute-start | bytes 344072 | tf_op jit(solution)/shard_map/ppermute | solution.py:49
  319.6 2.0 collective-permute-start.30
  321.7 3.5 collective-permute-start.31
  325.3 2.9 collective-permute-done.29.refs_5_
  328.2 0.6 copy-done.18
  328.8 2.2 shard_map.67
  331.1 1.5 collective-permute-start.32
  332.7 7.7 %collective-permute-start.39 = (s16[112,512]{1,0:T(8,128)(2,1)}, s16[112,512]{1,0:T(8,128)(2,1)S(1)}, u32[]{:S(2)}, u32[]{:S(2)}) collective-permute-start(s16[112,512]{1,0:T(8,128)(2,1)} %shard_map.67), channel_id=1, source_target_pairs={{0,112},{1,96},{2,80},{3,64},{4,48},{5,32},{6,16},{7,0},{8,120},{9... | collective-permute-start | bytes 344072 | tf_op jit(solution)/shard_map/ppermute | solution.py:556
  340.4 2.2 collective-permute-start.38
  342.5 0.4 collective-permute-start.37
  343.0 0.4 collective-permute-start.36
  343.4 2.9 collective-permute-start.33
  346.3 4.9 collective-permute-done.33
  351.2 4.4 collective-permute-start.34
  355.7 2.8 collective-permute-done.34
  358.4 3.9 collective-permute-start.35
  362.3 4.4 collective-permute-done.35
  366.8 11.7 %collective-permute-start.40 = (s16[8,112,512]{2,1,0:T(8,128)(2,1)S(1)}, s16[8,112,512]{2,1,0:T(8,128)(2,1)}, u32[]{:S(2)}, u32[]{:S(2)}) collective-permute-start(s16[8,112,512]{2,1,0:T(8,128)(2,1)S(1)} %bitcast_dynamic-update-slice_fusion.4.gown), channel_id=1, source_target_pairs={{0,8},{1,9},{2,10},{3,11},{4,12},{5,13},{6,14},{7,15},{8,0},{9,1},... | collective-permute-start | bytes 2752520 | tf_op jit(solution)/shard_map/ppermute | solution.py:49
  378.5 60.5 %shard_map.65.inv = f32[512,512]{1,0:T(8,128)S(1)} custom-call(f32[512,512]{1,0:T(8,128)S(1)} %bitcast.115), custom_call_target="tpu_custom_call" | custom-call | flops 17179869184 | bytes 2097152 | tf_op jit(solution)/shard_map/pallas_call | solution.py:336
  439.0 1.0 copy-done.12
  440.0 39.1 %all-gather = s16[896,512]{1,0:T(8,128)(2,1)S(1)} all-gather(s16[112,512]{1,0:T(8,128)(2,1)S(1)} %copy-done.13), channel_id=2, replica_groups=mesh['child'=2,'x'=4,'core'=2,'z'=4,'yh'=2] {'z','yh'}, dimensions={0}, use_global_device_ids=true | all-gather | bytes 1032192 | tf_op jit(solution)/shard_map/all_gather | solution.py:578
  479.1 36.0 %shard_map.69 = f32[768,1536]{1,0:T(8,128)} custom-call(s32[8]{0:T(128)S(1)} %copy-done.9, s32[2,32]{1,0:T(2,128)S(1)} %copy-done.7, s32[48]{0:T(128)S(1)} %copy-done.11, f32[512,512]{1,0:T(8,128)} %bitcast.116, f32[512,512]{1,0:T(8,128)} %copy-done.12, s16[8,112,512]{2,1,0:T(8,128)(2,1)S(1)} %bitcast.117, ...), custom_call_target="tpu_custom_call" | custom-call | flops 8589934592 | bytes 20971520 | tf_op jit(solution)/shard_map/pallas_call | solution.py:456
  (101 shorter events, 2.2 us)
Async XLA Ops:
  0.0 12.7 %copy-start.1 = (bf16[1,1024,1024]{2,1,0:T(8,128)(2,1)S(1)}, bf16[1,1024,1024]{2,1,0:T(8,128)(2,1)}, u32[]{:S(2)}) copy-start(bf16[1,1024,1024]{2,1,0:T(8,128)(2,1)} %param.7) | copy-start | bytes 6291460
  2.4 7.2 %collective-permute-start.6 = (bf16[256,1024]{1,0:T(8,128)(2,1)}, bf16[256,1024]{1,0:T(8,128)(2,1)}, u32[]{:S(2)}, u32[]{:S(2)}) collective-permute-start(bf16[256,1024]{1,0:T(8,128)(2,1)} %get-tuple-element.33), channel_id=1, source_target_pairs={{4,48},{6,56},{13,49},{15,57},{22,2},{16,10},{31,3},{25,11},{32,20... | collective-permute-start | bytes 1572872 | tf_op jit(solution)/shard_map/ppermute | solution.py:506
  3.9 7.3 %collective-permute-start.5 = (bf16[256,1024]{1,0:T(8,128)(2,1)}, bf16[256,1024]{1,0:T(8,128)(2,1)}, u32[]{:S(2)}, u32[]{:S(2)}) collective-permute-start(bf16[256,1024]{1,0:T(8,128)(2,1)} %get-tuple-element.33), channel_id=1, source_target_pairs={{4,32},{6,40},{13,33},{15,41},{22,50},{16,58},{31,51},{25,59},{32,... | collective-permute-start | bytes 1572872 | tf_op jit(solution)/shard_map/ppermute | solution.py:506
  5.5 7.2 %collective-permute-start.3 = (bf16[2,256,1024]{2,1,0:T(8,128)(2,1)S(1)}, bf16[2,256,1024]{2,1,0:T(8,128)(2,1)}, u32[]{:S(2)}, u32[]{:S(2)}) collective-permute-start(bf16[2,256,1024]{2,1,0:T(8,128)(2,1)S(1)} %pad_maximum_fusion.1), channel_id=1, source_target_pairs={{0,8},{9,1},{18,26},{27,19},{36,44},{45,37},{54,62},{63,55},{64,72... | collective-permute-start | bytes 3145736 | tf_op jit(solution)/shard_map/ppermute | solution.py:515
  6.8 5.9 %collective-permute-start.4 = (bf16[256,1024]{1,0:T(8,128)(2,1)}, bf16[256,1024]{1,0:T(8,128)(2,1)}, u32[]{:S(2)}, u32[]{:S(2)}) collective-permute-start(bf16[256,1024]{1,0:T(8,128)(2,1)} %get-tuple-element.33), channel_id=1, source_target_pairs={{4,16},{6,24},{13,17},{15,25},{22,34},{16,42},{31,35},{25,43},{32,... | collective-permute-start | bytes 1572872 | tf_op jit(solution)/shard_map/ppermute | solution.py:506
  8.2 4.4 collective-permute-start.2
  9.7 2.9 collective-permute-start.1
  11.1 1.5 collective-permute-start
  15.2 28.0 %collective-permute-start.7 = (bf16[2,256,1024]{2,1,0:T(8,128)(2,1)}, bf16[2,256,1024]{2,1,0:T(8,128)(2,1)}, u32[]{:S(2)}, u32[]{:S(2)}) collective-permute-start(bf16[2,256,1024]{2,1,0:T(8,128)(2,1)} %pad_maximum_fusion.2), channel_id=1, source_target_pairs={{0,8},{1,9},{2,10},{3,11},{4,12},{5,13},{6,14},{7,15},{8,0},{9,1},... | collective-permute-start | bytes 3145736 | tf_op jit(solution)/shard_map/ppermute | solution.py:49
  40.7 4.5 copy-start.8
  44.6 0.8 copy-start.5
  44.8 2.2 copy-start.2
  44.9 2.2 copy-start.6
  44.9 2.2 copy-start.10
  113.6 30.4 %collective-permute-start.24 = (s16[8,272,1024]{2,1,0:T(8,128)(2,1)}, s16[8,272,1024]{2,1,0:T(8,128)(2,1)}, u32[]{:S(2)}, u32[]{:S(2)}) collective-permute-start(s16[8,272,1024]{2,1,0:T(8,128)(2,1)} %all_to_all.10.own), channel_id=1, source_target_pairs={{0,8},{1,9},{2,10},{3,11},{4,12},{5,13},{6,14},{7,15},{8,0},{9,1},... | collective-permute-start | bytes 13369352 | tf_op jit(solution)/shard_map/ppermute | solution.py:49
  115.3 14.8 %collective-permute-start.8 = (f32[128,512]{1,0:T(8,128)S(1)}, f32[128,512]{1,0:T(8,128)S(1)}, u32[]{:S(2)}, u32[]{:S(2)}) collective-permute-start(f32[128,512]{1,0:T(8,128)S(1)} %get-tuple-element.34), channel_id=1, source_target_pairs={{0,16},{1,17},{2,18},{3,19},{4,20},{5,21},{6,22},{7,23},{8,24},{9,... | collective-permute-start | bytes 786440 | tf_op jit(solution)/shard_map/ppermute | solution.py:49
  115.9 14.2 %collective-permute-start.10 = (f32[128,512]{1,0:T(8,128)S(1)}, f32[128,512]{1,0:T(8,128)S(1)}, u32[]{:S(2)}, u32[]{:S(2)}) collective-permute-start(f32[128,512]{1,0:T(8,128)S(1)} %get-tuple-element.35), channel_id=1, source_target_pairs={{0,32},{1,33},{2,34},{3,35},{4,36},{5,37},{6,38},{7,39},{8,40},{9,... | collective-permute-start | bytes 786440 | tf_op jit(solution)/shard_map/ppermute | solution.py:49
  117.3 13.1 %collective-permute-start.9 = (f32[128,512]{1,0:T(8,128)S(1)}, f32[128,512]{1,0:T(8,128)S(1)}, u32[]{:S(2)}, u32[]{:S(2)}) collective-permute-start(f32[128,512]{1,0:T(8,128)S(1)} %get-tuple-element.36), channel_id=1, source_target_pairs={{0,48},{1,49},{2,50},{3,51},{4,52},{5,53},{6,54},{7,55},{8,56},{9,... | collective-permute-start | bytes 786440 | tf_op jit(solution)/shard_map/ppermute | solution.py:49
  130.5 4.9 collective-permute-start.11
  130.6 5.2 %collective-permute-start.13 = (f32[32,512]{1,0:T(8,128)S(1)}, f32[32,512]{1,0:T(8,128)S(1)}, u32[]{:S(2)}, u32[]{:S(2)}) collective-permute-start(f32[32,512]{1,0:T(8,128)S(1)} %get-tuple-element.42), channel_id=1, source_target_pairs={{0,4},{1,5},{2,6},{3,7},{4,0},{5,1},{6,2},{7,3},{8,12},{9,13},{10,... | collective-permute-start | bytes 196616 | tf_op jit(solution)/shard_map/ppermute | solution.py:49
  132.6 3.8 collective-permute-start.12
  136.5 3.2 collective-permute-start.14
  139.7 81.8 %collective-permute-start.17 = (f32[32,512]{1,0:T(8,128)S(1)}, f32[32,512]{1,0:T(8,128)S(1)}, u32[]{:S(2)}, u32[]{:S(2)}) collective-permute-start(f32[32,512]{1,0:T(8,128)S(1)} %add.218), channel_id=1, source_target_pairs={{0,1},{1,0},{2,3},{3,2},{4,5},{5,4},{6,7},{7,6},{8,9},{9,8},{10,11... | collective-permute-start | bytes 196616 | tf_op jit(solution)/shard_map/ppermute | solution.py:49
  143.7 77.9 %collective-permute-start.16 = (f32[32,512]{1,0:T(8,128)S(1)}, f32[32,512]{1,0:T(8,128)S(1)}, u32[]{:S(2)}, u32[]{:S(2)}) collective-permute-start(f32[32,512]{1,0:T(8,128)S(1)} %add.218), channel_id=1, source_target_pairs={{0,64},{1,65},{2,66},{3,67},{4,68},{5,69},{6,70},{7,71},{8,72},{9,... | collective-permute-start | bytes 196616 | tf_op jit(solution)/shard_map/ppermute | solution.py:49
  143.7 77.9 %collective-permute-start.15 = (f32[32,512]{1,0:T(8,128)S(1)}, f32[32,512]{1,0:T(8,128)S(1)}, u32[]{:S(2)}, u32[]{:S(2)}) collective-permute-start(f32[32,512]{1,0:T(8,128)S(1)} %add.218), channel_id=1, source_target_pairs={{0,65},{1,64},{2,67},{3,66},{4,69},{5,68},{6,71},{7,70},{8,73},{9,... | collective-permute-start | bytes 196616 | tf_op jit(solution)/shard_map/ppermute | solution.py:49
  216.4 262.6 %all-to-all-start.1 = ((s16[8,6,272,256]{3,2,1,0:T(8,128)(2,1)}), s16[8,6,272,256]{3,2,1,0:T(8,128)(2,1)}, u32[]{:S(2)}, u32[]{:S(2)}) async-start(s16[8,6,272,256]{3,2,1,0:T(8,128)(2,1)} %shard_map.68), calls=%async_computation.1 | async-start | bytes 13369344 | tf_op jit(solution)/shard_map/all_to_all | solution.py:574
  221.6 77.8 %copy-start.7 = (s32[2,32]{1,0:T(2,128)S(1)}, s32[2,32]{1,0:T(2,128)}, u32[]{:S(2)}) copy-start(s32[2,32]{1,0:T(2,128)} %maps.7) | copy-start | bytes 772
  221.6 77.8 %copy-start.9 = (s32[8]{0:T(128)S(1)}, s32[8]{0:T(128)}, u32[]{:S(2)}) copy-start(s32[8]{0:T(128)} %copy-done.8) | copy-start | bytes 100
  221.6 77.8 %copy-start.11 = (s32[48]{0:T(128)S(1)}, s32[48]{0:T(128)}, u32[]{:S(2)}) copy-start(s32[48]{0:T(128)} %place.7) | copy-start | bytes 580
  221.7 53.9 %collective-permute-start.18 = (f32[32,512]{1,0:T(8,128)S(1)}, f32[32,512]{1,0:T(8,128)S(1)}, u32[]{:S(2)}, u32[]{:S(2)}) collective-permute-start(f32[32,512]{1,0:T(8,128)S(1)} %get-tuple-element.26), channel_id=1, source_target_pairs={{0,2},{1,3},{2,4},{3,5},{4,6},{5,7},{6,0},{7,1},{8,10},{9,11},{10,... | collective-permute-start | bytes 196616 | tf_op jit(solution)/shard_map/ppermute | solution.py:49
  223.2 72.3 %collective-permute-start.19 = (f32[32,512]{1,0:T(8,128)S(1)}, f32[32,512]{1,0:T(8,128)S(1)}, u32[]{:S(2)}, u32[]{:S(2)}) collective-permute-start(f32[32,512]{1,0:T(8,128)S(1)} %get-tuple-element.26), channel_id=1, source_target_pairs={{0,6},{1,7},{2,0},{3,1},{4,2},{5,3},{6,4},{7,5},{8,14},{9,15},{10,... | collective-permute-start | bytes 196616 | tf_op jit(solution)/shard_map/ppermute | solution.py:49
  224.5 71.0 %collective-permute-start.20 = (f32[32,512]{1,0:T(8,128)S(1)}, f32[32,512]{1,0:T(8,128)S(1)}, u32[]{:S(2)}, u32[]{:S(2)}) collective-permute-start(f32[32,512]{1,0:T(8,128)S(1)} %get-tuple-element.26), channel_id=1, source_target_pairs={{0,4},{1,5},{2,6},{3,7},{4,0},{5,1},{6,2},{7,3},{8,12},{9,13},{10,... | collective-permute-start | bytes 196616 | tf_op jit(solution)/shard_map/ppermute | solution.py:49
  295.6 17.2 %collective-permute-start.21 = (f32[128,512]{1,0:T(8,128)S(1)}, f32[128,512]{1,0:T(8,128)S(1)}, u32[]{:S(2)}, u32[]{:S(2)}) collective-permute-start(f32[128,512]{1,0:T(8,128)S(1)} %bitcast.120), channel_id=1, source_target_pairs={{0,16},{1,17},{2,18},{3,19},{4,20},{5,21},{6,22},{7,23},{8,24},{9,... | collective-permute-start | bytes 786440 | tf_op jit(solution)/shard_map/ppermute | solution.py:49
  296.3 36.4 %collective-permute-start.23 = (f32[128,512]{1,0:T(8,128)S(1)}, f32[128,512]{1,0:T(8,128)S(1)}, u32[]{:S(2)}, u32[]{:S(2)}) collective-permute-start(f32[128,512]{1,0:T(8,128)S(1)} %bitcast.121), channel_id=1, source_target_pairs={{0,32},{1,33},{2,34},{3,35},{4,36},{5,37},{6,38},{7,39},{8,40},{9,... | collective-permute-start | bytes 786440 | tf_op jit(solution)/shard_map/ppermute | solution.py:49
  299.2 13.6 %collective-permute-start.22 = (f32[128,512]{1,0:T(8,128)S(1)}, f32[128,512]{1,0:T(8,128)S(1)}, u32[]{:S(2)}, u32[]{:S(2)}) collective-permute-start(f32[128,512]{1,0:T(8,128)S(1)} %bitcast.122), channel_id=1, source_target_pairs={{0,48},{1,49},{2,50},{3,51},{4,52},{5,53},{6,54},{7,55},{8,56},{9,... | collective-permute-start | bytes 786440 | tf_op jit(solution)/shard_map/ppermute | solution.py:49
  299.3 2.3 copy-start
  311.8 13.4 %copy-start.4 = (s16[112,512]{1,0:T(8,128)(2,1)}, s16[112,512]{1,0:T(8,128)(2,1)S(1)}, u32[]{:S(2)}) copy-start(s16[112,512]{1,0:T(8,128)(2,1)S(1)} %get-tuple-element.17.refs_0_) | copy-start | bytes 344068
  311.9 7.7 %collective-permute-start.25 = (s16[112,512]{1,0:T(8,128)(2,1)S(1)}, s16[112,512]{1,0:T(8,128)(2,1)S(1)}, u32[]{:S(2)}, u32[]{:S(2)}) collective-permute-start(s16[112,512]{1,0:T(8,128)(2,1)S(1)} %get-tuple-element.18), channel_id=1, source_target_pairs={{0,1},{1,0},{2,3},{3,2},{4,5},{5,4},{6,7},{7,6},{8,9},{9,8},{10,11... | collective-permute-start | bytes 344072 | tf_op jit(solution)/shard_map/ppermute | solution.py:49
  311.9 7.7 %collective-permute-start.26 = (s16[112,512]{1,0:T(8,128)(2,1)S(1)}, s16[112,512]{1,0:T(8,128)(2,1)S(1)}, u32[]{:S(2)}, u32[]{:S(2)}) collective-permute-start(s16[112,512]{1,0:T(8,128)(2,1)S(1)} %get-tuple-element.19), channel_id=1, source_target_pairs={{0,2},{1,3},{2,4},{3,5},{4,6},{5,7},{6,0},{7,1},{8,10},{9,11},{10,... | collective-permute-start | bytes 344072 | tf_op jit(solution)/shard_map/ppermute | solution.py:49
  312.8 8.9 %collective-permute-start.27 = (s16[112,512]{1,0:T(8,128)(2,1)S(1)}, s16[112,512]{1,0:T(8,128)(2,1)S(1)}, u32[]{:S(2)}, u32[]{:S(2)}) collective-permute-start(s16[112,512]{1,0:T(8,128)(2,1)S(1)} %get-tuple-element.20), channel_id=1, source_target_pairs={{0,3},{1,2},{2,5},{3,4},{4,7},{5,6},{6,1},{7,0},{8,11},{9,10},{10,... | collective-permute-start | bytes 344072 | tf_op jit(solution)/shard_map/ppermute | solution.py:49
  312.8 12.4 %collective-permute-start.28 = (s16[112,512]{1,0:T(8,128)(2,1)S(1)}, s16[112,512]{1,0:T(8,128)(2,1)S(1)}, u32[]{:S(2)}, u32[]{:S(2)}) collective-permute-start(s16[112,512]{1,0:T(8,128)(2,1)S(1)} %get-tuple-element.21), channel_id=1, source_target_pairs={{0,4},{1,5},{2,6},{3,7},{4,0},{5,1},{6,2},{7,3},{8,12},{9,13},{10,... | collective-permute-start | bytes 344072 | tf_op jit(solution)/shard_map/ppermute | solution.py:49
  319.5 8.6 %copy-start.14 = (s16[112,512]{1,0:T(8,128)(2,1)}, s16[112,512]{1,0:T(8,128)(2,1)S(1)}, u32[]{:S(2)}) copy-start(s16[112,512]{1,0:T(8,128)(2,1)S(1)} %collective-permute-done.25.refs_1_) | copy-start | bytes 344068
  319.5 8.6 %collective-permute-start.29 = (s16[112,512]{1,0:T(8,128)(2,1)S(1)}, s16[112,512]{1,0:T(8,128)(2,1)S(1)}, u32[]{:S(2)}, u32[]{:S(2)}) collective-permute-start(s16[112,512]{1,0:T(8,128)(2,1)S(1)} %get-tuple-element.22), channel_id=1, source_target_pairs={{0,5},{1,4},{2,7},{3,6},{4,1},{5,0},{6,3},{7,2},{8,13},{9,12},{10,... | collective-permute-start | bytes 344072 | tf_op jit(solution)/shard_map/ppermute | solution.py:49
  319.6 8.5 %copy-start.15 = (s16[112,512]{1,0:T(8,128)(2,1)}, s16[112,512]{1,0:T(8,128)(2,1)S(1)}, u32[]{:S(2)}) copy-start(s16[112,512]{1,0:T(8,128)(2,1)S(1)} %collective-permute-done.26.refs_2_) | copy-start | bytes 344068
  319.6 8.5 %collective-permute-start.30 = (s16[112,512]{1,0:T(8,128)(2,1)S(1)}, s16[112,512]{1,0:T(8,128)(2,1)S(1)}, u32[]{:S(2)}, u32[]{:S(2)}) collective-permute-start(s16[112,512]{1,0:T(8,128)(2,1)S(1)} %get-tuple-element.23), channel_id=1, source_target_pairs={{0,6},{1,7},{2,0},{3,1},{4,2},{5,3},{6,4},{7,5},{8,14},{9,15},{10,... | collective-permute-start | bytes 344072 | tf_op jit(solution)/shard_map/ppermute | solution.py:49
  321.7 6.4 %copy-start.16 = (s16[112,512]{1,0:T(8,128)(2,1)}, s16[112,512]{1,0:T(8,128)(2,1)S(1)}, u32[]{:S(2)}) copy-start(s16[112,512]{1,0:T(8,128)(2,1)S(1)} %collective-permute-done.27.refs_3_) | copy-start | bytes 344068
  321.7 6.4 %collective-permute-start.31 = (s16[112,512]{1,0:T(8,128)(2,1)S(1)}, s16[112,512]{1,0:T(8,128)(2,1)S(1)}, u32[]{:S(2)}, u32[]{:S(2)}) collective-permute-start(s16[112,512]{1,0:T(8,128)(2,1)S(1)} %get-tuple-element.24), channel_id=1, source_target_pairs={{0,7},{1,6},{2,1},{3,0},{4,3},{5,2},{6,5},{7,4},{8,15},{9,14},{10,... | collective-permute-start | bytes 344072 | tf_op jit(solution)/shard_map/ppermute | solution.py:49
  325.2 2.9 copy-start.17
  328.1 0.7 copy-start.18
  328.1 0.7 copy-start.19
  328.1 0.7 copy-start.20
  331.1 12.3 %collective-permute-start.32 = (s16[112,512]{1,0:T(8,128)(2,1)}, s16[112,512]{1,0:T(8,128)(2,1)S(1)}, u32[]{:S(2)}, u32[]{:S(2)}) collective-permute-start(s16[112,512]{1,0:T(8,128)(2,1)} %shard_map.67), channel_id=1, source_target_pairs={{0,0},{1,16},{2,32},{3,48},{4,64},{5,80},{6,96},{7,112},{8,8},{9,2... | collective-permute-start | bytes 344072 | tf_op jit(solution)/shard_map/ppermute | solution.py:556
  332.7 106.3 %copy-start.3 = (f32[4,128,512]{2,1,0:T(8,128)}, f32[4,128,512]{2,1,0:T(8,128)S(1)}, u32[]{:S(2)}) copy-start(f32[4,128,512]{2,1,0:T(8,128)S(1)} %bitcast_dynamic-update-slice_fusion) | copy-start | bytes 3145732
  332.7 34.1 %collective-permute-start.39 = (s16[112,512]{1,0:T(8,128)(2,1)}, s16[112,512]{1,0:T(8,128)(2,1)S(1)}, u32[]{:S(2)}, u32[]{:S(2)}) collective-permute-start(s16[112,512]{1,0:T(8,128)(2,1)} %shard_map.67), channel_id=1, source_target_pairs={{0,112},{1,96},{2,80},{3,64},{4,48},{5,32},{6,16},{7,0},{8,120},{9... | collective-permute-start | bytes 344072 | tf_op jit(solution)/shard_map/ppermute | solution.py:556
  340.4 26.4 %collective-permute-start.38 = (s16[112,512]{1,0:T(8,128)(2,1)}, s16[112,512]{1,0:T(8,128)(2,1)S(1)}, u32[]{:S(2)}, u32[]{:S(2)}) collective-permute-start(s16[112,512]{1,0:T(8,128)(2,1)} %shard_map.67), channel_id=1, source_target_pairs={{0,96},{1,112},{2,64},{3,80},{4,32},{5,48},{6,0},{7,16},{8,104},{9... | collective-permute-start | bytes 344072 | tf_op jit(solution)/shard_map/ppermute | solution.py:556
  342.5 24.2 %collective-permute-start.37 = (s16[112,512]{1,0:T(8,128)(2,1)}, s16[112,512]{1,0:T(8,128)(2,1)S(1)}, u32[]{:S(2)}, u32[]{:S(2)}) collective-permute-start(s16[112,512]{1,0:T(8,128)(2,1)} %shard_map.67), channel_id=1, source_target_pairs={{0,80},{1,64},{2,112},{3,96},{4,16},{5,0},{6,48},{7,32},{8,88},{9,... | collective-permute-start | bytes 344072 | tf_op jit(solution)/shard_map/ppermute | solution.py:556
  343.0 23.7 %collective-permute-start.36 = (s16[112,512]{1,0:T(8,128)(2,1)}, s16[112,512]{1,0:T(8,128)(2,1)S(1)}, u32[]{:S(2)}, u32[]{:S(2)}) collective-permute-start(s16[112,512]{1,0:T(8,128)(2,1)} %shard_map.67), channel_id=1, source_target_pairs={{0,64},{1,80},{2,96},{3,112},{4,0},{5,16},{6,32},{7,48},{8,72},{9,... | collective-permute-start | bytes 344072 | tf_op jit(solution)/shard_map/ppermute | solution.py:556
  343.4 7.8 %collective-permute-start.33 = (s16[112,512]{1,0:T(8,128)(2,1)}, s16[112,512]{1,0:T(8,128)(2,1)S(1)}, u32[]{:S(2)}, u32[]{:S(2)}) collective-permute-start(s16[112,512]{1,0:T(8,128)(2,1)} %shard_map.67), channel_id=1, source_target_pairs={{0,16},{1,0},{2,48},{3,32},{4,80},{5,64},{6,112},{7,96},{8,24},{9,... | collective-permute-start | bytes 344072 | tf_op jit(solution)/shard_map/ppermute | solution.py:556
  351.2 7.2 %collective-permute-start.34 = (s16[112,512]{1,0:T(8,128)(2,1)}, s16[112,512]{1,0:T(8,128)(2,1)S(1)}, u32[]{:S(2)}, u32[]{:S(2)}) collective-permute-start(s16[112,512]{1,0:T(8,128)(2,1)} %shard_map.67), channel_id=1, source_target_pairs={{0,32},{1,48},{2,0},{3,16},{4,96},{5,112},{6,64},{7,80},{8,40},{9,... | collective-permute-start | bytes 344072 | tf_op jit(solution)/shard_map/ppermute | solution.py:556
  358.4 8.3 %collective-permute-start.35 = (s16[112,512]{1,0:T(8,128)(2,1)}, s16[112,512]{1,0:T(8,128)(2,1)S(1)}, u32[]{:S(2)}, u32[]{:S(2)}) collective-permute-start(s16[112,512]{1,0:T(8,128)(2,1)} %shard_map.67), channel_id=1, source_target_pairs={{0,48},{1,32},{2,16},{3,0},{4,112},{5,96},{6,80},{7,64},{8,56},{9,... | collective-permute-start | bytes 344072 | tf_op jit(solution)/shard_map/ppermute | solution.py:556
  366.8 112.3 %collective-permute-start.40 = (s16[8,112,512]{2,1,0:T(8,128)(2,1)S(1)}, s16[8,112,512]{2,1,0:T(8,128)(2,1)}, u32[]{:S(2)}, u32[]{:S(2)}) collective-permute-start(s16[8,112,512]{2,1,0:T(8,128)(2,1)S(1)} %bitcast_dynamic-update-slice_fusion.4.gown), channel_id=1, source_target_pairs={{0,8},{1,9},{2,10},{3,11},{4,12},{5,13},{6,14},{7,15},{8,0},{9,1},... | collective-permute-start | bytes 2752520 | tf_op jit(solution)/shard_map/ppermute | solution.py:49
  378.5 61.5 %copy-start.13 = (s16[112,512]{1,0:T(8,128)(2,1)S(1)}, s16[112,512]{1,0:T(8,128)(2,1)}, u32[]{:S(2)}) copy-start(s16[112,512]{1,0:T(8,128)(2,1)} %shard_map.67) | copy-start | bytes 344068
  439.0 1.0 copy-start.12

commit v2 on v1

--- a/solution.py
+++ b/solution.py
@@ -180,10 +180,11 @@
             num_scalar_prefetch=3,
             grid=(1,),
             in_specs=[pl.BlockSpec(memory_space=pl.ANY)] * 2,
-            out_specs=pl.BlockSpec(memory_space=pl.ANY),
+            out_specs=pl.BlockSpec((8, 2 * RT, TILE + CODE, TILE), lambda i, *s: (0, 0, 0, 0)),
             scratch_shapes=[pltpu.SemaphoreType.DMA((24,))],
         ),
         out_shape=jax.ShapeDtypeStruct((8, 2 * RT, TILE + CODE, TILE), I16),
+        compiler_params=pltpu.CompilerParams(vmem_limit_bytes=32 * MIB),
         cost_estimate=pl.CostEstimate(flops=0, bytes_accessed=8 * MIB, transcendentals=0),
     )(ids, maps, place, own, other)
 
@@ -291,6 +292,7 @@
 
 
 NB = 128
+WAYS = 4
 
 
 def inverse_kernel(a_ref, out, w, f):
@@ -310,15 +312,42 @@
         w[:, :NB] = f[blk(k), blk(k)]
         w[:, NB:] = jnp.where(eye, 1.0, 0.0).astype(F32)
 
-        def step(j, _):
-            line = w[pl.ds(j, 1), :]
-            pivot = jnp.sum(jnp.where(lanes == j, line, 0.0), axis=1, keepdims=True)
-            column = jnp.sum(jnp.where(col == j, w[:, :NB], 0.0), axis=1, keepdims=True)
-            factor = jnp.where(sub > j, column / pivot, 0.0)
-            w[...] = w[...] - factor * line
+        def step(n4, _):
+            j = n4 * WAYS
+            lines = [w[pl.ds(j + a, 1), :] for a in range(WAYS)]
+            square = w[:, :NB]
+            columns = [
+                jnp.sum(jnp.where(col == j + a, square, 0.0), axis=1, keepdims=True)
+                for a in range(WAYS)
+            ]
+            small = [
+                [
+                    jnp.sum(jnp.where(lanes == j + b, lines[a], 0.0), axis=1, keepdims=True)
+                    if b >= a
+                    else None
+                    for b in range(WAYS)
+                ]
+                for a in range(WAYS)
+            ]
+            factors = []
+            for a in range(WAYS):
+                inverse = 1.0 / small[a][a]
+                for b in range(a + 1, WAYS):
+                    times = small[a][b] * inverse
+                    for d in range(b, WAYS):
+                        small[b][d] = small[b][d] - times * small[a][d]
+                    lines[b] = lines[b] - times * lines[a]
+                    columns[b] = columns[b] - times * columns[a]
+                factors.append(jnp.where(sub >= j + WAYS, columns[a] * inverse, 0.0))
+            total = w[...]
+            for a in range(WAYS):
+                total = total - factors[a] * lines[a]
+            w[...] = total
+            for a in range(1, WAYS):
+                w[pl.ds(j + a, 1), :] = lines[a]
             return 0
 
-        lax.fori_loop(0, NB, step, 0)
+        lax.fori_loop(0, NB // WAYS, step, 0)
         d = jnp.sum(jnp.where(eye, w[:, :NB], 0.0), axis=1, keepdims=True)
         inv = w[:, NB:] * (1.0 / jnp.sqrt(d))
         out[blk(k), blk(k)] = inv
@@ -354,59 +383,76 @@
     return one(a[0], b[0]) + (one(a[0], b[1]) + one(a[1], b[0]))
 
 
-def final_kernel(
-    ids, maps, place, diag, inv, gr, gown, goth, recv, front, out,
-    gbuf, ph, plo, rows_f, tiles, inv_h, inv_l, tsem,
-):
+def panel_kernel(ids, maps, place, diag, inv, gr, gown, goth, ph, plo, rows_f, gbuf):
+    c, g, core, k, z, yh = ids[2], ids[3], ids[4], ids[7], ids[5], ids[6]
+    e = (place[0], place[1])
+    inv2 = split(inv[...])
+
+    def fill(base, ref, order, first):
+        for s in range(8):
+            v = decode_strip(ref, (order(s),))
+            for t in range(RT):
+                gbuf[base + t * TILE + s * STRIP : base + t * TILE + (s + 1) * STRIP, :] = v[
+                    t * STRIP : (t + 1) * STRIP, :
+                ]
+        for t in range(RT):
+            for a in range(2):
+
+                @pl.when(first + t == e[a])
+                def _():
+                    gbuf[base + t * TILE : base + (t + 1) * TILE, :] = diag[
+                        a * TILE : (a + 1) * TILE, :
+                    ]
+
+    fill(
+        0, gr, lambda s: lax.rem((yh + s) % 2, 2) * 4 + lax.rem(z - s // 2 + 4, 4), g * RT
+    )
+    for b in range(2):
+        base = RT * TILE * (1 + b)
+
+        @pl.when(core == b)
+        def _():
+            fill(base, gown, lambda s: k ^ s, c * QT + b * RT)
+
+        @pl.when(core != b)
+        def _():
+            fill(base, goth, lambda s: k ^ s, c * QT + b * RT)
+
+    for t in range(9):
+        rows = slice(t * TILE, (t + 1) * TILE)
+        v = dot3(split(gbuf[rows, :]), inv2)
+        hi, lo = split(v)
+        ph[rows, :] = hi
+        plo[rows, :] = lo
+        if t < RT:
+            rows_f[rows, :] = v
+
+
+def panel_rows(ids, maps, place, diag, inv, gr, gown, goth):
+    def whole(*shape):
+        return pl.BlockSpec(shape, lambda i, *s: (0,) * len(shape))
+
+    return pl.pallas_call(
+        panel_kernel,
+        grid_spec=pltpu.PrefetchScalarGridSpec(
+            num_scalar_prefetch=3,
+            grid=(1,),
+            in_specs=[whole(PANEL, PANEL)] * 2 + [whole(8, SROWS, PANEL)] * 3,
+            out_specs=[whole(9 * TILE, PANEL)] * 2 + [whole(RT * TILE, PANEL)],
+            scratch_shapes=[pltpu.VMEM((9 * TILE, PANEL), F32)],
+        ),
+        out_shape=[jax.ShapeDtypeStruct((9 * TILE, PANEL), BF16)] * 2
+        + [jax.ShapeDtypeStruct((RT * TILE, PANEL), F32)],
+        compiler_params=pltpu.CompilerParams(vmem_limit_bytes=52 * MIB),
+        cost_estimate=pl.CostEstimate(flops=1 << 33, bytes_accessed=16 * MIB, transcendentals=0),
+    )(ids, maps, place, diag, inv, gr, gown, goth)
+
+
+def final_kernel(ids, maps, place, ph, plo, rows_f, recv, front, out, tiles, tsem):
     p = pl.program_id(0)
-    c, g, core, k = ids[2], ids[3], ids[4], ids[7]
+    c, g = ids[2], ids[3]
     e = (place[0], place[1])
-
-    @pl.when(p == 0)
-    def _():
-        hi, lo = split(inv[...])
-        inv_h[...] = hi
-        inv_l[...] = lo
-
-        def fill(base, ref, order, first):
-            for s in range(8):
-                v = decode_strip(ref, (order(s),))
-                for t in range(RT):
-                    gbuf[base + t * TILE + s * STRIP : base + t * TILE + (s + 1) * STRIP, :] = v[
-                        t * STRIP : (t + 1) * STRIP, :
-                    ]
-            for t in range(RT):
-                for a in range(2):
-
-                    @pl.when(first + t == e[a])
-                    def _():
-                        gbuf[base + t * TILE : base + (t + 1) * TILE, :] = diag[
-                            a * TILE : (a + 1) * TILE, :
-                        ]
-
-        fill(0, gr, lambda s: s, g * RT)
-        for b in range(2):
-            base = RT * TILE * (1 + b)
-
-            @pl.when(core == b)
-            def _():
-                fill(base, gown, lambda s: k ^ s, c * QT + b * RT)
-
-            @pl.when(core != b)
-            def _():
-                fill(base, goth, lambda s: k ^ s, c * QT + b * RT)
-
-        for t in range(9):
-            rows = slice(t * TILE, (t + 1) * TILE)
-            v = dot3(split(gbuf[rows, :]), (inv_h[...], inv_l[...]))
-            hi, lo = split(v)
-            ph[rows, :] = hi
-            plo[rows, :] = lo
-            if t < RT:
-                rows_f[rows, :] = v
-
     pr = pl.ds(pl.multiple_of(p * TILE, TILE), TILE)
-    left = (ph[pr, :], plo[pr, :])
     srow = g * RT + p
     there = [find(maps, place, ch, srow) >= 0 for ch in range(2)]
     js = [[find(maps, place, ch, c * QT + t) for t in range(QT)] for ch in range(2)]
@@ -426,6 +472,7 @@
                     )
 
     each(lambda copy: copy.start())
+    left = (ph[pr, :], plo[pr, :])
     for t in range(QT):
         cols = slice(t * TILE, (t + 1) * TILE)
         right = slice((RT + t) * TILE, (RT + t + 1) * TILE)
@@ -445,10 +492,10 @@
 
             @pl.when(c * QT + t == e[a])
             def _():
-                out[:, cols] = rows_f[pr, a * TILE : (a + 1) * TILE]
-
-
-def final(ids, maps, place, diag, inv, gr, gown, goth, recv, front):
+                out[:, cols] = rows_f[:, a * TILE : (a + 1) * TILE]
+
+
+def final(ids, maps, place, ph, plo, rows_f, recv, front):
     def whole(*shape):
         return pl.BlockSpec(shape, lambda i, *s: (0,) * len(shape))
 
@@ -459,30 +506,22 @@
             num_scalar_prefetch=3,
             grid=(RT,),
             in_specs=[
-                whole(PANEL, PANEL),
-                whole(PANEL, PANEL),
-                whole(8, SROWS, PANEL),
-                whole(8, SROWS, PANEL),
-                whole(8, SROWS, PANEL),
+                whole(9 * TILE, PANEL),
+                whole(9 * TILE, PANEL),
+                pl.BlockSpec((TILE, PANEL), lambda i, *s: (i, 0)),
                 pl.BlockSpec(memory_space=pl.ANY),
                 line,
             ],
             out_specs=line,
             scratch_shapes=[
-                pltpu.VMEM((9 * TILE, PANEL), F32),
-                pltpu.VMEM((9 * TILE, PANEL), BF16),
-                pltpu.VMEM((9 * TILE, PANEL), BF16),
-                pltpu.VMEM((RT * TILE, PANEL), F32),
                 pltpu.VMEM((2 * QT, TILE + CODE, TILE), I16),
-                pltpu.VMEM((PANEL, PANEL), BF16),
-                pltpu.VMEM((PANEL, PANEL), BF16),
                 pltpu.SemaphoreType.DMA((2 * QT,)),
             ],
         ),
         out_shape=jax.ShapeDtypeStruct((RT * TILE, QT * TILE), F32),
         compiler_params=pltpu.CompilerParams(vmem_limit_bytes=52 * MIB),
-        cost_estimate=pl.CostEstimate(flops=1 << 33, bytes_accessed=20 * MIB, transcendentals=0),
-    )(ids, maps, place, diag, inv, gr, gown, goth, recv, front)
+        cost_estimate=pl.CostEstimate(flops=1 << 32, bytes_accessed=20 * MIB, transcendentals=0),
+    )(ids, maps, place, ph, plo, rows_f, recv, front)
 
 
 def pick(v, at):
@@ -567,18 +606,20 @@
         ids, maps, place, child_patterns, child_blocks[0], panel, partner, parent_front
     )
     own = lax.all_to_all(send, ("child", "x"), split_axis=0, concat_axis=0, tiled=True)
+    diag = sum_everywhere(diag, x, z)
+    own, diag = lax.optimization_barrier((own, diag))
     other = shift(own, dk=1)
-    diag = sum_everywhere(diag, x, z)
-    inv = inverse_factor(diag)
     send = route(ids, maps, place, own, other)
     recv = lax.all_to_all(send, ("z", "yh"), split_axis=0, concat_axis=0, tiled=True)
     parts = strips(ids, maps, place, own, other, parent_front)
     parts = [parts[0]] + [shift(parts[m], dz=m // 2, dy=m % 2) for m in range(1, 8)]
+    inv = inverse_factor(diag)
     strip = merge(parts)
-    gr = lax.all_gather(strip, ("z", "yh"))
-    gown = jnp.stack([cross(strip, m) for m in range(8)])
-    goth = shift(gown, dk=1)
-    return final(ids, maps, place, diag, inv, gr, gown, goth, recv, parent_front)
+    crossed = jnp.stack([cross(strip, m) for m in range(8)])
+    line = jnp.stack([strip] + [shift(strip, dz=d) for d in range(1, 4)])
+    gr = jnp.concatenate([line, shift(line, dy=1)])
+    ph, plo, rows_f = panel_rows(ids, maps, place, diag, inv, gr, crossed, shift(crossed, dk=1))
+    return final(ids, maps, place, ph, plo, rows_f, recv, parent_front)
 
 
 def solution(mesh):

time: 525 us -> 442 us (0.84)
  Pallas kernels: 192 us -> 89.3 us
  blocking collectives: 94.4 us -> 0 us
  waiting for transfers between devices: 102 us -> 178 us
  starting transfers between devices: 113 us -> 142 us
  local copies, waits for them, and re-layouts: 9.1 us -> 20.8 us
    ppermute x26 -> x30, waiting for transfers between devices: 89.6 us -> 170 us  [shift(): return lax.ppermute(v, AXES, pairs)]
    pallas_call x1, Pallas kernels: 72.3 us -> 4.45 us  [route(): pl.pallas_call(route_kernel, grid_spec=pltpu.PrefetchScalarGridSpec(num_s...]
    all_to_all x1 -> x0, blocking collectives: 55.3 us -> none  [body(): lax.all_to_all(send, ('child', 'x'), split_axis=0, concat_axis=0, tiled=T...]
    all_gather x1 -> x0, blocking collectives: 39.1 us -> none  [body(): gr = lax.all_gather(strip, ('z', 'yh'))]
    pallas_call x1, Pallas kernels: 60.5 us -> 29.7 us  [inverse_factor(): pl.pallas_call(inverse_kernel, out_shape=jax.ShapeDtypeStruct((PANEL, PAN...]
    ppermute x26 -> x30, starting transfers between devices: 73.8 us -> 86.9 us  [shift(): return lax.ppermute(v, AXES, pairs)]
    unnamed x49 -> x57, local copies, waits for them, and re-layouts: 6 us -> 17.7 us
    ppermute x8, starting transfers between devices: 23.5 us -> 34.9 us  [cross(): return lax.ppermute(v, AXES, pairs)]
  transfers between devices with their start and end apart: 42 -> 47, of which waited for: 13 -> 20; matrix products, arithmetic and copies ran while one was open for 0% -> 0% of each run, Pallas kernels for 28% -> 10%
where the time goes in v2:
time: 442 us; the launch traced here: 436 us
  waiting for transfers between devices  178 us (40%)
  starting transfers between devices  142 us (32%)
  Pallas kernels  89.3 us (20%)
  local copies, waits for them, and re-layouts  20.8 us (5%)
  other arithmetic  4.61 us (1%)
    ppermute x30, waiting for transfers between devices, shift(): return lax.ppermute(v, AXES, pairs)  170 us
    ppermute x30, starting transfers between devices, shift(): return lax.ppermute(v, AXES, pairs)  86.9 us
    ppermute x8, starting transfers between devices, cross(): return lax.ppermute(v, AXES, pairs)  34.9 us
    pallas_call x1, Pallas kernels, final(): pl.pallas_call(final_kernel, grid_spec=pltpu.PrefetchScalarGridSpec(num_s...  29.8 us
    pallas_call x1, Pallas kernels, inverse_factor(): pl.pallas_call(inverse_kernel, out_shape=jax.ShapeDtypeStruct((PANEL, PAN...  29.7 us
    unnamed x57, local copies, waits for them, and re-layouts  17.7 us
    pallas_call x1, Pallas kernels, update(): pl.pallas_call(update_kernel, grid_spec=pltpu.PrefetchScalarGridSpec(num_...  10.3 us
    pallas_call x1, Pallas kernels, panel_rows(): pl.pallas_call(panel_kernel, grid_spec=pltpu.PrefetchScalarGridSpec(num_s...  9.82 us
  transfers between devices with their start and end apart: 47, of which 20 were waited for; matrix products, arithmetic and copies ran while one was open for 0% of the time, Pallas kernels for 10%

profile of v2, /device:TPU:1, one launch (start us, length us, event | category | flops | bytes accessed | tf_op | source)
XLA Modules:
  0.0 435.7 jit_solution(1349726913427226452)
XLA Ops:
  0.0 2.4 constant_dynamic-slice_fusion.1
  2.4 1.5 collective-permute-start.6
  3.9 1.5 collective-permute-start.5
  5.5 1.3 collective-permute-start.3
  6.8 1.5 collective-permute-start.4
  8.2 1.4 collective-permute-start.2
  9.7 1.5 collective-permute-start.1
  11.2 1.5 collective-permute-start
  12.7 1.5 fusion.9
  15.3 25.4 %collective-permute-start.7 = (bf16[2,256,1024]{2,1,0:T(8,128)(2,1)}, bf16[2,256,1024]{2,1,0:T(8,128)(2,1)}, u32[]{:S(2)}, u32[]{:S(2)}) collective-permute-start(bf16[2,256,1024]{2,1,0:T(8,128)(2,1)} %pad_maximum_fusion.2), channel_id=1, source_target_pairs={{0,8},{1,9},{2,10},{3,11},{4,12},{5,13},{6,14},{7,15},{8,0},{9,1},... | collective-permute-start | bytes 3145736 | tf_op jit(solution)/shard_map/ppermute | solution.py:49
  40.7 2.5 collective-permute-done.7
  43.3 1.5 broadcast_select_fusion.1
  45.5 1.7 copy-done.6
  47.2 10.3 %shard_map.64 = (s16[8,272,1024]{2,1,0:T(8,128)(2,1)S(1)}, f32[512,512]{1,0:T(8,128)S(1)}) custom-call(s32[8]{0:T(128)S(1)} %stack.94.ids, s32[2,32]{1,0:T(2,128)S(1)} %copy-done.11, s32[48]{0:T(128)S(1)} %copy-done.12, s32[2,32,32]{2,1,0:T(8,128)S(1)} %copy-done.10, f32[1024,1024]{1,0:T(8,128)S(1)} %bitcast.119, bf16[1024,1024]{1,0:T(8,128)(2,1)S(1)} %bitcast.117, ...), custom_call_target="tpu_custom_call" | custom-call | flops 2147483648 | bytes 14680064 | tf_op jit(solution)/shard_map/pallas_call | solution.py:116
  57.5 2.1 copy-done.5
  59.6 4.8 %all-to-all-start = ((s16[8,272,1024]{2,1,0:T(8,128)(2,1)}), s16[8,272,1024]{2,1,0:T(8,128)(2,1)}, u32[]{:S(2)}, u32[]{:S(2)}) async-start(s16[8,272,1024]{2,1,0:T(8,128)(2,1)} %copy-done.5), calls=%async_computation | async-start | bytes 8912896 | tf_op jit(solution)/shard_map/all_to_all | solution.py:608
  64.5 2.4 collective-permute-start.8
  66.9 1.5 collective-permute-start.10
  69.6 51.9 %collective-permute-done.8 = f32[128,512]{1,0:T(8,128)S(1)} collective-permute-done((f32[128,512]{1,0:T(8,128)S(1)}, f32[128,512]{1,0:T(8,128)S(1)}, u32[]{:S(2)}, u32[]{:S(2)}) %collective-permute-start.8) | collective-permute-done | bytes 262176 | tf_op jit(solution)/shard_map/ppermute | solution.py:49
  121.5 12.7 %collective-permute-done.10 = f32[128,512]{1,0:T(8,128)S(1)} collective-permute-done((f32[128,512]{1,0:T(8,128)S(1)}, f32[128,512]{1,0:T(8,128)S(1)}, u32[]{:S(2)}, u32[]{:S(2)}) %collective-permute-start.10) | collective-permute-done | bytes 262176 | tf_op jit(solution)/shard_map/ppermute | solution.py:49
  134.2 7.4 %collective-permute-done.9 = f32[128,512]{1,0:T(8,128)S(1)} collective-permute-done((f32[128,512]{1,0:T(8,128)S(1)}, f32[128,512]{1,0:T(8,128)S(1)}, u32[]{:S(2)}, u32[]{:S(2)}) %collective-permute-start.9) | collective-permute-done | bytes 262176 | tf_op jit(solution)/shard_map/ppermute | solution.py:49
  141.8 2.5 collective-permute-start.13
  145.2 1.6 collective-permute-done.11
  147.8 2.7 collective-permute-start.14
  151.4 5.0 %collective-permute-start.17 = (f32[32,512]{1,0:T(8,128)S(1)}, f32[32,512]{1,0:T(8,128)S(1)}, u32[]{:S(2)}, u32[]{:S(2)}) collective-permute-start(f32[32,512]{1,0:T(8,128)S(1)} %add.218), channel_id=1, source_target_pairs={{0,1},{1,0},{2,3},{3,2},{4,5},{5,4},{6,7},{7,6},{8,9},{9,8},{10,11... | collective-permute-start | bytes 196616 | tf_op jit(solution)/shard_map/ppermute | solution.py:49
  157.0 1.6 collective-permute-done.17
  158.6 1.9 collective-permute-done.16
  161.5 2.6 collective-permute-start.19
  164.1 1.6 collective-permute-done.18
  166.0 2.8 collective-permute-done.20
  169.1 2.5 collective-permute-start.22
  171.8 10.0 %collective-permute-done.21 = f32[128,512]{1,0:T(8,128)S(1)} collective-permute-done((f32[128,512]{1,0:T(8,128)S(1)}, f32[128,512]{1,0:T(8,128)S(1)}, u32[]{:S(2)}, u32[]{:S(2)}) %collective-permute-start.21) | collective-permute-done | bytes 262176 | tf_op jit(solution)/shard_map/ppermute | solution.py:49
  181.9 3.4 collective-permute-start.24
  185.3 7.4 %collective-permute-done.24.other = s16[8,272,1024]{2,1,0:T(8,128)(2,1)S(1)} collective-permute-done((s16[8,272,1024]{2,1,0:T(8,128)(2,1)}, s16[8,272,1024]{2,1,0:T(8,128)(2,1)S(1)}, u32[]{:S(2)}, u32[]{:S(2)}) %collective-permute-start.24) | collective-permute-done | bytes 4456480 | tf_op jit(solution)/shard_map/ppermute | solution.py:49
  192.7 4.4 %shard_map.69 = s16[8,6,272,256]{3,2,1,0:T(8,128)(2,1)S(1)} custom-call(s32[8]{0:T(128)S(1)} %stack.94.ids, s32[2,32]{1,0:T(2,128)S(1)} %copy-done.11, s32[48]{0:T(128)S(1)} %copy-done.12, s16[8,272,1024]{2,1,0:T(8,128)(2,1)} %all-to-all-done.own, s16[8,272,1024]{2,1,0:T(8,128)(2,1)S(1)} %collective-permute-done.24.other), custom_call_target="tpu_custom_call" | custom-call | bytes 8388608 | tf_op jit(solution)/shard_map/pallas_call | solution.py:177
  197.1 2.8 copy-done.1
  200.0 2.1 copy-done.2
  202.1 5.0 %all-to-all-start.1 = ((s16[8,6,272,256]{3,2,1,0:T(8,128)(2,1)}), s16[8,6,272,256]{3,2,1,0:T(8,128)(2,1)}, u32[]{:S(2)}, u32[]{:S(2)}) async-start(s16[8,6,272,256]{3,2,1,0:T(8,128)(2,1)} %copy-done.1), calls=%async_computation.1 | async-start | bytes 13369344 | tf_op jit(solution)/shard_map/all_to_all | solution.py:613
  207.1 2.3 copy-done
  209.4 2.3 copy-done.3
  211.7 3.1 shard_map.66
  214.7 2.7 collective-permute-start.25
  217.5 4.4 %collective-permute-start.26 = (s16[112,512]{1,0:T(8,128)(2,1)S(1)}, s16[112,512]{1,0:T(8,128)(2,1)S(1)}, u32[]{:S(2)}, u32[]{:S(2)}) collective-permute-start(s16[112,512]{1,0:T(8,128)(2,1)S(1)} %get-tuple-element.26), channel_id=1, source_target_pairs={{0,2},{1,3},{2,4},{3,5},{4,6},{5,7},{6,0},{7,1},{8,10},{9,11},{10,... | collective-permute-start | bytes 344072 | tf_op jit(solution)/shard_map/ppermute | solution.py:49
  222.8 4.5 %collective-permute-start.29 = (s16[112,512]{1,0:T(8,128)(2,1)S(1)}, s16[112,512]{1,0:T(8,128)(2,1)S(1)}, u32[]{:S(2)}, u32[]{:S(2)}) collective-permute-start(s16[112,512]{1,0:T(8,128)(2,1)S(1)} %get-tuple-element.29), channel_id=1, source_target_pairs={{0,5},{1,4},{2,7},{3,6},{4,1},{5,0},{6,3},{7,2},{8,13},{9,12},{10,... | collective-permute-start | bytes 344072 | tf_op jit(solution)/shard_map/ppermute | solution.py:49
  227.3 57.2 %collective-permute-done.25.refs_1_ = s16[112,512]{1,0:T(8,128)(2,1)S(1)} collective-permute-done((s16[112,512]{1,0:T(8,128)(2,1)S(1)}, s16[112,512]{1,0:T(8,128)(2,1)S(1)}, u32[]{:S(2)}, u32[]{:S(2)}) %collective-permute-start.25) | collective-permute-done | bytes 114720 | tf_op jit(solution)/shard_map/ppermute | solution.py:49
  284.5 1.7 collective-permute-start.30
  286.6 29.7 %shard_map.65.inv = f32[512,512]{1,0:T(8,128)S(1)} custom-call(f32[512,512]{1,0:T(8,128)S(1)} %bitcast.122), custom_call_target="tpu_custom_call" | custom-call | flops 17179869184 | bytes 2097152 | tf_op jit(solution)/shard_map/pallas_call | solution.py:365
  317.1 2.2 shard_map.67
  319.3 2.4 collective-permute-start.43
  321.8 1.4 collective-permute-start.42
  323.2 2.4 collective-permute-start.41
  326.5 1.5 collective-permute-start.36
  328.9 13.1 %collective-permute-start.37 = (s16[112,512]{1,0:T(8,128)(2,1)}, s16[112,512]{1,0:T(8,128)(2,1)S(1)}, u32[]{:S(2)}, u32[]{:S(2)}) collective-permute-start(s16[112,512]{1,0:T(8,128)(2,1)} %shard_map.67), channel_id=1, source_target_pairs={{0,16},{1,0},{2,48},{3,32},{4,80},{5,64},{6,112},{7,96},{8,24},{9,... | collective-permute-start | bytes 344072 | tf_op jit(solution)/shard_map/ppermute | solution.py:595
  342.1 2.1 collective-permute-done.37
  344.2 4.6 %collective-permute-start.38 = (s16[112,512]{1,0:T(8,128)(2,1)}, s16[112,512]{1,0:T(8,128)(2,1)S(1)}, u32[]{:S(2)}, u32[]{:S(2)}) collective-permute-start(s16[112,512]{1,0:T(8,128)(2,1)} %shard_map.67), channel_id=1, source_target_pairs={{0,32},{1,48},{2,0},{3,16},{4,96},{5,112},{6,64},{7,80},{8,40},{9,... | collective-permute-start | bytes 344072 | tf_op jit(solution)/shard_map/ppermute | solution.py:595
  348.8 3.8 collective-permute-done.38
  352.7 8.4 %collective-permute-start.39 = (s16[112,512]{1,0:T(8,128)(2,1)}, s16[112,512]{1,0:T(8,128)(2,1)S(1)}, u32[]{:S(2)}, u32[]{:S(2)}) collective-permute-start(s16[112,512]{1,0:T(8,128)(2,1)} %shard_map.67), channel_id=1, source_target_pairs={{0,48},{1,32},{2,16},{3,0},{4,112},{5,96},{6,80},{7,64},{8,56},{9,... | collective-permute-start | bytes 344072 | tf_op jit(solution)/shard_map/ppermute | solution.py:595
  361.1 2.1 collective-permute-done.39
  363.2 8.6 %collective-permute-start.34 = (s16[112,512]{1,0:T(8,128)(2,1)}, s16[112,512]{1,0:T(8,128)(2,1)S(1)}, u32[]{:S(2)}, u32[]{:S(2)}) collective-permute-start(s16[112,512]{1,0:T(8,128)(2,1)} %shard_map.67), channel_id=1, source_target_pairs={{0,6},{1,7},{2,0},{3,1},{4,2},{5,3},{6,4},{7,5},{8,14},{9,15},{10,... | collective-permute-start | bytes 344072 | tf_op jit(solution)/shard_map/ppermute | solution.py:49
  372.6 11.8 %collective-permute-start.44 = (s16[8,112,512]{2,1,0:T(8,128)(2,1)S(1)}, s16[8,112,512]{2,1,0:T(8,128)(2,1)S(1)}, u32[]{:S(2)}, u32[]{:S(2)}) collective-permute-start(s16[8,112,512]{2,1,0:T(8,128)(2,1)S(1)} %bitcast_dynamic-update-slice_fusion.4.gown), channel_id=1, source_target_pairs={{0,8},{1,9},{2,10},{3,11},{4,12},{5,13},{6,14},{7,15},{8,0},{9,1},... | collective-permute-start | bytes 2752520 | tf_op jit(solution)/shard_map/ppermute | solution.py:49
  384.7 8.8 %collective-permute-done.35 = s16[4,112,512]{2,1,0:T(8,128)(2,1)S(1)} collective-permute-done((s16[4,112,512]{2,1,0:T(8,128)(2,1)S(1)}, s16[4,112,512]{2,1,0:T(8,128)(2,1)S(1)}, u32[]{:S(2)}, u32[]{:S(2)}) %collective-permute-start.35) | collective-permute-done | bytes 458784 | tf_op jit(solution)/shard_map/ppermute | solution.py:49
  394.5 9.8 %shard_map.68 = (bf16[2304,512]{1,0:T(8,128)(2,1)}, bf16[2304,512]{1,0:T(8,128)(2,1)}, f32[768,512]{1,0:T(8,128)}) custom-call(s32[8]{0:T(128)S(1)} %stack.94.ids, s32[2,32]{1,0:T(2,128)S(1)} %copy-done.11, s32[48]{0:T(128)S(1)} %copy-done.12, f32[512,512]{1,0:T(8,128)} %bitcast.123, f32[512,512]{1,0:T(8,128)} %copy-done.13, ...), custom_call_target="tpu_custom_call" | custom-call | flops 8589934592 | bytes 16777216 | tf_op jit(solution)/shard_map/pallas_call | solution.py:435
  404.3 1.4 copy-done.7
  405.7 29.8 %shard_map.70 = f32[768,1536]{1,0:T(8,128)} custom-call(s32[8]{0:T(128)S(1)} %stack.94.ids, s32[2,32]{1,0:T(2,128)S(1)} %copy-done.11, s32[48]{0:T(128)S(1)} %copy-done.12, bf16[2304,512]{1,0:T(8,128)(2,1)} %get-tuple-element.32.ph, bf16[2304,512]{1,0:T(8,128)(2,1)} %get-tuple-element.33.plo, f32[768,512]{1,0:T(8,128)S(1)} %copy-done.7, ...), custom_call_target="tpu_custom_call" | custom-call | flops 4294967296 | bytes 20971520 | tf_op jit(solution)/shard_map/pallas_call | solution.py:503
  (120 shorter events, 14.2 us)
Async XLA Ops:
  0.0 12.7 %copy-start.4 = (bf16[1,1024,1024]{2,1,0:T(8,128)(2,1)S(1)}, bf16[1,1024,1024]{2,1,0:T(8,128)(2,1)}, u32[]{:S(2)}) copy-start(bf16[1,1024,1024]{2,1,0:T(8,128)(2,1)} %param.7) | copy-start | bytes 6291460
  2.4 7.3 %collective-permute-start.6 = (bf16[256,1024]{1,0:T(8,128)(2,1)}, bf16[256,1024]{1,0:T(8,128)(2,1)}, u32[]{:S(2)}, u32[]{:S(2)}) collective-permute-start(bf16[256,1024]{1,0:T(8,128)(2,1)} %get-tuple-element.43), channel_id=1, source_target_pairs={{4,48},{6,56},{13,49},{15,57},{22,2},{16,10},{31,3},{25,11},{32,20... | collective-permute-start | bytes 1572872 | tf_op jit(solution)/shard_map/ppermute | solution.py:545
  3.9 7.2 %collective-permute-start.5 = (bf16[256,1024]{1,0:T(8,128)(2,1)}, bf16[256,1024]{1,0:T(8,128)(2,1)}, u32[]{:S(2)}, u32[]{:S(2)}) collective-permute-start(bf16[256,1024]{1,0:T(8,128)(2,1)} %get-tuple-element.43), channel_id=1, source_target_pairs={{4,32},{6,40},{13,33},{15,41},{22,50},{16,58},{31,51},{25,59},{32,... | collective-permute-start | bytes 1572872 | tf_op jit(solution)/shard_map/ppermute | solution.py:545
  5.5 7.2 %collective-permute-start.3 = (bf16[2,256,1024]{2,1,0:T(8,128)(2,1)S(1)}, bf16[2,256,1024]{2,1,0:T(8,128)(2,1)}, u32[]{:S(2)}, u32[]{:S(2)}) collective-permute-start(bf16[2,256,1024]{2,1,0:T(8,128)(2,1)S(1)} %pad_maximum_fusion.1), channel_id=1, source_target_pairs={{0,8},{9,1},{18,26},{27,19},{36,44},{45,37},{54,62},{63,55},{64,72... | collective-permute-start | bytes 3145736 | tf_op jit(solution)/shard_map/ppermute | solution.py:554
  6.8 5.9 %collective-permute-start.4 = (bf16[256,1024]{1,0:T(8,128)(2,1)}, bf16[256,1024]{1,0:T(8,128)(2,1)}, u32[]{:S(2)}, u32[]{:S(2)}) collective-permute-start(bf16[256,1024]{1,0:T(8,128)(2,1)} %get-tuple-element.43), channel_id=1, source_target_pairs={{4,16},{6,24},{13,17},{15,25},{22,34},{16,42},{31,35},{25,43},{32,... | collective-permute-start | bytes 1572872 | tf_op jit(solution)/shard_map/ppermute | solution.py:545
  8.2 4.4 %collective-permute-start.2 = (bf16[256,1024]{1,0:T(8,128)(2,1)}, bf16[256,1024]{1,0:T(8,128)(2,1)}, u32[]{:S(2)}, u32[]{:S(2)}) collective-permute-start(bf16[256,1024]{1,0:T(8,128)(2,1)} %get-tuple-element.43), channel_id=1, source_target_pairs={{0,48},{2,56},{9,49},{11,57},{18,2},{20,10},{27,3},{29,11},{36,20}... | collective-permute-start | bytes 1572872 | tf_op jit(solution)/shard_map/ppermute | solution.py:545
  9.7 3.0 collective-permute-start.1
  11.2 1.5 collective-permute-start
  15.3 28.0 %collective-permute-start.7 = (bf16[2,256,1024]{2,1,0:T(8,128)(2,1)}, bf16[2,256,1024]{2,1,0:T(8,128)(2,1)}, u32[]{:S(2)}, u32[]{:S(2)}) collective-permute-start(bf16[2,256,1024]{2,1,0:T(8,128)(2,1)} %pad_maximum_fusion.2), channel_id=1, source_target_pairs={{0,8},{1,9},{2,10},{3,11},{4,12},{5,13},{6,14},{7,15},{8,0},{9,1},... | collective-permute-start | bytes 3145736 | tf_op jit(solution)/shard_map/ppermute | solution.py:49
  45.0 2.2 copy-start.6
  45.0 2.2 copy-start.11
  45.0 2.2 copy-start.12
  57.5 2.1 copy-start.5
  59.6 122.3 %all-to-all-start = ((s16[8,272,1024]{2,1,0:T(8,128)(2,1)}), s16[8,272,1024]{2,1,0:T(8,128)(2,1)}, u32[]{:S(2)}, u32[]{:S(2)}) async-start(s16[8,272,1024]{2,1,0:T(8,128)(2,1)} %copy-done.5), calls=%async_computation | async-start | bytes 8912896 | tf_op jit(solution)/shard_map/all_to_all | solution.py:608
  64.5 57.0 %collective-permute-start.8 = (f32[128,512]{1,0:T(8,128)S(1)}, f32[128,512]{1,0:T(8,128)S(1)}, u32[]{:S(2)}, u32[]{:S(2)}) collective-permute-start(f32[128,512]{1,0:T(8,128)S(1)} %get-tuple-element.44), channel_id=1, source_target_pairs={{0,16},{1,17},{2,18},{3,19},{4,20},{5,21},{6,22},{7,23},{8,24},{9,... | collective-permute-start | bytes 786440 | tf_op jit(solution)/shard_map/ppermute | solution.py:49
  66.9 67.3 %collective-permute-start.10 = (f32[128,512]{1,0:T(8,128)S(1)}, f32[128,512]{1,0:T(8,128)S(1)}, u32[]{:S(2)}, u32[]{:S(2)}) collective-permute-start(f32[128,512]{1,0:T(8,128)S(1)} %get-tuple-element.45), channel_id=1, source_target_pairs={{0,32},{1,33},{2,34},{3,35},{4,36},{5,37},{6,38},{7,39},{8,40},{9,... | collective-permute-start | bytes 786440 | tf_op jit(solution)/shard_map/ppermute | solution.py:49
  68.4 73.2 %collective-permute-start.9 = (f32[128,512]{1,0:T(8,128)S(1)}, f32[128,512]{1,0:T(8,128)S(1)}, u32[]{:S(2)}, u32[]{:S(2)}) collective-permute-start(f32[128,512]{1,0:T(8,128)S(1)} %get-tuple-element.46), channel_id=1, source_target_pairs={{0,48},{1,49},{2,50},{3,51},{4,52},{5,53},{6,54},{7,55},{8,56},{9,... | collective-permute-start | bytes 786440 | tf_op jit(solution)/shard_map/ppermute | solution.py:49
  141.7 5.1 %collective-permute-start.11 = (f32[32,512]{1,0:T(8,128)S(1)}, f32[32,512]{1,0:T(8,128)S(1)}, u32[]{:S(2)}, u32[]{:S(2)}) collective-permute-start(f32[32,512]{1,0:T(8,128)S(1)} %get-tuple-element.51), channel_id=1, source_target_pairs={{0,2},{1,3},{2,4},{3,5},{4,6},{5,7},{6,0},{7,1},{8,10},{9,11},{10,... | collective-permute-start | bytes 196616 | tf_op jit(solution)/shard_map/ppermute | solution.py:49
  141.8 5.0 %collective-permute-start.13 = (f32[32,512]{1,0:T(8,128)S(1)}, f32[32,512]{1,0:T(8,128)S(1)}, u32[]{:S(2)}, u32[]{:S(2)}) collective-permute-start(f32[32,512]{1,0:T(8,128)S(1)} %get-tuple-element.52), channel_id=1, source_target_pairs={{0,4},{1,5},{2,6},{3,7},{4,0},{5,1},{6,2},{7,3},{8,12},{9,13},{10,... | collective-permute-start | bytes 196616 | tf_op jit(solution)/shard_map/ppermute | solution.py:49
  144.3 3.4 collective-permute-start.12
  147.8 3.6 collective-permute-start.14
  151.4 7.2 %collective-permute-start.17 = (f32[32,512]{1,0:T(8,128)S(1)}, f32[32,512]{1,0:T(8,128)S(1)}, u32[]{:S(2)}, u32[]{:S(2)}) collective-permute-start(f32[32,512]{1,0:T(8,128)S(1)} %add.218), channel_id=1, source_target_pairs={{0,1},{1,0},{2,3},{3,2},{4,5},{5,4},{6,7},{7,6},{8,9},{9,8},{10,11... | collective-permute-start | bytes 196616 | tf_op jit(solution)/shard_map/ppermute | solution.py:49
  156.4 4.1 collective-permute-start.16
  157.0 4.3 collective-permute-start.15
  161.4 4.4 %collective-permute-start.18 = (f32[32,512]{1,0:T(8,128)S(1)}, f32[32,512]{1,0:T(8,128)S(1)}, u32[]{:S(2)}, u32[]{:S(2)}) collective-permute-start(f32[32,512]{1,0:T(8,128)S(1)} %get-tuple-element.36), channel_id=1, source_target_pairs={{0,2},{1,3},{2,4},{3,5},{4,6},{5,7},{6,0},{7,1},{8,10},{9,11},{10,... | collective-permute-start | bytes 196616 | tf_op jit(solution)/shard_map/ppermute | solution.py:49
  161.5 4.5 %collective-permute-start.19 = (f32[32,512]{1,0:T(8,128)S(1)}, f32[32,512]{1,0:T(8,128)S(1)}, u32[]{:S(2)}, u32[]{:S(2)}) collective-permute-start(f32[32,512]{1,0:T(8,128)S(1)} %get-tuple-element.36), channel_id=1, source_target_pairs={{0,6},{1,7},{2,0},{3,1},{4,2},{5,3},{6,4},{7,5},{8,14},{9,15},{10,... | collective-permute-start | bytes 196616 | tf_op jit(solution)/shard_map/ppermute | solution.py:49
  164.1 4.7 %collective-permute-start.20 = (f32[32,512]{1,0:T(8,128)S(1)}, f32[32,512]{1,0:T(8,128)S(1)}, u32[]{:S(2)}, u32[]{:S(2)}) collective-permute-start(f32[32,512]{1,0:T(8,128)S(1)} %get-tuple-element.36), channel_id=1, source_target_pairs={{0,4},{1,5},{2,6},{3,7},{4,0},{5,1},{6,2},{7,3},{8,12},{9,13},{10,... | collective-permute-start | bytes 196616 | tf_op jit(solution)/shard_map/ppermute | solution.py:49
  168.9 12.9 %collective-permute-start.21 = (f32[128,512]{1,0:T(8,128)S(1)}, f32[128,512]{1,0:T(8,128)S(1)}, u32[]{:S(2)}, u32[]{:S(2)}) collective-permute-start(f32[128,512]{1,0:T(8,128)S(1)} %bitcast.126), channel_id=1, source_target_pairs={{0,16},{1,17},{2,18},{3,19},{4,20},{5,21},{6,22},{7,23},{8,24},{9,... | collective-permute-start | bytes 786440 | tf_op jit(solution)/shard_map/ppermute | solution.py:49
  169.0 12.8 %collective-permute-start.23 = (f32[128,512]{1,0:T(8,128)S(1)}, f32[128,512]{1,0:T(8,128)S(1)}, u32[]{:S(2)}, u32[]{:S(2)}) collective-permute-start(f32[128,512]{1,0:T(8,128)S(1)} %bitcast.127), channel_id=1, source_target_pairs={{0,32},{1,33},{2,34},{3,35},{4,36},{5,37},{6,38},{7,39},{8,40},{9,... | collective-permute-start | bytes 786440 | tf_op jit(solution)/shard_map/ppermute | solution.py:49
  169.1 12.7 %collective-permute-start.22 = (f32[128,512]{1,0:T(8,128)S(1)}, f32[128,512]{1,0:T(8,128)S(1)}, u32[]{:S(2)}, u32[]{:S(2)}) collective-permute-start(f32[128,512]{1,0:T(8,128)S(1)} %bitcast.128), channel_id=1, source_target_pairs={{0,48},{1,49},{2,50},{3,51},{4,52},{5,53},{6,54},{7,55},{8,56},{9,... | collective-permute-start | bytes 786440 | tf_op jit(solution)/shard_map/ppermute | solution.py:49
  181.9 104.7 %copy-start.8 = (f32[4,128,512]{2,1,0:T(8,128)}, f32[4,128,512]{2,1,0:T(8,128)S(1)}, u32[]{:S(2)}) copy-start(f32[4,128,512]{2,1,0:T(8,128)S(1)} %bitcast_dynamic-update-slice_fusion) | copy-start | bytes 3145732
  181.9 10.8 %collective-permute-start.24 = (s16[8,272,1024]{2,1,0:T(8,128)(2,1)}, s16[8,272,1024]{2,1,0:T(8,128)(2,1)S(1)}, u32[]{:S(2)}, u32[]{:S(2)}) collective-permute-start(s16[8,272,1024]{2,1,0:T(8,128)(2,1)} %all-to-all-done.own), channel_id=1, source_target_pairs={{0,8},{1,9},{2,10},{3,11},{4,12},{5,13},{6,14},{7,15},{8,0},{9,1},... | collective-permute-start | bytes 13369352 | tf_op jit(solution)/shard_map/ppermute | solution.py:49
  197.1 2.8 copy-start.1
  200.0 2.1 copy-start.2
  202.1 202.2 %all-to-all-start.1 = ((s16[8,6,272,256]{3,2,1,0:T(8,128)(2,1)}), s16[8,6,272,256]{3,2,1,0:T(8,128)(2,1)}, u32[]{:S(2)}, u32[]{:S(2)}) async-start(s16[8,6,272,256]{3,2,1,0:T(8,128)(2,1)} %copy-done.1), calls=%async_computation.1 | async-start | bytes 13369344 | tf_op jit(solution)/shard_map/all_to_all | solution.py:613
  207.1 2.3 copy-start
  209.4 2.3 copy-start.3
  214.7 101.5 %copy-start.9 = (s16[112,512]{1,0:T(8,128)(2,1)}, s16[112,512]{1,0:T(8,128)(2,1)S(1)}, u32[]{:S(2)}) copy-start(s16[112,512]{1,0:T(8,128)(2,1)S(1)} %get-tuple-element.24.refs_0_) | copy-start | bytes 344068
  214.7 69.7 %collective-permute-start.25 = (s16[112,512]{1,0:T(8,128)(2,1)S(1)}, s16[112,512]{1,0:T(8,128)(2,1)S(1)}, u32[]{:S(2)}, u32[]{:S(2)}) collective-permute-start(s16[112,512]{1,0:T(8,128)(2,1)S(1)} %get-tuple-element.25), channel_id=1, source_target_pairs={{0,1},{1,0},{2,3},{3,2},{4,5},{5,4},{6,7},{7,6},{8,9},{9,8},{10,11... | collective-permute-start | bytes 344072 | tf_op jit(solution)/shard_map/ppermute | solution.py:49
  217.5 68.7 %collective-permute-start.26 = (s16[112,512]{1,0:T(8,128)(2,1)S(1)}, s16[112,512]{1,0:T(8,128)(2,1)S(1)}, u32[]{:S(2)}, u32[]{:S(2)}) collective-permute-start(s16[112,512]{1,0:T(8,128)(2,1)S(1)} %get-tuple-element.26), channel_id=1, source_target_pairs={{0,2},{1,3},{2,4},{3,5},{4,6},{5,7},{6,0},{7,1},{8,10},{9,11},{10,... | collective-permute-start | bytes 344072 | tf_op jit(solution)/shard_map/ppermute | solution.py:49
  221.9 94.4 %collective-permute-start.27 = (s16[112,512]{1,0:T(8,128)(2,1)S(1)}, s16[112,512]{1,0:T(8,128)(2,1)S(1)}, u32[]{:S(2)}, u32[]{:S(2)}) collective-permute-start(s16[112,512]{1,0:T(8,128)(2,1)S(1)} %get-tuple-element.27), channel_id=1, source_target_pairs={{0,3},{1,2},{2,5},{3,4},{4,7},{5,6},{6,1},{7,0},{8,11},{9,10},{10,... | collective-permute-start | bytes 344072 | tf_op jit(solution)/shard_map/ppermute | solution.py:49
  221.9 94.4 %collective-permute-start.28 = (s16[112,512]{1,0:T(8,128)(2,1)S(1)}, s16[112,512]{1,0:T(8,128)(2,1)S(1)}, u32[]{:S(2)}, u32[]{:S(2)}) collective-permute-start(s16[112,512]{1,0:T(8,128)(2,1)S(1)} %get-tuple-element.28), channel_id=1, source_target_pairs={{0,4},{1,5},{2,6},{3,7},{4,0},{5,1},{6,2},{7,3},{8,12},{9,13},{10,... | collective-permute-start | bytes 344072 | tf_op jit(solution)/shard_map/ppermute | solution.py:49
  222.8 93.5 %collective-permute-start.29 = (s16[112,512]{1,0:T(8,128)(2,1)S(1)}, s16[112,512]{1,0:T(8,128)(2,1)S(1)}, u32[]{:S(2)}, u32[]{:S(2)}) collective-permute-start(s16[112,512]{1,0:T(8,128)(2,1)S(1)} %get-tuple-element.29), channel_id=1, source_target_pairs={{0,5},{1,4},{2,7},{3,6},{4,1},{5,0},{6,3},{7,2},{8,13},{9,12},{10,... | collective-permute-start | bytes 344072 | tf_op jit(solution)/shard_map/ppermute | solution.py:49
  284.5 31.8 %copy-start.15 = (s16[112,512]{1,0:T(8,128)(2,1)}, s16[112,512]{1,0:T(8,128)(2,1)S(1)}, u32[]{:S(2)}) copy-start(s16[112,512]{1,0:T(8,128)(2,1)S(1)} %collective-permute-done.25.refs_1_) | copy-start | bytes 344068
  284.5 31.9 %collective-permute-start.30 = (s16[112,512]{1,0:T(8,128)(2,1)S(1)}, s16[112,512]{1,0:T(8,128)(2,1)S(1)}, u32[]{:S(2)}, u32[]{:S(2)}) collective-permute-start(s16[112,512]{1,0:T(8,128)(2,1)S(1)} %get-tuple-element.30), channel_id=1, source_target_pairs={{0,6},{1,7},{2,0},{3,1},{4,2},{5,3},{6,4},{7,5},{8,14},{9,15},{10,... | collective-permute-start | bytes 344072 | tf_op jit(solution)/shard_map/ppermute | solution.py:49
  286.1 30.1 %copy-start.16 = (s16[112,512]{1,0:T(8,128)(2,1)}, s16[112,512]{1,0:T(8,128)(2,1)S(1)}, u32[]{:S(2)}) copy-start(s16[112,512]{1,0:T(8,128)(2,1)S(1)} %collective-permute-done.26.refs_2_) | copy-start | bytes 344068
  286.1 30.2 %collective-permute-start.31 = (s16[112,512]{1,0:T(8,128)(2,1)S(1)}, s16[112,512]{1,0:T(8,128)(2,1)S(1)}, u32[]{:S(2)}, u32[]{:S(2)}) collective-permute-start(s16[112,512]{1,0:T(8,128)(2,1)S(1)} %get-tuple-element.31), channel_id=1, source_target_pairs={{0,7},{1,6},{2,1},{3,0},{4,3},{5,2},{6,5},{7,4},{8,15},{9,14},{10,... | collective-permute-start | bytes 344072 | tf_op jit(solution)/shard_map/ppermute | solution.py:49
  316.2 68.4 %copy-start.13 = (f32[512,512]{1,0:T(8,128)}, f32[512,512]{1,0:T(8,128)S(1)}, u32[]{:S(2)}) copy-start(f32[512,512]{1,0:T(8,128)S(1)} %shard_map.65.inv) | copy-start | bytes 3145732
  319.3 65.2 %copy-start.14 = (s16[112,512]{1,0:T(8,128)(2,1)S(1)}, s16[112,512]{1,0:T(8,128)(2,1)}, u32[]{:S(2)}) copy-start(s16[112,512]{1,0:T(8,128)(2,1)} %shard_map.67) | copy-start | bytes 344068
  319.3 53.3 %collective-permute-start.43 = (s16[112,512]{1,0:T(8,128)(2,1)}, s16[112,512]{1,0:T(8,128)(2,1)S(1)}, u32[]{:S(2)}, u32[]{:S(2)}) collective-permute-start(s16[112,512]{1,0:T(8,128)(2,1)} %shard_map.67), channel_id=1, source_target_pairs={{0,112},{1,96},{2,80},{3,64},{4,48},{5,32},{6,16},{7,0},{8,120},{9... | collective-permute-start | bytes 344072 | tf_op jit(solution)/shard_map/ppermute | solution.py:595
  321.8 50.8 %collective-permute-start.42 = (s16[112,512]{1,0:T(8,128)(2,1)}, s16[112,512]{1,0:T(8,128)(2,1)S(1)}, u32[]{:S(2)}, u32[]{:S(2)}) collective-permute-start(s16[112,512]{1,0:T(8,128)(2,1)} %shard_map.67), channel_id=1, source_target_pairs={{0,96},{1,112},{2,64},{3,80},{4,32},{5,48},{6,0},{7,16},{8,104},{9... | collective-permute-start | bytes 344072 | tf_op jit(solution)/shard_map/ppermute | solution.py:595
  323.2 48.7 %collective-permute-start.41 = (s16[112,512]{1,0:T(8,128)(2,1)}, s16[112,512]{1,0:T(8,128)(2,1)S(1)}, u32[]{:S(2)}, u32[]{:S(2)}) collective-permute-start(s16[112,512]{1,0:T(8,128)(2,1)} %shard_map.67), channel_id=1, source_target_pairs={{0,80},{1,64},{2,112},{3,96},{4,16},{5,0},{6,48},{7,32},{8,88},{9,... | collective-permute-start | bytes 344072 | tf_op jit(solution)/shard_map/ppermute | solution.py:595
  325.6 46.2 %collective-permute-start.40 = (s16[112,512]{1,0:T(8,128)(2,1)}, s16[112,512]{1,0:T(8,128)(2,1)S(1)}, u32[]{:S(2)}, u32[]{:S(2)}) collective-permute-start(s16[112,512]{1,0:T(8,128)(2,1)} %shard_map.67), channel_id=1, source_target_pairs={{0,64},{1,80},{2,96},{3,112},{4,0},{5,16},{6,32},{7,48},{8,72},{9,... | collective-permute-start | bytes 344072 | tf_op jit(solution)/shard_map/ppermute | solution.py:595
  326.5 2.5 collective-permute-start.36
  328.9 15.2 %collective-permute-start.37 = (s16[112,512]{1,0:T(8,128)(2,1)}, s16[112,512]{1,0:T(8,128)(2,1)S(1)}, u32[]{:S(2)}, u32[]{:S(2)}) collective-permute-start(s16[112,512]{1,0:T(8,128)(2,1)} %shard_map.67), channel_id=1, source_target_pairs={{0,16},{1,0},{2,48},{3,32},{4,80},{5,64},{6,112},{7,96},{8,24},{9,... | collective-permute-start | bytes 344072 | tf_op jit(solution)/shard_map/ppermute | solution.py:595
  344.2 8.5 %collective-permute-start.38 = (s16[112,512]{1,0:T(8,128)(2,1)}, s16[112,512]{1,0:T(8,128)(2,1)S(1)}, u32[]{:S(2)}, u32[]{:S(2)}) collective-permute-start(s16[112,512]{1,0:T(8,128)(2,1)} %shard_map.67), channel_id=1, source_target_pairs={{0,32},{1,48},{2,0},{3,16},{4,96},{5,112},{6,64},{7,80},{8,40},{9,... | collective-permute-start | bytes 344072 | tf_op jit(solution)/shard_map/ppermute | solution.py:595
  352.7 10.5 %collective-permute-start.39 = (s16[112,512]{1,0:T(8,128)(2,1)}, s16[112,512]{1,0:T(8,128)(2,1)S(1)}, u32[]{:S(2)}, u32[]{:S(2)}) collective-permute-start(s16[112,512]{1,0:T(8,128)(2,1)} %shard_map.67), channel_id=1, source_target_pairs={{0,48},{1,32},{2,16},{3,0},{4,112},{5,96},{6,80},{7,64},{8,56},{9,... | collective-permute-start | bytes 344072 | tf_op jit(solution)/shard_map/ppermute | solution.py:595
  363.2 21.3 %collective-permute-start.34 = (s16[112,512]{1,0:T(8,128)(2,1)}, s16[112,512]{1,0:T(8,128)(2,1)S(1)}, u32[]{:S(2)}, u32[]{:S(2)}) collective-permute-start(s16[112,512]{1,0:T(8,128)(2,1)} %shard_map.67), channel_id=1, source_target_pairs={{0,6},{1,7},{2,0},{3,1},{4,2},{5,3},{6,4},{7,5},{8,14},{9,15},{10,... | collective-permute-start | bytes 344072 | tf_op jit(solution)/shard_map/ppermute | solution.py:49
  371.8 12.7 %collective-permute-start.33 = (s16[112,512]{1,0:T(8,128)(2,1)}, s16[112,512]{1,0:T(8,128)(2,1)S(1)}, u32[]{:S(2)}, u32[]{:S(2)}) collective-permute-start(s16[112,512]{1,0:T(8,128)(2,1)} %shard_map.67), channel_id=1, source_target_pairs={{0,4},{1,5},{2,6},{3,7},{4,0},{5,1},{6,2},{7,3},{8,12},{9,13},{10,... | collective-permute-start | bytes 344072 | tf_op jit(solution)/shard_map/ppermute | solution.py:49
  371.9 12.6 %collective-permute-start.32 = (s16[112,512]{1,0:T(8,128)(2,1)}, s16[112,512]{1,0:T(8,128)(2,1)S(1)}, u32[]{:S(2)}, u32[]{:S(2)}) collective-permute-start(s16[112,512]{1,0:T(8,128)(2,1)} %shard_map.67), channel_id=1, source_target_pairs={{0,2},{1,3},{2,4},{3,5},{4,6},{5,7},{6,0},{7,1},{8,10},{9,11},{10,... | collective-permute-start | bytes 344072 | tf_op jit(solution)/shard_map/ppermute | solution.py:49
  372.6 20.9 %collective-permute-start.44 = (s16[8,112,512]{2,1,0:T(8,128)(2,1)S(1)}, s16[8,112,512]{2,1,0:T(8,128)(2,1)S(1)}, u32[]{:S(2)}, u32[]{:S(2)}) collective-permute-start(s16[8,112,512]{2,1,0:T(8,128)(2,1)S(1)} %bitcast_dynamic-update-slice_fusion.4.gown), channel_id=1, source_target_pairs={{0,8},{1,9},{2,10},{3,11},{4,12},{5,13},{6,14},{7,15},{8,0},{9,1},... | collective-permute-start | bytes 2752520 | tf_op jit(solution)/shard_map/ppermute | solution.py:49
  384.6 8.9 %collective-permute-start.35 = (s16[4,112,512]{2,1,0:T(8,128)(2,1)S(1)}, s16[4,112,512]{2,1,0:T(8,128)(2,1)S(1)}, u32[]{:S(2)}, u32[]{:S(2)}) collective-permute-start(s16[4,112,512]{2,1,0:T(8,128)(2,1)S(1)} %pad_add_fusion), channel_id=1, source_target_pairs={{0,1},{1,0},{2,3},{3,2},{4,5},{5,4},{6,7},{7,6},{8,9},{9,8},{10,11... | collective-permute-start | bytes 1376264 | tf_op jit(solution)/shard_map/ppermute | solution.py:49
  393.5 1.0 copy-start.22
  404.3 1.4 copy-start.7
  (6 other events, 4.4 us)

commit v3 on v2

v3 whole, which is shorter than its diff:
```python
import jax
import jax.numpy as jnp
from jax import lax
from jax.experimental import pallas as pl
from jax.experimental.pallas import tpu as pltpu
from jax.sharding import Mesh
from jax.sharding import PartitionSpec as P

TILE = 256
PANEL = 512
CODE = 16
CT = 4
RT = 3
QT = 6
STRIP = 32
SROWS = RT * STRIP + CODE
AXES = ("child", "x", "core", "z", "yh")
SIZES = (2, 4, 2, 4, 2)
MIB = 1 << 20
F32 = jnp.float32
I32 = jnp.int32
I16 = jnp.int16
BF16 = jnp.bfloat16
HIGHEST = lax.Precision.HIGHEST


def flat(c, x, k, z, y):
    return (((c * 4 + x) * 2 + k) * 4 + z) * 2 + y


def everyone():
    return [
        (c, x, k, z, y)
        for c in range(2)
        for x in range(4)
        for k in range(2)
        for z in range(4)
        for y in range(2)
    ]


def shift(v, dc=0, dx=0, dk=0, dz=0, dy=0):
    pairs = [
        (flat(c, x, k, z, y), flat(c ^ dc, (x + dx) % 4, k ^ dk, (z + dz) % 4, y ^ dy))
        for c, x, k, z, y in everyone()
    ]
    return lax.ppermute(v, AXES, pairs)


def encode(u):
    top = jnp.max(jnp.abs(u), axis=0, keepdims=True)
    code = jnp.ceil(jnp.log2(jnp.maximum(top, 1e-30)) * 128.0)
    q = jnp.clip(jnp.floor(u * jnp.exp2(15.0 - code * (1.0 / 128.0)) + 0.5), -32767.0, 32767.0)
    return q.astype(I32).astype(I16), code


def scale_rows(code):
    return jnp.broadcast_to(code, (CODE, code.shape[1])).astype(I32).astype(I16)


def as_float(q):
    return q.astype(I32).astype(F32)


def column_scale(codes):
    return jnp.exp2(as_float(codes)[0:1, :] * (1.0 / 128.0) - 15.0)


def update_kernel(ids, slots, pat, blk, pan, par, front, send, diag, gcol, tile, sem):
    i = pl.program_id(0)
    ch, r, c, g = ids[0], ids[1], ids[2], ids[3]
    e = (ids[8], ids[9])

    @pl.when(i == 0)
    def _():
        diag[...] = jnp.zeros_like(diag)
        for a in range(2):
            for b in range(2):

                @pl.when((e[a] // RT == g) & (e[b] // QT == c))
                def _():
                    rows = pl.multiple_of((e[a] % RT) * TILE, TILE)
                    cols = pl.multiple_of((e[b] % QT) * TILE, TILE)
                    copy = pltpu.make_async_copy(
                        front.at[pl.ds(rows, TILE), pl.ds(cols, TILE)], tile, sem
                    )
                    copy.start()
                    copy.wait()
                    diag[a * TILE : (a + 1) * TILE, b * TILE : (b + 1) * TILE] = tile[...]

    si = slots[ch, r * CT + i]
    for j in range(CT):
        cols = slice(j * TILE, (j + 1) * TILE)
        prod = lax.dot_general(
            pan[...], par[cols, :], (((1,), (1,)), ((), ())), preferred_element_type=F32
        )
        u = (blk[:, cols] - prod) * pat[ch, r * CT + i, c * CT + j].astype(F32)
        q, code = encode(u)
        send[0, 0:TILE, cols] = q
        send[0, TILE:, cols] = scale_rows(code)
        sj = slots[ch, c * CT + j]
        for b in range(2):
            at = slice(b * TILE, (b + 1) * TILE)

            @pl.when(sj == e[b])
            def _():
                gcol[:, at] = u
                for a in range(2):

                    @pl.when(si == e[a])
                    def _():
                        diag[a * TILE : (a + 1) * TILE, at] += u


def update(ids, slots, pat, blk, pan, par, front):
    def slot(i, ids, slots, pat):
        return slots[ids[0], ids[1] * CT + i] // QT, 0, 0

    return pl.pallas_call(
        update_kernel,
        grid_spec=pltpu.PrefetchScalarGridSpec(
            num_scalar_prefetch=3,
            grid=(CT,),
            in_specs=[
                pl.BlockSpec((TILE, 1024), lambda i, *s: (i, 0)),
                pl.BlockSpec((TILE, 1024), lambda i, *s: (i, 0)),
                pl.BlockSpec((1024, 1024), lambda i, *s: (0, 0)),
                pl.BlockSpec(memory_space=pl.ANY),
            ],
            out_specs=[
                pl.BlockSpec((1, TILE + CODE, 1024), slot),
                pl.BlockSpec((PANEL, PANEL), lambda i, *s: (0, 0)),
                pl.BlockSpec((TILE, PANEL), lambda i, *s: (i, 0)),
            ],
            scratch_shapes=[pltpu.VMEM((TILE, TILE), F32), pltpu.SemaphoreType.DMA],
        ),
        out_shape=[
            jax.ShapeDtypeStruct((8, TILE + CODE, 1024), I16),
            jax.ShapeDtypeStruct((PANEL, PANEL), F32),
            jax.ShapeDtypeStruct((CT * TILE, PANEL), F32),
        ],
        compiler_params=pltpu.CompilerParams(vmem_limit_bytes=40 * MIB),
        cost_estimate=pl.CostEstimate(flops=1 << 31, bytes_accessed=14 * MIB, transcendentals=0),
    )(ids, slots, pat, blk, pan, par, front)


def strips_kernel(ids, gcol, front, *rest):
    outs, (wide, sem) = rest[:4], rest[4:]
    c, z = ids[2], ids[5]
    for a in range(2):
        e = ids[8 + a]

        @pl.when(e // QT == c)
        def _():
            at = pl.multiple_of((e % QT) * TILE, TILE)
            copy = pltpu.make_async_copy(
                front.at[:, pl.ds(at, TILE)], wide.at[:, pl.ds(a * TILE, TILE)], sem
            )
            copy.start()
            copy.wait()

    for d in range(4):
        for f in range(2):
            s = ((z + d) % 4) * 2 + f
            at = 0
            for ref, n in ((gcol, CT), (wide, RT)):
                parts = [
                    ref[pl.ds(pl.multiple_of(p * TILE + s * STRIP, STRIP), STRIP), :]
                    for p in range(n)
                ]
                q, code = encode(jnp.concatenate(parts, 0))
                outs[d][f, at : at + n * STRIP, :] = q
                outs[d][f, at + n * STRIP : at + n * STRIP + CODE, :] = scale_rows(code)
                at += n * STRIP + CODE


def strips(ids, gcol, front):
    return pl.pallas_call(
        strips_kernel,
        grid_spec=pltpu.PrefetchScalarGridSpec(
            num_scalar_prefetch=1,
            grid=(1,),
            in_specs=[
                pl.BlockSpec((CT * TILE, PANEL), lambda i, *s: (0, 0)),
                pl.BlockSpec(memory_space=pl.ANY),
            ],
            out_specs=[pl.BlockSpec((2, TILE, PANEL), lambda i, *s: (0, 0, 0))] * 4,
            scratch_shapes=[pltpu.VMEM((RT * TILE, PANEL), F32), pltpu.SemaphoreType.DMA],
        ),
        out_shape=[jax.ShapeDtypeStruct((2, TILE, PANEL), I16)] * 4,
        compiler_params=pltpu.CompilerParams(vmem_limit_bytes=24 * MIB),
        cost_estimate=pl.CostEstimate(flops=0, bytes_accessed=6 * MIB, transcendentals=0),
    )(ids, gcol, front)


CHILD_CODE = CT * STRIP
FRONT = CHILD_CODE + CODE
FRONT_CODE = FRONT + RT * STRIP


def compose_kernel(ids, where, own, other, out, acc, kept):
    q = pl.program_id(0)
    ch, core, k, x = ids[0], ids[4], ids[7], ids[10]
    half = lax.broadcasted_iota(I32, (STRIP, PANEL), 1) < TILE

    def group(q):
        first = q * QT + core * RT
        d, f = lax.rem(x - q % 4 + 4, 4), lax.rem(ch + q // 4, 2)
        acc[...] = as_float(own[d, f, FRONT:FRONT_CODE, :]) * column_scale(
            own[d, f, FRONT_CODE:, :]
        )
        for m in range(2):
            known = [(where[m, ids[8 + a]] >= 0).astype(I32) for a in range(2)]
            mask = jnp.where(half, known[0], known[1]) > 0
            for p in range(RT):
                i = where[m, first + p]
                for here, ref in ((True, own), (False, other)):

                    @pl.when((i >= 0) & (((i // CT) % 2 == core) == here))
                    def _():
                        dm, fm = lax.rem(x - i // 8 + 4, 4), lax.rem(ch + m, 2)
                        row = pl.multiple_of((i % CT) * STRIP, STRIP)
                        v = as_float(ref[dm, fm, pl.ds(row, STRIP), :]) * column_scale(
                            ref[dm, fm, CHILD_CODE:FRONT, :]
                        )
                        acc[p * STRIP : (p + 1) * STRIP, :] += jnp.where(mask, v, 0.0)

        return encode(acc[...])

    @pl.when(q == 0)
    def _():
        v, code = group(k)
        kept[0 : RT * STRIP, :] = v
        kept[RT * STRIP :, :] = scale_rows(code)

    v, code = group(q)
    out[0, 0] = kept[...]
    out[0, 1, 0 : RT * STRIP, :] = v
    out[0, 1, RT * STRIP :, :] = scale_rows(code)


def compose(ids, where, own, other):
    whole = pl.BlockSpec((4, 2, TILE, PANEL), lambda i, *s: (0, 0, 0, 0))
    return pl.pallas_call(
        compose_kernel,
        grid_spec=pltpu.PrefetchScalarGridSpec(
            num_scalar_prefetch=2,
            grid=(8,),
            in_specs=[whole] * 2,
            out_specs=pl.BlockSpec((1, 2, SROWS, PANEL), lambda i, *s: (i, 0, 0, 0)),
            scratch_shapes=[
                pltpu.VMEM((RT * STRIP, PANEL), F32),
                pltpu.VMEM((SROWS, PANEL), I16),
            ],
        ),
        out_shape=jax.ShapeDtypeStruct((8, 2, SROWS, PANEL), I16),
        compiler_params=pltpu.CompilerParams(vmem_limit_bytes=24 * MIB),
        cost_estimate=pl.CostEstimate(flops=0, bytes_accessed=6 * MIB, transcendentals=0),
    )(ids, where, own, other)


def route_kernel(ids, slots, where, own, other, send, sems):
    c, g, core = ids[2], ids[3], ids[4]

    def each(act):
        for ch in range(2):
            for p in range(RT):
                i = rows[ch * RT + p]
                src = ch * 4 + i // 8
                for j in range(CT):
                    q = slots[ch, c * CT + j] // QT
                    sem = sems.at[(ch * RT + p) * CT + j]
                    for here, buf in ((True, own), (False, other)):

                        @pl.when((i >= 0) & (((i // 4) % 2 == core) == here))
                        def _():
                            copy = pltpu.make_async_copy(
                                buf.at[src, :, pl.ds(j * TILE, TILE)],
                                send.at[q, ch * RT + p],
                                sem,
                            )
                            act(copy)

    rows = [where[ch, g * RT + p] for ch in range(2) for p in range(RT)]
    each(lambda copy: copy.start())
    each(lambda copy: copy.wait())


def route(ids, slots, where, own, other):
    return pl.pallas_call(
        route_kernel,
        grid_spec=pltpu.PrefetchScalarGridSpec(
            num_scalar_prefetch=3,
            grid=(1,),
            in_specs=[pl.BlockSpec(memory_space=pl.ANY)] * 2,
            out_specs=pl.BlockSpec((8, 2 * RT, TILE + CODE, TILE), lambda i, *s: (0, 0, 0, 0)),
            scratch_shapes=[pltpu.SemaphoreType.DMA((24,))],
        ),
        out_shape=jax.ShapeDtypeStruct((8, 2 * RT, TILE + CODE, TILE), I16),
        compiler_params=pltpu.CompilerParams(vmem_limit_bytes=32 * MIB),
        cost_estimate=pl.CostEstimate(flops=0, bytes_accessed=8 * MIB, transcendentals=0),
    )(ids, slots, where, own, other)


def decode_strip(ref, lead=()):
    q = ref[lead + (slice(0, RT * STRIP), slice(None))]
    codes = ref[lead + (slice(RT * STRIP, SROWS), slice(None))]
    return as_float(q) * column_scale(codes)


def nt(a, b):
    return lax.dot_general(
        a, b, (((1,), (1,)), ((), ())), precision=HIGHEST, preferred_element_type=F32
    )


def nn(a, b):
    return lax.dot_general(
        a, b, (((1,), (0,)), ((), ())), precision=HIGHEST, preferred_element_type=F32
    )


NB = 128
WAYS = 4


def inverse_kernel(a_ref, out, w, f):
    n = PANEL // NB
    out[...] = jnp.zeros_like(out)
    row = lax.broadcasted_iota(I32, (NB, NB), 0)
    col = lax.broadcasted_iota(I32, (NB, NB), 1)
    eye = row == col
    lanes = lax.broadcasted_iota(I32, (1, 2 * NB), 1)
    sub = lax.broadcasted_iota(I32, (NB, 1), 0)

    def blk(i):
        return slice(i * NB, (i + 1) * NB)

    f[...] = a_ref[...]
    for k in range(n):
        w[:, :NB] = f[blk(k), blk(k)]
        w[:, NB:] = jnp.where(eye, 1.0, 0.0).astype(F32)

        def step(n4, _):
            j = n4 * WAYS
            lines = [w[pl.ds(j + a, 1), :] for a in range(WAYS)]
            square = w[:, :NB]
            columns = [
                jnp.sum(jnp.where(col == j + a, square, 0.0), axis=1, keepdims=True)
                for a in range(WAYS)
            ]
            small = [
                [
                    jnp.sum(jnp.where(lanes == j + b, lines[a], 0.0), axis=1, keepdims=True)
                    if b >= a
                    else None
                    for b in range(WAYS)
                ]
                for a in range(WAYS)
            ]
            factors = []
            for a in range(WAYS):
                inverse = 1.0 / small[a][a]
                for b in range(a + 1, WAYS):
                    times = small[a][b] * inverse
                    for d in range(b, WAYS):
                        small[b][d] = small[b][d] - times * small[a][d]
                    lines[b] = lines[b] - times * lines[a]
                    columns[b] = columns[b] - times * columns[a]
                factors.append(jnp.where(sub >= j + WAYS, columns[a] * inverse, 0.0))
            total = w[...]
            for a in range(WAYS):
                total = total - factors[a] * lines[a]
            w[...] = total
            for a in range(1, WAYS):
                w[pl.ds(j + a, 1), :] = lines[a]
            return 0

        lax.fori_loop(0, NB // WAYS, step, 0)
        d = jnp.sum(jnp.where(eye, w[:, :NB], 0.0), axis=1, keepdims=True)
        inv = w[:, NB:] * (1.0 / jnp.sqrt(d))
        out[blk(k), blk(k)] = inv
        rest = (k + 1) * NB
        if rest < PANEL:
            below = nt(f[rest:, blk(k)], inv)
            f[rest:, blk(k)] = below
            f[rest:, rest:] = f[rest:, rest:] - nt(below, below)
    for k in range(1, n):
        acc = nn(f[blk(k), : k * NB], out[: k * NB, : k * NB])
        out[blk(k), : k * NB] = -nn(out[blk(k), blk(k)], acc)


def inverse_factor(a):
    return pl.pallas_call(
        inverse_kernel,
        out_shape=jax.ShapeDtypeStruct((PANEL, PANEL), F32),
        scratch_shapes=[pltpu.VMEM((NB, 2 * NB), F32), pltpu.VMEM((PANEL, PANEL), F32)],
        compiler_params=pltpu.CompilerParams(vmem_limit_bytes=24 * MIB),
        cost_estimate=pl.CostEstimate(flops=1 << 34, bytes_accessed=2 * MIB, transcendentals=0),
    )(a)


def split(v):
    hi = v.astype(BF16)
    return hi, (v - hi.astype(F32)).astype(BF16)


def dot3(a, b):
    def one(x, y):
        return lax.dot_general(x, y, (((1,), (1,)), ((), ())), preferred_element_type=F32)

    return one(a[0], b[0]) + (one(a[0], b[1]) + one(a[1], b[0]))


def panel_kernel(ids, diag, inv, gx, goth, ph, plo, rows_f, gbuf):
    c, g, core = ids[2], ids[3], ids[4]
    inv2 = split(inv[...])

    def fill(base, ref, lead, first):
        for s in range(8):
            v = decode_strip(ref, lead(s))
            for t in range(RT):
                gbuf[base + t * TILE + s * STRIP : base + t * TILE + (s + 1) * STRIP, :] = v[
                    t * STRIP : (t + 1) * STRIP, :
                ]
        for t in range(RT):
            for a in range(2):

                @pl.when(first + t == ids[8 + a])
                def _():
                    gbuf[base + t * TILE : base + (t + 1) * TILE, :] = diag[
                        a * TILE : (a + 1) * TILE, :
                    ]

    fill(0, gx, lambda s: (s, 0), g * RT)
    for b in range(2):
        base = RT * TILE * (1 + b)

        @pl.when(core == b)
        def _():
            fill(base, gx, lambda s: (s, 1), c * QT + b * RT)

        @pl.when(core != b)
        def _():
            fill(base, goth, lambda s: (s,), c * QT + b * RT)

    for t in range(3):
        rows = slice(t * RT * TILE, (t + 1) * RT * TILE)
        v = dot3(split(gbuf[rows, :]), inv2)
        hi, lo = split(v)
        ph[rows, :] = hi
        plo[rows, :] = lo
        if t == 0:
            rows_f[...] = v


def panel_rows(ids, diag, inv, gx, goth):
    def whole(*shape):
        return pl.BlockSpec(shape, lambda i, *s: (0,) * len(shape))

    return pl.pallas_call(
        panel_kernel,
        grid_spec=pltpu.PrefetchScalarGridSpec(
            num_scalar_prefetch=1,
            grid=(1,),
            in_specs=[whole(PANEL, PANEL)] * 2
            + [whole(8, 2, SROWS, PANEL), whole(8, SROWS, PANEL)],
            out_specs=[whole(9 * TILE, PANEL)] * 2 + [whole(RT * TILE, PANEL)],
            scratch_shapes=[pltpu.VMEM((9 * TILE, PANEL), F32)],
        ),
        out_shape=[jax.ShapeDtypeStruct((9 * TILE, PANEL), BF16)] * 2
        + [jax.ShapeDtypeStruct((RT * TILE, PANEL), F32)],
        compiler_params=pltpu.CompilerParams(vmem_limit_bytes=52 * MIB),
        cost_estimate=pl.CostEstimate(flops=1 << 33, bytes_accessed=16 * MIB, transcendentals=0),
    )(ids, diag, inv, gx, goth)


def final_kernel(ids, where, lh, ll, rh, rl, rows_f, recv, front, out, tiles, tsem):
    t = pl.program_id(0)
    c, g = ids[2], ids[3]
    col = c * QT + t
    js = [where[ch, col] for ch in range(2)]
    there = [[where[ch, g * RT + p] >= 0 for p in range(RT)] for ch in range(2)]

    def each(act):
        for ch in range(2):
            for p in range(RT):

                @pl.when(there[ch][p] & (js[ch] >= 0))
                def _():
                    act(
                        pltpu.make_async_copy(
                            recv.at[js[ch] // CT, ch * RT + p],
                            tiles.at[ch * RT + p],
                            tsem.at[ch * RT + p],
                        )
                    )

    each(lambda copy: copy.start())
    out[...] = front[...] - dot3((lh[...], ll[...]), (rh[...], rl[...]))
    each(lambda copy: copy.wait())
    for p in range(RT):
        rows = slice(p * TILE, (p + 1) * TILE)
        for ch in range(2):

            @pl.when(there[ch][p] & (js[ch] >= 0))
            def _():
                out[rows, :] += as_float(tiles[ch * RT + p, 0:TILE, :]) * column_scale(
                    tiles[ch * RT + p, TILE:, :]
                )

    for a in range(2):

        @pl.when(col == ids[8 + a])
        def _():
            out[...] = rows_f[:, a * TILE : (a + 1) * TILE]


def final(ids, where, ph, plo, rows_f, recv, front):
    line = pl.BlockSpec((RT * TILE, TILE), lambda i, *s: (0, i))
    left = pl.BlockSpec((RT * TILE, PANEL), lambda i, *s: (0, 0))
    right = pl.BlockSpec((TILE, PANEL), lambda i, *s: (RT + i, 0))
    return pl.pallas_call(
        final_kernel,
        grid_spec=pltpu.PrefetchScalarGridSpec(
            num_scalar_prefetch=2,
            grid=(QT,),
            in_specs=[
                left,
                left,
                right,
                right,
                left,
                pl.BlockSpec(memory_space=pl.ANY),
                line,
            ],
            out_specs=line,
            scratch_shapes=[
                pltpu.VMEM((2 * RT, TILE + CODE, TILE), I16),
                pltpu.SemaphoreType.DMA((2 * RT,)),
            ],
        ),
        out_shape=jax.ShapeDtypeStruct((RT * TILE, QT * TILE), F32),
        compiler_params=pltpu.CompilerParams(vmem_limit_bytes=52 * MIB),
        cost_estimate=pl.CostEstimate(flops=1 << 32, bytes_accessed=20 * MIB, transcendentals=0),
    )(ids, where, ph, plo, ph, plo, rows_f, recv, front)


def pick(v, at):
    return lax.dynamic_index_in_dim(v, at, 0, keepdims=False)


def fetch_partner(panel, x, core, z, yh):
    tiles = panel.reshape(4, TILE, 1024)
    piece = pick(tiles, (z - x) % 4)
    halves = []
    for h in range(2):
        came = []
        for dx in (1, 2, 3):
            pairs = [
                (flat(c, xs, y, (xs + 2 * h + b) % 4, y), flat(c, (xs + dx) % 4, b, xs, y))
                for c in range(2)
                for xs in range(4)
                for y in range(2)
                for b in range(2)
            ]
            came.append(lax.ppermute(piece, AXES, pairs))
        halves.append(came)
    two = jnp.stack([pick(tiles, 1 - core), pick(tiles, 3 - core)])
    pairs = [
        (flat(c, x, y, x, y), flat(c, x, 1 - y, x, y))
        for c in range(2)
        for x in range(4)
        for y in range(2)
    ]
    beside = lax.ppermute(two, AXES, pairs)
    owner = (x == z) & (core == yh)
    way = (x - z) % 4
    mine = []
    for h in range(2):
        a, b, d = halves[h]
        got = jnp.where(way == 1, a, jnp.where(way == 2, b, jnp.where(way == 3, d, beside[h])))
        mine.append(jnp.where(owner, pick(tiles, core + 2 * h), got))
    mine = jnp.stack(mine)
    other = shift(mine, dk=1)
    even = jnp.where(core == 0, mine, other)
    odd = jnp.where(core == 0, other, mine)
    return jnp.stack([even[0], odd[0], even[1], odd[1]]).reshape(1024, 1024)


def sum_first(v, core, z):
    v = v.reshape(2, 256, PANEL)
    v = pick(v, core) + shift(pick(v, 1 - core), dk=1)
    v = v.reshape(4, 64, PANEL)
    got = [shift(pick(v, (z + d) % 4), dz=d) for d in (1, 3, 2)]
    return pick(v, z) + got[0] + got[1] + got[2]


def gathered(v, at, **axis):
    (name,) = axis
    full = jnp.zeros((4,) + v.shape, v.dtype)
    full = lax.dynamic_update_index_in_dim(full, v, at, 0)
    for d in (1, 3, 2):
        full = lax.dynamic_update_index_in_dim(full, shift(v, **{name: d}), (at - d) % 4, 0)
    return full


def sum_second(v, x, z):
    v = v.reshape(4, 16, PANEL)
    got = [shift(pick(v, (x + d) % 4), dx=d) for d in (1, 3, 2)]
    v = pick(v, x) + got[0] + got[1] + got[2]
    v = (v + shift(v, dc=1, dy=1)) + (shift(v, dc=1) + shift(v, dy=1))
    return gathered(v, z, dz=0)


def sum_third(v, x, core):
    v = gathered(v, x, dx=0)
    v = jnp.transpose(v, (1, 0, 2, 3)).reshape(256, PANEL)
    other = shift(v, dk=1)
    return jnp.concatenate([jnp.where(core == 0, v, other), jnp.where(core == 0, other, v)])


def tables(child_maps, parent_place):
    hit = child_maps[:, :, None] == jnp.arange(48, dtype=I32)
    slots = jnp.sum(jnp.where(hit, parent_place, 0), axis=2)
    hit = slots[:, :, None] == jnp.arange(48, dtype=I32)
    where = jnp.max(jnp.where(hit, jnp.arange(32, dtype=I32)[None, :, None], -1), axis=1)
    return slots, where


def body(child_blocks, child_panels, child_patterns, child_maps, parent_place, parent_front):
    ch, x, core, z, yh = (lax.axis_index(n).astype(I32) for n in AXES)
    r, c = x * 2 + core, z * 2 + yh
    slots, where = tables(child_maps, parent_place)
    e = parent_place[0], parent_place[1]
    ids = jnp.stack([ch, r, c, ch * 8 + r, core, z, yh, ch * 4 + x, e[0], e[1], x])
    panel = child_panels[0]
    partner = fetch_partner(panel, x, core, z, yh)
    send, diag, gcol = update(
        ids, slots, child_patterns, child_blocks[0], panel, partner, parent_front
    )
    own = lax.all_to_all(send, ("child", "x"), split_axis=0, concat_axis=0, tiled=True)

    diag = sum_first(diag, core, z)
    parts = strips(ids, gcol, parent_front)
    held = [pick(pick(where, ch), e[a]) // CT for a in range(2)]
    fronts = [e[a] // QT for a in range(2)]
    row = lax.broadcasted_iota(I32, (TILE, PANEL), 0)
    first = lax.broadcasted_iota(I32, (TILE, PANEL), 1) < TILE
    holder = jnp.where(
        row < FRONT,
        jnp.where(first, held[0], held[1]),
        jnp.where(first, fronts[0], fronts[1]),
    )
    away = (z - holder // 2 + 4) % 4
    strip = parts[0]
    for d in (1, 3, 2):
        strip = jnp.where(away == d, shift(parts[d], dz=d), strip)
    own, diag, strip = lax.optimization_barrier((own, diag, strip))

    other = shift(own, dk=1)
    send = route(ids, slots, where, own, other)
    kept, moved = pick(strip, yh), shift(pick(strip, 1 - yh), dy=1)
    strip = jnp.where(holder % 2 == yh, kept, moved)
    strip = jnp.stack([strip, shift(strip, dc=1)])
    diag = sum_second(diag, x, z)
    send, diag, strip = lax.optimization_barrier((send, diag, strip))
    recv = lax.all_to_all(send, ("z", "yh"), split_axis=0, concat_axis=0, tiled=True)

    diag = sum_third(diag, x, core)
    line = jnp.stack([strip] + [shift(strip, dx=d) for d in range(1, 4)])
    inv = inverse_factor(diag)
    gsend = compose(ids, where, line, shift(line, dk=1))
    recv, inv, gsend = lax.optimization_barrier((recv, inv, gsend))
    gx = lax.all_to_all(gsend, ("z", "yh"), split_axis=0, concat_axis=0, tiled=True)
    ph, plo, rows_f = panel_rows(ids, diag, inv, gx, shift(gx[:, 1], dk=1))
    return final(ids, where, ph, plo, rows_f, recv, parent_front)


def solution(mesh):
    fine = Mesh(mesh.devices.reshape(SIZES), AXES)
    rows, cols = ("x", "core"), ("z", "yh")
    return jax.shard_map(
        body,
        mesh=fine,
        in_specs=(
            P("child", rows, cols),
            P("child", rows, None),
            P(),
            P(),
            P(),
            P(("child", "x", "core"), cols),
        ),
        out_specs=P(("child", "x", "core"), cols),
        check_vma=False,
    )
```

time: 442 us -> 302 us (0.68); the launches traced: 436 us -> 301 us
  waiting for transfers between devices: 178 us -> 52.5 us
  starting transfers between devices: 142 us -> 104 us
  blocking collectives: 0 us -> 34.9 us
  Pallas kernels: 89.3 us -> 73.6 us
  between operations: 0.94 us -> 12.6 us
  local copies, waits for them, and re-layouts: 20.8 us -> 15.8 us
    ppermute x30 -> x29, waiting for transfers between devices: 170 us -> 51.6 us  [shift(): return lax.ppermute(v, AXES, pairs)]
    all_to_all x0 -> x1, blocking collectives: none -> 34.9 us  [body(): lax.all_to_all(gsend, ('z', 'yh'), split_axis=0, concat_axis=0, tiled=True)]
    ppermute x8 -> x0, starting transfers between devices: 34.9 us -> none  [cross(): return lax.ppermute(v, AXES, pairs)]
    pallas_call x1, Pallas kernels: 29.8 us -> 14.1 us  [final(): pl.pallas_call(final_kernel, grid_spec=pltpu.PrefetchScalarGridSpec(num_s...]
    ppermute x8 -> x0, waiting for transfers between devices: 8.03 us -> none  [cross(): return lax.ppermute(v, AXES, pairs)]
    unnamed x57 -> x24, local copies, waits for them, and re-layouts: 17.7 us -> 10.8 us
    ppermute x30 -> x29, starting transfers between devices: 86.9 us -> 84.2 us  [shift(): return lax.ppermute(v, AXES, pairs)]
  transfers between devices with their start and end apart: 47 -> 38, of which waited for: 20 -> 17; matrix products, arithmetic and copies ran while one was open for 0% -> 2% of each run, Pallas kernels for 10% -> 12%
where the time goes in v3:
time: 302 us; the launch traced here: 301 us
  starting transfers between devices  104 us (34%)
  Pallas kernels  73.6 us (24%)
  waiting for transfers between devices  52.5 us (17%)
  blocking collectives  34.9 us (12%)
  local copies, waits for them, and re-layouts  15.8 us (5%)
  between operations  12.6 us (4%)
  other arithmetic  7.95 us (3%)
    ppermute x29, starting transfers between devices, shift(): return lax.ppermute(v, AXES, pairs)  84.2 us
    ppermute x29, waiting for transfers between devices, shift(): return lax.ppermute(v, AXES, pairs)  51.6 us
    all_to_all x1, blocking collectives, body(): lax.all_to_all(gsend, ('z', 'yh'), split_axis=0, concat_axis=0, tiled=True)  34.9 us
    pallas_call x1, Pallas kernels, inverse_factor(): pl.pallas_call(inverse_kernel, out_shape=jax.ShapeDtypeStruct((PANEL, PAN...  29.7 us
    pallas_call x1, Pallas kernels, final(): pl.pallas_call(final_kernel, grid_spec=pltpu.PrefetchScalarGridSpec(num_s...  14.1 us
    pallas_call x1, Pallas kernels, update(): pl.pallas_call(update_kernel, grid_spec=pltpu.PrefetchScalarGridSpec(num_...  11 us
    unnamed x24, local copies, waits for them, and re-layouts  10.8 us
    pallas_call x1, Pallas kernels, panel_rows(): pl.pallas_call(panel_kernel, grid_spec=pltpu.PrefetchScalarGridSpec(num_s...  10.2 us
  transfers between devices with their start and end apart: 38, of which 17 were waited for; matrix products, arithmetic and copies ran while one was open for 2% of the time, Pallas kernels for 12%

profile of v3, /device:TPU:1, one launch (start us, length us, event | category | flops | bytes accessed | tf_op | source)
XLA Modules:
  0.0 301.4 jit_solution(14216683428570731257)
XLA Ops:
  0.0 2.4 constant_dynamic-slice_fusion.1
  2.4 1.5 collective-permute-start.6
  3.9 1.4 collective-permute-start.5
  5.5 1.3 collective-permute-start.3
  6.8 1.5 collective-permute-start.4
  8.2 1.4 collective-permute-start.2
  9.7 1.5 collective-permute-start.1
  11.2 1.5 collective-permute-start
  12.7 1.5 fusion.16
  14.2 1.1 pad_maximum_fusion.2
  15.3 25.4 %collective-permute-start.7 = (bf16[2,256,1024]{2,1,0:T(8,128)(2,1)}, bf16[2,256,1024]{2,1,0:T(8,128)(2,1)}, u32[]{:S(2)}, u32[]{:S(2)}) collective-permute-start(bf16[2,256,1024]{2,1,0:T(8,128)(2,1)} %pad_maximum_fusion.2), channel_id=1, source_target_pairs={{0,8},{1,9},{2,10},{3,11},{4,12},{5,13},{6,14},{7,15},{8,0},{9,1},... | collective-permute-start | bytes 3145736 | tf_op jit(solution)/shard_map/ppermute | solution.py:47
  41.0 2.4 collective-permute-done.7
  43.3 1.5 broadcast_select_fusion.1
  45.6 1.6 copy-done.3
  47.2 11.0 %shard_map.64 = (s16[8,272,1024]{2,1,0:T(8,128)(2,1)}, f32[512,512]{1,0:T(8,128)S(1)}, f32[1024,512]{1,0:T(8,128)S(1)}) custom-call(s32[11]{0:T(128)S(1)} %stack.80.ids, s32[2,32]{1,0:T(2,128)S(1)} %select_reduce_fusion.1.slots, s32[2,32,32]{2,1,0:T(8,128)S(1)} %copy-done.7, f32[1024,1024]{1,0:T(8,128)S(1)} %bitcast.128, bf16[1024,1024]{1,0:T(8,128)(2,1)S(1)} %bitcast.126, ...), custom_call_target="tpu_custom_call" | custom-call | flops 2147483648 | bytes 14680064 | tf_op jit(solution)/shard_map/pallas_call | solution.py:119
  58.2 1.3 copy-done.4
  59.5 4.9 %all-to-all-start = ((s16[8,272,1024]{2,1,0:T(8,128)(2,1)}), s16[8,272,1024]{2,1,0:T(8,128)(2,1)}, u32[]{:S(2)}, u32[]{:S(2)}) async-start(s16[8,272,1024]{2,1,0:T(8,128)(2,1)} %get-tuple-element.24), calls=%async_computation | async-start | bytes 8912896 | tf_op jit(solution)/shard_map/all_to_all | solution.py:642
  65.1 0.8 dynamic-slice_bitcast_fusion
  65.9 1.2 collective-permute-start.8
  79.8 2.3 copy-done
  82.1 1.7 shard_map.65
  83.8 1.5 collective-permute-start.12
  85.4 1.5 collective-permute-start.14
  86.8 0.8 broadcast_compare_fusion
  87.7 1.2 bitcast_add_fusion
  88.9 2.4 collective-permute-start.11
  91.3 7.8 %collective-permute-done.12 = s16[2,256,512]{2,1,0:T(8,128)(2,1)S(1)} collective-permute-done((s16[2,256,512]{2,1,0:T(8,128)(2,1)S(1)}, s16[2,256,512]{2,1,0:T(8,128)(2,1)S(1)}, u32[]{:S(2)}, u32[]{:S(2)}) %collective-permute-start.12) | collective-permute-done | bytes 524320 | tf_op jit(solution)/shard_map/ppermute | solution.py:47
  99.4 8.8 %collective-permute-done.13 = s16[2,256,512]{2,1,0:T(8,128)(2,1)S(1)} collective-permute-done((s16[2,256,512]{2,1,0:T(8,128)(2,1)S(1)}, s16[2,256,512]{2,1,0:T(8,128)(2,1)S(1)}, u32[]{:S(2)}, u32[]{:S(2)}) %collective-permute-start.13) | collective-permute-done | bytes 524320 | tf_op jit(solution)/shard_map/ppermute | solution.py:47
  108.2 2.4 collective-permute-done.14
  111.0 2.7 collective-permute-done.9
  113.7 2.3 collective-permute-done.11
  116.0 0.9 all-to-all-done.own
  116.9 0.9 collective-permute-start.15
  117.7 12.5 %collective-permute-start.16 = (f32[16,512]{1,0:T(8,128)S(1)}, f32[16,512]{1,0:T(8,128)S(1)}, u32[]{:S(2)}, u32[]{:S(2)}) collective-permute-start(f32[16,512]{1,0:T(8,128)S(1)} %get-tuple-element.61), channel_id=1, source_target_pairs={{0,16},{1,17},{2,18},{3,19},{4,20},{5,21},{6,22},{7,23},{8,24},{9,... | collective-permute-start | bytes 98312 | tf_op jit(solution)/shard_map/ppermute | solution.py:47
  130.2 4.4 %collective-permute-start.18 = (f32[16,512]{1,0:T(8,128)S(1)}, f32[16,512]{1,0:T(8,128)S(1)}, u32[]{:S(2)}, u32[]{:S(2)}) collective-permute-start(f32[16,512]{1,0:T(8,128)S(1)} %get-tuple-element.62), channel_id=1, source_target_pairs={{0,32},{1,33},{2,34},{3,35},{4,36},{5,37},{6,38},{7,39},{8,40},{9,... | collective-permute-start | bytes 98312 | tf_op jit(solution)/shard_map/ppermute | solution.py:47
  135.2 1.4 collective-permute-done.18
  136.6 0.8 collective-permute-done.17
  137.4 1.8 collective-permute-start.21
  139.8 1.2 collective-permute-start.19
  141.0 1.5 collective-permute-start.25
  142.5 1.7 collective-permute-done.19
  145.0 3.4 %collective-permute-start.23 = (f32[16,512]{1,0:T(8,128)S(1)}, f32[16,512]{1,0:T(8,128)S(1)}, u32[]{:S(2)}, u32[]{:S(2)}) collective-permute-start(f32[16,512]{1,0:T(8,128)S(1)} %get-tuple-element.44), channel_id=1, source_target_pairs={{0,6},{1,7},{2,0},{3,1},{4,2},{5,3},{6,4},{7,5},{8,14},{9,15},{10,... | collective-permute-start | bytes 98312 | tf_op jit(solution)/shard_map/ppermute | solution.py:47
  148.3 1.0 collective-permute-start.24
  150.3 2.3 collective-permute-done.24
  152.6 3.1 %collective-permute-done.26 = s16[256,512]{1,0:T(8,128)(2,1)S(1)} collective-permute-done((s16[256,512]{1,0:T(8,128)(2,1)S(1)}, s16[256,512]{1,0:T(8,128)(2,1)S(1)}, u32[]{:S(2)}, u32[]{:S(2)}) %collective-permute-start.26) | collective-permute-done | bytes 262176 | tf_op jit(solution)/shard_map/ppermute | solution.py:47
  155.8 2.7 shard_map.66
  158.5 2.8 copy-done.1
  161.3 4.9 %all-to-all-start.1 = ((s16[8,6,272,256]{3,2,1,0:T(8,128)(2,1)}), s16[8,6,272,256]{3,2,1,0:T(8,128)(2,1)}, u32[]{:S(2)}, u32[]{:S(2)}) async-start(s16[8,6,272,256]{3,2,1,0:T(8,128)(2,1)} %copy-done.1), calls=%async_computation.1 | async-start | bytes 13369344 | tf_op jit(solution)/shard_map/all_to_all | solution.py:668
  166.2 1.4 collective-permute-start.29
  167.6 0.8 collective-permute-start.28
  169.1 2.0 collective-permute-start.33
  171.2 2.3 collective-permute-done.27
  173.5 12.6 %collective-permute-start.30 = (f32[256,512]{1,0:T(8,128)S(1)}, f32[256,512]{1,0:T(8,128)S(1)}, u32[]{:S(2)}, u32[]{:S(2)}) collective-permute-start(f32[256,512]{1,0:T(8,128)S(1)} %bitcast.131), channel_id=1, source_target_pairs={{0,8},{1,9},{2,10},{3,11},{4,12},{5,13},{6,14},{7,15},{8,0},{9,1},... | collective-permute-start | bytes 1572872 | tf_op jit(solution)/shard_map/ppermute | solution.py:47
  186.1 10.6 %collective-permute-done.31 = s16[2,256,512]{2,1,0:T(8,128)(2,1)S(1)} collective-permute-done((s16[2,256,512]{2,1,0:T(8,128)(2,1)S(1)}, s16[2,256,512]{2,1,0:T(8,128)(2,1)S(1)}, u32[]{:S(2)}, u32[]{:S(2)}) %collective-permute-start.31) | collective-permute-done | bytes 524320 | tf_op jit(solution)/shard_map/ppermute | solution.py:47
  197.0 4.3 %collective-permute-start.34 = (s16[4,2,256,512]{3,2,1,0:T(8,128)(2,1)S(1)}, s16[4,2,256,512]{3,2,1,0:T(8,128)(2,1)S(1)}, u32[]{:S(2)}, u32[]{:S(2)}) collective-permute-start(s16[4,2,256,512]{3,2,1,0:T(8,128)(2,1)S(1)} %pad_add_fusion.own), channel_id=1, source_target_pairs={{0,8},{1,9},{2,10},{3,11},{4,12},{5,13},{6,14},{7,15},{8,0},{9,1},... | collective-permute-start | bytes 6291464 | tf_op jit(solution)/shard_map/ppermute | solution.py:47
  201.5 29.7 %shard_map.67.inv = f32[512,512]{1,0:T(8,128)S(1)} custom-call(f32[512,512]{1,0:T(8,128)S(1)} %pad_maximum_fusion.3.a_ref.diag), custom_call_target="tpu_custom_call" | custom-call | flops 17179869184 | bytes 2097152 | tf_op jit(solution)/shard_map/pallas_call | solution.py:394
  231.2 0.9 copy-done.8
  232.1 4.2 %shard_map.68 = s16[8,2,112,512]{3,2,1,0:T(8,128)(2,1)S(1)} custom-call(s32[11]{0:T(128)S(1)} %stack.80.ids, s32[2,48]{1,0:T(2,128)S(1)} %select_reduce_fusion.where, s16[4,2,256,512]{3,2,1,0:T(8,128)(2,1)S(1)} %pad_add_fusion.own, s16[4,2,256,512]{3,2,1,0:T(8,128)(2,1)S(1)} %collective-permute-done.34.other), custom_call_target="tpu_custom_call" | custom-call | bytes 6291456 | tf_op jit(solution)/shard_map/pallas_call | solution.py:244
  236.4 34.9 %all_to_all.15.gx = s16[8,2,112,512]{3,2,1,0:T(8,128)(2,1)S(1)} all-to-all(s16[8,2,112,512]{3,2,1,0:T(8,128)(2,1)S(1)} %shard_map.68), channel_id=1, replica_groups=mesh['child'=2,'x'=4,'core'=2,'z'=4,'yh'=2] {'z','yh'}, dimensions={0} | all-to-all | bytes 3670016 | tf_op jit(solution)/shard_map/all_to_all | solution.py:675
  271.4 2.0 collective-permute-start.35
  273.4 2.1 collective-permute-done.35.goth
  275.5 10.2 %shard_map.69 = (bf16[2304,512]{1,0:T(8,128)(2,1)}, bf16[2304,512]{1,0:T(8,128)(2,1)}, f32[768,512]{1,0:T(8,128)}) custom-call(s32[11]{0:T(128)S(1)} %stack.80.ids, f32[512,512]{1,0:T(8,128)S(1)} %pad_maximum_fusion.3.a_ref.diag, f32[512,512]{1,0:T(8,128)} %copy-done.8, s16[8,2,112,512]{3,2,1,0:T(8,128)(2,1)} %copy-done.9, ...), custom_call_target="tpu_custom_call" | custom-call | flops 8589934592 | bytes 16777216 | tf_op jit(solution)/shard_map/pallas_call | solution.py:461
  285.7 1.4 copy-done.6
  287.1 14.1 %shard_map.70 = f32[768,1536]{1,0:T(8,128)} custom-call(s32[11]{0:T(128)S(1)} %stack.80.ids, s32[2,48]{1,0:T(2,128)S(1)} %select_reduce_fusion.where, bf16[2304,512]{1,0:T(8,128)(2,1)} %get-tuple-element.39.lh.rh, bf16[2304,512]{1,0:T(8,128)(2,1)} %get-tuple-element.40.ll.rl, bf16[2304,512]{1,0:T(8,128)(2,1)} %get-tuple-element.39.lh.rh, ...), custom_call_target="tpu_custom_call" | custom-call | flops 4294967296 | bytes 20971520 | tf_op jit(solution)/shard_map/pallas_call | solution.py:523
  (83 shorter events, 7.5 us)
Async XLA Ops:
  0.0 12.6 %copy-start.2 = (bf16[1,1024,1024]{2,1,0:T(8,128)(2,1)S(1)}, bf16[1,1024,1024]{2,1,0:T(8,128)(2,1)}, u32[]{:S(2)}) copy-start(bf16[1,1024,1024]{2,1,0:T(8,128)(2,1)} %param.7) | copy-start | bytes 6291460
  2.4 7.2 %collective-permute-start.6 = (bf16[256,1024]{1,0:T(8,128)(2,1)}, bf16[256,1024]{1,0:T(8,128)(2,1)}, u32[]{:S(2)}, u32[]{:S(2)}) collective-permute-start(bf16[256,1024]{1,0:T(8,128)(2,1)} %get-tuple-element.51), channel_id=1, source_target_pairs={{4,48},{6,56},{13,49},{15,57},{22,2},{16,10},{31,3},{25,11},{32,20... | collective-permute-start | bytes 1572872 | tf_op jit(solution)/shard_map/ppermute | solution.py:567
  3.9 7.2 %collective-permute-start.5 = (bf16[256,1024]{1,0:T(8,128)(2,1)}, bf16[256,1024]{1,0:T(8,128)(2,1)}, u32[]{:S(2)}, u32[]{:S(2)}) collective-permute-start(bf16[256,1024]{1,0:T(8,128)(2,1)} %get-tuple-element.51), channel_id=1, source_target_pairs={{4,32},{6,40},{13,33},{15,41},{22,50},{16,58},{31,51},{25,59},{32,... | collective-permute-start | bytes 1572872 | tf_op jit(solution)/shard_map/ppermute | solution.py:567
  5.5 7.2 %collective-permute-start.3 = (bf16[2,256,1024]{2,1,0:T(8,128)(2,1)S(1)}, bf16[2,256,1024]{2,1,0:T(8,128)(2,1)}, u32[]{:S(2)}, u32[]{:S(2)}) collective-permute-start(bf16[2,256,1024]{2,1,0:T(8,128)(2,1)S(1)} %pad_maximum_fusion.1), channel_id=1, source_target_pairs={{0,8},{9,1},{18,26},{27,19},{36,44},{45,37},{54,62},{63,55},{64,72... | collective-permute-start | bytes 3145736 | tf_op jit(solution)/shard_map/ppermute | solution.py:576
  6.8 5.9 %collective-permute-start.4 = (bf16[256,1024]{1,0:T(8,128)(2,1)}, bf16[256,1024]{1,0:T(8,128)(2,1)}, u32[]{:S(2)}, u32[]{:S(2)}) collective-permute-start(bf16[256,1024]{1,0:T(8,128)(2,1)} %get-tuple-element.51), channel_id=1, source_target_pairs={{4,16},{6,24},{13,17},{15,25},{22,34},{16,42},{31,35},{25,43},{32,... | collective-permute-start | bytes 1572872 | tf_op jit(solution)/shard_map/ppermute | solution.py:567
  8.2 4.4 %collective-permute-start.2 = (bf16[256,1024]{1,0:T(8,128)(2,1)}, bf16[256,1024]{1,0:T(8,128)(2,1)}, u32[]{:S(2)}, u32[]{:S(2)}) collective-permute-start(bf16[256,1024]{1,0:T(8,128)(2,1)} %get-tuple-element.51), channel_id=1, source_target_pairs={{0,48},{2,56},{9,49},{11,57},{18,2},{20,10},{27,3},{29,11},{36,20}... | collective-permute-start | bytes 1572872 | tf_op jit(solution)/shard_map/ppermute | solution.py:567
  9.7 2.9 collective-permute-start.1
  11.2 1.5 collective-permute-start
  14.2 26.5 %copy-start.10 = (s32[48]{0:T(128)S(1)}, s32[48]{0:T(128)}, u32[]{:S(2)}) copy-start(s32[48]{0:T(128)} %param.10) | copy-start | bytes 580
  14.2 26.6 %copy-start.11 = (s32[2,32]{1,0:T(2,128)S(1)}, s32[2,32]{1,0:T(2,128)}, u32[]{:S(2)}) copy-start(s32[2,32]{1,0:T(2,128)} %param.9) | copy-start | bytes 772
  15.3 28.0 %collective-permute-start.7 = (bf16[2,256,1024]{2,1,0:T(8,128)(2,1)}, bf16[2,256,1024]{2,1,0:T(8,128)(2,1)}, u32[]{:S(2)}, u32[]{:S(2)}) collective-permute-start(bf16[2,256,1024]{2,1,0:T(8,128)(2,1)} %pad_maximum_fusion.2), channel_id=1, source_target_pairs={{0,8},{1,9},{2,10},{3,11},{4,12},{5,13},{6,14},{7,15},{8,0},{9,1},... | collective-permute-start | bytes 3145736 | tf_op jit(solution)/shard_map/ppermute | solution.py:47
  44.8 0.8 copy-start.7
  45.0 2.2 copy-start.3
  58.2 1.4 copy-start.4
  59.5 20.2 %copy-start.5 = (f32[1024,512]{1,0:T(8,128)S(1)}, f32[1024,512]{1,0:T(8,128)}, u32[]{:S(2)}) copy-start(f32[1024,512]{1,0:T(8,128)} %copy-done.4) | copy-start | bytes 6291460
  59.5 57.4 %all-to-all-start = ((s16[8,272,1024]{2,1,0:T(8,128)(2,1)}), s16[8,272,1024]{2,1,0:T(8,128)(2,1)}, u32[]{:S(2)}, u32[]{:S(2)}) async-start(s16[8,272,1024]{2,1,0:T(8,128)(2,1)} %get-tuple-element.24), calls=%async_computation | async-start | bytes 8912896 | tf_op jit(solution)/shard_map/all_to_all | solution.py:642
  65.9 21.7 %collective-permute-start.8 = (f32[256,512]{1,0:T(8,128)}, f32[256,512]{1,0:T(8,128)}, u32[]{:S(2)}, u32[]{:S(2)}) collective-permute-start(f32[256,512]{1,0:T(8,128)} %dynamic-slice_bitcast_fusion), channel_id=1, source_target_pairs={{0,8},{1,9},{2,10},{3,11},{4,12},{5,13},{6,14},{7,15},{8,0},{9,1},... | collective-permute-start | bytes 1572872 | tf_op jit(solution)/shard_map/ppermute | solution.py:47
  79.8 2.3 copy-start
  83.8 15.3 %collective-permute-start.12 = (s16[2,256,512]{2,1,0:T(8,128)(2,1)S(1)}, s16[2,256,512]{2,1,0:T(8,128)(2,1)S(1)}, u32[]{:S(2)}, u32[]{:S(2)}) collective-permute-start(s16[2,256,512]{2,1,0:T(8,128)(2,1)S(1)} %get-tuple-element.27), channel_id=1, source_target_pairs={{0,4},{1,5},{2,6},{3,7},{4,0},{5,1},{6,2},{7,3},{8,12},{9,13},{10,... | collective-permute-start | bytes 1572872 | tf_op jit(solution)/shard_map/ppermute | solution.py:47
  85.3 22.9 %collective-permute-start.13 = (s16[2,256,512]{2,1,0:T(8,128)(2,1)S(1)}, s16[2,256,512]{2,1,0:T(8,128)(2,1)S(1)}, u32[]{:S(2)}, u32[]{:S(2)}) collective-permute-start(s16[2,256,512]{2,1,0:T(8,128)(2,1)S(1)} %get-tuple-element.28), channel_id=1, source_target_pairs={{0,6},{1,7},{2,0},{3,1},{4,2},{5,3},{6,4},{7,5},{8,14},{9,15},{10,... | collective-permute-start | bytes 1572872 | tf_op jit(solution)/shard_map/ppermute | solution.py:47
  85.4 25.3 %collective-permute-start.14 = (s16[2,256,512]{2,1,0:T(8,128)(2,1)S(1)}, s16[2,256,512]{2,1,0:T(8,128)(2,1)S(1)}, u32[]{:S(2)}, u32[]{:S(2)}) collective-permute-start(s16[2,256,512]{2,1,0:T(8,128)(2,1)S(1)} %get-tuple-element.29), channel_id=1, source_target_pairs={{0,2},{1,3},{2,4},{3,5},{4,6},{5,7},{6,0},{7,1},{8,10},{9,11},{10,... | collective-permute-start | bytes 1572872 | tf_op jit(solution)/shard_map/ppermute | solution.py:47
  88.9 24.8 %collective-permute-start.9 = (f32[64,512]{1,0:T(8,128)S(1)}, f32[64,512]{1,0:T(8,128)S(1)}, u32[]{:S(2)}, u32[]{:S(2)}) collective-permute-start(f32[64,512]{1,0:T(8,128)S(1)} %get-tuple-element.58), channel_id=1, source_target_pairs={{0,2},{1,3},{2,4},{3,5},{4,6},{5,7},{6,0},{7,1},{8,10},{9,11},{10,... | collective-permute-start | bytes 393224 | tf_op jit(solution)/shard_map/ppermute | solution.py:47
  88.9 27.0 %collective-permute-start.11 = (f32[64,512]{1,0:T(8,128)S(1)}, f32[64,512]{1,0:T(8,128)S(1)}, u32[]{:S(2)}, u32[]{:S(2)}) collective-permute-start(f32[64,512]{1,0:T(8,128)S(1)} %get-tuple-element.59), channel_id=1, source_target_pairs={{0,4},{1,5},{2,6},{3,7},{4,0},{5,1},{6,2},{7,3},{8,12},{9,13},{10,... | collective-permute-start | bytes 393224 | tf_op jit(solution)/shard_map/ppermute | solution.py:47
  99.1 16.9 %collective-permute-start.10 = (f32[64,512]{1,0:T(8,128)S(1)}, f32[64,512]{1,0:T(8,128)S(1)}, u32[]{:S(2)}, u32[]{:S(2)}) collective-permute-start(f32[64,512]{1,0:T(8,128)S(1)} %get-tuple-element.60), channel_id=1, source_target_pairs={{0,6},{1,7},{2,0},{3,1},{4,2},{5,3},{6,4},{7,5},{8,14},{9,15},{10,... | collective-permute-start | bytes 393224 | tf_op jit(solution)/shard_map/ppermute | solution.py:47
  116.9 38.9 %collective-permute-start.15 = (s16[8,272,1024]{2,1,0:T(8,128)(2,1)}, s16[8,272,1024]{2,1,0:T(8,128)(2,1)}, u32[]{:S(2)}, u32[]{:S(2)}) collective-permute-start(s16[8,272,1024]{2,1,0:T(8,128)(2,1)} %all-to-all-done.own), channel_id=1, source_target_pairs={{0,8},{1,9},{2,10},{3,11},{4,12},{5,13},{6,14},{7,15},{8,0},{9,1},... | collective-permute-start | bytes 13369352 | tf_op jit(solution)/shard_map/ppermute | solution.py:47
  117.7 17.4 %collective-permute-start.16 = (f32[16,512]{1,0:T(8,128)S(1)}, f32[16,512]{1,0:T(8,128)S(1)}, u32[]{:S(2)}, u32[]{:S(2)}) collective-permute-start(f32[16,512]{1,0:T(8,128)S(1)} %get-tuple-element.61), channel_id=1, source_target_pairs={{0,16},{1,17},{2,18},{3,19},{4,20},{5,21},{6,22},{7,23},{8,24},{9,... | collective-permute-start | bytes 98312 | tf_op jit(solution)/shard_map/ppermute | solution.py:47
  130.2 6.3 %collective-permute-start.18 = (f32[16,512]{1,0:T(8,128)S(1)}, f32[16,512]{1,0:T(8,128)S(1)}, u32[]{:S(2)}, u32[]{:S(2)}) collective-permute-start(f32[16,512]{1,0:T(8,128)S(1)} %get-tuple-element.62), channel_id=1, source_target_pairs={{0,32},{1,33},{2,34},{3,35},{4,36},{5,37},{6,38},{7,39},{8,40},{9,... | collective-permute-start | bytes 98312 | tf_op jit(solution)/shard_map/ppermute | solution.py:47
  134.6 2.8 collective-permute-start.17
  137.4 5.1 %collective-permute-start.21 = (f32[16,512]{1,0:T(8,128)S(1)}, f32[16,512]{1,0:T(8,128)S(1)}, u32[]{:S(2)}, u32[]{:S(2)}) collective-permute-start(f32[16,512]{1,0:T(8,128)S(1)} %fusion.23), channel_id=1, source_target_pairs={{0,1},{1,0},{2,3},{3,2},{4,5},{5,4},{6,7},{7,6},{8,9},{9,8},{10,11... | collective-permute-start | bytes 98312 | tf_op jit(solution)/shard_map/ppermute | solution.py:47
  139.2 3.4 %collective-permute-start.20 = (f32[16,512]{1,0:T(8,128)S(1)}, f32[16,512]{1,0:T(8,128)S(1)}, u32[]{:S(2)}, u32[]{:S(2)}) collective-permute-start(f32[16,512]{1,0:T(8,128)S(1)} %fusion.23), channel_id=1, source_target_pairs={{0,64},{1,65},{2,66},{3,67},{4,68},{5,69},{6,70},{7,71},{8,72},{9,... | collective-permute-start | bytes 98312 | tf_op jit(solution)/shard_map/ppermute | solution.py:47
  139.8 4.4 %collective-permute-start.19 = (f32[16,512]{1,0:T(8,128)S(1)}, f32[16,512]{1,0:T(8,128)S(1)}, u32[]{:S(2)}, u32[]{:S(2)}) collective-permute-start(f32[16,512]{1,0:T(8,128)S(1)} %fusion.23), channel_id=1, source_target_pairs={{0,65},{1,64},{2,67},{3,66},{4,69},{5,68},{6,71},{7,70},{8,73},{9,... | collective-permute-start | bytes 98312 | tf_op jit(solution)/shard_map/ppermute | solution.py:47
  141.0 8.8 %collective-permute-start.25 = (s16[256,512]{1,0:T(8,128)(2,1)S(1)}, s16[256,512]{1,0:T(8,128)(2,1)S(1)}, u32[]{:S(2)}, u32[]{:S(2)}) collective-permute-start(s16[256,512]{1,0:T(8,128)(2,1)S(1)} %dynamic-slice_bitcast_fusion.2), channel_id=1, source_target_pairs={{0,1},{1,0},{2,3},{3,2},{4,5},{5,4},{6,7},{7,6},{8,9},{9,8},{10,11... | collective-permute-start | bytes 786440 | tf_op jit(solution)/shard_map/ppermute | solution.py:47
  144.2 5.6 %collective-permute-start.22 = (f32[16,512]{1,0:T(8,128)S(1)}, f32[16,512]{1,0:T(8,128)S(1)}, u32[]{:S(2)}, u32[]{:S(2)}) collective-permute-start(f32[16,512]{1,0:T(8,128)S(1)} %get-tuple-element.44), channel_id=1, source_target_pairs={{0,2},{1,3},{2,4},{3,5},{4,6},{5,7},{6,0},{7,1},{8,10},{9,11},{10,... | collective-permute-start | bytes 98312 | tf_op jit(solution)/shard_map/ppermute | solution.py:47
  145.0 5.3 %collective-permute-start.23 = (f32[16,512]{1,0:T(8,128)S(1)}, f32[16,512]{1,0:T(8,128)S(1)}, u32[]{:S(2)}, u32[]{:S(2)}) collective-permute-start(f32[16,512]{1,0:T(8,128)S(1)} %get-tuple-element.44), channel_id=1, source_target_pairs={{0,6},{1,7},{2,0},{3,1},{4,2},{5,3},{6,4},{7,5},{8,14},{9,15},{10,... | collective-permute-start | bytes 98312 | tf_op jit(solution)/shard_map/ppermute | solution.py:47
  148.3 4.3 %collective-permute-start.24 = (f32[16,512]{1,0:T(8,128)S(1)}, f32[16,512]{1,0:T(8,128)S(1)}, u32[]{:S(2)}, u32[]{:S(2)}) collective-permute-start(f32[16,512]{1,0:T(8,128)S(1)} %get-tuple-element.44), channel_id=1, source_target_pairs={{0,4},{1,5},{2,6},{3,7},{4,0},{5,1},{6,2},{7,3},{8,12},{9,13},{10,... | collective-permute-start | bytes 98312 | tf_op jit(solution)/shard_map/ppermute | solution.py:47
  150.2 5.6 %collective-permute-start.26 = (s16[256,512]{1,0:T(8,128)(2,1)S(1)}, s16[256,512]{1,0:T(8,128)(2,1)S(1)}, u32[]{:S(2)}, u32[]{:S(2)}) collective-permute-start(s16[256,512]{1,0:T(8,128)(2,1)S(1)} %fusion.18), channel_id=1, source_target_pairs={{0,64},{1,65},{2,66},{3,67},{4,68},{5,69},{6,70},{7,71},{8,72},{9,... | collective-permute-start | bytes 786440 | tf_op jit(solution)/shard_map/ppermute | solution.py:47
  158.5 2.8 copy-start.1
  161.3 75.0 %all-to-all-start.1 = ((s16[8,6,272,256]{3,2,1,0:T(8,128)(2,1)}), s16[8,6,272,256]{3,2,1,0:T(8,128)(2,1)}, u32[]{:S(2)}, u32[]{:S(2)}) async-start(s16[8,6,272,256]{3,2,1,0:T(8,128)(2,1)} %copy-done.1), calls=%async_computation.1 | async-start | bytes 13369344 | tf_op jit(solution)/shard_map/all_to_all | solution.py:668
  166.2 7.2 %collective-permute-start.29 = (f32[4,16,512]{2,1,0:T(8,128)S(1)}, f32[4,16,512]{2,1,0:T(8,128)S(1)}, u32[]{:S(2)}, u32[]{:S(2)}) collective-permute-start(f32[4,16,512]{2,1,0:T(8,128)S(1)} %bitcast_dynamic-update-slice_fusion.4), channel_id=1, source_target_pairs={{0,32},{1,33},{2,34},{3,35},{4,36},{5,37},{6,38},{7,39},{8,40},{9,... | collective-permute-start | bytes 393224 | tf_op jit(solution)/shard_map/ppermute | solution.py:47
  167.6 5.8 %collective-permute-start.28 = (f32[4,16,512]{2,1,0:T(8,128)S(1)}, f32[4,16,512]{2,1,0:T(8,128)S(1)}, u32[]{:S(2)}, u32[]{:S(2)}) collective-permute-start(f32[4,16,512]{2,1,0:T(8,128)S(1)} %bitcast_dynamic-update-slice_fusion.4), channel_id=1, source_target_pairs={{0,48},{1,49},{2,50},{3,51},{4,52},{5,53},{6,54},{7,55},{8,56},{9,... | collective-permute-start | bytes 393224 | tf_op jit(solution)/shard_map/ppermute | solution.py:47
  168.4 5.0 %collective-permute-start.27 = (f32[4,16,512]{2,1,0:T(8,128)S(1)}, f32[4,16,512]{2,1,0:T(8,128)S(1)}, u32[]{:S(2)}, u32[]{:S(2)}) collective-permute-start(f32[4,16,512]{2,1,0:T(8,128)S(1)} %bitcast_dynamic-update-slice_fusion.4), channel_id=1, source_target_pairs={{0,16},{1,17},{2,18},{3,19},{4,20},{5,21},{6,22},{7,23},{8,24},{9,... | collective-permute-start | bytes 393224 | tf_op jit(solution)/shard_map/ppermute | solution.py:47
  169.1 17.0 %collective-permute-start.33 = (s16[2,256,512]{2,1,0:T(8,128)(2,1)S(1)}, s16[2,256,512]{2,1,0:T(8,128)(2,1)S(1)}, u32[]{:S(2)}, u32[]{:S(2)}) collective-permute-start(s16[2,256,512]{2,1,0:T(8,128)(2,1)S(1)} %pad_add_fusion.1), channel_id=1, source_target_pairs={{0,48},{1,49},{2,50},{3,51},{4,52},{5,53},{6,54},{7,55},{8,56},{9,... | collective-permute-start | bytes 1572872 | tf_op jit(solution)/shard_map/ppermute | solution.py:47
  171.1 15.1 %collective-permute-start.32 = (s16[2,256,512]{2,1,0:T(8,128)(2,1)S(1)}, s16[2,256,512]{2,1,0:T(8,128)(2,1)S(1)}, u32[]{:S(2)}, u32[]{:S(2)}) collective-permute-start(s16[2,256,512]{2,1,0:T(8,128)(2,1)S(1)} %pad_add_fusion.1), channel_id=1, source_target_pairs={{0,32},{1,33},{2,34},{3,35},{4,36},{5,37},{6,38},{7,39},{8,40},{9,... | collective-permute-start | bytes 1572872 | tf_op jit(solution)/shard_map/ppermute | solution.py:47
  173.4 23.3 %collective-permute-start.31 = (s16[2,256,512]{2,1,0:T(8,128)(2,1)S(1)}, s16[2,256,512]{2,1,0:T(8,128)(2,1)S(1)}, u32[]{:S(2)}, u32[]{:S(2)}) collective-permute-start(s16[2,256,512]{2,1,0:T(8,128)(2,1)S(1)} %pad_add_fusion.1), channel_id=1, source_target_pairs={{0,16},{1,17},{2,18},{3,19},{4,20},{5,21},{6,22},{7,23},{8,24},{9,... | collective-permute-start | bytes 1572872 | tf_op jit(solution)/shard_map/ppermute | solution.py:47
  173.5 27.8 %collective-permute-start.30 = (f32[256,512]{1,0:T(8,128)S(1)}, f32[256,512]{1,0:T(8,128)S(1)}, u32[]{:S(2)}, u32[]{:S(2)}) collective-permute-start(f32[256,512]{1,0:T(8,128)S(1)} %bitcast.131), channel_id=1, source_target_pairs={{0,8},{1,9},{2,10},{3,11},{4,12},{5,13},{6,14},{7,15},{8,0},{9,1},... | collective-permute-start | bytes 1572872 | tf_op jit(solution)/shard_map/ppermute | solution.py:47
  197.0 35.2 %collective-permute-start.34 = (s16[4,2,256,512]{3,2,1,0:T(8,128)(2,1)S(1)}, s16[4,2,256,512]{3,2,1,0:T(8,128)(2,1)S(1)}, u32[]{:S(2)}, u32[]{:S(2)}) collective-permute-start(s16[4,2,256,512]{3,2,1,0:T(8,128)(2,1)S(1)} %pad_add_fusion.own), channel_id=1, source_target_pairs={{0,8},{1,9},{2,10},{3,11},{4,12},{5,13},{6,14},{7,15},{8,0},{9,1},... | collective-permute-start | bytes 6291464 | tf_op jit(solution)/shard_map/ppermute | solution.py:47
  231.2 1.0 copy-start.8
  271.3 4.2 %copy-start.9 = (s16[8,2,112,512]{3,2,1,0:T(8,128)(2,1)}, s16[8,2,112,512]{3,2,1,0:T(8,128)(2,1)S(1)}, u32[]{:S(2)}) copy-start(s16[8,2,112,512]{3,2,1,0:T(8,128)(2,1)S(1)} %all_to_all.15.gx) | copy-start | bytes 5505028
  271.4 4.1 %collective-permute-start.35 = (s16[8,112,512]{2,1,0:T(8,128)(2,1)S(1)}, s16[8,112,512]{2,1,0:T(8,128)(2,1)S(1)}, u32[]{:S(2)}, u32[]{:S(2)}) collective-permute-start(s16[8,112,512]{2,1,0:T(8,128)(2,1)S(1)} %slice_bitcast_fusion), channel_id=1, source_target_pairs={{0,8},{1,9},{2,10},{3,11},{4,12},{5,13},{6,14},{7,15},{8,0},{9,1},... | collective-permute-start | bytes 2752520 | tf_op jit(solution)/shard_map/ppermute | solution.py:47
  285.7 1.4 copy-start.6

commit v4 on v3

--- a/solution.py
+++ b/solution.py
@@ -13,7 +13,8 @@
 RT = 3
 QT = 6
 STRIP = 32
-SROWS = RT * STRIP + CODE
+GROWS = 2 * RT * STRIP + CODE
+CROWS = 2 * RT * TILE + CODE
 AXES = ("child", "x", "core", "z", "yh")
 SIZES = (2, 4, 2, 4, 2)
 MIB = 1 << 20
@@ -50,8 +51,9 @@
 def encode(u):
     top = jnp.max(jnp.abs(u), axis=0, keepdims=True)
     code = jnp.ceil(jnp.log2(jnp.maximum(top, 1e-30)) * 128.0)
-    q = jnp.clip(jnp.floor(u * jnp.exp2(15.0 - code * (1.0 / 128.0)) + 0.5), -32767.0, 32767.0)
-    return q.astype(I32).astype(I16), code
+    scale = jnp.exp2(15.0 - code * (1.0 / 128.0)) * (32766.0 / 32768.0)
+    q = (u * scale + 32768.5).astype(I32) - 32768
+    return q.astype(I16), code
 
 
 def scale_rows(code):
@@ -62,11 +64,12 @@
     return q.astype(I32).astype(F32)
 
 
-def column_scale(codes):
-    return jnp.exp2(as_float(codes)[0:1, :] * (1.0 / 128.0) - 15.0)
-
-
-def update_kernel(ids, slots, pat, blk, pan, par, front, send, diag, gcol, tile, sem):
+def column_scale(codes, row=0):
+    code = as_float(codes)[row : row + 1, :]
+    return jnp.exp2(code * (1.0 / 128.0) - 15.0) * (32768.0 / 32766.0)
+
+
+def update_kernel(ids, slots, pat, blk, pan, mine, other, front, send, diag, gcol, tile, sem):
     i = pl.program_id(0)
     ch, r, c, g = ids[0], ids[1], ids[2], ids[3]
     e = (ids[8], ids[9])
@@ -89,10 +92,15 @@
                     diag[a * TILE : (a + 1) * TILE, b * TILE : (b + 1) * TILE] = tile[...]
 
     si = slots[ch, r * CT + i]
-    for j in range(CT):
-        cols = slice(j * TILE, (j + 1) * TILE)
+    for n in range(CT):
+        half = mine if n < 2 else other
+        j = (ids[4] if n < 2 else 1 - ids[4]) * 2 + n % 2
+        cols = pl.ds(pl.multiple_of(j * TILE, TILE), TILE)
         prod = lax.dot_general(
-            pan[...], par[cols, :], (((1,), (1,)), ((), ())), preferred_element_type=F32
+            pan[...],
+            half[(n % 2) * TILE : (n % 2 + 1) * TILE, :],
+            (((1,), (1,)), ((), ())),
+            preferred_element_type=F32,
         )
         u = (blk[:, cols] - prod) * pat[ch, r * CT + i, c * CT + j].astype(F32)
         q, code = encode(u)
@@ -112,7 +120,7 @@
                         diag[a * TILE : (a + 1) * TILE, at] += u
 
 
-def update(ids, slots, pat, blk, pan, par, front):
+def update(ids, slots, pat, blk, pan, mine, other, front):
     def slot(i, ids, slots, pat):
         return slots[ids[0], ids[1] * CT + i] // QT, 0, 0
 
@@ -124,7 +132,8 @@
             in_specs=[
                 pl.BlockSpec((TILE, 1024), lambda i, *s: (i, 0)),
                 pl.BlockSpec((TILE, 1024), lambda i, *s: (i, 0)),
-                pl.BlockSpec((1024, 1024), lambda i, *s: (0, 0)),
+                pl.BlockSpec((512, 1024), lambda i, *s: (0, 0)),
+                pl.BlockSpec((512, 1024), lambda i, *s: (0, 0)),
                 pl.BlockSpec(memory_space=pl.ANY),
             ],
             out_specs=[
@@ -135,13 +144,13 @@
             scratch_shapes=[pltpu.VMEM((TILE, TILE), F32), pltpu.SemaphoreType.DMA],
         ),
         out_shape=[
-            jax.ShapeDtypeStruct((8, TILE + CODE, 1024), I16),
-            jax.ShapeDtypeStruct((PANEL, PANEL), F32),
-            jax.ShapeDtypeStruct((CT * TILE, PANEL), F32),
+            pltpu.HBM((8, TILE + CODE, 1024), I16),
+            pltpu.HBM((PANEL, PANEL), F32),
+            pltpu.HBM((CT * TILE, PANEL), F32),
         ],
         compiler_params=pltpu.CompilerParams(vmem_limit_bytes=40 * MIB),
         cost_estimate=pl.CostEstimate(flops=1 << 31, bytes_accessed=14 * MIB, transcendentals=0),
-    )(ids, slots, pat, blk, pan, par, front)
+    )(ids, slots, pat, blk, pan, mine, other, front)
 
 
 def strips_kernel(ids, gcol, front, *rest):
@@ -198,7 +207,7 @@
 FRONT_CODE = FRONT + RT * STRIP
 
 
-def compose_kernel(ids, where, own, other, out, acc, kept):
+def compose_kernel(ids, where, own, other, out, acc, kept, kcode):
     q = pl.program_id(0)
     ch, core, k, x = ids[0], ids[4], ids[7], ids[10]
     half = lax.broadcasted_iota(I32, (STRIP, PANEL), 1) < TILE
@@ -230,13 +239,15 @@
     @pl.when(q == 0)
     def _():
         v, code = group(k)
-        kept[0 : RT * STRIP, :] = v
-        kept[RT * STRIP :, :] = scale_rows(code)
+        kept[...] = v
+        kcode[...] = jnp.broadcast_to(code, kcode.shape)
 
     v, code = group(q)
-    out[0, 0] = kept[...]
-    out[0, 1, 0 : RT * STRIP, :] = v
-    out[0, 1, RT * STRIP :, :] = scale_rows(code)
+    out[0, 0 : RT * STRIP, :] = kept[...]
+    out[0, RT * STRIP : 2 * RT * STRIP, :] = v
+    row = lax.broadcasted_iota(I32, (CODE, PANEL), 0)
+    both = jnp.where(row == 0, kcode[0:1, :], code)
+    out[0, 2 * RT * STRIP :, :] = both.astype(I32).astype(I16)
 
 
 def compose(ids, where, own, other):
@@ -247,43 +258,59 @@
             num_scalar_prefetch=2,
             grid=(8,),
             in_specs=[whole] * 2,
-            out_specs=pl.BlockSpec((1, 2, SROWS, PANEL), lambda i, *s: (i, 0, 0, 0)),
+            out_specs=pl.BlockSpec((1, GROWS, PANEL), lambda i, *s: (i, 0, 0)),
             scratch_shapes=[
                 pltpu.VMEM((RT * STRIP, PANEL), F32),
-                pltpu.VMEM((SROWS, PANEL), I16),
+                pltpu.VMEM((RT * STRIP, PANEL), I16),
+                pltpu.VMEM((8, PANEL), F32),
             ],
         ),
-        out_shape=jax.ShapeDtypeStruct((8, 2, SROWS, PANEL), I16),
+        out_shape=pltpu.HBM((8, GROWS, PANEL), I16),
         compiler_params=pltpu.CompilerParams(vmem_limit_bytes=24 * MIB),
         cost_estimate=pl.CostEstimate(flops=0, bytes_accessed=6 * MIB, transcendentals=0),
     )(ids, where, own, other)
 
 
-def route_kernel(ids, slots, where, own, other, send, sems):
+def route_kernel(ids, slots, where, own, other, send, codes, sems):
     c, g, core = ids[2], ids[3], ids[4]
+    rows = [where[ch, g * RT + p] for ch in range(2) for p in range(RT)]
 
     def each(act):
-        for ch in range(2):
-            for p in range(RT):
-                i = rows[ch * RT + p]
-                src = ch * 4 + i // 8
-                for j in range(CT):
-                    q = slots[ch, c * CT + j] // QT
-                    sem = sems.at[(ch * RT + p) * CT + j]
-                    for here, buf in ((True, own), (False, other)):
-
-                        @pl.when((i >= 0) & (((i // 4) % 2 == core) == here))
-                        def _():
-                            copy = pltpu.make_async_copy(
-                                buf.at[src, :, pl.ds(j * TILE, TILE)],
-                                send.at[q, ch * RT + p],
-                                sem,
+        for m in range(2 * RT):
+            i = rows[m]
+            src = (m // RT) * 4 + i // 8
+            for here, buf in ((True, own), (False, other)):
+
+                @pl.when((i >= 0) & (((i // CT) % 2 == core) == here))
+                def _():
+                    act(
+                        pltpu.make_async_copy(
+                            buf.at[src, pl.ds(TILE, CODE), :], codes.at[m], sems.at[m * 5 + CT]
+                        )
+                    )
+                    for j in range(CT):
+                        q = slots[m // RT, c * CT + j] // QT
+                        act(
+                            pltpu.make_async_copy(
+                                buf.at[src, pl.ds(0, TILE), pl.ds(j * TILE, TILE)],
+                                send.at[q, pl.ds(m * TILE, TILE), :],
+                                sems.at[m * 5 + j],
                             )
-                            act(copy)
-
-    rows = [where[ch, g * RT + p] for ch in range(2) for p in range(RT)]
+                        )
+
     each(lambda copy: copy.start())
     each(lambda copy: copy.wait())
+    line = lax.broadcasted_iota(I32, (CODE, TILE), 0)
+    for ch in range(2):
+        for j in range(CT):
+            q = slots[ch, c * CT + j] // QT
+            at = (q, slice(2 * RT * TILE, CROWS), slice(None))
+            v = send[at].astype(I32)
+            for p in range(RT):
+                m = ch * RT + p
+                own_codes = codes[m, :, j * TILE : (j + 1) * TILE].astype(I32)
+                v = jnp.where(line == m, own_codes, v)
+            send[at] = v.astype(I16)
 
 
 def route(ids, slots, where, own, other):
@@ -293,19 +320,16 @@
             num_scalar_prefetch=3,
             grid=(1,),
             in_specs=[pl.BlockSpec(memory_space=pl.ANY)] * 2,
-            out_specs=pl.BlockSpec((8, 2 * RT, TILE + CODE, TILE), lambda i, *s: (0, 0, 0, 0)),
-            scratch_shapes=[pltpu.SemaphoreType.DMA((24,))],
+            out_specs=pl.BlockSpec((8, CROWS, TILE), lambda i, *s: (0, 0, 0)),
+            scratch_shapes=[
+                pltpu.VMEM((2 * RT, CODE, 1024), I16),
+                pltpu.SemaphoreType.DMA((2 * RT * 5,)),
+            ],
         ),
-        out_shape=jax.ShapeDtypeStruct((8, 2 * RT, TILE + CODE, TILE), I16),
+        out_shape=pltpu.HBM((8, CROWS, TILE), I16),
         compiler_params=pltpu.CompilerParams(vmem_limit_bytes=32 * MIB),
         cost_estimate=pl.CostEstimate(flops=0, bytes_accessed=8 * MIB, transcendentals=0),
     )(ids, slots, where, own, other)
-
-
-def decode_strip(ref, lead=()):
-    q = ref[lead + (slice(0, RT * STRIP), slice(None))]
-    codes = ref[lead + (slice(RT * STRIP, SROWS), slice(None))]
-    return as_float(q) * column_scale(codes)
 
 
 def nt(a, b):
@@ -412,102 +436,101 @@
     return one(a[0], b[0]) + (one(a[0], b[1]) + one(a[1], b[0]))
 
 
-def panel_kernel(ids, diag, inv, gx, goth, ph, plo, rows_f, gbuf):
+def final_kernel(
+    ids, where, diag, inv, gx, goth, recv, front, out,
+    gbuf, rows_f, lh, ll, ih, il, tiles, codes, tsem,
+):
+    t = pl.program_id(0)
     c, g, core = ids[2], ids[3], ids[4]
-    inv2 = split(inv[...])
-
-    def fill(base, ref, lead, first):
-        for s in range(8):
-            v = decode_strip(ref, lead(s))
-            for t in range(RT):
-                gbuf[base + t * TILE + s * STRIP : base + t * TILE + (s + 1) * STRIP, :] = v[
-                    t * STRIP : (t + 1) * STRIP, :
-                ]
-        for t in range(RT):
-            for a in range(2):
-
-                @pl.when(first + t == ids[8 + a])
-                def _():
-                    gbuf[base + t * TILE : base + (t + 1) * TILE, :] = diag[
-                        a * TILE : (a + 1) * TILE, :
-                    ]
-
-    fill(0, gx, lambda s: (s, 0), g * RT)
-    for b in range(2):
-        base = RT * TILE * (1 + b)
-
-        @pl.when(core == b)
-        def _():
-            fill(base, gx, lambda s: (s, 1), c * QT + b * RT)
-
-        @pl.when(core != b)
-        def _():
-            fill(base, goth, lambda s: (s,), c * QT + b * RT)
-
-    for t in range(3):
-        rows = slice(t * RT * TILE, (t + 1) * RT * TILE)
-        v = dot3(split(gbuf[rows, :]), inv2)
-        hi, lo = split(v)
-        ph[rows, :] = hi
-        plo[rows, :] = lo
-        if t == 0:
-            rows_f[...] = v
-
-
-def panel_rows(ids, diag, inv, gx, goth):
-    def whole(*shape):
-        return pl.BlockSpec(shape, lambda i, *s: (0,) * len(shape))
-
-    return pl.pallas_call(
-        panel_kernel,
-        grid_spec=pltpu.PrefetchScalarGridSpec(
-            num_scalar_prefetch=1,
-            grid=(1,),
-            in_specs=[whole(PANEL, PANEL)] * 2
-            + [whole(8, 2, SROWS, PANEL), whole(8, SROWS, PANEL)],
-            out_specs=[whole(9 * TILE, PANEL)] * 2 + [whole(RT * TILE, PANEL)],
-            scratch_shapes=[pltpu.VMEM((9 * TILE, PANEL), F32)],
-        ),
-        out_shape=[jax.ShapeDtypeStruct((9 * TILE, PANEL), BF16)] * 2
-        + [jax.ShapeDtypeStruct((RT * TILE, PANEL), F32)],
-        compiler_params=pltpu.CompilerParams(vmem_limit_bytes=52 * MIB),
-        cost_estimate=pl.CostEstimate(flops=1 << 33, bytes_accessed=16 * MIB, transcendentals=0),
-    )(ids, diag, inv, gx, goth)
-
-
-def final_kernel(ids, where, lh, ll, rh, rl, rows_f, recv, front, out, tiles, tsem):
-    t = pl.program_id(0)
-    c, g = ids[2], ids[3]
     col = c * QT + t
     js = [where[ch, col] for ch in range(2)]
     there = [[where[ch, g * RT + p] >= 0 for p in range(RT)] for ch in range(2)]
 
     def each(act):
         for ch in range(2):
+            src = js[ch] // CT
+
+            @pl.when(js[ch] >= 0)
+            def _():
+                act(
+                    pltpu.make_async_copy(
+                        recv.at[src, pl.ds(2 * RT * TILE, CODE), :],
+                        codes.at[ch],
+                        tsem.at[2 * RT + ch],
+                    )
+                )
+
             for p in range(RT):
+                m = ch * RT + p
 
                 @pl.when(there[ch][p] & (js[ch] >= 0))
                 def _():
                     act(
                         pltpu.make_async_copy(
-                            recv.at[js[ch] // CT, ch * RT + p],
-                            tiles.at[ch * RT + p],
-                            tsem.at[ch * RT + p],
+                            recv.at[src, pl.ds(m * TILE, TILE), :], tiles.at[m], tsem.at[m]
                         )
                     )
 
     each(lambda copy: copy.start())
-    out[...] = front[...] - dot3((lh[...], ll[...]), (rh[...], rl[...]))
+
+    @pl.when(t == 0)
+    def _():
+        hi, lo = split(inv[...])
+        ih[...] = hi
+        il[...] = lo
+        for s in range(8):
+            scale = column_scale(gx[s, 2 * RT * STRIP :, :], 0)
+            v = as_float(gx[s, 0 : RT * STRIP, :]) * scale
+            for p in range(RT):
+                gbuf[p * TILE + s * STRIP : p * TILE + (s + 1) * STRIP, :] = v[
+                    p * STRIP : (p + 1) * STRIP, :
+                ]
+        for p in range(RT):
+            for a in range(2):
+
+                @pl.when(g * RT + p == ids[8 + a])
+                def _():
+                    gbuf[p * TILE : (p + 1) * TILE, :] = diag[a * TILE : (a + 1) * TILE, :]
+
+        v = dot3(split(gbuf[...]), (ih[...], il[...]))
+        rows_f[...] = v
+        hi, lo = split(v)
+        lh[...] = hi
+        ll[...] = lo
+
+    side = pl.multiple_of((t % RT) * STRIP, STRIP)
+
+    @pl.when(t // RT == core)
+    def _():
+        for s in range(8):
+            gbuf[s * STRIP : (s + 1) * STRIP, :] = as_float(
+                gx[s, pl.ds(RT * STRIP + side, STRIP), :]
+            ) * column_scale(gx[s, 2 * RT * STRIP :, :], 1)
+
+    @pl.when(t // RT != core)
+    def _():
+        for s in range(8):
+            gbuf[s * STRIP : (s + 1) * STRIP, :] = as_float(
+                goth[s, pl.ds(side, STRIP), :]
+            ) * column_scale(goth[s, RT * STRIP :, :], 1)
+
+    for a in range(2):
+
+        @pl.when(col == ids[8 + a])
+        def _():
+            gbuf[0:TILE, :] = diag[a * TILE : (a + 1) * TILE, :]
+
+    right = split(dot3(split(gbuf[0:TILE, :]), (ih[...], il[...])))
+    out[...] = front[...] - dot3((lh[...], ll[...]), right)
     each(lambda copy: copy.wait())
     for p in range(RT):
         rows = slice(p * TILE, (p + 1) * TILE)
         for ch in range(2):
+            m = ch * RT + p
 
             @pl.when(there[ch][p] & (js[ch] >= 0))
             def _():
-                out[rows, :] += as_float(tiles[ch * RT + p, 0:TILE, :]) * column_scale(
-                    tiles[ch * RT + p, TILE:, :]
-                )
+                out[rows, :] += as_float(tiles[m]) * column_scale(codes[ch], m)
 
     for a in range(2):
 
@@ -516,34 +539,41 @@
             out[...] = rows_f[:, a * TILE : (a + 1) * TILE]
 
 
-def final(ids, where, ph, plo, rows_f, recv, front):
+def final(ids, where, diag, inv, gx, goth, recv, front):
+    def whole(*shape):
+        return pl.BlockSpec(shape, lambda i, *s: (0,) * len(shape))
+
     line = pl.BlockSpec((RT * TILE, TILE), lambda i, *s: (0, i))
-    left = pl.BlockSpec((RT * TILE, PANEL), lambda i, *s: (0, 0))
-    right = pl.BlockSpec((TILE, PANEL), lambda i, *s: (RT + i, 0))
     return pl.pallas_call(
         final_kernel,
         grid_spec=pltpu.PrefetchScalarGridSpec(
             num_scalar_prefetch=2,
             grid=(QT,),
             in_specs=[
-                left,
-                left,
-                right,
-                right,
-                left,
+                whole(PANEL, PANEL),
+                whole(PANEL, PANEL),
+                whole(8, GROWS, PANEL),
+                whole(8, GROWS - RT * STRIP, PANEL),
                 pl.BlockSpec(memory_space=pl.ANY),
                 line,
             ],
             out_specs=line,
             scratch_shapes=[
-                pltpu.VMEM((2 * RT, TILE + CODE, TILE), I16),
-                pltpu.SemaphoreType.DMA((2 * RT,)),
+                pltpu.VMEM((RT * TILE, PANEL), F32),
+                pltpu.VMEM((RT * TILE, PANEL), F32),
+                pltpu.VMEM((RT * TILE, PANEL), BF16),
+                pltpu.VMEM((RT * TILE, PANEL), BF16),
+                pltpu.VMEM((PANEL, PANEL), BF16),
+                pltpu.VMEM((PANEL, PANEL), BF16),
+                pltpu.VMEM((2 * RT, TILE, TILE), I16),
+                pltpu.VMEM((2, CODE, TILE), I16),
+                pltpu.SemaphoreType.DMA((2 * RT + 2,)),
             ],
         ),
         out_shape=jax.ShapeDtypeStruct((RT * TILE, QT * TILE), F32),
         compiler_params=pltpu.CompilerParams(vmem_limit_bytes=52 * MIB),
-        cost_estimate=pl.CostEstimate(flops=1 << 32, bytes_accessed=20 * MIB, transcendentals=0),
-    )(ids, where, ph, plo, ph, plo, rows_f, recv, front)
+        cost_estimate=pl.CostEstimate(flops=1 << 33, bytes_accessed=20 * MIB, transcendentals=0),
+    )(ids, where, diag, inv, gx, goth, recv, front)
 
 
 def pick(v, at):
@@ -551,41 +581,29 @@
 
 
 def fetch_partner(panel, x, core, z, yh):
-    tiles = panel.reshape(4, TILE, 1024)
-    piece = pick(tiles, (z - x) % 4)
-    halves = []
-    for h in range(2):
-        came = []
-        for dx in (1, 2, 3):
-            pairs = [
-                (flat(c, xs, y, (xs + 2 * h + b) % 4, y), flat(c, (xs + dx) % 4, b, xs, y))
-                for c in range(2)
-                for xs in range(4)
-                for y in range(2)
-                for b in range(2)
-            ]
-            came.append(lax.ppermute(piece, AXES, pairs))
-        halves.append(came)
-    two = jnp.stack([pick(tiles, 1 - core), pick(tiles, 3 - core)])
+    halves = panel.reshape(2, 512, 1024)
+    piece = pick(halves, ((z - x + 4) % 4) // 2)
+    came = []
+    for dx in (1, 2, 3):
+        pairs = [
+            (flat(c, xs, y, (xs + 2 * b) % 4, y), flat(c, (xs + dx) % 4, b, xs, y))
+            for c in range(2)
+            for xs in range(4)
+            for y in range(2)
+            for b in range(2)
+        ]
+        came.append(lax.ppermute(piece, AXES, pairs))
     pairs = [
         (flat(c, x, y, x, y), flat(c, x, 1 - y, x, y))
         for c in range(2)
         for x in range(4)
         for y in range(2)
     ]
-    beside = lax.ppermute(two, AXES, pairs)
-    owner = (x == z) & (core == yh)
-    way = (x - z) % 4
-    mine = []
-    for h in range(2):
-        a, b, d = halves[h]
-        got = jnp.where(way == 1, a, jnp.where(way == 2, b, jnp.where(way == 3, d, beside[h])))
-        mine.append(jnp.where(owner, pick(tiles, core + 2 * h), got))
-    mine = jnp.stack(mine)
-    other = shift(mine, dk=1)
-    even = jnp.where(core == 0, mine, other)
-    odd = jnp.where(core == 0, other, mine)
-    return jnp.stack([even[0], odd[0], even[1], odd[1]]).reshape(1024, 1024)
+    beside = lax.ppermute(pick(halves, 1 - core), AXES, pairs)
+    way = (x - z + 4) % 4
+    mine = jnp.where(way == 1, came[0], jnp.where(way == 2, came[1], came[2]))
+    mine = jnp.where(way == 0, jnp.where(core == yh, pick(halves, core), beside), mine)
+    return mine, shift(mine, dk=1)
 
 
 def sum_first(v, core, z):
@@ -593,7 +611,8 @@
     v = pick(v, core) + shift(pick(v, 1 - core), dk=1)
     v = v.reshape(4, 64, PANEL)
     got = [shift(pick(v, (z + d) % 4), dz=d) for d in (1, 3, 2)]
-    return pick(v, z) + got[0] + got[1] + got[2]
+    v = pick(v, z) + got[0] + got[1] + got[2]
+    return gathered(v, z, dz=0).reshape(256, PANEL)
 
 
 def gathered(v, at, **axis):
@@ -605,17 +624,15 @@
     return full
 
 
-def sum_second(v, x, z):
-    v = v.reshape(4, 16, PANEL)
+def sum_second(v, x):
+    v = v.reshape(4, 64, PANEL)
     got = [shift(pick(v, (x + d) % 4), dx=d) for d in (1, 3, 2)]
     v = pick(v, x) + got[0] + got[1] + got[2]
-    v = (v + shift(v, dc=1, dy=1)) + (shift(v, dc=1) + shift(v, dy=1))
-    return gathered(v, z, dz=0)
+    return (v + shift(v, dc=1, dy=1)) + (shift(v, dc=1) + shift(v, dy=1))
 
 
 def sum_third(v, x, core):
-    v = gathered(v, x, dx=0)
-    v = jnp.transpose(v, (1, 0, 2, 3)).reshape(256, PANEL)
+    v = gathered(v, x, dx=0).reshape(256, PANEL)
     other = shift(v, dk=1)
     return jnp.concatenate([jnp.where(core == 0, v, other), jnp.where(core == 0, other, v)])
 
@@ -635,9 +652,11 @@
     e = parent_place[0], parent_place[1]
     ids = jnp.stack([ch, r, c, ch * 8 + r, core, z, yh, ch * 4 + x, e[0], e[1], x])
     panel = child_panels[0]
-    partner = fetch_partner(panel, x, core, z, yh)
+    parent_front = pltpu.with_memory_space_constraint(parent_front, pltpu.HBM)
+    block = pltpu.with_memory_space_constraint(child_blocks[0], pltpu.HBM)
+    mine, theirs = fetch_partner(panel, x, core, z, yh)
     send, diag, gcol = update(
-        ids, slots, child_patterns, child_blocks[0], panel, partner, parent_front
+        ids, slots, child_patterns, block, panel, mine, theirs, parent_front
     )
     own = lax.all_to_all(send, ("child", "x"), split_axis=0, concat_axis=0, tiled=True)
 
@@ -663,7 +682,7 @@
     kept, moved = pick(strip, yh), shift(pick(strip, 1 - yh), dy=1)
     strip = jnp.where(holder % 2 == yh, kept, moved)
     strip = jnp.stack([strip, shift(strip, dc=1)])
-    diag = sum_second(diag, x, z)
+    diag = sum_second(diag, x)
     send, diag, strip = lax.optimization_barrier((send, diag, strip))
     recv = lax.all_to_all(send, ("z", "yh"), split_axis=0, concat_axis=0, tiled=True)
 
@@ -673,8 +692,8 @@
     gsend = compose(ids, where, line, shift(line, dk=1))
     recv, inv, gsend = lax.optimization_barrier((recv, inv, gsend))
     gx = lax.all_to_all(gsend, ("z", "yh"), split_axis=0, concat_axis=0, tiled=True)
-    ph, plo, rows_f = panel_rows(ids, diag, inv, gx, shift(gx[:, 1], dk=1))
-    return final(ids, where, ph, plo, rows_f, recv, parent_front)
+    goth = shift(gx[:, RT * STRIP :], dk=1)
+    return final(ids, where, diag, inv, gx, goth, recv, parent_front)
 
 
 def solution(mesh):

time: 302 us -> 294 us (0.974)
  local copies, waits for them, and re-layouts: 15.8 us -> 8.85 us
  blocking collectives: 34.9 us -> 30.9 us
  waiting for transfers between devices: 52.5 us -> 56.2 us
    pallas_call x1 -> x0, Pallas kernels: 10.2 us -> none  [panel_rows(): pl.pallas_call(panel_kernel, grid_spec=pltpu.PrefetchScalarGridSpec(num_s...]
    unnamed x24 -> x26, local copies, waits for them, and re-layouts: 10.8 us -> 1.82 us
    ppermute x29, waiting for transfers between devices: 51.6 us -> 56.2 us  [shift(): return lax.ppermute(v, AXES, pairs)]
    squeeze x4 -> x5, local copies, waits for them, and re-layouts: 0.89 us -> 5.4 us  [pick(): return lax.dynamic_index_in_dim(v, at, 0, keepdims=False)]
    all_to_all x1, blocking collectives: 34.9 us -> 30.9 us  [body(): lax.all_to_all(gsend, ('z', 'yh'), split_axis=0, concat_axis=0, tiled=True)]
    ppermute x6 -> x3, starting transfers between devices: 8.76 us -> 4.91 us  [fetch_partner(): came.append(lax.ppermute(piece, AXES, pairs))]
  transfers between devices with their start and end apart: 38 -> 35, of which waited for: 17 -> 14; matrix products, arithmetic and copies ran while one was open for 2% -> 4% of each run, Pallas kernels for 12% -> 13%
where the time goes in v4:
time: 294 us
  starting transfers between devices  101 us (34%)
  Pallas kernels  73.1 us (25%)
  waiting for transfers between devices  56.2 us (19%)
  blocking collectives  30.9 us (11%)
  between operations  13.3 us (5%)
  other arithmetic  9.94 us (3%)
  local copies, waits for them, and re-layouts  8.85 us (3%)
    ppermute x29, starting transfers between devices, shift(): return lax.ppermute(v, AXES, pairs)  85.3 us
    ppermute x29, waiting for transfers between devices, shift(): return lax.ppermute(v, AXES, pairs)  56.2 us
    all_to_all x1, blocking collectives, body(): lax.all_to_all(gsend, ('z', 'yh'), split_axis=0, concat_axis=0, tiled=True)  30.9 us
    pallas_call x1, Pallas kernels, inverse_factor(): pl.pallas_call(inverse_kernel, out_shape=jax.ShapeDtypeStruct((PANEL, PAN...  29.7 us
    pallas_call x1, Pallas kernels, final(): pl.pallas_call(final_kernel, grid_spec=pltpu.PrefetchScalarGridSpec(num_s...  15.5 us
    pallas_call x1, Pallas kernels, update(): pl.pallas_call(update_kernel, grid_spec=pltpu.PrefetchScalarGridSpec(num_...  13.1 us
    pallas_call x1, Pallas kernels, compose(): pl.pallas_call(compose_kernel, grid_spec=pltpu.PrefetchScalarGridSpec(num...  7.11 us
  transfers between devices with their start and end apart: 35, of which 14 were waited for; matrix products, arithmetic and copies ran while one was open for 4% of the time, Pallas kernels for 13%

profile of v4, /device:TPU:1, one launch (start us, length us, event | category | flops | bytes accessed | tf_op | source)
XLA Modules:
  0.0 293.7 jit_solution(14753875233137397081)
XLA Ops:
  0.0 2.8 dynamic-slice_bitcast_fusion
  2.8 1.3 collective-permute-start
  4.1 1.7 collective-permute-start.3
  5.8 1.6 collective-permute-start.2
  7.4 1.6 collective-permute-start.1
  9.1 1.8 fusion.mine
  10.9 31.3 %collective-permute-start.4 = (bf16[512,1024]{1,0:T(8,128)(2,1)S(1)}, bf16[512,1024]{1,0:T(8,128)(2,1)}, u32[]{:S(2)}, u32[]{:S(2)}) collective-permute-start(bf16[512,1024]{1,0:T(8,128)(2,1)S(1)} %fusion.mine), channel_id=1, source_target_pairs={{0,8},{1,9},{2,10},{3,11},{4,12},{5,13},{6,14},{7,15},{8,0},{9,1},... | collective-permute-start | bytes 3145736 | tf_op jit(solution)/shard_map/ppermute | solution.py:48
  42.4 2.1 collective-permute-done.4.other
  44.6 13.1 %shard_map.64 = (s16[8,272,1024]{2,1,0:T(8,128)(2,1)}, f32[512,512]{1,0:T(8,128)}, f32[1024,512]{1,0:T(8,128)}) custom-call(s32[11]{0:T(128)S(1)} %stack.63.ids, s32[2,32]{1,0:T(2,128)S(1)} %select_reduce_fusion.1.slots, s32[2,32,32]{2,1,0:T(8,128)S(1)} %copy-done.2, f32[1024,1024]{1,0:T(8,128)} %bitcast.90, bf16[1024,1024]{1,0:T(8,128)(2,1)S(1)} %bitcast.89, ...), custom_call_target="tpu_custom_call" | custom-call | flops 2147483648 | bytes 14680064 | tf_op jit(solution)/shard_map/pallas_call | solution.py:127
  57.7 5.1 %all-to-all-start = ((s16[8,272,1024]{2,1,0:T(8,128)(2,1)}), s16[8,272,1024]{2,1,0:T(8,128)(2,1)}, u32[]{:S(2)}, u32[]{:S(2)}) async-start(s16[8,272,1024]{2,1,0:T(8,128)(2,1)} %get-tuple-element.21), calls=%async_computation | async-start | bytes 8912896 | tf_op jit(solution)/shard_map/all_to_all | solution.py:661
  62.8 0.8 dynamic-slice_bitcast_fusion.2
  63.6 0.7 collective-permute-start.5
  64.3 0.6 fusion.19
  65.0 1.2 collective-permute-done.5
  66.2 1.9 bitcast_add_fusion
  68.1 1.7 dynamic-slice_bitcast_fusion.9
  69.8 0.5 iota_compare_fusion.3
  77.9 0.7 fusion.18
  83.7 2.3 shard_map.65
  86.0 1.1 collective-permute-start.12
  87.1 2.8 collective-permute-start.13
  90.0 0.5 collective-permute-start.14
  90.5 1.8 collective-permute-start.8
  92.3 2.1 collective-permute-start.7
  94.4 0.8 broadcast_compare_fusion
  95.3 19.9 %collective-permute-done.8 = f32[64,512]{1,0:T(8,128)S(1)} collective-permute-done((f32[64,512]{1,0:T(8,128)S(1)}, f32[64,512]{1,0:T(8,128)S(1)}, u32[]{:S(2)}, u32[]{:S(2)}) %collective-permute-start.8) | collective-permute-done | bytes 131104 | tf_op jit(solution)/shard_map/ppermute | solution.py:48
  115.2 3.9 %collective-permute-done.7 = f32[64,512]{1,0:T(8,128)} collective-permute-done((f32[64,512]{1,0:T(8,128)S(1)}, f32[64,512]{1,0:T(8,128)}, u32[]{:S(2)}, u32[]{:S(2)}) %collective-permute-start.7) | collective-permute-done | bytes 131104 | tf_op jit(solution)/shard_map/ppermute | solution.py:48
  119.2 1.0 bitcast_dynamic-update-slice_fusion.7
  120.2 1.0 collective-permute-start.9
  121.2 0.8 copy-done.6
  122.0 1.6 select_select_fusion.1
  123.7 2.1 collective-permute-start.10
  125.7 1.2 collective-permute-start.11
  127.0 1.0 collective-permute-done.10
  128.0 3.0 %collective-permute-done.11 = f32[64,512]{1,0:T(8,128)S(1)} collective-permute-done((f32[64,512]{1,0:T(8,128)S(1)}, f32[64,512]{1,0:T(8,128)S(1)}, u32[]{:S(2)}, u32[]{:S(2)}) %collective-permute-start.11) | collective-permute-done | bytes 131104 | tf_op jit(solution)/shard_map/ppermute | solution.py:48
  131.1 3.0 %collective-permute-start.15 = (s16[8,272,1024]{2,1,0:T(8,128)(2,1)}, s16[8,272,1024]{2,1,0:T(8,128)(2,1)}, u32[]{:S(2)}, u32[]{:S(2)}) collective-permute-start(s16[8,272,1024]{2,1,0:T(8,128)(2,1)} %all-to-all-done.own), channel_id=1, source_target_pairs={{0,8},{1,9},{2,10},{3,11},{4,12},{5,13},{6,14},{7,15},{8,0},{9,1},... | collective-permute-start | bytes 13369352 | tf_op jit(solution)/shard_map/ppermute | solution.py:48
  134.1 2.1 collective-permute-start.16
  136.2 2.1 collective-permute-start.18
  138.3 1.2 collective-permute-start.17
  139.5 3.4 %collective-permute-start.22 = (s16[256,512]{1,0:T(8,128)(2,1)S(1)}, s16[256,512]{1,0:T(8,128)(2,1)S(1)}, u32[]{:S(2)}, u32[]{:S(2)}) collective-permute-start(s16[256,512]{1,0:T(8,128)(2,1)S(1)} %dynamic-slice_bitcast_fusion.3), channel_id=1, source_target_pairs={{0,1},{1,0},{2,3},{3,2},{4,5},{5,4},{6,7},{7,6},{8,9},{9,8},{10,11... | collective-permute-start | bytes 786440 | tf_op jit(solution)/shard_map/ppermute | solution.py:48
  142.9 1.8 collective-permute-done.18
  144.7 2.7 collective-permute-start.21
  147.5 0.5 collective-permute-start.20
  149.0 0.7 collective-permute-start.23
  149.7 2.1 collective-permute-done.21
  151.8 2.3 collective-permute-done.20
  154.2 5.6 %collective-permute-done.23 = s16[256,512]{1,0:T(8,128)(2,1)S(1)} collective-permute-done((s16[256,512]{1,0:T(8,128)(2,1)S(1)}, s16[256,512]{1,0:T(8,128)(2,1)S(1)}, u32[]{:S(2)}, u32[]{:S(2)}) %collective-permute-start.23) | collective-permute-done | bytes 262176 | tf_op jit(solution)/shard_map/ppermute | solution.py:48
  159.9 5.4 %shard_map.66 = s16[8,1552,256]{2,1,0:T(8,128)(2,1)} custom-call(s32[11]{0:T(128)S(1)} %stack.63.ids, s32[2,32]{1,0:T(2,128)S(1)} %select_reduce_fusion.1.slots, s32[2,48]{1,0:T(2,128)S(1)} %select_reduce_fusion.where, s16[8,272,1024]{2,1,0:T(8,128)(2,1)} %all-to-all-done.own, s16[8,272,1024]{2,1,0:T(8,128)(2,1)} %collective-permute-done.15.other), custom_call_target="tpu_custom_call" | custom-call | bytes 8388608 | tf_op jit(solution)/shard_map/pallas_call | solution.py:317
  165.2 4.8 %all-to-all-start.1 = ((s16[8,1552,256]{2,1,0:T(8,128)(2,1)}), s16[8,1552,256]{2,1,0:T(8,128)(2,1)}, u32[]{:S(2)}, u32[]{:S(2)}) async-start(s16[8,1552,256]{2,1,0:T(8,128)(2,1)} %shard_map.66), calls=%async_computation.1 | async-start | bytes 12713984 | tf_op jit(solution)/shard_map/all_to_all | solution.py:687
  170.1 1.7 collective-permute-start.26
  171.8 1.4 collective-permute-start.25
  173.2 2.6 collective-permute-start.30
  176.0 3.7 %collective-permute-done.24 = f32[64,512]{1,0:T(8,128)S(1)} collective-permute-done((f32[64,512]{1,0:T(8,128)S(1)}, f32[64,512]{1,0:T(8,128)S(1)}, u32[]{:S(2)}, u32[]{:S(2)}) %collective-permute-start.24) | collective-permute-done | bytes 131104 | tf_op jit(solution)/shard_map/ppermute | solution.py:48
  179.7 12.6 %collective-permute-start.27 = (f32[256,512]{1,0:T(8,128)S(1)}, f32[256,512]{1,0:T(8,128)}, u32[]{:S(2)}, u32[]{:S(2)}) collective-permute-start(f32[256,512]{1,0:T(8,128)S(1)} %bitcast.91), channel_id=1, source_target_pairs={{0,8},{1,9},{2,10},{3,11},{4,12},{5,13},{6,14},{7,15},{8,0},{9,1},... | collective-permute-start | bytes 1572872 | tf_op jit(solution)/shard_map/ppermute | solution.py:48
  192.4 7.0 %collective-permute-done.28 = s16[2,256,512]{2,1,0:T(8,128)(2,1)S(1)} collective-permute-done((s16[2,256,512]{2,1,0:T(8,128)(2,1)S(1)}, s16[2,256,512]{2,1,0:T(8,128)(2,1)S(1)}, u32[]{:S(2)}, u32[]{:S(2)}) %collective-permute-start.28) | collective-permute-done | bytes 524320 | tf_op jit(solution)/shard_map/ppermute | solution.py:48
  199.6 4.7 %collective-permute-start.31 = (s16[4,2,256,512]{3,2,1,0:T(8,128)(2,1)S(1)}, s16[4,2,256,512]{3,2,1,0:T(8,128)(2,1)}, u32[]{:S(2)}, u32[]{:S(2)}) collective-permute-start(s16[4,2,256,512]{3,2,1,0:T(8,128)(2,1)S(1)} %pad_add_fusion.own), channel_id=1, source_target_pairs={{0,8},{1,9},{2,10},{3,11},{4,12},{5,13},{6,14},{7,15},{8,0},{9,1},... | collective-permute-start | bytes 6291464 | tf_op jit(solution)/shard_map/ppermute | solution.py:48
  204.3 1.2 broadcast_select_fusion.1
  205.5 29.7 %shard_map.67.inv = f32[512,512]{1,0:T(8,128)S(1)} custom-call(f32[512,512]{1,0:T(8,128)S(1)} %pad_maximum_fusion.a_ref.diag), custom_call_target="tpu_custom_call" | custom-call | flops 17179869184 | bytes 2097152 | tf_op jit(solution)/shard_map/pallas_call | solution.py:418
  235.2 1.0 copy-done.3
  236.2 7.1 %shard_map.68 = s16[8,208,512]{2,1,0:T(8,128)(2,1)} custom-call(s32[11]{0:T(128)S(1)} %stack.63.ids, s32[2,48]{1,0:T(2,128)S(1)} %select_reduce_fusion.where, s16[4,2,256,512]{3,2,1,0:T(8,128)(2,1)S(1)} %pad_add_fusion.own, s16[4,2,256,512]{3,2,1,0:T(8,128)(2,1)} %collective-permute-done.31.other), custom_call_target="tpu_custom_call" | custom-call | bytes 6291456 | tf_op jit(solution)/shard_map/pallas_call | solution.py:255
  243.3 30.9 %all_to_all.15.gx = s16[8,208,512]{2,1,0:T(8,128)(2,1)S(1)} all-to-all(s16[8,208,512]{2,1,0:T(8,128)(2,1)} %shard_map.68), channel_id=1, replica_groups=mesh['child'=2,'x'=4,'core'=2,'z'=4,'yh'=2] {'z','yh'}, dimensions={0} | all-to-all | bytes 3407872 | tf_op jit(solution)/shard_map/all_to_all | solution.py:694
  274.3 1.6 collective-permute-start.32
  275.9 2.1 collective-permute-done.32.goth
  278.0 15.5 %shard_map.69 = f32[768,1536]{1,0:T(8,128)} custom-call(s32[11]{0:T(128)S(1)} %stack.63.ids, s32[2,48]{1,0:T(2,128)S(1)} %select_reduce_fusion.where, f32[512,512]{1,0:T(8,128)S(1)} %pad_maximum_fusion.a_ref.diag, f32[512,512]{1,0:T(8,128)} %copy-done.3, s16[8,208,512]{2,1,0:T(8,128)(2,1)} %copy-done.4, ...), custom_call_target="tpu_custom_call" | custom-call | flops 8589934592 | bytes 20971520 | tf_op jit(solution)/shard_map/pallas_call | solution.py:547
  (73 shorter events, 2.3 us)
Async XLA Ops:
  0.0 9.1 %copy-start = (bf16[1,1024,1024]{2,1,0:T(8,128)(2,1)S(1)}, bf16[1,1024,1024]{2,1,0:T(8,128)(2,1)}, u32[]{:S(2)}) copy-start(bf16[1,1024,1024]{2,1,0:T(8,128)(2,1)} %param.7) | copy-start | bytes 6291460
  2.8 6.2 %collective-permute-start = (bf16[512,1024]{1,0:T(8,128)(2,1)}, bf16[512,1024]{1,0:T(8,128)(2,1)}, u32[]{:S(2)}, u32[]{:S(2)}) collective-permute-start(bf16[512,1024]{1,0:T(8,128)(2,1)} %get-tuple-element.40), channel_id=1, source_target_pairs={{0,8},{9,1},{18,26},{27,19},{36,44},{45,37},{54,62},{63,55},{64,72... | collective-permute-start | bytes 3145736 | tf_op jit(solution)/shard_map/ppermute | solution.py:602
  4.1 4.9 %collective-permute-start.3 = (bf16[512,1024]{1,0:T(8,128)(2,1)S(1)}, bf16[512,1024]{1,0:T(8,128)(2,1)}, u32[]{:S(2)}, u32[]{:S(2)}) collective-permute-start(bf16[512,1024]{1,0:T(8,128)(2,1)S(1)} %get-tuple-element.39), channel_id=1, source_target_pairs={{0,48},{4,56},{9,49},{13,57},{18,2},{22,10},{27,3},{31,11},{36,20}... | collective-permute-start | bytes 3145736 | tf_op jit(solution)/shard_map/ppermute | solution.py:595
  5.8 3.3 %collective-permute-start.2 = (bf16[512,1024]{1,0:T(8,128)(2,1)S(1)}, bf16[512,1024]{1,0:T(8,128)(2,1)}, u32[]{:S(2)}, u32[]{:S(2)}) collective-permute-start(bf16[512,1024]{1,0:T(8,128)(2,1)S(1)} %get-tuple-element.39), channel_id=1, source_target_pairs={{0,32},{4,40},{9,33},{13,41},{18,50},{22,58},{27,51},{31,59},{36,4... | collective-permute-start | bytes 3145736 | tf_op jit(solution)/shard_map/ppermute | solution.py:595
  7.4 1.7 collective-permute-start.1
  9.0 33.1 %copy-start.9 = (s32[48]{0:T(128)S(1)}, s32[48]{0:T(128)}, u32[]{:S(2)}) copy-start(s32[48]{0:T(128)} %param.10) | copy-start | bytes 580
  9.0 33.2 %copy-start.12 = (s32[2,32]{1,0:T(2,128)S(1)}, s32[2,32]{1,0:T(2,128)}, u32[]{:S(2)}) copy-start(s32[2,32]{1,0:T(2,128)} %param.9) | copy-start | bytes 772
  9.0 35.6 %copy-start.2 = (s32[2,32,32]{2,1,0:T(8,128)S(1)}, s32[2,32,32]{2,1,0:T(8,128)}, u32[]{:S(2)}) copy-start(s32[2,32,32]{2,1,0:T(8,128)} %pat.1) | copy-start | bytes 24580
  10.9 33.7 %collective-permute-start.4 = (bf16[512,1024]{1,0:T(8,128)(2,1)S(1)}, bf16[512,1024]{1,0:T(8,128)(2,1)}, u32[]{:S(2)}, u32[]{:S(2)}) collective-permute-start(bf16[512,1024]{1,0:T(8,128)(2,1)S(1)} %fusion.mine), channel_id=1, source_target_pairs={{0,8},{1,9},{2,10},{3,11},{4,12},{5,13},{6,14},{7,15},{8,0},{9,1},... | collective-permute-start | bytes 3145736 | tf_op jit(solution)/shard_map/ppermute | solution.py:48
  57.7 5.1 %copy-start.5 = (f32[512,512]{1,0:T(8,128)S(1)}, f32[512,512]{1,0:T(8,128)}, u32[]{:S(2)}) copy-start(f32[512,512]{1,0:T(8,128)} %get-tuple-element.22) | copy-start | bytes 3145732
  57.7 73.3 %all-to-all-start = ((s16[8,272,1024]{2,1,0:T(8,128)(2,1)}), s16[8,272,1024]{2,1,0:T(8,128)(2,1)}, u32[]{:S(2)}, u32[]{:S(2)}) async-start(s16[8,272,1024]{2,1,0:T(8,128)(2,1)} %get-tuple-element.21), calls=%async_computation | async-start | bytes 8912896 | tf_op jit(solution)/shard_map/all_to_all | solution.py:661
  62.8 20.9 %copy-start.1 = (f32[1024,512]{1,0:T(8,128)S(1)}, f32[1024,512]{1,0:T(8,128)}, u32[]{:S(2)}) copy-start(f32[1024,512]{1,0:T(8,128)} %get-tuple-element.23.gcol) | copy-start | bytes 6291460
  63.6 2.5 collective-permute-start.5
  69.8 22.5 %collective-permute-start.6 = (f32[64,512]{1,0:T(8,128)}, f32[64,512]{1,0:T(8,128)S(1)}, u32[]{:S(2)}, u32[]{:S(2)}) collective-permute-start(f32[64,512]{1,0:T(8,128)} %get-tuple-element.46), channel_id=1, source_target_pairs={{0,2},{1,3},{2,4},{3,5},{4,6},{5,7},{6,0},{7,1},{8,10},{9,11},{10,... | collective-permute-start | bytes 393224 | tf_op jit(solution)/shard_map/ppermute | solution.py:48
  83.7 10.7 %copy-start.7 = (s32[512]{0:T(512)}, s32[512]{0:T(512)S(1)}, u32[]{:S(2)}) copy-start(s32[512]{0:T(512)S(1)} %get-tuple-element.57) | copy-start | bytes 6148
  83.7 10.7 %copy-start.10 = (pred[256]{0:T(512)(128)(4,1)S(1)}, pred[256]{0:T(512)(128)(4,1)}, u32[]{:S(2)}) copy-start(pred[256]{0:T(512)(128)(4,1)} %iota_compare_fusion.3) | copy-start | bytes 772
  86.0 35.1 %collective-permute-start.12 = (s16[2,256,512]{2,1,0:T(8,128)(2,1)}, s16[2,256,512]{2,1,0:T(8,128)(2,1)S(1)}, u32[]{:S(2)}, u32[]{:S(2)}) collective-permute-start(s16[2,256,512]{2,1,0:T(8,128)(2,1)} %get-tuple-element.24), channel_id=1, source_target_pairs={{0,4},{1,5},{2,6},{3,7},{4,0},{5,1},{6,2},{7,3},{8,12},{9,13},{10,... | collective-permute-start | bytes 1572872 | tf_op jit(solution)/shard_map/ppermute | solution.py:48
  87.1 34.1 %collective-permute-start.13 = (s16[2,256,512]{2,1,0:T(8,128)(2,1)}, s16[2,256,512]{2,1,0:T(8,128)(2,1)S(1)}, u32[]{:S(2)}, u32[]{:S(2)}) collective-permute-start(s16[2,256,512]{2,1,0:T(8,128)(2,1)} %get-tuple-element.25), channel_id=1, source_target_pairs={{0,6},{1,7},{2,0},{3,1},{4,2},{5,3},{6,4},{7,5},{8,14},{9,15},{10,... | collective-permute-start | bytes 1572872 | tf_op jit(solution)/shard_map/ppermute | solution.py:48
  90.0 31.2 %collective-permute-start.14 = (s16[2,256,512]{2,1,0:T(8,128)(2,1)S(1)}, s16[2,256,512]{2,1,0:T(8,128)(2,1)}, u32[]{:S(2)}, u32[]{:S(2)}) collective-permute-start(s16[2,256,512]{2,1,0:T(8,128)(2,1)S(1)} %get-tuple-element.26), channel_id=1, source_target_pairs={{0,2},{1,3},{2,4},{3,5},{4,6},{5,7},{6,0},{7,1},{8,10},{9,11},{10,... | collective-permute-start | bytes 1572872 | tf_op jit(solution)/shard_map/ppermute | solution.py:48
  90.5 24.7 %collective-permute-start.8 = (f32[64,512]{1,0:T(8,128)S(1)}, f32[64,512]{1,0:T(8,128)S(1)}, u32[]{:S(2)}, u32[]{:S(2)}) collective-permute-start(f32[64,512]{1,0:T(8,128)S(1)} %get-tuple-element.47), channel_id=1, source_target_pairs={{0,4},{1,5},{2,6},{3,7},{4,0},{5,1},{6,2},{7,3},{8,12},{9,13},{10,... | collective-permute-start | bytes 393224 | tf_op jit(solution)/shard_map/ppermute | solution.py:48
  92.3 26.8 %collective-permute-start.7 = (f32[64,512]{1,0:T(8,128)S(1)}, f32[64,512]{1,0:T(8,128)}, u32[]{:S(2)}, u32[]{:S(2)}) collective-permute-start(f32[64,512]{1,0:T(8,128)S(1)} %get-tuple-element.48), channel_id=1, source_target_pairs={{0,6},{1,7},{2,0},{3,1},{4,2},{5,3},{6,4},{7,5},{8,14},{9,15},{10,... | collective-permute-start | bytes 393224 | tf_op jit(solution)/shard_map/ppermute | solution.py:48
  120.2 6.8 %collective-permute-start.9 = (f32[64,512]{1,0:T(8,128)S(1)}, f32[64,512]{1,0:T(8,128)S(1)}, u32[]{:S(2)}, u32[]{:S(2)}) collective-permute-start(f32[64,512]{1,0:T(8,128)S(1)} %get-tuple-element.38), channel_id=1, source_target_pairs={{0,2},{1,3},{2,4},{3,5},{4,6},{5,7},{6,0},{7,1},{8,10},{9,11},{10,... | collective-permute-start | bytes 393224 | tf_op jit(solution)/shard_map/ppermute | solution.py:48
  121.2 0.8 copy-start.6
  123.6 25.0 %copy-start.8 = (s32[512]{0:T(512)S(1)}, s32[512]{0:T(512)}, u32[]{:S(2)}) copy-start(s32[512]{0:T(512)} %copy-done.7) | copy-start | bytes 6148
  123.7 25.0 %copy-start.11 = (pred[256]{0:T(512)(128)(4,1)S(1)}, pred[256]{0:T(512)(128)(4,1)}, u32[]{:S(2)}) copy-start(pred[256]{0:T(512)(128)(4,1)} %iota_compare_fusion.3) | copy-start | bytes 772
  123.7 4.3 %collective-permute-start.10 = (f32[64,512]{1,0:T(8,128)S(1)}, f32[64,512]{1,0:T(8,128)S(1)}, u32[]{:S(2)}, u32[]{:S(2)}) collective-permute-start(f32[64,512]{1,0:T(8,128)S(1)} %get-tuple-element.38), channel_id=1, source_target_pairs={{0,6},{1,7},{2,0},{3,1},{4,2},{5,3},{6,4},{7,5},{8,14},{9,15},{10,... | collective-permute-start | bytes 393224 | tf_op jit(solution)/shard_map/ppermute | solution.py:48
  125.7 5.3 %collective-permute-start.11 = (f32[64,512]{1,0:T(8,128)S(1)}, f32[64,512]{1,0:T(8,128)S(1)}, u32[]{:S(2)}, u32[]{:S(2)}) collective-permute-start(f32[64,512]{1,0:T(8,128)S(1)} %get-tuple-element.38), channel_id=1, source_target_pairs={{0,4},{1,5},{2,6},{3,7},{4,0},{5,1},{6,2},{7,3},{8,12},{9,13},{10,... | collective-permute-start | bytes 393224 | tf_op jit(solution)/shard_map/ppermute | solution.py:48
  131.1 28.8 %collective-permute-start.15 = (s16[8,272,1024]{2,1,0:T(8,128)(2,1)}, s16[8,272,1024]{2,1,0:T(8,128)(2,1)}, u32[]{:S(2)}, u32[]{:S(2)}) collective-permute-start(s16[8,272,1024]{2,1,0:T(8,128)(2,1)} %all-to-all-done.own), channel_id=1, source_target_pairs={{0,8},{1,9},{2,10},{3,11},{4,12},{5,13},{6,14},{7,15},{8,0},{9,1},... | collective-permute-start | bytes 13369352 | tf_op jit(solution)/shard_map/ppermute | solution.py:48
  134.1 8.7 %collective-permute-start.16 = (f32[64,512]{1,0:T(8,128)S(1)}, f32[64,512]{1,0:T(8,128)S(1)}, u32[]{:S(2)}, u32[]{:S(2)}) collective-permute-start(f32[64,512]{1,0:T(8,128)S(1)} %get-tuple-element.43), channel_id=1, source_target_pairs={{0,16},{1,17},{2,18},{3,19},{4,20},{5,21},{6,22},{7,23},{8,24},{9,... | collective-permute-start | bytes 393224 | tf_op jit(solution)/shard_map/ppermute | solution.py:48
  136.2 8.5 %collective-permute-start.18 = (f32[64,512]{1,0:T(8,128)S(1)}, f32[64,512]{1,0:T(8,128)S(1)}, u32[]{:S(2)}, u32[]{:S(2)}) collective-permute-start(f32[64,512]{1,0:T(8,128)S(1)} %get-tuple-element.44), channel_id=1, source_target_pairs={{0,32},{1,33},{2,34},{3,35},{4,36},{5,37},{6,38},{7,39},{8,40},{9,... | collective-permute-start | bytes 393224 | tf_op jit(solution)/shard_map/ppermute | solution.py:48
  138.3 6.4 %collective-permute-start.17 = (f32[64,512]{1,0:T(8,128)S(1)}, f32[64,512]{1,0:T(8,128)S(1)}, u32[]{:S(2)}, u32[]{:S(2)}) collective-permute-start(f32[64,512]{1,0:T(8,128)S(1)} %get-tuple-element.45), channel_id=1, source_target_pairs={{0,48},{1,49},{2,50},{3,51},{4,52},{5,53},{6,54},{7,55},{8,56},{9,... | collective-permute-start | bytes 393224 | tf_op jit(solution)/shard_map/ppermute | solution.py:48
  139.5 9.1 %collective-permute-start.22 = (s16[256,512]{1,0:T(8,128)(2,1)S(1)}, s16[256,512]{1,0:T(8,128)(2,1)S(1)}, u32[]{:S(2)}, u32[]{:S(2)}) collective-permute-start(s16[256,512]{1,0:T(8,128)(2,1)S(1)} %dynamic-slice_bitcast_fusion.3), channel_id=1, source_target_pairs={{0,1},{1,0},{2,3},{3,2},{4,5},{5,4},{6,7},{7,6},{8,9},{9,8},{10,11... | collective-permute-start | bytes 786440 | tf_op jit(solution)/shard_map/ppermute | solution.py:48
  144.7 7.1 %collective-permute-start.21 = (f32[64,512]{1,0:T(8,128)S(1)}, f32[64,512]{1,0:T(8,128)S(1)}, u32[]{:S(2)}, u32[]{:S(2)}) collective-permute-start(f32[64,512]{1,0:T(8,128)S(1)} %fusion.12), channel_id=1, source_target_pairs={{0,1},{1,0},{2,3},{3,2},{4,5},{5,4},{6,7},{7,6},{8,9},{9,8},{10,11... | collective-permute-start | bytes 393224 | tf_op jit(solution)/shard_map/ppermute | solution.py:48
  147.5 6.7 %collective-permute-start.20 = (f32[64,512]{1,0:T(8,128)S(1)}, f32[64,512]{1,0:T(8,128)S(1)}, u32[]{:S(2)}, u32[]{:S(2)}) collective-permute-start(f32[64,512]{1,0:T(8,128)S(1)} %fusion.12), channel_id=1, source_target_pairs={{0,64},{1,65},{2,66},{3,67},{4,68},{5,69},{6,70},{7,71},{8,72},{9,... | collective-permute-start | bytes 393224 | tf_op jit(solution)/shard_map/ppermute | solution.py:48
  147.9 6.3 %collective-permute-start.19 = (f32[64,512]{1,0:T(8,128)S(1)}, f32[64,512]{1,0:T(8,128)S(1)}, u32[]{:S(2)}, u32[]{:S(2)}) collective-permute-start(f32[64,512]{1,0:T(8,128)S(1)} %fusion.12), channel_id=1, source_target_pairs={{0,65},{1,64},{2,67},{3,66},{4,69},{5,68},{6,71},{7,70},{8,73},{9,... | collective-permute-start | bytes 393224 | tf_op jit(solution)/shard_map/ppermute | solution.py:48
  149.0 10.8 %collective-permute-start.23 = (s16[256,512]{1,0:T(8,128)(2,1)S(1)}, s16[256,512]{1,0:T(8,128)(2,1)S(1)}, u32[]{:S(2)}, u32[]{:S(2)}) collective-permute-start(s16[256,512]{1,0:T(8,128)(2,1)S(1)} %fusion.9), channel_id=1, source_target_pairs={{0,64},{1,65},{2,66},{3,67},{4,68},{5,69},{6,70},{7,71},{8,72},{9,... | collective-permute-start | bytes 786440 | tf_op jit(solution)/shard_map/ppermute | solution.py:48
  165.2 78.1 %all-to-all-start.1 = ((s16[8,1552,256]{2,1,0:T(8,128)(2,1)}), s16[8,1552,256]{2,1,0:T(8,128)(2,1)}, u32[]{:S(2)}, u32[]{:S(2)}) async-start(s16[8,1552,256]{2,1,0:T(8,128)(2,1)} %shard_map.66), calls=%async_computation.1 | async-start | bytes 12713984 | tf_op jit(solution)/shard_map/all_to_all | solution.py:687
  170.1 9.6 %collective-permute-start.26 = (f32[64,512]{1,0:T(8,128)S(1)}, f32[64,512]{1,0:T(8,128)S(1)}, u32[]{:S(2)}, u32[]{:S(2)}) collective-permute-start(f32[64,512]{1,0:T(8,128)S(1)} %add_add_fusion), channel_id=1, source_target_pairs={{0,32},{1,33},{2,34},{3,35},{4,36},{5,37},{6,38},{7,39},{8,40},{9,... | collective-permute-start | bytes 393224 | tf_op jit(solution)/shard_map/ppermute | solution.py:48
  171.8 7.9 %collective-permute-start.25 = (f32[64,512]{1,0:T(8,128)S(1)}, f32[64,512]{1,0:T(8,128)S(1)}, u32[]{:S(2)}, u32[]{:S(2)}) collective-permute-start(f32[64,512]{1,0:T(8,128)S(1)} %add_add_fusion), channel_id=1, source_target_pairs={{0,48},{1,49},{2,50},{3,51},{4,52},{5,53},{6,54},{7,55},{8,56},{9,... | collective-permute-start | bytes 393224 | tf_op jit(solution)/shard_map/ppermute | solution.py:48
  173.2 6.4 %collective-permute-start.24 = (f32[64,512]{1,0:T(8,128)S(1)}, f32[64,512]{1,0:T(8,128)S(1)}, u32[]{:S(2)}, u32[]{:S(2)}) collective-permute-start(f32[64,512]{1,0:T(8,128)S(1)} %add_add_fusion), channel_id=1, source_target_pairs={{0,16},{1,17},{2,18},{3,19},{4,20},{5,21},{6,22},{7,23},{8,24},{9,... | collective-permute-start | bytes 393224 | tf_op jit(solution)/shard_map/ppermute | solution.py:48
  173.2 19.1 %collective-permute-start.30 = (s16[2,256,512]{2,1,0:T(8,128)(2,1)S(1)}, s16[2,256,512]{2,1,0:T(8,128)(2,1)S(1)}, u32[]{:S(2)}, u32[]{:S(2)}) collective-permute-start(s16[2,256,512]{2,1,0:T(8,128)(2,1)S(1)} %pad_add_fusion.1), channel_id=1, source_target_pairs={{0,48},{1,49},{2,50},{3,51},{4,52},{5,53},{6,54},{7,55},{8,56},{9,... | collective-permute-start | bytes 1572872 | tf_op jit(solution)/shard_map/ppermute | solution.py:48
  175.9 16.5 %collective-permute-start.29 = (s16[2,256,512]{2,1,0:T(8,128)(2,1)S(1)}, s16[2,256,512]{2,1,0:T(8,128)(2,1)S(1)}, u32[]{:S(2)}, u32[]{:S(2)}) collective-permute-start(s16[2,256,512]{2,1,0:T(8,128)(2,1)S(1)} %pad_add_fusion.1), channel_id=1, source_target_pairs={{0,32},{1,33},{2,34},{3,35},{4,36},{5,37},{6,38},{7,39},{8,40},{9,... | collective-permute-start | bytes 1572872 | tf_op jit(solution)/shard_map/ppermute | solution.py:48
  179.7 19.7 %collective-permute-start.28 = (s16[2,256,512]{2,1,0:T(8,128)(2,1)S(1)}, s16[2,256,512]{2,1,0:T(8,128)(2,1)S(1)}, u32[]{:S(2)}, u32[]{:S(2)}) collective-permute-start(s16[2,256,512]{2,1,0:T(8,128)(2,1)S(1)} %pad_add_fusion.1), channel_id=1, source_target_pairs={{0,16},{1,17},{2,18},{3,19},{4,20},{5,21},{6,22},{7,23},{8,24},{9,... | collective-permute-start | bytes 1572872 | tf_op jit(solution)/shard_map/ppermute | solution.py:48
  179.7 24.5 %collective-permute-start.27 = (f32[256,512]{1,0:T(8,128)S(1)}, f32[256,512]{1,0:T(8,128)}, u32[]{:S(2)}, u32[]{:S(2)}) collective-permute-start(f32[256,512]{1,0:T(8,128)S(1)} %bitcast.91), channel_id=1, source_target_pairs={{0,8},{1,9},{2,10},{3,11},{4,12},{5,13},{6,14},{7,15},{8,0},{9,1},... | collective-permute-start | bytes 1572872 | tf_op jit(solution)/shard_map/ppermute | solution.py:48
  199.6 36.6 %collective-permute-start.31 = (s16[4,2,256,512]{3,2,1,0:T(8,128)(2,1)S(1)}, s16[4,2,256,512]{3,2,1,0:T(8,128)(2,1)}, u32[]{:S(2)}, u32[]{:S(2)}) collective-permute-start(s16[4,2,256,512]{3,2,1,0:T(8,128)(2,1)S(1)} %pad_add_fusion.own), channel_id=1, source_target_pairs={{0,8},{1,9},{2,10},{3,11},{4,12},{5,13},{6,14},{7,15},{8,0},{9,1},... | collective-permute-start | bytes 6291464 | tf_op jit(solution)/shard_map/ppermute | solution.py:48
  235.2 1.0 copy-start.3
  274.2 3.8 %copy-start.4 = (s16[8,208,512]{2,1,0:T(8,128)(2,1)}, s16[8,208,512]{2,1,0:T(8,128)(2,1)S(1)}, u32[]{:S(2)}) copy-start(s16[8,208,512]{2,1,0:T(8,128)(2,1)S(1)} %all_to_all.15.gx) | copy-start | bytes 5111812
  274.3 3.7 %collective-permute-start.32 = (s16[8,112,512]{2,1,0:T(8,128)(2,1)S(1)}, s16[8,112,512]{2,1,0:T(8,128)(2,1)S(1)}, u32[]{:S(2)}, u32[]{:S(2)}) collective-permute-start(s16[8,112,512]{2,1,0:T(8,128)(2,1)S(1)} %slice.16), channel_id=1, source_target_pairs={{0,8},{1,9},{2,10},{3,11},{4,12},{5,13},{6,14},{7,15},{8,0},{9,1},... | collective-permute-start | bytes 2752520 | tf_op jit(solution)/shard_map/ppermute | solution.py:48

commit v5 on v4

--- a/solution.py
+++ b/solution.py
@@ -52,8 +52,7 @@
     top = jnp.max(jnp.abs(u), axis=0, keepdims=True)
     code = jnp.ceil(jnp.log2(jnp.maximum(top, 1e-30)) * 128.0)
     scale = jnp.exp2(15.0 - code * (1.0 / 128.0)) * (32766.0 / 32768.0)
-    q = (u * scale + 32768.5).astype(I32) - 32768
-    return q.astype(I16), code
+    return jnp.floor(u * scale + 0.5).astype(I32).astype(I16), code
 
 
 def scale_rows(code):
@@ -205,6 +204,64 @@
 CHILD_CODE = CT * STRIP
 FRONT = CHILD_CODE + CODE
 FRONT_CODE = FRONT + RT * STRIP
+
+
+def regions(ids, where, child):
+    for a in range(2):
+        cols = slice(a * TILE, (a + 1) * TILE)
+        yield slice(0, FRONT), cols, where[child, ids[8 + a]] // CT
+        yield slice(FRONT, TILE), cols, ids[8 + a] // QT
+
+
+def choose_z_kernel(ids, where, *refs):
+    for rows, cols, holder in regions(ids, where, ids[0]):
+        for d in range(4):
+
+            @pl.when(lax.rem(ids[5] - holder // 2 + 4, 4) == d)
+            def _():
+                refs[4][:, rows, cols] = refs[d][:, rows, cols]
+
+
+def choose_z(ids, where, parts):
+    whole = pl.BlockSpec((2, TILE, PANEL), lambda i, *s: (0, 0, 0))
+    return pl.pallas_call(
+        choose_z_kernel,
+        grid_spec=pltpu.PrefetchScalarGridSpec(
+            num_scalar_prefetch=2, grid=(1,), in_specs=[whole] * 4, out_specs=whole
+        ),
+        out_shape=jax.ShapeDtypeStruct((2, TILE, PANEL), I16),
+        cost_estimate=pl.CostEstimate(flops=0, bytes_accessed=3 * MIB, transcendentals=0),
+    )(ids, where, *parts)
+
+
+def choose_y_kernel(ids, where, kept, beside, across, both, out):
+    for n, (near, far) in enumerate(((kept, beside), (across, both))):
+        child = lax.rem(ids[0] + n, 2)
+        for rows, cols, holder in regions(ids, where, child):
+            here = lax.rem(holder + 8, 2) == ids[6]
+
+            @pl.when(here)
+            def _():
+                out[n, rows, cols] = near[rows, cols]
+
+            @pl.when(jnp.logical_not(here))
+            def _():
+                out[n, rows, cols] = far[rows, cols]
+
+
+def choose_y(ids, where, parts):
+    whole = pl.BlockSpec((TILE, PANEL), lambda i, *s: (0, 0))
+    return pl.pallas_call(
+        choose_y_kernel,
+        grid_spec=pltpu.PrefetchScalarGridSpec(
+            num_scalar_prefetch=2,
+            grid=(1,),
+            in_specs=[whole] * 4,
+            out_specs=pl.BlockSpec((2, TILE, PANEL), lambda i, *s: (0, 0, 0)),
+        ),
+        out_shape=jax.ShapeDtypeStruct((2, TILE, PANEL), I16),
+        cost_estimate=pl.CostEstimate(flops=0, bytes_accessed=2 * MIB, transcendentals=0),
+    )(ids, where, *parts)
 
 
 def compose_kernel(ids, where, own, other, out, acc, kept, kcode):
@@ -611,8 +668,7 @@
     v = pick(v, core) + shift(pick(v, 1 - core), dk=1)
     v = v.reshape(4, 64, PANEL)
     got = [shift(pick(v, (z + d) % 4), dz=d) for d in (1, 3, 2)]
-    v = pick(v, z) + got[0] + got[1] + got[2]
-    return gathered(v, z, dz=0).reshape(256, PANEL)
+    return pick(v, z) + got[0] + got[1] + got[2]
 
 
 def gathered(v, at, **axis):
@@ -655,33 +711,25 @@
     parent_front = pltpu.with_memory_space_constraint(parent_front, pltpu.HBM)
     block = pltpu.with_memory_space_constraint(child_blocks[0], pltpu.HBM)
     mine, theirs = fetch_partner(panel, x, core, z, yh)
+    mine, theirs, ids, slots, where = lax.optimization_barrier((mine, theirs, ids, slots, where))
     send, diag, gcol = update(
         ids, slots, child_patterns, block, panel, mine, theirs, parent_front
     )
     own = lax.all_to_all(send, ("child", "x"), split_axis=0, concat_axis=0, tiled=True)
 
     diag = sum_first(diag, core, z)
+    diag, gcol = lax.optimization_barrier((diag, gcol))
     parts = strips(ids, gcol, parent_front)
-    held = [pick(pick(where, ch), e[a]) // CT for a in range(2)]
-    fronts = [e[a] // QT for a in range(2)]
-    row = lax.broadcasted_iota(I32, (TILE, PANEL), 0)
-    first = lax.broadcasted_iota(I32, (TILE, PANEL), 1) < TILE
-    holder = jnp.where(
-        row < FRONT,
-        jnp.where(first, held[0], held[1]),
-        jnp.where(first, fronts[0], fronts[1]),
-    )
-    away = (z - holder // 2 + 4) % 4
-    strip = parts[0]
-    for d in (1, 3, 2):
-        strip = jnp.where(away == d, shift(parts[d], dz=d), strip)
+    parts = [parts[0]] + [shift(parts[d], dz=d) for d in range(1, 4)]
+    diag = gathered(diag, z, dz=0).reshape(256, PANEL)
+    strip = choose_z(ids, where, parts)
     own, diag, strip = lax.optimization_barrier((own, diag, strip))
 
     other = shift(own, dk=1)
     send = route(ids, slots, where, own, other)
-    kept, moved = pick(strip, yh), shift(pick(strip, 1 - yh), dy=1)
-    strip = jnp.where(holder % 2 == yh, kept, moved)
-    strip = jnp.stack([strip, shift(strip, dc=1)])
+    kept, moved = pick(strip, yh), pick(strip, 1 - yh)
+    moves = [shift(moved, dy=1), shift(kept, dc=1), shift(moved, dc=1, dy=1)]
+    strip = choose_y(ids, where, [kept] + moves)
     diag = sum_second(diag, x)
     send, diag, strip = lax.optimization_barrier((send, diag, strip))
     recv = lax.all_to_all(send, ("z", "yh"), split_axis=0, concat_axis=0, tiled=True)

time: 294 us -> 294 us (level)
  starting transfers between devices: 101 us -> 116 us
  between operations: 13.3 us -> 0.68 us
  Pallas kernels: 73.1 us -> 78.3 us
  other arithmetic: 9.94 us -> 5.45 us
    ppermute x29 -> x30, starting transfers between devices: 85.3 us -> 100 us  [shift(): return lax.ppermute(v, AXES, pairs)]
    pallas_call x0 -> x2, Pallas kernels: none -> 6.1 us  [the longest x1 3.25 us: choose_z(): pl.pallas_call(choose_z_kernel, grid_spec=pltpu.PrefetchScalarGridSpec(nu...]
    ppermute x29 -> x30, waiting for transfers between devices: 56.2 us -> 50.8 us  [shift(): return lax.ppermute(v, AXES, pairs)]
  transfers between devices with their start and end apart: 35 -> 36, of which waited for: 14 -> 14; matrix products, arithmetic and copies ran while one was open for 4% -> 2% of each run, Pallas kernels for 13% -> 15%
where the time goes in v5:
time: 294 us; the launch traced here: 293 us
  starting transfers between devices  116 us (39%)
  Pallas kernels  78.3 us (27%)
  waiting for transfers between devices  53.3 us (18%)
  blocking collectives  30.7 us (10%)
  local copies, waits for them, and re-layouts  8.45 us (3%)
  other arithmetic  5.45 us (2%)
    ppermute x30, starting transfers between devices, shift(): return lax.ppermute(v, AXES, pairs)  100 us
    ppermute x30, waiting for transfers between devices, shift(): return lax.ppermute(v, AXES, pairs)  50.8 us
    all_to_all x1, blocking collectives, body(): lax.all_to_all(gsend, ('z', 'yh'), split_axis=0, concat_axis=0, tiled=True)  30.7 us
    pallas_call x1, Pallas kernels, inverse_factor(): pl.pallas_call(inverse_kernel, out_shape=jax.ShapeDtypeStruct((PANEL, PAN...  29.6 us
    pallas_call x1, Pallas kernels, final(): pl.pallas_call(final_kernel, grid_spec=pltpu.PrefetchScalarGridSpec(num_s...  15.5 us
    pallas_call x1, Pallas kernels, update(): pl.pallas_call(update_kernel, grid_spec=pltpu.PrefetchScalarGridSpec(num_...  13.1 us
    pallas_call x1, Pallas kernels, compose(): pl.pallas_call(compose_kernel, grid_spec=pltpu.PrefetchScalarGridSpec(num...  7.12 us
  transfers between devices with their start and end apart: 36, of which 14 were waited for; matrix products, arithmetic and copies ran while one was open for 2% of the time, Pallas kernels for 15%

profile of v5, /device:TPU:1, one launch (start us, length us, event | category | flops | bytes accessed | tf_op | source)
XLA Modules:
  0.0 292.9 jit_solution(13578053073100997805)
XLA Ops:
  0.0 2.8 dynamic-slice_bitcast_fusion
  2.8 1.3 collective-permute-start
  4.1 1.6 collective-permute-start.3
  5.8 1.6 collective-permute-start.2
  7.4 1.6 collective-permute-start.1
  9.1 1.9 fusion.mine
  11.0 31.3 %collective-permute-start.4 = (bf16[512,1024]{1,0:T(8,128)(2,1)S(1)}, bf16[512,1024]{1,0:T(8,128)(2,1)}, u32[]{:S(2)}, u32[]{:S(2)}) collective-permute-start(bf16[512,1024]{1,0:T(8,128)(2,1)S(1)} %fusion.mine), channel_id=1, source_target_pairs={{0,8},{1,9},{2,10},{3,11},{4,12},{5,13},{6,14},{7,15},{8,0},{9,1},... | collective-permute-start | bytes 3145736 | tf_op jit(solution)/shard_map/ppermute | solution.py:48
  42.6 0.6 select_reduce_fusion.where
  43.2 1.5 collective-permute-done.4.other
  44.7 13.1 %shard_map.64 = (s16[8,272,1024]{2,1,0:T(8,128)(2,1)}, f32[512,512]{1,0:T(8,128)}, f32[1024,512]{1,0:T(8,128)}) custom-call(s32[11]{0:T(128)S(1)} %stack.55.ids, s32[2,32]{1,0:T(2,128)S(1)} %select_reduce_fusion.1.slots, s32[2,32,32]{2,1,0:T(8,128)S(1)} %copy-done.3, f32[1024,1024]{1,0:T(8,128)} %bitcast.83, bf16[1024,1024]{1,0:T(8,128)(2,1)S(1)} %bitcast.82, ...), custom_call_target="tpu_custom_call" | custom-call | flops 2147483648 | bytes 14680064 | tf_op jit(solution)/shard_map/pallas_call | solution.py:126
  57.8 5.1 %all-to-all-start = ((s16[8,272,1024]{2,1,0:T(8,128)(2,1)}), s16[8,272,1024]{2,1,0:T(8,128)(2,1)}, u32[]{:S(2)}, u32[]{:S(2)}) async-start(s16[8,272,1024]{2,1,0:T(8,128)(2,1)} %get-tuple-element.33), calls=%async_computation | async-start | bytes 8912896 | tf_op jit(solution)/shard_map/all_to_all | solution.py:718
  62.9 0.8 dynamic-slice_bitcast_fusion.2
  63.7 0.7 collective-permute-start.5
  64.4 1.7 collective-permute-done.5
  66.1 1.1 bitcast_add_fusion
  67.4 1.1 collective-permute-start.8
  68.5 2.0 collective-permute-start.7
  70.5 5.8 %collective-permute-done.6 = f32[64,512]{1,0:T(8,128)S(1)} collective-permute-done((f32[64,512]{1,0:T(8,128)S(1)}, f32[64,512]{1,0:T(8,128)S(1)}, u32[]{:S(2)}, u32[]{:S(2)}) %collective-permute-start.6) | collective-permute-done | bytes 131104 | tf_op jit(solution)/shard_map/ppermute | solution.py:48
  76.5 1.1 collective-permute-start.11
  77.6 2.5 collective-permute-start.10
  80.1 0.5 collective-permute-start.9
  80.6 1.5 shard_map.65
  82.1 0.8 copy-done.2
  82.9 1.5 collective-permute-start.12
  84.3 1.9 collective-permute-start.13
  86.3 1.7 collective-permute-start.14
  88.1 9.9 %collective-permute-done.12.refs_1_ = s16[2,256,512]{2,1,0:T(8,128)(2,1)S(1)} collective-permute-done((s16[2,256,512]{2,1,0:T(8,128)(2,1)S(1)}, s16[2,256,512]{2,1,0:T(8,128)(2,1)S(1)}, u32[]{:S(2)}, u32[]{:S(2)}) %collective-permute-start.12) | collective-permute-done | bytes 524320 | tf_op jit(solution)/shard_map/ppermute | solution.py:48
  98.0 10.0 %collective-permute-done.13.refs_2_ = s16[2,256,512]{2,1,0:T(8,128)(2,1)S(1)} collective-permute-done((s16[2,256,512]{2,1,0:T(8,128)(2,1)S(1)}, s16[2,256,512]{2,1,0:T(8,128)(2,1)S(1)}, u32[]{:S(2)}, u32[]{:S(2)}) %collective-permute-start.13) | collective-permute-done | bytes 524320 | tf_op jit(solution)/shard_map/ppermute | solution.py:48
  108.0 0.9 collective-permute-done.14.refs_3_
  108.8 0.8 copy-done.14
  109.6 3.2 %shard_map.66 = s16[2,256,512]{2,1,0:T(8,128)(2,1)} custom-call(s32[11]{0:T(128)} %copy-done.5, s32[2,48]{1,0:T(2,128)} %select_reduce_fusion.where, s16[2,256,512]{2,1,0:T(8,128)(2,1)} %copy-done.2, s16[2,256,512]{2,1,0:T(8,128)(2,1)} %copy-done.12, s16[2,256,512]{2,1,0:T(8,128)(2,1)} %copy-done.13, s16[2,256,512]{2,1,0:T(8,128)(2,1)} %copy-done.14), custom_call_target="tpu_custom_call" | custom-call | bytes 3145728 | tf_op jit(solution)/shard_map/pallas_call | solution.py:227
  112.9 2.5 all-to-all-done.own
  115.3 0.8 collective-permute-start.15
  116.2 13.0 %collective-permute-start.16 = (f32[64,512]{1,0:T(8,128)S(1)}, f32[64,512]{1,0:T(8,128)S(1)}, u32[]{:S(2)}, u32[]{:S(2)}) collective-permute-start(f32[64,512]{1,0:T(8,128)S(1)} %get-tuple-element.57), channel_id=1, source_target_pairs={{0,16},{1,17},{2,18},{3,19},{4,20},{5,21},{6,22},{7,23},{8,24},{9,... | collective-permute-start | bytes 393224 | tf_op jit(solution)/shard_map/ppermute | solution.py:48
  129.2 4.4 %collective-permute-start.18 = (f32[64,512]{1,0:T(8,128)S(1)}, f32[64,512]{1,0:T(8,128)S(1)}, u32[]{:S(2)}, u32[]{:S(2)}) collective-permute-start(f32[64,512]{1,0:T(8,128)S(1)} %get-tuple-element.58), channel_id=1, source_target_pairs={{0,32},{1,33},{2,34},{3,35},{4,36},{5,37},{6,38},{7,39},{8,40},{9,... | collective-permute-start | bytes 393224 | tf_op jit(solution)/shard_map/ppermute | solution.py:48
  133.6 1.1 dynamic-slice_bitcast_fusion.3
  134.6 4.2 %collective-permute-start.24 = (s16[256,512]{1,0:T(8,128)(2,1)S(1)}, s16[256,512]{1,0:T(8,128)(2,1)S(1)}, u32[]{:S(2)}, u32[]{:S(2)}) collective-permute-start(s16[256,512]{1,0:T(8,128)(2,1)S(1)} %get-tuple-element.55), channel_id=1, source_target_pairs={{0,65},{1,64},{2,67},{3,66},{4,69},{5,68},{6,71},{7,70},{8,73},{9,... | collective-permute-start | bytes 786440 | tf_op jit(solution)/shard_map/ppermute | solution.py:48
  138.8 1.5 collective-permute-start.22
  140.3 0.9 collective-permute-start.23
  141.2 4.2 %collective-permute-start.21 = (f32[64,512]{1,0:T(8,128)S(1)}, f32[64,512]{1,0:T(8,128)S(1)}, u32[]{:S(2)}, u32[]{:S(2)}) collective-permute-start(f32[64,512]{1,0:T(8,128)S(1)} %fusion.2), channel_id=1, source_target_pairs={{0,1},{1,0},{2,3},{3,2},{4,5},{5,4},{6,7},{7,6},{8,9},{9,8},{10,11... | collective-permute-start | bytes 393224 | tf_op jit(solution)/shard_map/ppermute | solution.py:48
  145.4 5.2 %collective-permute-done.24.both = s16[256,512]{1,0:T(8,128)(2,1)S(1)} collective-permute-done((s16[256,512]{1,0:T(8,128)(2,1)S(1)}, s16[256,512]{1,0:T(8,128)(2,1)S(1)}, u32[]{:S(2)}, u32[]{:S(2)}) %collective-permute-start.24) | collective-permute-done | bytes 262176 | tf_op jit(solution)/shard_map/ppermute | solution.py:48
  150.6 2.4 collective-permute-start.19
  153.1 0.7 copy-done.17
  153.8 2.8 shard_map.68
  156.6 1.4 collective-permute-done.20
  158.1 0.6 collective-permute-done.19
  158.8 5.3 %shard_map.67 = s16[8,1552,256]{2,1,0:T(8,128)(2,1)} custom-call(s32[11]{0:T(128)S(1)} %copy-done.6, s32[2,32]{1,0:T(2,128)S(1)} %select_reduce_fusion.1.slots, s32[2,48]{1,0:T(2,128)S(1)} %copy-done.4, s16[8,272,1024]{2,1,0:T(8,128)(2,1)} %all-to-all-done.own, s16[8,272,1024]{2,1,0:T(8,128)(2,1)} %collective-permute-done.15.other), custom_call_target="tpu_custom_call" | custom-call | bytes 8388608 | tf_op jit(solution)/shard_map/pallas_call | solution.py:374
  164.1 4.9 %all-to-all-start.1 = ((s16[8,1552,256]{2,1,0:T(8,128)(2,1)}), s16[8,1552,256]{2,1,0:T(8,128)(2,1)}, u32[]{:S(2)}, u32[]{:S(2)}) async-start(s16[8,1552,256]{2,1,0:T(8,128)(2,1)} %shard_map.67), calls=%async_computation.1 | async-start | bytes 12713984 | tf_op jit(solution)/shard_map/all_to_all | solution.py:735
  169.1 1.2 collective-permute-start.27
  170.2 2.9 collective-permute-start.26
  173.2 2.7 collective-permute-start.31
  175.9 2.7 collective-permute-done.25
  178.7 12.3 %collective-permute-start.28 = (f32[256,512]{1,0:T(8,128)S(1)}, f32[256,512]{1,0:T(8,128)}, u32[]{:S(2)}, u32[]{:S(2)}) collective-permute-start(f32[256,512]{1,0:T(8,128)S(1)} %bitcast.84), channel_id=1, source_target_pairs={{0,8},{1,9},{2,10},{3,11},{4,12},{5,13},{6,14},{7,15},{8,0},{9,1},... | collective-permute-start | bytes 1572872 | tf_op jit(solution)/shard_map/ppermute | solution.py:48
  191.0 8.7 %collective-permute-done.29 = s16[2,256,512]{2,1,0:T(8,128)(2,1)S(1)} collective-permute-done((s16[2,256,512]{2,1,0:T(8,128)(2,1)S(1)}, s16[2,256,512]{2,1,0:T(8,128)(2,1)S(1)}, u32[]{:S(2)}, u32[]{:S(2)}) %collective-permute-start.29) | collective-permute-done | bytes 524320 | tf_op jit(solution)/shard_map/ppermute | solution.py:48
  199.7 0.2 pad_add_fusion.own
  200.0 3.8 %collective-permute-start.32 = (s16[4,2,256,512]{3,2,1,0:T(8,128)(2,1)S(1)}, s16[4,2,256,512]{3,2,1,0:T(8,128)(2,1)}, u32[]{:S(2)}, u32[]{:S(2)}) collective-permute-start(s16[4,2,256,512]{3,2,1,0:T(8,128)(2,1)S(1)} %pad_add_fusion.own), channel_id=1, source_target_pairs={{0,8},{1,9},{2,10},{3,11},{4,12},{5,13},{6,14},{7,15},{8,0},{9,1},... | collective-permute-start | bytes 6291464 | tf_op jit(solution)/shard_map/ppermute | solution.py:48
  203.8 1.2 broadcast_select_fusion.1
  205.1 29.6 %shard_map.69.inv = f32[512,512]{1,0:T(8,128)S(1)} custom-call(f32[512,512]{1,0:T(8,128)S(1)} %pad_maximum_fusion.a_ref.diag), custom_call_target="tpu_custom_call" | custom-call | flops 17179869184 | bytes 2097152 | tf_op jit(solution)/shard_map/pallas_call | solution.py:475
  234.7 1.0 copy-done.7
  235.7 7.1 %shard_map.70 = s16[8,208,512]{2,1,0:T(8,128)(2,1)} custom-call(s32[11]{0:T(128)S(1)} %copy-done.6, s32[2,48]{1,0:T(2,128)S(1)} %copy-done.4, s16[4,2,256,512]{3,2,1,0:T(8,128)(2,1)S(1)} %pad_add_fusion.own, s16[4,2,256,512]{3,2,1,0:T(8,128)(2,1)} %collective-permute-done.32.other), custom_call_target="tpu_custom_call" | custom-call | bytes 6291456 | tf_op jit(solution)/shard_map/pallas_call | solution.py:312
  242.8 30.7 %all_to_all.15.gx = s16[8,208,512]{2,1,0:T(8,128)(2,1)S(1)} all-to-all(s16[8,208,512]{2,1,0:T(8,128)(2,1)} %shard_map.70), channel_id=1, replica_groups=mesh['child'=2,'x'=4,'core'=2,'z'=4,'yh'=2] {'z','yh'}, dimensions={0} | all-to-all | bytes 3407872 | tf_op jit(solution)/shard_map/all_to_all | solution.py:742
  273.5 1.6 collective-permute-start.33
  275.1 2.1 collective-permute-done.33.goth
  277.2 15.5 %shard_map.71 = f32[768,1536]{1,0:T(8,128)} custom-call(s32[11]{0:T(128)S(1)} %copy-done.6, s32[2,48]{1,0:T(2,128)S(1)} %copy-done.4, f32[512,512]{1,0:T(8,128)S(1)} %pad_maximum_fusion.a_ref.diag, f32[512,512]{1,0:T(8,128)} %copy-done.7, s16[8,208,512]{2,1,0:T(8,128)(2,1)} %copy-done.8, s16[8,112,512]{2,1,0:T(8,128)(2,1)S(1)} %collective-permute-done.33.goth, ...), custom_call_target="tpu_custom_call" | custom-call | flops 8589934592 | bytes 20971520 | tf_op jit(solution)/shard_map/pallas_call | solution.py:604
  (84 shorter events, 1.2 us)
Async XLA Ops:
  0.0 9.1 %copy-start = (bf16[1,1024,1024]{2,1,0:T(8,128)(2,1)S(1)}, bf16[1,1024,1024]{2,1,0:T(8,128)(2,1)}, u32[]{:S(2)}) copy-start(bf16[1,1024,1024]{2,1,0:T(8,128)(2,1)} %param.7) | copy-start | bytes 6291460
  2.8 6.2 %collective-permute-start = (bf16[512,1024]{1,0:T(8,128)(2,1)}, bf16[512,1024]{1,0:T(8,128)(2,1)}, u32[]{:S(2)}, u32[]{:S(2)}) collective-permute-start(bf16[512,1024]{1,0:T(8,128)(2,1)} %get-tuple-element.52), channel_id=1, source_target_pairs={{0,8},{9,1},{18,26},{27,19},{36,44},{45,37},{54,62},{63,55},{64,72... | collective-permute-start | bytes 3145736 | tf_op jit(solution)/shard_map/ppermute | solution.py:659
  4.1 4.9 %collective-permute-start.3 = (bf16[512,1024]{1,0:T(8,128)(2,1)S(1)}, bf16[512,1024]{1,0:T(8,128)(2,1)}, u32[]{:S(2)}, u32[]{:S(2)}) collective-permute-start(bf16[512,1024]{1,0:T(8,128)(2,1)S(1)} %get-tuple-element.51), channel_id=1, source_target_pairs={{0,48},{4,56},{9,49},{13,57},{18,2},{22,10},{27,3},{31,11},{36,20}... | collective-permute-start | bytes 3145736 | tf_op jit(solution)/shard_map/ppermute | solution.py:652
  5.8 3.3 %collective-permute-start.2 = (bf16[512,1024]{1,0:T(8,128)(2,1)S(1)}, bf16[512,1024]{1,0:T(8,128)(2,1)}, u32[]{:S(2)}, u32[]{:S(2)}) collective-permute-start(bf16[512,1024]{1,0:T(8,128)(2,1)S(1)} %get-tuple-element.51), channel_id=1, source_target_pairs={{0,32},{4,40},{9,33},{13,41},{18,50},{22,58},{27,51},{31,59},{36,4... | collective-permute-start | bytes 3145736 | tf_op jit(solution)/shard_map/ppermute | solution.py:652
  7.4 1.7 collective-permute-start.1
  9.0 33.3 %copy-start.18 = (s32[48]{0:T(128)S(1)}, s32[48]{0:T(128)}, u32[]{:S(2)}) copy-start(s32[48]{0:T(128)} %param.10) | copy-start | bytes 580
  9.0 33.4 %copy-start.19 = (s32[2,32]{1,0:T(2,128)S(1)}, s32[2,32]{1,0:T(2,128)}, u32[]{:S(2)}) copy-start(s32[2,32]{1,0:T(2,128)} %param.9) | copy-start | bytes 772
  9.0 35.7 %copy-start.3 = (s32[2,32,32]{2,1,0:T(8,128)S(1)}, s32[2,32,32]{2,1,0:T(8,128)}, u32[]{:S(2)}) copy-start(s32[2,32,32]{2,1,0:T(8,128)} %pat.1) | copy-start | bytes 24580
  11.0 33.7 %collective-permute-start.4 = (bf16[512,1024]{1,0:T(8,128)(2,1)S(1)}, bf16[512,1024]{1,0:T(8,128)(2,1)}, u32[]{:S(2)}, u32[]{:S(2)}) collective-permute-start(bf16[512,1024]{1,0:T(8,128)(2,1)S(1)} %fusion.mine), channel_id=1, source_target_pairs={{0,8},{1,9},{2,10},{3,11},{4,12},{5,13},{6,14},{7,15},{8,0},{9,1},... | collective-permute-start | bytes 3145736 | tf_op jit(solution)/shard_map/ppermute | solution.py:48
  42.4 38.2 %copy-start.5 = (s32[11]{0:T(128)}, s32[11]{0:T(128)S(1)}, u32[]{:S(2)}) copy-start(s32[11]{0:T(128)S(1)} %stack.55.ids) | copy-start | bytes 136
  57.8 5.1 %copy-start.11 = (f32[512,512]{1,0:T(8,128)S(1)}, f32[512,512]{1,0:T(8,128)}, u32[]{:S(2)}) copy-start(f32[512,512]{1,0:T(8,128)} %get-tuple-element.34) | copy-start | bytes 3145732
  57.8 57.5 %all-to-all-start = ((s16[8,272,1024]{2,1,0:T(8,128)(2,1)}), s16[8,272,1024]{2,1,0:T(8,128)(2,1)}, u32[]{:S(2)}, u32[]{:S(2)}) async-start(s16[8,272,1024]{2,1,0:T(8,128)(2,1)} %get-tuple-element.33), calls=%async_computation | async-start | bytes 8912896 | tf_op jit(solution)/shard_map/all_to_all | solution.py:718
  62.9 17.7 %copy-start.1 = (f32[1024,512]{1,0:T(8,128)S(1)}, f32[1024,512]{1,0:T(8,128)}, u32[]{:S(2)}) copy-start(f32[1024,512]{1,0:T(8,128)} %get-tuple-element.37.gcol) | copy-start | bytes 6291460
  63.7 2.4 collective-permute-start.5
  67.3 9.0 %collective-permute-start.6 = (f32[64,512]{1,0:T(8,128)S(1)}, f32[64,512]{1,0:T(8,128)S(1)}, u32[]{:S(2)}, u32[]{:S(2)}) collective-permute-start(f32[64,512]{1,0:T(8,128)S(1)} %get-tuple-element.60), channel_id=1, source_target_pairs={{0,2},{1,3},{2,4},{3,5},{4,6},{5,7},{6,0},{7,1},{8,10},{9,11},{10,... | collective-permute-start | bytes 393224 | tf_op jit(solution)/shard_map/ppermute | solution.py:48
  67.4 8.9 %collective-permute-start.8 = (f32[64,512]{1,0:T(8,128)S(1)}, f32[64,512]{1,0:T(8,128)S(1)}, u32[]{:S(2)}, u32[]{:S(2)}) collective-permute-start(f32[64,512]{1,0:T(8,128)S(1)} %get-tuple-element.61), channel_id=1, source_target_pairs={{0,4},{1,5},{2,6},{3,7},{4,0},{5,1},{6,2},{7,3},{8,12},{9,13},{10,... | collective-permute-start | bytes 393224 | tf_op jit(solution)/shard_map/ppermute | solution.py:48
  68.5 8.0 %collective-permute-start.7 = (f32[64,512]{1,0:T(8,128)S(1)}, f32[64,512]{1,0:T(8,128)S(1)}, u32[]{:S(2)}, u32[]{:S(2)}) collective-permute-start(f32[64,512]{1,0:T(8,128)S(1)} %get-tuple-element.62), channel_id=1, source_target_pairs={{0,6},{1,7},{2,0},{3,1},{4,2},{5,3},{6,4},{7,5},{8,14},{9,15},{10,... | collective-permute-start | bytes 393224 | tf_op jit(solution)/shard_map/ppermute | solution.py:48
  76.5 11.6 %collective-permute-start.11 = (f32[64,512]{1,0:T(8,128)S(1)}, f32[64,512]{1,0:T(8,128)S(1)}, u32[]{:S(2)}, u32[]{:S(2)}) collective-permute-start(f32[64,512]{1,0:T(8,128)S(1)} %fusion.4), channel_id=1, source_target_pairs={{0,4},{1,5},{2,6},{3,7},{4,0},{5,1},{6,2},{7,3},{8,12},{9,13},{10,... | collective-permute-start | bytes 393224 | tf_op jit(solution)/shard_map/ppermute | solution.py:48
  77.6 10.4 %collective-permute-start.10 = (f32[64,512]{1,0:T(8,128)S(1)}, f32[64,512]{1,0:T(8,128)S(1)}, u32[]{:S(2)}, u32[]{:S(2)}) collective-permute-start(f32[64,512]{1,0:T(8,128)S(1)} %fusion.4), channel_id=1, source_target_pairs={{0,6},{1,7},{2,0},{3,1},{4,2},{5,3},{6,4},{7,5},{8,14},{9,15},{10,... | collective-permute-start | bytes 393224 | tf_op jit(solution)/shard_map/ppermute | solution.py:48
  80.1 6.2 %collective-permute-start.9 = (f32[64,512]{1,0:T(8,128)S(1)}, f32[64,512]{1,0:T(8,128)S(1)}, u32[]{:S(2)}, u32[]{:S(2)}) collective-permute-start(f32[64,512]{1,0:T(8,128)S(1)} %fusion.4), channel_id=1, source_target_pairs={{0,2},{1,3},{2,4},{3,5},{4,6},{5,7},{6,0},{7,1},{8,10},{9,11},{10,... | collective-permute-start | bytes 393224 | tf_op jit(solution)/shard_map/ppermute | solution.py:48
  82.1 0.8 copy-start.2
  82.9 15.1 %collective-permute-start.12 = (s16[2,256,512]{2,1,0:T(8,128)(2,1)S(1)}, s16[2,256,512]{2,1,0:T(8,128)(2,1)S(1)}, u32[]{:S(2)}, u32[]{:S(2)}) collective-permute-start(s16[2,256,512]{2,1,0:T(8,128)(2,1)S(1)} %get-tuple-element.39), channel_id=1, source_target_pairs={{0,2},{1,3},{2,4},{3,5},{4,6},{5,7},{6,0},{7,1},{8,10},{9,11},{10,... | collective-permute-start | bytes 1572872 | tf_op jit(solution)/shard_map/ppermute | solution.py:48
  84.3 23.6 %collective-permute-start.13 = (s16[2,256,512]{2,1,0:T(8,128)(2,1)S(1)}, s16[2,256,512]{2,1,0:T(8,128)(2,1)S(1)}, u32[]{:S(2)}, u32[]{:S(2)}) collective-permute-start(s16[2,256,512]{2,1,0:T(8,128)(2,1)S(1)} %get-tuple-element.40), channel_id=1, source_target_pairs={{0,4},{1,5},{2,6},{3,7},{4,0},{5,1},{6,2},{7,3},{8,12},{9,13},{10,... | collective-permute-start | bytes 1572872 | tf_op jit(solution)/shard_map/ppermute | solution.py:48
  86.3 22.5 %collective-permute-start.14 = (s16[2,256,512]{2,1,0:T(8,128)(2,1)S(1)}, s16[2,256,512]{2,1,0:T(8,128)(2,1)S(1)}, u32[]{:S(2)}, u32[]{:S(2)}) collective-permute-start(s16[2,256,512]{2,1,0:T(8,128)(2,1)S(1)} %get-tuple-element.41), channel_id=1, source_target_pairs={{0,6},{1,7},{2,0},{3,1},{4,2},{5,3},{6,4},{7,5},{8,14},{9,15},{10,... | collective-permute-start | bytes 1572872 | tf_op jit(solution)/shard_map/ppermute | solution.py:48
  98.0 10.9 %copy-start.12 = (s16[2,256,512]{2,1,0:T(8,128)(2,1)}, s16[2,256,512]{2,1,0:T(8,128)(2,1)S(1)}, u32[]{:S(2)}) copy-start(s16[2,256,512]{2,1,0:T(8,128)(2,1)S(1)} %collective-permute-done.12.refs_1_) | copy-start | bytes 1572868
  108.0 0.9 copy-start.13
  108.8 0.8 copy-start.14
  115.3 43.4 %collective-permute-start.15 = (s16[8,272,1024]{2,1,0:T(8,128)(2,1)}, s16[8,272,1024]{2,1,0:T(8,128)(2,1)}, u32[]{:S(2)}, u32[]{:S(2)}) collective-permute-start(s16[8,272,1024]{2,1,0:T(8,128)(2,1)} %all-to-all-done.own), channel_id=1, source_target_pairs={{0,8},{1,9},{2,10},{3,11},{4,12},{5,13},{6,14},{7,15},{8,0},{9,1},... | collective-permute-start | bytes 13369352 | tf_op jit(solution)/shard_map/ppermute | solution.py:48
  116.2 42.6 %copy-start.4 = (s32[2,48]{1,0:T(2,128)S(1)}, s32[2,48]{1,0:T(2,128)}, u32[]{:S(2)}) copy-start(s32[2,48]{1,0:T(2,128)} %select_reduce_fusion.where) | copy-start | bytes 1156
  116.2 42.6 %copy-start.6 = (s32[11]{0:T(128)S(1)}, s32[11]{0:T(128)}, u32[]{:S(2)}) copy-start(s32[11]{0:T(128)} %copy-done.5) | copy-start | bytes 136
  116.2 22.6 %collective-permute-start.16 = (f32[64,512]{1,0:T(8,128)S(1)}, f32[64,512]{1,0:T(8,128)S(1)}, u32[]{:S(2)}, u32[]{:S(2)}) collective-permute-start(f32[64,512]{1,0:T(8,128)S(1)} %get-tuple-element.57), channel_id=1, source_target_pairs={{0,16},{1,17},{2,18},{3,19},{4,20},{5,21},{6,22},{7,23},{8,24},{9,... | collective-permute-start | bytes 393224 | tf_op jit(solution)/shard_map/ppermute | solution.py:48
  129.2 11.1 %collective-permute-start.18 = (f32[64,512]{1,0:T(8,128)S(1)}, f32[64,512]{1,0:T(8,128)S(1)}, u32[]{:S(2)}, u32[]{:S(2)}) collective-permute-start(f32[64,512]{1,0:T(8,128)S(1)} %get-tuple-element.58), channel_id=1, source_target_pairs={{0,32},{1,33},{2,34},{3,35},{4,36},{5,37},{6,38},{7,39},{8,40},{9,... | collective-permute-start | bytes 393224 | tf_op jit(solution)/shard_map/ppermute | solution.py:48
  133.5 7.7 %collective-permute-start.17 = (f32[64,512]{1,0:T(8,128)S(1)}, f32[64,512]{1,0:T(8,128)S(1)}, u32[]{:S(2)}, u32[]{:S(2)}) collective-permute-start(f32[64,512]{1,0:T(8,128)S(1)} %get-tuple-element.59), channel_id=1, source_target_pairs={{0,48},{1,49},{2,50},{3,51},{4,52},{5,53},{6,54},{7,55},{8,56},{9,... | collective-permute-start | bytes 393224 | tf_op jit(solution)/shard_map/ppermute | solution.py:48
  134.6 18.4 %copy-start.10 = (s16[256,512]{1,0:T(8,128)(2,1)}, s16[256,512]{1,0:T(8,128)(2,1)S(1)}, u32[]{:S(2)}) copy-start(s16[256,512]{1,0:T(8,128)(2,1)S(1)} %get-tuple-element.56.kept) | copy-start | bytes 786436
  134.6 16.0 %collective-permute-start.24 = (s16[256,512]{1,0:T(8,128)(2,1)S(1)}, s16[256,512]{1,0:T(8,128)(2,1)S(1)}, u32[]{:S(2)}, u32[]{:S(2)}) collective-permute-start(s16[256,512]{1,0:T(8,128)(2,1)S(1)} %get-tuple-element.55), channel_id=1, source_target_pairs={{0,65},{1,64},{2,67},{3,66},{4,69},{5,68},{6,71},{7,70},{8,73},{9,... | collective-permute-start | bytes 786440 | tf_op jit(solution)/shard_map/ppermute | solution.py:48
  138.8 11.8 %collective-permute-start.22 = (s16[256,512]{1,0:T(8,128)(2,1)S(1)}, s16[256,512]{1,0:T(8,128)(2,1)S(1)}, u32[]{:S(2)}, u32[]{:S(2)}) collective-permute-start(s16[256,512]{1,0:T(8,128)(2,1)S(1)} %get-tuple-element.55), channel_id=1, source_target_pairs={{0,1},{1,0},{2,3},{3,2},{4,5},{5,4},{6,7},{7,6},{8,9},{9,8},{10,11... | collective-permute-start | bytes 786440 | tf_op jit(solution)/shard_map/ppermute | solution.py:48
  140.3 12.7 %collective-permute-start.23 = (s16[256,512]{1,0:T(8,128)(2,1)S(1)}, s16[256,512]{1,0:T(8,128)(2,1)S(1)}, u32[]{:S(2)}, u32[]{:S(2)}) collective-permute-start(s16[256,512]{1,0:T(8,128)(2,1)S(1)} %get-tuple-element.56.kept), channel_id=1, source_target_pairs={{0,64},{1,65},{2,66},{3,67},{4,68},{5,69},{6,70},{7,71},{8,72},{9,... | collective-permute-start | bytes 786440 | tf_op jit(solution)/shard_map/ppermute | solution.py:48
  141.2 15.4 %collective-permute-start.21 = (f32[64,512]{1,0:T(8,128)S(1)}, f32[64,512]{1,0:T(8,128)S(1)}, u32[]{:S(2)}, u32[]{:S(2)}) collective-permute-start(f32[64,512]{1,0:T(8,128)S(1)} %fusion.2), channel_id=1, source_target_pairs={{0,1},{1,0},{2,3},{3,2},{4,5},{5,4},{6,7},{7,6},{8,9},{9,8},{10,11... | collective-permute-start | bytes 393224 | tf_op jit(solution)/shard_map/ppermute | solution.py:48
  150.6 2.5 copy-start.15
  150.6 7.5 %collective-permute-start.20 = (f32[64,512]{1,0:T(8,128)S(1)}, f32[64,512]{1,0:T(8,128)S(1)}, u32[]{:S(2)}, u32[]{:S(2)}) collective-permute-start(f32[64,512]{1,0:T(8,128)S(1)} %fusion.2), channel_id=1, source_target_pairs={{0,64},{1,65},{2,66},{3,67},{4,68},{5,69},{6,70},{7,71},{8,72},{9,... | collective-permute-start | bytes 393224 | tf_op jit(solution)/shard_map/ppermute | solution.py:48
  150.6 2.5 copy-start.16
  150.6 8.1 %collective-permute-start.19 = (f32[64,512]{1,0:T(8,128)S(1)}, f32[64,512]{1,0:T(8,128)S(1)}, u32[]{:S(2)}, u32[]{:S(2)}) collective-permute-start(f32[64,512]{1,0:T(8,128)S(1)} %fusion.2), channel_id=1, source_target_pairs={{0,65},{1,64},{2,67},{3,66},{4,69},{5,68},{6,71},{7,70},{8,73},{9,... | collective-permute-start | bytes 393224 | tf_op jit(solution)/shard_map/ppermute | solution.py:48
  153.1 0.7 copy-start.17
  164.1 9.0 %copy-start.9 = (s16[2,256,512]{2,1,0:T(8,128)(2,1)S(1)}, s16[2,256,512]{2,1,0:T(8,128)(2,1)}, u32[]{:S(2)}) copy-start(s16[2,256,512]{2,1,0:T(8,128)(2,1)} %shard_map.68) | copy-start | bytes 1572868
  164.1 78.7 %all-to-all-start.1 = ((s16[8,1552,256]{2,1,0:T(8,128)(2,1)}), s16[8,1552,256]{2,1,0:T(8,128)(2,1)}, u32[]{:S(2)}, u32[]{:S(2)}) async-start(s16[8,1552,256]{2,1,0:T(8,128)(2,1)} %shard_map.67), calls=%async_computation.1 | async-start | bytes 12713984 | tf_op jit(solution)/shard_map/all_to_all | solution.py:735
  169.1 9.6 %collective-permute-start.27 = (f32[64,512]{1,0:T(8,128)S(1)}, f32[64,512]{1,0:T(8,128)S(1)}, u32[]{:S(2)}, u32[]{:S(2)}) collective-permute-start(f32[64,512]{1,0:T(8,128)S(1)} %add_add_fusion), channel_id=1, source_target_pairs={{0,32},{1,33},{2,34},{3,35},{4,36},{5,37},{6,38},{7,39},{8,40},{9,... | collective-permute-start | bytes 393224 | tf_op jit(solution)/shard_map/ppermute | solution.py:48
  170.2 8.4 %collective-permute-start.26 = (f32[64,512]{1,0:T(8,128)S(1)}, f32[64,512]{1,0:T(8,128)S(1)}, u32[]{:S(2)}, u32[]{:S(2)}) collective-permute-start(f32[64,512]{1,0:T(8,128)S(1)} %add_add_fusion), channel_id=1, source_target_pairs={{0,48},{1,49},{2,50},{3,51},{4,52},{5,53},{6,54},{7,55},{8,56},{9,... | collective-permute-start | bytes 393224 | tf_op jit(solution)/shard_map/ppermute | solution.py:48
  173.1 5.5 %collective-permute-start.25 = (f32[64,512]{1,0:T(8,128)S(1)}, f32[64,512]{1,0:T(8,128)S(1)}, u32[]{:S(2)}, u32[]{:S(2)}) collective-permute-start(f32[64,512]{1,0:T(8,128)S(1)} %add_add_fusion), channel_id=1, source_target_pairs={{0,16},{1,17},{2,18},{3,19},{4,20},{5,21},{6,22},{7,23},{8,24},{9,... | collective-permute-start | bytes 393224 | tf_op jit(solution)/shard_map/ppermute | solution.py:48
  173.2 17.9 %collective-permute-start.31 = (s16[2,256,512]{2,1,0:T(8,128)(2,1)S(1)}, s16[2,256,512]{2,1,0:T(8,128)(2,1)S(1)}, u32[]{:S(2)}, u32[]{:S(2)}) collective-permute-start(s16[2,256,512]{2,1,0:T(8,128)(2,1)S(1)} %copy-done.9), channel_id=1, source_target_pairs={{0,48},{1,49},{2,50},{3,51},{4,52},{5,53},{6,54},{7,55},{8,56},{9,... | collective-permute-start | bytes 1572872 | tf_op jit(solution)/shard_map/ppermute | solution.py:48
  175.8 15.2 %collective-permute-start.30 = (s16[2,256,512]{2,1,0:T(8,128)(2,1)S(1)}, s16[2,256,512]{2,1,0:T(8,128)(2,1)S(1)}, u32[]{:S(2)}, u32[]{:S(2)}) collective-permute-start(s16[2,256,512]{2,1,0:T(8,128)(2,1)S(1)} %copy-done.9), channel_id=1, source_target_pairs={{0,32},{1,33},{2,34},{3,35},{4,36},{5,37},{6,38},{7,39},{8,40},{9,... | collective-permute-start | bytes 1572872 | tf_op jit(solution)/shard_map/ppermute | solution.py:48
  178.7 21.1 %collective-permute-start.29 = (s16[2,256,512]{2,1,0:T(8,128)(2,1)S(1)}, s16[2,256,512]{2,1,0:T(8,128)(2,1)S(1)}, u32[]{:S(2)}, u32[]{:S(2)}) collective-permute-start(s16[2,256,512]{2,1,0:T(8,128)(2,1)S(1)} %copy-done.9), channel_id=1, source_target_pairs={{0,16},{1,17},{2,18},{3,19},{4,20},{5,21},{6,22},{7,23},{8,24},{9,... | collective-permute-start | bytes 1572872 | tf_op jit(solution)/shard_map/ppermute | solution.py:48
  178.7 25.0 %collective-permute-start.28 = (f32[256,512]{1,0:T(8,128)S(1)}, f32[256,512]{1,0:T(8,128)}, u32[]{:S(2)}, u32[]{:S(2)}) collective-permute-start(f32[256,512]{1,0:T(8,128)S(1)} %bitcast.84), channel_id=1, source_target_pairs={{0,8},{1,9},{2,10},{3,11},{4,12},{5,13},{6,14},{7,15},{8,0},{9,1},... | collective-permute-start | bytes 1572872 | tf_op jit(solution)/shard_map/ppermute | solution.py:48
  200.0 35.7 %collective-permute-start.32 = (s16[4,2,256,512]{3,2,1,0:T(8,128)(2,1)S(1)}, s16[4,2,256,512]{3,2,1,0:T(8,128)(2,1)}, u32[]{:S(2)}, u32[]{:S(2)}) collective-permute-start(s16[4,2,256,512]{3,2,1,0:T(8,128)(2,1)S(1)} %pad_add_fusion.own), channel_id=1, source_target_pairs={{0,8},{1,9},{2,10},{3,11},{4,12},{5,13},{6,14},{7,15},{8,0},{9,1},... | collective-permute-start | bytes 6291464 | tf_op jit(solution)/shard_map/ppermute | solution.py:48
  234.7 1.0 copy-start.7
  273.5 3.8 %copy-start.8 = (s16[8,208,512]{2,1,0:T(8,128)(2,1)}, s16[8,208,512]{2,1,0:T(8,128)(2,1)S(1)}, u32[]{:S(2)}) copy-start(s16[8,208,512]{2,1,0:T(8,128)(2,1)S(1)} %all_to_all.15.gx) | copy-start | bytes 5111812
  273.5 3.7 %collective-permute-start.33 = (s16[8,112,512]{2,1,0:T(8,128)(2,1)S(1)}, s16[8,112,512]{2,1,0:T(8,128)(2,1)S(1)}, u32[]{:S(2)}, u32[]{:S(2)}) collective-permute-start(s16[8,112,512]{2,1,0:T(8,128)(2,1)S(1)} %slice.10), channel_id=1, source_target_pairs={{0,8},{1,9},{2,10},{3,11},{4,12},{5,13},{6,14},{7,15},{8,0},{9,1},... | collective-permute-start | bytes 2752520 | tf_op jit(solution)/shard_map/ppermute | solution.py:48

commit v6 on v5

--- a/solution.py
+++ b/solution.py
@@ -214,53 +214,71 @@
 
 
 def choose_z_kernel(ids, where, *refs):
-    for rows, cols, holder in regions(ids, where, ids[0]):
-        for d in range(4):
-
-            @pl.when(lax.rem(ids[5] - holder // 2 + 4, 4) == d)
-            def _():
-                refs[4][:, rows, cols] = refs[d][:, rows, cols]
+    out, sems = refs[4], refs[5]
+
+    def each(act):
+        for n, (rows, cols, holder) in enumerate(regions(ids, where, ids[0])):
+            for d in range(4):
+
+                @pl.when(lax.rem(ids[5] - holder // 2 + 4, 4) == d)
+                def _():
+                    act(
+                        pltpu.make_async_copy(
+                            refs[d].at[:, rows, cols], out.at[:, rows, cols], sems.at[n]
+                        )
+                    )
+
+    each(lambda copy: copy.start())
+    each(lambda copy: copy.wait())
 
 
 def choose_z(ids, where, parts):
-    whole = pl.BlockSpec((2, TILE, PANEL), lambda i, *s: (0, 0, 0))
     return pl.pallas_call(
         choose_z_kernel,
         grid_spec=pltpu.PrefetchScalarGridSpec(
-            num_scalar_prefetch=2, grid=(1,), in_specs=[whole] * 4, out_specs=whole
+            num_scalar_prefetch=2,
+            grid=(1,),
+            in_specs=[pl.BlockSpec(memory_space=pl.ANY)] * 4,
+            out_specs=pl.BlockSpec((2, TILE, PANEL), lambda i, *s: (0, 0, 0)),
+            scratch_shapes=[pltpu.SemaphoreType.DMA((4,))],
         ),
         out_shape=jax.ShapeDtypeStruct((2, TILE, PANEL), I16),
-        cost_estimate=pl.CostEstimate(flops=0, bytes_accessed=3 * MIB, transcendentals=0),
+        cost_estimate=pl.CostEstimate(flops=0, bytes_accessed=MIB, transcendentals=0),
     )(ids, where, *parts)
 
 
-def choose_y_kernel(ids, where, kept, beside, across, both, out):
-    for n, (near, far) in enumerate(((kept, beside), (across, both))):
-        child = lax.rem(ids[0] + n, 2)
-        for rows, cols, holder in regions(ids, where, child):
-            here = lax.rem(holder + 8, 2) == ids[6]
-
-            @pl.when(here)
-            def _():
-                out[n, rows, cols] = near[rows, cols]
-
-            @pl.when(jnp.logical_not(here))
-            def _():
-                out[n, rows, cols] = far[rows, cols]
+def choose_y_kernel(ids, where, kept, beside, across, both, out, sems):
+    def each(act):
+        for n, (near, far) in enumerate(((kept, beside), (across, both))):
+            child = lax.rem(ids[0] + n, 2)
+            for m, (rows, cols, holder) in enumerate(regions(ids, where, child)):
+                here = lax.rem(holder + 8, 2) == ids[6]
+                for side, ref in ((True, near), (False, far)):
+
+                    @pl.when(here == side)
+                    def _():
+                        act(
+                            pltpu.make_async_copy(
+                                ref.at[rows, cols], out.at[n, rows, cols], sems.at[n * 4 + m]
+                            )
+                        )
+
+    each(lambda copy: copy.start())
+    each(lambda copy: copy.wait())
 
 
 def choose_y(ids, where, parts):
-    whole = pl.BlockSpec((TILE, PANEL), lambda i, *s: (0, 0))
     return pl.pallas_call(
         choose_y_kernel,
         grid_spec=pltpu.PrefetchScalarGridSpec(
             num_scalar_prefetch=2,
             grid=(1,),
-            in_specs=[whole] * 4,
+            in_specs=[pl.BlockSpec(memory_space=pl.ANY)] * 4,
             out_specs=pl.BlockSpec((2, TILE, PANEL), lambda i, *s: (0, 0, 0)),
+            scratch_shapes=[pltpu.SemaphoreType.DMA((8,))],
         ),
         out_shape=jax.ShapeDtypeStruct((2, TILE, PANEL), I16),
-        cost_estimate=pl.CostEstimate(flops=0, bytes_accessed=2 * MIB, transcendentals=0),
+        cost_estimate=pl.CostEstimate(flops=0, bytes_accessed=MIB, transcendentals=0),
     )(ids, where, *parts)
 
 
@@ -322,52 +340,64 @@
                 pltpu.VMEM((8, PANEL), F32),
             ],
         ),
-        out_shape=pltpu.HBM((8, GROWS, PANEL), I16),
+        out_shape=jax.ShapeDtypeStruct((8, GROWS, PANEL), I16),
         compiler_params=pltpu.CompilerParams(vmem_limit_bytes=24 * MIB),
         cost_estimate=pl.CostEstimate(flops=0, bytes_accessed=6 * MIB, transcendentals=0),
     )(ids, where, own, other)
 
 
-def route_kernel(ids, slots, where, own, other, send, codes, sems):
+def route_kernel(ids, slots, where, own, other, send, lines, codes, isem, osem, csem):
     c, g, core = ids[2], ids[3], ids[4]
     rows = [where[ch, g * RT + p] for ch in range(2) for p in range(RT)]
-
-    def each(act):
-        for m in range(2 * RT):
-            i = rows[m]
-            src = (m // RT) * 4 + i // 8
-            for here, buf in ((True, own), (False, other)):
-
-                @pl.when((i >= 0) & (((i // CT) % 2 == core) == here))
-                def _():
-                    act(
-                        pltpu.make_async_copy(
-                            buf.at[src, pl.ds(TILE, CODE), :], codes.at[m], sems.at[m * 5 + CT]
-                        )
+    to = [[slots[ch, c * CT + j] // QT for j in range(CT)] for ch in range(2)]
+
+    def come(m, act):
+        i = rows[m]
+        src = (m // RT) * 4 + i // 8
+        for here, buf in ((True, own), (False, other)):
+
+            @pl.when((i >= 0) & (((i // CT) % 2 == core) == here))
+            def _():
+                act(pltpu.make_async_copy(buf.at[src], lines.at[m], isem.at[m]))
+
+    def leave(m, act):
+        @pl.when(rows[m] >= 0)
+        def _():
+            for j in range(CT):
+                act(
+                    pltpu.make_async_copy(
+                        lines.at[m, pl.ds(0, TILE), pl.ds(j * TILE, TILE)],
+                        send.at[to[m // RT][j], pl.ds(m * TILE, TILE), :],
+                        osem.at[m * CT + j],
                     )
-                    for j in range(CT):
-                        q = slots[m // RT, c * CT + j] // QT
-                        act(
-                            pltpu.make_async_copy(
-                                buf.at[src, pl.ds(0, TILE), pl.ds(j * TILE, TILE)],
-                                send.at[q, pl.ds(m * TILE, TILE), :],
-                                sems.at[m * 5 + j],
-                            )
-                        )
-
-    each(lambda copy: copy.start())
-    each(lambda copy: copy.wait())
+                )
+
+    for m in range(2 * RT):
+        come(m, lambda copy: copy.start())
+    for m in range(2 * RT):
+        come(m, lambda copy: copy.wait())
+        leave(m, lambda copy: copy.start())
     line = lax.broadcasted_iota(I32, (CODE, TILE), 0)
+    codes[...] = jnp.zeros_like(codes)
     for ch in range(2):
         for j in range(CT):
-            q = slots[ch, c * CT + j] // QT
-            at = (q, slice(2 * RT * TILE, CROWS), slice(None))
-            v = send[at].astype(I32)
+            q = to[ch][j]
+            v = codes[q].astype(I32)
             for p in range(RT):
                 m = ch * RT + p
-                own_codes = codes[m, :, j * TILE : (j + 1) * TILE].astype(I32)
-                v = jnp.where(line == m, own_codes, v)
-            send[at] = v.astype(I16)
+                mine = lines[m, TILE:, j * TILE : (j + 1) * TILE].astype(I32)
+                v = jnp.where(line == m, mine, v)
+            codes[q] = v.astype(I16)
+    tails = [
+        pltpu.make_async_copy(codes.at[q], send.at[q, pl.ds(2 * RT * TILE, CODE), :], csem.at[q])
+        for q in range(8)
+    ]
+    for copy in tails:
+        copy.start()
+    for m in range(2 * RT):
+        leave(m, lambda copy: copy.wait())
+    for copy in tails:
+        copy.wait()
 
 
 def route(ids, slots, where, own, other):
@@ -377,10 +407,13 @@
             num_scalar_prefetch=3,
             grid=(1,),
             in_specs=[pl.BlockSpec(memory_space=pl.ANY)] * 2,
-            out_specs=pl.BlockSpec((8, CROWS, TILE), lambda i, *s: (0, 0, 0)),
+            out_specs=pl.BlockSpec(memory_space=pl.ANY),
             scratch_shapes=[
-                pltpu.VMEM((2 * RT, CODE, 1024), I16),
-                pltpu.SemaphoreType.DMA((2 * RT * 5,)),
+                pltpu.VMEM((2 * RT, TILE + CODE, 1024), I16),
+                pltpu.VMEM((8, CODE, TILE), I16),
+                pltpu.SemaphoreType.DMA((2 * RT,)),
+                pltpu.SemaphoreType.DMA((2 * RT * CT,)),
+                pltpu.SemaphoreType.DMA((8,)),
             ],
         ),
         out_shape=pltpu.HBM((8, CROWS, TILE), I16),
@@ -401,8 +434,8 @@
     )
 
 
-NB = 128
-WAYS = 4
+NB = 64
+WAYS = 8
 
 
 def inverse_kernel(a_ref, out, w, f):
@@ -493,12 +526,9 @@
     return one(a[0], b[0]) + (one(a[0], b[1]) + one(a[1], b[0]))
 
 
-def final_kernel(
-    ids, where, diag, inv, gx, goth, recv, front, out,
-    gbuf, rows_f, lh, ll, ih, il, tiles, codes, tsem,
-):
+def base_kernel(ids, where, recv, front, out, tiles, codes, tsem):
     t = pl.program_id(0)
-    c, g, core = ids[2], ids[3], ids[4]
+    c, g = ids[2], ids[3]
     col = c * QT + t
     js = [where[ch, col] for ch in range(2)]
     there = [[where[ch, g * RT + p] >= 0 for p in range(RT)] for ch in range(2)]
@@ -530,6 +560,46 @@
 
     each(lambda copy: copy.start())
 
+    out[...] = front[...]
+    each(lambda copy: copy.wait())
+    for p in range(RT):
+        rows = slice(p * TILE, (p + 1) * TILE)
+        for ch in range(2):
+            m = ch * RT + p
+
+            @pl.when(there[ch][p] & (js[ch] >= 0))
+            def _():
+                out[rows, :] += as_float(tiles[m]) * column_scale(codes[ch], m)
+
+
+def base(ids, where, recv, front):
+    line = pl.BlockSpec((RT * TILE, TILE), lambda i, *s: (0, i))
+    return pl.pallas_call(
+        base_kernel,
+        grid_spec=pltpu.PrefetchScalarGridSpec(
+            num_scalar_prefetch=2,
+            grid=(QT,),
+            in_specs=[pl.BlockSpec(memory_space=pl.ANY), line],
+            out_specs=line,
+            scratch_shapes=[
+                pltpu.VMEM((2 * RT, TILE, TILE), I16),
+                pltpu.VMEM((2, CODE, TILE), I16),
+                pltpu.SemaphoreType.DMA((2 * RT + 2,)),
+            ],
+        ),
+        out_shape=jax.ShapeDtypeStruct((RT * TILE, QT * TILE), F32),
+        compiler_params=pltpu.CompilerParams(vmem_limit_bytes=24 * MIB),
+        cost_estimate=pl.CostEstimate(flops=0, bytes_accessed=20 * MIB, transcendentals=0),
+    )(ids, where, recv, front)
+
+
+def final_kernel(
+    ids, diag, inv, gx, goth, front, out,
+    gbuf, rows_f, lh, ll, ih, il,
+):
+    t = pl.program_id(0)
+    c, g, core = ids[2], ids[3], ids[4]
+    col = c * QT + t
     @pl.when(t == 0)
     def _():
         hi, lo = split(inv[...])
@@ -579,16 +649,6 @@
 
     right = split(dot3(split(gbuf[0:TILE, :]), (ih[...], il[...])))
     out[...] = front[...] - dot3((lh[...], ll[...]), right)
-    each(lambda copy: copy.wait())
-    for p in range(RT):
-        rows = slice(p * TILE, (p + 1) * TILE)
-        for ch in range(2):
-            m = ch * RT + p
-
-            @pl.when(there[ch][p] & (js[ch] >= 0))
-            def _():
-                out[rows, :] += as_float(tiles[m]) * column_scale(codes[ch], m)
-
     for a in range(2):
 
         @pl.when(col == ids[8 + a])
@@ -596,7 +656,7 @@
             out[...] = rows_f[:, a * TILE : (a + 1) * TILE]
 
 
-def final(ids, where, diag, inv, gx, goth, recv, front):
+def final(ids, diag, inv, gx, goth, front):
     def whole(*shape):
         return pl.BlockSpec(shape, lambda i, *s: (0,) * len(shape))
 
@@ -604,14 +664,13 @@
     return pl.pallas_call(
         final_kernel,
         grid_spec=pltpu.PrefetchScalarGridSpec(
-            num_scalar_prefetch=2,
+            num_scalar_prefetch=1,
             grid=(QT,),
             in_specs=[
                 whole(PANEL, PANEL),
                 whole(PANEL, PANEL),
                 whole(8, GROWS, PANEL),
                 whole(8, GROWS - RT * STRIP, PANEL),
-                pl.BlockSpec(memory_space=pl.ANY),
                 line,
             ],
             out_specs=line,
@@ -622,15 +681,12 @@
                 pltpu.VMEM((RT * TILE, PANEL), BF16),
                 pltpu.VMEM((PANEL, PANEL), BF16),
                 pltpu.VMEM((PANEL, PANEL), BF16),
-                pltpu.VMEM((2 * RT, TILE, TILE), I16),
-                pltpu.VMEM((2, CODE, TILE), I16),
-                pltpu.SemaphoreType.DMA((2 * RT + 2,)),
             ],
         ),
         out_shape=jax.ShapeDtypeStruct((RT * TILE, QT * TILE), F32),
         compiler_params=pltpu.CompilerParams(vmem_limit_bytes=52 * MIB),
         cost_estimate=pl.CostEstimate(flops=1 << 33, bytes_accessed=20 * MIB, transcendentals=0),
-    )(ids, where, diag, inv, gx, goth, recv, front)
+    )(ids, diag, inv, gx, goth, front)
 
 
 def pick(v, at):
@@ -680,10 +736,13 @@
     return full
 
 
-def sum_second(v, x):
+def sum_x(v, x):
     v = v.reshape(4, 64, PANEL)
     got = [shift(pick(v, (x + d) % 4), dx=d) for d in (1, 3, 2)]
-    v = pick(v, x) + got[0] + got[1] + got[2]
+    return pick(v, x) + got[0] + got[1] + got[2]
+
+
+def sum_y(v):
     return (v + shift(v, dc=1, dy=1)) + (shift(v, dc=1) + shift(v, dy=1))
 
 
@@ -721,7 +780,7 @@
     diag, gcol = lax.optimization_barrier((diag, gcol))
     parts = strips(ids, gcol, parent_front)
     parts = [parts[0]] + [shift(parts[d], dz=d) for d in range(1, 4)]
-    diag = gathered(diag, z, dz=0).reshape(256, PANEL)
+    diag = sum_x(gathered(diag, z, dz=0).reshape(256, PANEL), x)
     strip = choose_z(ids, where, parts)
     own, diag, strip = lax.optimization_barrier((own, diag, strip))
 
@@ -730,7 +789,7 @@
     kept, moved = pick(strip, yh), pick(strip, 1 - yh)
     moves = [shift(moved, dy=1), shift(kept, dc=1), shift(moved, dc=1, dy=1)]
     strip = choose_y(ids, where, [kept] + moves)
-    diag = sum_second(diag, x)
+    diag = sum_y(diag)
     send, diag, strip = lax.optimization_barrier((send, diag, strip))
     recv = lax.all_to_all(send, ("z", "yh"), split_axis=0, concat_axis=0, tiled=True)
 
@@ -740,8 +799,10 @@
     gsend = compose(ids, where, line, shift(line, dk=1))
     recv, inv, gsend = lax.optimization_barrier((recv, inv, gsend))
     gx = lax.all_to_all(gsend, ("z", "yh"), split_axis=0, concat_axis=0, tiled=True)
+    with_children = base(ids, where, recv, parent_front)
+    gx, with_children = lax.optimization_barrier((gx, with_children))
     goth = shift(gx[:, RT * STRIP :], dk=1)
-    return final(ids, where, diag, inv, gx, goth, recv, parent_front)
+    return final(ids, diag, inv, gx, goth, with_children)
 
 
 def solution(mesh):

time: 294 us -> 299 us (1.017)
  waiting for transfers between devices: 53.3 us -> 97.3 us
  blocking collectives: 30.7 us -> 0 us
  starting transfers between devices: 116 us -> 102 us
  local copies, waits for them, and re-layouts: 8.45 us -> 12 us
    ppermute x30, waiting for transfers between devices: 50.8 us -> 82.7 us  [shift(): return lax.ppermute(v, AXES, pairs)]
    all_to_all x1 -> x0, blocking collectives: 30.7 us -> none  [body(): lax.all_to_all(gsend, ('z', 'yh'), split_axis=0, concat_axis=0, tiled=True)]
    ppermute x30, starting transfers between devices: 100 us -> 73.7 us  [shift(): return lax.ppermute(v, AXES, pairs)]
    pallas_call x0 -> x1, Pallas kernels: none -> 10.1 us  [base(): pl.pallas_call(base_kernel, grid_spec=pltpu.PrefetchScalarGridSpec(num_sc...]
    all_to_all x0 -> x1, waiting for transfers between devices: none -> 9.8 us  [body(): lax.all_to_all(gsend, ('z', 'yh'), split_axis=0, concat_axis=0, tiled=True)]
    all_to_all x1, starting transfers between devices: 4.89 us -> 9.85 us  [body(): lax.all_to_all(send, ('z', 'yh'), split_axis=0, concat_axis=0, tiled=True)]
    all_to_all x1, waiting for transfers between devices: 0.01 us -> 4.85 us  [body(): lax.all_to_all(send, ('z', 'yh'), split_axis=0, concat_axis=0, tiled=True)]
    all_to_all x0 -> x1, starting transfers between devices: none -> 3.93 us  [body(): lax.all_to_all(gsend, ('z', 'yh'), split_axis=0, concat_axis=0, tiled=True)]
  transfers between devices with their start and end apart: 36 -> 37, of which waited for: 14 -> 18; matrix products, arithmetic and copies ran while one was open for 2% -> 2% of each run, Pallas kernels for 15% -> 17%
where the time goes in v6:
time: 299 us; the launch traced here: 298 us
  starting transfers between devices  102 us (34%)
  waiting for transfers between devices  97.3 us (33%)
  Pallas kernels  80.9 us (27%)
  local copies, waits for them, and re-layouts  12 us (4%)
  other arithmetic  5.49 us (2%)
    ppermute x30, waiting for transfers between devices, shift(): return lax.ppermute(v, AXES, pairs)  82.7 us
    ppermute x30, starting transfers between devices, shift(): return lax.ppermute(v, AXES, pairs)  73.7 us
    pallas_call x1, Pallas kernels, inverse_factor(): pl.pallas_call(inverse_kernel, out_shape=jax.ShapeDtypeStruct((PANEL, PAN...  26.5 us
    pallas_call x1, Pallas kernels, final(): pl.pallas_call(final_kernel, grid_spec=pltpu.PrefetchScalarGridSpec(num_s...  14.3 us
    pallas_call x1, Pallas kernels, update(): pl.pallas_call(update_kernel, grid_spec=pltpu.PrefetchScalarGridSpec(num_...  13.1 us
    pallas_call x1, Pallas kernels, base(): pl.pallas_call(base_kernel, grid_spec=pltpu.PrefetchScalarGridSpec(num_sc...  10.1 us
    all_to_all x1, starting transfers between devices, body(): lax.all_to_all(send, ('z', 'yh'), split_axis=0, concat_axis=0, tiled=True)  9.85 us
    all_to_all x1, waiting for transfers between devices, body(): lax.all_to_all(gsend, ('z', 'yh'), split_axis=0, concat_axis=0, tiled=True)  9.8 us
  transfers between devices with their start and end apart: 37, of which 18 were waited for; matrix products, arithmetic and copies ran while one was open for 2% of the time, Pallas kernels for 17%

profile of v6, /device:TPU:1, one launch (start us, length us, event | category | flops | bytes accessed | tf_op | source)
XLA Modules:
  0.0 298.0 jit_solution(3213188191314894997)
XLA Ops:
  0.0 2.8 dynamic-slice_bitcast_fusion
  2.8 1.3 collective-permute-start
  4.1 1.7 collective-permute-start.1
  5.8 1.6 collective-permute-start.2
  7.4 1.6 collective-permute-start.3
  9.1 1.9 fusion.mine
  11.0 23.6 %collective-permute-start.4 = (bf16[512,1024]{1,0:T(8,128)(2,1)S(1)}, bf16[512,1024]{1,0:T(8,128)(2,1)}, u32[]{:S(2)}, u32[]{:S(2)}) collective-permute-start(bf16[512,1024]{1,0:T(8,128)(2,1)S(1)} %fusion.mine), channel_id=1, source_target_pairs={{0,8},{1,9},{2,10},{3,11},{4,12},{5,13},{6,14},{7,15},{8,0},{9,1},... | collective-permute-start | bytes 3145736 | tf_op jit(solution)/shard_map/ppermute | solution.py:48
  35.6 1.5 collective-permute-done.4.other
  37.1 13.1 %shard_map.64 = (s16[8,272,1024]{2,1,0:T(8,128)(2,1)}, f32[512,512]{1,0:T(8,128)}, f32[1024,512]{1,0:T(8,128)}) custom-call(s32[11]{0:T(128)S(1)} %stack.55.ids, s32[2,32]{1,0:T(2,128)S(1)} %select_reduce_fusion.1.slots, s32[2,32,32]{2,1,0:T(8,128)S(1)} %copy-done.8, f32[1024,1024]{1,0:T(8,128)} %bitcast.81, bf16[1024,1024]{1,0:T(8,128)(2,1)S(1)} %bitcast.80, ...), custom_call_target="tpu_custom_call" | custom-call | flops 2147483648 | bytes 14680064 | tf_op jit(solution)/shard_map/pallas_call | solution.py:126
  50.2 8.1 %all-to-all-start = ((s16[8,272,1024]{2,1,0:T(8,128)(2,1)}), s16[8,272,1024]{2,1,0:T(8,128)(2,1)}, u32[]{:S(2)}, u32[]{:S(2)}) async-start(s16[8,272,1024]{2,1,0:T(8,128)(2,1)} %get-tuple-element.35), calls=%async_computation | async-start | bytes 8912896 | tf_op jit(solution)/shard_map/all_to_all | solution.py:777
  58.3 0.8 dynamic-slice_bitcast_fusion.2
  59.5 1.7 collective-permute-done.5
  61.3 1.1 bitcast_add_fusion
  62.4 5.5 %collective-permute-start.8 = (f32[64,512]{1,0:T(8,128)S(1)}, f32[64,512]{1,0:T(8,128)S(1)}, u32[]{:S(2)}, u32[]{:S(2)}) collective-permute-start(f32[64,512]{1,0:T(8,128)S(1)} %get-tuple-element.65), channel_id=1, source_target_pairs={{0,4},{1,5},{2,6},{3,7},{4,0},{5,1},{6,2},{7,3},{8,12},{9,13},{10,... | collective-permute-start | bytes 393224 | tf_op jit(solution)/shard_map/ppermute | solution.py:48
  68.0 3.1 %collective-permute-start.7 = (f32[64,512]{1,0:T(8,128)S(1)}, f32[64,512]{1,0:T(8,128)S(1)}, u32[]{:S(2)}, u32[]{:S(2)}) collective-permute-start(f32[64,512]{1,0:T(8,128)S(1)} %get-tuple-element.66), channel_id=1, source_target_pairs={{0,6},{1,7},{2,0},{3,1},{4,2},{5,3},{6,4},{7,5},{8,14},{9,15},{10,... | collective-permute-start | bytes 393224 | tf_op jit(solution)/shard_map/ppermute | solution.py:48
  71.8 4.0 %collective-permute-done.7 = f32[64,512]{1,0:T(8,128)S(1)} collective-permute-done((f32[64,512]{1,0:T(8,128)S(1)}, f32[64,512]{1,0:T(8,128)S(1)}, u32[]{:S(2)}, u32[]{:S(2)}) %collective-permute-start.7) | collective-permute-done | bytes 131104 | tf_op jit(solution)/shard_map/ppermute | solution.py:48
  76.3 1.2 collective-permute-start.9
  77.6 1.5 collective-permute-start.10
  79.1 0.9 collective-permute-start.11
  80.0 2.2 shard_map.65
  82.2 0.8 copy-done.4
  83.0 1.9 collective-permute-start.15
  85.7 1.7 collective-permute-start.17
  87.6 3.4 %collective-permute-start.14 = (f32[64,512]{1,0:T(8,128)S(1)}, f32[64,512]{1,0:T(8,128)S(1)}, u32[]{:S(2)}, u32[]{:S(2)}) collective-permute-start(f32[64,512]{1,0:T(8,128)S(1)} %get-tuple-element.62), channel_id=1, source_target_pairs={{0,32},{1,33},{2,34},{3,35},{4,36},{5,37},{6,38},{7,39},{8,40},{9,... | collective-permute-start | bytes 393224 | tf_op jit(solution)/shard_map/ppermute | solution.py:48
  91.7 29.9 %collective-permute-done.14 = f32[64,512]{1,0:T(8,128)S(1)} collective-permute-done((f32[64,512]{1,0:T(8,128)S(1)}, f32[64,512]{1,0:T(8,128)S(1)}, u32[]{:S(2)}, u32[]{:S(2)}) %collective-permute-start.14) | collective-permute-done | bytes 131104 | tf_op jit(solution)/shard_map/ppermute | solution.py:48
  121.6 4.5 %collective-permute-start.12 = (f32[64,512]{1,0:T(8,128)S(1)}, f32[64,512]{1,0:T(8,128)S(1)}, u32[]{:S(2)}, u32[]{:S(2)}) collective-permute-start(f32[64,512]{1,0:T(8,128)S(1)} %get-tuple-element.61), channel_id=1, source_target_pairs={{0,16},{1,17},{2,18},{3,19},{4,20},{5,21},{6,22},{7,23},{8,24},{9,... | collective-permute-start | bytes 393224 | tf_op jit(solution)/shard_map/ppermute | solution.py:48
  126.1 3.5 %collective-permute-done.13 = f32[64,512]{1,0:T(8,128)S(1)} collective-permute-done((f32[64,512]{1,0:T(8,128)S(1)}, f32[64,512]{1,0:T(8,128)S(1)}, u32[]{:S(2)}, u32[]{:S(2)}) %collective-permute-start.13) | collective-permute-done | bytes 131104 | tf_op jit(solution)/shard_map/ppermute | solution.py:48
  129.7 1.9 collective-permute-done.12
  132.7 2.8 shard_map.66
  135.5 3.1 %collective-permute-start.18 = (s16[8,272,1024]{2,1,0:T(8,128)(2,1)}, s16[8,272,1024]{2,1,0:T(8,128)(2,1)}, u32[]{:S(2)}, u32[]{:S(2)}) collective-permute-start(s16[8,272,1024]{2,1,0:T(8,128)(2,1)} %all-to-all-done.own), channel_id=1, source_target_pairs={{0,8},{1,9},{2,10},{3,11},{4,12},{5,13},{6,14},{7,15},{8,0},{9,1},... | collective-permute-start | bytes 13369352 | tf_op jit(solution)/shard_map/ppermute | solution.py:48
  138.6 1.2 collective-permute-start.20
  139.8 1.7 collective-permute-start.21
  141.5 0.9 collective-permute-start.19
  142.4 1.1 dynamic-slice_bitcast_fusion.3
  144.1 1.8 collective-permute-start.23
  145.9 2.0 collective-permute-done.21
  147.9 0.9 collective-permute-start.24
  148.9 7.2 %collective-permute-done.19 = f32[64,512]{1,0:T(8,128)S(1)} collective-permute-done((f32[64,512]{1,0:T(8,128)S(1)}, f32[64,512]{1,0:T(8,128)S(1)}, u32[]{:S(2)}, u32[]{:S(2)}) %collective-permute-start.19) | collective-permute-done | bytes 131104 | tf_op jit(solution)/shard_map/ppermute | solution.py:48
  156.1 0.8 collective-permute-done.23.across
  157.0 4.7 %collective-permute-done.24.both = s16[256,512]{1,0:T(8,128)(2,1)S(1)} collective-permute-done((s16[256,512]{1,0:T(8,128)(2,1)S(1)}, s16[256,512]{1,0:T(8,128)(2,1)S(1)}, u32[]{:S(2)}, u32[]{:S(2)}) %collective-permute-start.24) | collective-permute-done | bytes 262176 | tf_op jit(solution)/shard_map/ppermute | solution.py:48
  162.4 2.7 shard_map.68
  165.1 3.6 %shard_map.67 = s16[8,1552,256]{2,1,0:T(8,128)(2,1)} custom-call(s32[11]{0:T(128)S(1)} %copy-done.7, s32[2,32]{1,0:T(2,128)S(1)} %select_reduce_fusion.1.slots, s32[2,48]{1,0:T(2,128)S(1)} %copy-done.5, s16[8,272,1024]{2,1,0:T(8,128)(2,1)} %all-to-all-done.own, s16[8,272,1024]{2,1,0:T(8,128)(2,1)} %collective-permute-done.18.other), custom_call_target="tpu_custom_call" | custom-call | bytes 8388608 | tf_op jit(solution)/shard_map/pallas_call | solution.py:404
  168.7 9.9 %all-to-all-start.1 = ((s16[8,1552,256]{2,1,0:T(8,128)(2,1)}), s16[8,1552,256]{2,1,0:T(8,128)(2,1)}, u32[]{:S(2)}, u32[]{:S(2)}) async-start(s16[8,1552,256]{2,1,0:T(8,128)(2,1)} %shard_map.67), calls=%async_computation.1 | async-start | bytes 12713984 | tf_op jit(solution)/shard_map/all_to_all | solution.py:794
  178.6 2.7 collective-permute-start.26
  181.5 1.0 collective-permute-start.31
  182.5 1.7 collective-permute-start.30
  184.3 0.9 collective-permute-start.29
  185.3 1.8 collective-permute-done.27
  187.1 3.6 %collective-permute-start.28 = (f32[256,512]{1,0:T(8,128)S(1)}, f32[256,512]{1,0:T(8,128)}, u32[]{:S(2)}, u32[]{:S(2)}) collective-permute-start(f32[256,512]{1,0:T(8,128)S(1)} %bitcast.82), channel_id=1, source_target_pairs={{0,8},{1,9},{2,10},{3,11},{4,12},{5,13},{6,14},{7,15},{8,0},{9,1},... | collective-permute-start | bytes 1572872 | tf_op jit(solution)/shard_map/ppermute | solution.py:48
  190.7 7.6 %collective-permute-done.31 = s16[2,256,512]{2,1,0:T(8,128)(2,1)S(1)} collective-permute-done((s16[2,256,512]{2,1,0:T(8,128)(2,1)S(1)}, s16[2,256,512]{2,1,0:T(8,128)(2,1)S(1)}, u32[]{:S(2)}, u32[]{:S(2)}) %collective-permute-start.31) | collective-permute-done | bytes 524320 | tf_op jit(solution)/shard_map/ppermute | solution.py:48
  198.3 12.5 %collective-permute-done.29 = s16[2,256,512]{2,1,0:T(8,128)(2,1)S(1)} collective-permute-done((s16[2,256,512]{2,1,0:T(8,128)(2,1)S(1)}, s16[2,256,512]{2,1,0:T(8,128)(2,1)S(1)}, u32[]{:S(2)}, u32[]{:S(2)}) %collective-permute-start.29) | collective-permute-done | bytes 524320 | tf_op jit(solution)/shard_map/ppermute | solution.py:48
  211.6 1.2 broadcast_select_fusion.1
  212.8 26.5 %shard_map.69.inv = f32[512,512]{1,0:T(8,128)S(1)} custom-call(f32[512,512]{1,0:T(8,128)S(1)} %pad_maximum_fusion.a_ref.diag), custom_call_target="tpu_custom_call" | custom-call | flops 17179869184 | bytes 2097152 | tf_op jit(solution)/shard_map/pallas_call | solution.py:508
  239.3 1.0 copy-done.9
  240.3 5.8 %shard_map.70 = s16[8,208,512]{2,1,0:T(8,128)(2,1)S(1)} custom-call(s32[11]{0:T(128)S(1)} %copy-done.7, s32[2,48]{1,0:T(2,128)S(1)} %copy-done.5, s16[4,2,256,512]{3,2,1,0:T(8,128)(2,1)S(1)} %pad_add_fusion.own, s16[4,2,256,512]{3,2,1,0:T(8,128)(2,1)} %collective-permute-done.32.other), custom_call_target="tpu_custom_call" | custom-call | bytes 6291456 | tf_op jit(solution)/shard_map/pallas_call | solution.py:330
  246.1 1.2 copy-done.1
  247.3 4.8 %all-to-all-done.1.recv = s16[8,1552,256]{2,1,0:T(8,128)(2,1)} async-done(((s16[8,1552,256]{2,1,0:T(8,128)(2,1)}), s16[8,1552,256]{2,1,0:T(8,128)(2,1)}, u32[]{:S(2)}, u32[]{:S(2)}) %all-to-all-start.1) | async-done | bytes 6357024 | tf_op jit(solution)/shard_map/all_to_all | solution.py:794
  252.1 3.9 %all-to-all-start.2 = ((s16[8,208,512]{2,1,0:T(8,128)(2,1)}), s16[8,208,512]{2,1,0:T(8,128)(2,1)S(1)}, u32[]{:S(2)}, u32[]{:S(2)}) async-start(s16[8,208,512]{2,1,0:T(8,128)(2,1)} %copy-done.1), calls=%async_computation.2 | async-start | bytes 3407872 | tf_op jit(solution)/shard_map/all_to_all | solution.py:801
  256.0 10.1 %shard_map.71.front = f32[768,1536]{1,0:T(8,128)S(1)} custom-call(s32[11]{0:T(128)S(1)} %copy-done.7, s32[2,48]{1,0:T(2,128)S(1)} %copy-done.5, s16[8,1552,256]{2,1,0:T(8,128)(2,1)} %all-to-all-done.1.recv, f32[768,1536]{1,0:T(8,128)} %front.5), custom_call_target="tpu_custom_call" | custom-call | bytes 20971520 | tf_op jit(solution)/shard_map/pallas_call | solution.py:577
  266.1 2.2 copy-done.2
  268.3 9.8 %all-to-all-done.2.gx = s16[8,208,512]{2,1,0:T(8,128)(2,1)S(1)} async-done(((s16[8,208,512]{2,1,0:T(8,128)(2,1)}), s16[8,208,512]{2,1,0:T(8,128)(2,1)S(1)}, u32[]{:S(2)}, u32[]{:S(2)}) %all-to-all-start.2) | async-done | bytes 1703968 | tf_op jit(solution)/shard_map/all_to_all | solution.py:801
  278.2 3.4 %collective-permute-start.33 = (s16[8,112,512]{2,1,0:T(8,128)(2,1)S(1)}, s16[8,112,512]{2,1,0:T(8,128)(2,1)S(1)}, u32[]{:S(2)}, u32[]{:S(2)}) collective-permute-start(s16[8,112,512]{2,1,0:T(8,128)(2,1)S(1)} %slice.9), channel_id=1, source_target_pairs={{0,8},{1,9},{2,10},{3,11},{4,12},{5,13},{6,14},{7,15},{8,0},{9,1},... | collective-permute-start | bytes 2752520 | tf_op jit(solution)/shard_map/ppermute | solution.py:48
  281.6 2.1 collective-permute-done.33.goth
  283.7 14.3 %shard_map.72 = f32[768,1536]{1,0:T(8,128)} custom-call(s32[11]{0:T(128)S(1)} %copy-done.7, f32[512,512]{1,0:T(8,128)S(1)} %pad_maximum_fusion.a_ref.diag, f32[512,512]{1,0:T(8,128)} %copy-done.9, s16[8,208,512]{2,1,0:T(8,128)(2,1)} %copy-done.10, s16[8,112,512]{2,1,0:T(8,128)(2,1)S(1)} %collective-permute-done.33.goth, f32[768,1536]{1,0:T(8,128)} %copy-done.2), custom_call_target="tpu_custom_call" | custom-call | flops 8589934592 | bytes 20971520 | tf_op jit(solution)/shard_map/pallas_call | solution.py:664
  (88 shorter events, 8.0 us)
Async XLA Ops:
  0.0 9.1 %copy-start = (bf16[1,1024,1024]{2,1,0:T(8,128)(2,1)S(1)}, bf16[1,1024,1024]{2,1,0:T(8,128)(2,1)}, u32[]{:S(2)}) copy-start(bf16[1,1024,1024]{2,1,0:T(8,128)(2,1)} %param.7) | copy-start | bytes 6291460
  2.8 6.2 %collective-permute-start = (bf16[512,1024]{1,0:T(8,128)(2,1)}, bf16[512,1024]{1,0:T(8,128)(2,1)}, u32[]{:S(2)}, u32[]{:S(2)}) collective-permute-start(bf16[512,1024]{1,0:T(8,128)(2,1)} %get-tuple-element.56), channel_id=1, source_target_pairs={{0,8},{9,1},{18,26},{27,19},{36,44},{45,37},{54,62},{63,55},{64,72... | collective-permute-start | bytes 3145736 | tf_op jit(solution)/shard_map/ppermute | solution.py:715
  4.1 4.9 %collective-permute-start.1 = (bf16[512,1024]{1,0:T(8,128)(2,1)S(1)}, bf16[512,1024]{1,0:T(8,128)(2,1)}, u32[]{:S(2)}, u32[]{:S(2)}) collective-permute-start(bf16[512,1024]{1,0:T(8,128)(2,1)S(1)} %get-tuple-element.55), channel_id=1, source_target_pairs={{0,16},{4,24},{9,17},{13,25},{18,34},{22,42},{27,35},{31,43},{36,5... | collective-permute-start | bytes 3145736 | tf_op jit(solution)/shard_map/ppermute | solution.py:708
  5.8 3.3 %collective-permute-start.2 = (bf16[512,1024]{1,0:T(8,128)(2,1)S(1)}, bf16[512,1024]{1,0:T(8,128)(2,1)}, u32[]{:S(2)}, u32[]{:S(2)}) collective-permute-start(bf16[512,1024]{1,0:T(8,128)(2,1)S(1)} %get-tuple-element.55), channel_id=1, source_target_pairs={{0,32},{4,40},{9,33},{13,41},{18,50},{22,58},{27,51},{31,59},{36,4... | collective-permute-start | bytes 3145736 | tf_op jit(solution)/shard_map/ppermute | solution.py:708
  7.4 1.7 collective-permute-start.3
  9.1 25.6 %copy-start.19 = (s32[48]{0:T(128)S(1)}, s32[48]{0:T(128)}, u32[]{:S(2)}) copy-start(s32[48]{0:T(128)} %param.10) | copy-start | bytes 580
  9.1 25.7 %copy-start.20 = (s32[2,32]{1,0:T(2,128)S(1)}, s32[2,32]{1,0:T(2,128)}, u32[]{:S(2)}) copy-start(s32[2,32]{1,0:T(2,128)} %param.9) | copy-start | bytes 772
  9.1 28.0 %copy-start.8 = (s32[2,32,32]{2,1,0:T(8,128)S(1)}, s32[2,32,32]{2,1,0:T(8,128)}, u32[]{:S(2)}) copy-start(s32[2,32,32]{2,1,0:T(8,128)} %pat.1) | copy-start | bytes 24580
  11.0 26.0 %collective-permute-start.4 = (bf16[512,1024]{1,0:T(8,128)(2,1)S(1)}, bf16[512,1024]{1,0:T(8,128)(2,1)}, u32[]{:S(2)}, u32[]{:S(2)}) collective-permute-start(bf16[512,1024]{1,0:T(8,128)(2,1)S(1)} %fusion.mine), channel_id=1, source_target_pairs={{0,8},{1,9},{2,10},{3,11},{4,12},{5,13},{6,14},{7,15},{8,0},{9,1},... | collective-permute-start | bytes 3145736 | tf_op jit(solution)/shard_map/ppermute | solution.py:48
  34.7 45.3 %copy-start.6 = (s32[11]{0:T(128)}, s32[11]{0:T(128)S(1)}, u32[]{:S(2)}) copy-start(s32[11]{0:T(128)S(1)} %stack.55.ids) | copy-start | bytes 136
  50.2 8.1 %copy-start.13 = (f32[512,512]{1,0:T(8,128)S(1)}, f32[512,512]{1,0:T(8,128)}, u32[]{:S(2)}) copy-start(f32[512,512]{1,0:T(8,128)} %get-tuple-element.36) | copy-start | bytes 3145732
  50.2 85.3 %all-to-all-start = ((s16[8,272,1024]{2,1,0:T(8,128)(2,1)}), s16[8,272,1024]{2,1,0:T(8,128)(2,1)}, u32[]{:S(2)}, u32[]{:S(2)}) async-start(s16[8,272,1024]{2,1,0:T(8,128)(2,1)} %get-tuple-element.35), calls=%async_computation | async-start | bytes 8912896 | tf_op jit(solution)/shard_map/all_to_all | solution.py:777
  58.2 21.8 %copy-start.3 = (f32[1024,512]{1,0:T(8,128)S(1)}, f32[1024,512]{1,0:T(8,128)}, u32[]{:S(2)}) copy-start(f32[1024,512]{1,0:T(8,128)} %get-tuple-element.39.gcol) | copy-start | bytes 6291460
  59.1 2.2 collective-permute-start.5
  62.4 9.3 %collective-permute-start.8 = (f32[64,512]{1,0:T(8,128)S(1)}, f32[64,512]{1,0:T(8,128)S(1)}, u32[]{:S(2)}, u32[]{:S(2)}) collective-permute-start(f32[64,512]{1,0:T(8,128)S(1)} %get-tuple-element.65), channel_id=1, source_target_pairs={{0,4},{1,5},{2,6},{3,7},{4,0},{5,1},{6,2},{7,3},{8,12},{9,13},{10,... | collective-permute-start | bytes 393224 | tf_op jit(solution)/shard_map/ppermute | solution.py:48
  68.0 7.9 %collective-permute-start.7 = (f32[64,512]{1,0:T(8,128)S(1)}, f32[64,512]{1,0:T(8,128)S(1)}, u32[]{:S(2)}, u32[]{:S(2)}) collective-permute-start(f32[64,512]{1,0:T(8,128)S(1)} %get-tuple-element.66), channel_id=1, source_target_pairs={{0,6},{1,7},{2,0},{3,1},{4,2},{5,3},{6,4},{7,5},{8,14},{9,15},{10,... | collective-permute-start | bytes 393224 | tf_op jit(solution)/shard_map/ppermute | solution.py:48
  71.0 5.3 %collective-permute-start.6 = (f32[64,512]{1,0:T(8,128)S(1)}, f32[64,512]{1,0:T(8,128)S(1)}, u32[]{:S(2)}, u32[]{:S(2)}) collective-permute-start(f32[64,512]{1,0:T(8,128)S(1)} %get-tuple-element.64), channel_id=1, source_target_pairs={{0,2},{1,3},{2,4},{3,5},{4,6},{5,7},{6,0},{7,1},{8,10},{9,11},{10,... | collective-permute-start | bytes 393224 | tf_op jit(solution)/shard_map/ppermute | solution.py:48
  76.3 9.4 %collective-permute-start.9 = (f32[64,512]{1,0:T(8,128)S(1)}, f32[64,512]{1,0:T(8,128)S(1)}, u32[]{:S(2)}, u32[]{:S(2)}) collective-permute-start(f32[64,512]{1,0:T(8,128)S(1)} %fusion.4), channel_id=1, source_target_pairs={{0,2},{1,3},{2,4},{3,5},{4,6},{5,7},{6,0},{7,1},{8,10},{9,11},{10,... | collective-permute-start | bytes 393224 | tf_op jit(solution)/shard_map/ppermute | solution.py:48
  77.6 9.9 %collective-permute-start.10 = (f32[64,512]{1,0:T(8,128)S(1)}, f32[64,512]{1,0:T(8,128)S(1)}, u32[]{:S(2)}, u32[]{:S(2)}) collective-permute-start(f32[64,512]{1,0:T(8,128)S(1)} %fusion.4), channel_id=1, source_target_pairs={{0,6},{1,7},{2,0},{3,1},{4,2},{5,3},{6,4},{7,5},{8,14},{9,15},{10,... | collective-permute-start | bytes 393224 | tf_op jit(solution)/shard_map/ppermute | solution.py:48
  79.1 8.4 %collective-permute-start.11 = (f32[64,512]{1,0:T(8,128)S(1)}, f32[64,512]{1,0:T(8,128)S(1)}, u32[]{:S(2)}, u32[]{:S(2)}) collective-permute-start(f32[64,512]{1,0:T(8,128)S(1)} %fusion.4), channel_id=1, source_target_pairs={{0,4},{1,5},{2,6},{3,7},{4,0},{5,1},{6,2},{7,3},{8,12},{9,13},{10,... | collective-permute-start | bytes 393224 | tf_op jit(solution)/shard_map/ppermute | solution.py:48
  82.2 0.8 copy-start.4
  83.0 48.7 %collective-permute-start.15 = (s16[2,256,512]{2,1,0:T(8,128)(2,1)}, s16[2,256,512]{2,1,0:T(8,128)(2,1)S(1)}, u32[]{:S(2)}, u32[]{:S(2)}) collective-permute-start(s16[2,256,512]{2,1,0:T(8,128)(2,1)} %get-tuple-element.41), channel_id=1, source_target_pairs={{0,2},{1,3},{2,4},{3,5},{4,6},{5,7},{6,0},{7,1},{8,10},{9,11},{10,... | collective-permute-start | bytes 1572872 | tf_op jit(solution)/shard_map/ppermute | solution.py:48
  84.9 46.8 %collective-permute-start.16 = (s16[2,256,512]{2,1,0:T(8,128)(2,1)S(1)}, s16[2,256,512]{2,1,0:T(8,128)(2,1)S(1)}, u32[]{:S(2)}, u32[]{:S(2)}) collective-permute-start(s16[2,256,512]{2,1,0:T(8,128)(2,1)S(1)} %get-tuple-element.42), channel_id=1, source_target_pairs={{0,4},{1,5},{2,6},{3,7},{4,0},{5,1},{6,2},{7,3},{8,12},{9,13},{10,... | collective-permute-start | bytes 1572872 | tf_op jit(solution)/shard_map/ppermute | solution.py:48
  85.7 46.0 %collective-permute-start.17 = (s16[2,256,512]{2,1,0:T(8,128)(2,1)S(1)}, s16[2,256,512]{2,1,0:T(8,128)(2,1)}, u32[]{:S(2)}, u32[]{:S(2)}) collective-permute-start(s16[2,256,512]{2,1,0:T(8,128)(2,1)S(1)} %get-tuple-element.43), channel_id=1, source_target_pairs={{0,6},{1,7},{2,0},{3,1},{4,2},{5,3},{6,4},{7,5},{8,14},{9,15},{10,... | collective-permute-start | bytes 1572872 | tf_op jit(solution)/shard_map/ppermute | solution.py:48
  87.6 34.0 %collective-permute-start.14 = (f32[64,512]{1,0:T(8,128)S(1)}, f32[64,512]{1,0:T(8,128)S(1)}, u32[]{:S(2)}, u32[]{:S(2)}) collective-permute-start(f32[64,512]{1,0:T(8,128)S(1)} %get-tuple-element.62), channel_id=1, source_target_pairs={{0,32},{1,33},{2,34},{3,35},{4,36},{5,37},{6,38},{7,39},{8,40},{9,... | collective-permute-start | bytes 393224 | tf_op jit(solution)/shard_map/ppermute | solution.py:48
  91.0 38.7 %collective-permute-start.13 = (f32[64,512]{1,0:T(8,128)S(1)}, f32[64,512]{1,0:T(8,128)S(1)}, u32[]{:S(2)}, u32[]{:S(2)}) collective-permute-start(f32[64,512]{1,0:T(8,128)S(1)} %get-tuple-element.63), channel_id=1, source_target_pairs={{0,48},{1,49},{2,50},{3,51},{4,52},{5,53},{6,54},{7,55},{8,56},{9,... | collective-permute-start | bytes 393224 | tf_op jit(solution)/shard_map/ppermute | solution.py:48
  121.6 10.0 %collective-permute-start.12 = (f32[64,512]{1,0:T(8,128)S(1)}, f32[64,512]{1,0:T(8,128)S(1)}, u32[]{:S(2)}, u32[]{:S(2)}) collective-permute-start(f32[64,512]{1,0:T(8,128)S(1)} %get-tuple-element.61), channel_id=1, source_target_pairs={{0,16},{1,17},{2,18},{3,19},{4,20},{5,21},{6,22},{7,23},{8,24},{9,... | collective-permute-start | bytes 393224 | tf_op jit(solution)/shard_map/ppermute | solution.py:48
  131.7 0.8 copy-start.14
  131.7 1.0 copy-start.15
  135.4 29.7 %copy-start.5 = (s32[2,48]{1,0:T(2,128)S(1)}, s32[2,48]{1,0:T(2,128)}, u32[]{:S(2)}) copy-start(s32[2,48]{1,0:T(2,128)} %select_reduce_fusion.where) | copy-start | bytes 1156
  135.4 29.7 %copy-start.7 = (s32[11]{0:T(128)S(1)}, s32[11]{0:T(128)}, u32[]{:S(2)}) copy-start(s32[11]{0:T(128)} %copy-done.6) | copy-start | bytes 136
  135.5 29.6 %collective-permute-start.18 = (s16[8,272,1024]{2,1,0:T(8,128)(2,1)}, s16[8,272,1024]{2,1,0:T(8,128)(2,1)}, u32[]{:S(2)}, u32[]{:S(2)}) collective-permute-start(s16[8,272,1024]{2,1,0:T(8,128)(2,1)} %all-to-all-done.own), channel_id=1, source_target_pairs={{0,8},{1,9},{2,10},{3,11},{4,12},{5,13},{6,14},{7,15},{8,0},{9,1},... | collective-permute-start | bytes 13369352 | tf_op jit(solution)/shard_map/ppermute | solution.py:48
  138.6 5.6 %collective-permute-start.20 = (f32[64,512]{1,0:T(8,128)S(1)}, f32[64,512]{1,0:T(8,128)S(1)}, u32[]{:S(2)}, u32[]{:S(2)}) collective-permute-start(f32[64,512]{1,0:T(8,128)S(1)} %fusion.2), channel_id=1, source_target_pairs={{0,64},{1,65},{2,66},{3,67},{4,68},{5,69},{6,70},{7,71},{8,72},{9,... | collective-permute-start | bytes 393224 | tf_op jit(solution)/shard_map/ppermute | solution.py:48
  139.8 8.2 %collective-permute-start.21 = (f32[64,512]{1,0:T(8,128)S(1)}, f32[64,512]{1,0:T(8,128)S(1)}, u32[]{:S(2)}, u32[]{:S(2)}) collective-permute-start(f32[64,512]{1,0:T(8,128)S(1)} %fusion.2), channel_id=1, source_target_pairs={{0,1},{1,0},{2,3},{3,2},{4,5},{5,4},{6,7},{7,6},{8,9},{9,8},{10,11... | collective-permute-start | bytes 393224 | tf_op jit(solution)/shard_map/ppermute | solution.py:48
  141.5 14.6 %collective-permute-start.19 = (f32[64,512]{1,0:T(8,128)S(1)}, f32[64,512]{1,0:T(8,128)S(1)}, u32[]{:S(2)}, u32[]{:S(2)}) collective-permute-start(f32[64,512]{1,0:T(8,128)S(1)} %fusion.2), channel_id=1, source_target_pairs={{0,65},{1,64},{2,67},{3,66},{4,69},{5,68},{6,71},{7,70},{8,73},{9,... | collective-permute-start | bytes 393224 | tf_op jit(solution)/shard_map/ppermute | solution.py:48
  143.5 18.2 %copy-start.12 = (s16[256,512]{1,0:T(8,128)(2,1)}, s16[256,512]{1,0:T(8,128)(2,1)S(1)}, u32[]{:S(2)}) copy-start(s16[256,512]{1,0:T(8,128)(2,1)S(1)} %get-tuple-element.60.kept) | copy-start | bytes 786436
  143.5 12.6 %collective-permute-start.22 = (s16[256,512]{1,0:T(8,128)(2,1)S(1)}, s16[256,512]{1,0:T(8,128)(2,1)S(1)}, u32[]{:S(2)}, u32[]{:S(2)}) collective-permute-start(s16[256,512]{1,0:T(8,128)(2,1)S(1)} %get-tuple-element.59), channel_id=1, source_target_pairs={{0,1},{1,0},{2,3},{3,2},{4,5},{5,4},{6,7},{7,6},{8,9},{9,8},{10,11... | collective-permute-start | bytes 786440 | tf_op jit(solution)/shard_map/ppermute | solution.py:48
  144.1 12.8 %collective-permute-start.23 = (s16[256,512]{1,0:T(8,128)(2,1)S(1)}, s16[256,512]{1,0:T(8,128)(2,1)S(1)}, u32[]{:S(2)}, u32[]{:S(2)}) collective-permute-start(s16[256,512]{1,0:T(8,128)(2,1)S(1)} %get-tuple-element.60.kept), channel_id=1, source_target_pairs={{0,64},{1,65},{2,66},{3,67},{4,68},{5,69},{6,70},{7,71},{8,72},{9,... | collective-permute-start | bytes 786440 | tf_op jit(solution)/shard_map/ppermute | solution.py:48
  147.9 13.8 %collective-permute-start.24 = (s16[256,512]{1,0:T(8,128)(2,1)S(1)}, s16[256,512]{1,0:T(8,128)(2,1)S(1)}, u32[]{:S(2)}, u32[]{:S(2)}) collective-permute-start(s16[256,512]{1,0:T(8,128)(2,1)S(1)} %get-tuple-element.59), channel_id=1, source_target_pairs={{0,65},{1,64},{2,67},{3,66},{4,69},{5,68},{6,71},{7,70},{8,73},{9,... | collective-permute-start | bytes 786440 | tf_op jit(solution)/shard_map/ppermute | solution.py:48
  156.1 5.6 %copy-start.16 = (s16[256,512]{1,0:T(8,128)(2,1)}, s16[256,512]{1,0:T(8,128)(2,1)S(1)}, u32[]{:S(2)}) copy-start(s16[256,512]{1,0:T(8,128)(2,1)S(1)} %collective-permute-done.22.beside) | copy-start | bytes 786436
  157.0 4.7 %copy-start.17 = (s16[256,512]{1,0:T(8,128)(2,1)}, s16[256,512]{1,0:T(8,128)(2,1)S(1)}, u32[]{:S(2)}) copy-start(s16[256,512]{1,0:T(8,128)(2,1)S(1)} %collective-permute-done.23.across) | copy-start | bytes 786436
  161.7 0.7 copy-start.18
  168.7 12.8 %copy-start.11 = (s16[2,256,512]{2,1,0:T(8,128)(2,1)S(1)}, s16[2,256,512]{2,1,0:T(8,128)(2,1)}, u32[]{:S(2)}) copy-start(s16[2,256,512]{2,1,0:T(8,128)(2,1)} %shard_map.68) | copy-start | bytes 1572868
  168.7 83.4 %all-to-all-start.1 = ((s16[8,1552,256]{2,1,0:T(8,128)(2,1)}), s16[8,1552,256]{2,1,0:T(8,128)(2,1)}, u32[]{:S(2)}, u32[]{:S(2)}) async-start(s16[8,1552,256]{2,1,0:T(8,128)(2,1)} %shard_map.67), calls=%async_computation.1 | async-start | bytes 12713984 | tf_op jit(solution)/shard_map/all_to_all | solution.py:794
  178.6 5.7 %collective-permute-start.25 = (f32[64,512]{1,0:T(8,128)S(1)}, f32[64,512]{1,0:T(8,128)S(1)}, u32[]{:S(2)}, u32[]{:S(2)}) collective-permute-start(f32[64,512]{1,0:T(8,128)S(1)} %add_add_fusion), channel_id=1, source_target_pairs={{0,16},{1,17},{2,18},{3,19},{4,20},{5,21},{6,22},{7,23},{8,24},{9,... | collective-permute-start | bytes 393224 | tf_op jit(solution)/shard_map/ppermute | solution.py:48
  178.6 6.7 %collective-permute-start.26 = (f32[64,512]{1,0:T(8,128)S(1)}, f32[64,512]{1,0:T(8,128)S(1)}, u32[]{:S(2)}, u32[]{:S(2)}) collective-permute-start(f32[64,512]{1,0:T(8,128)S(1)} %add_add_fusion), channel_id=1, source_target_pairs={{0,48},{1,49},{2,50},{3,51},{4,52},{5,53},{6,54},{7,55},{8,56},{9,... | collective-permute-start | bytes 393224 | tf_op jit(solution)/shard_map/ppermute | solution.py:48
  181.3 5.8 %collective-permute-start.27 = (f32[64,512]{1,0:T(8,128)S(1)}, f32[64,512]{1,0:T(8,128)S(1)}, u32[]{:S(2)}, u32[]{:S(2)}) collective-permute-start(f32[64,512]{1,0:T(8,128)S(1)} %add_add_fusion), channel_id=1, source_target_pairs={{0,32},{1,33},{2,34},{3,35},{4,36},{5,37},{6,38},{7,39},{8,40},{9,... | collective-permute-start | bytes 393224 | tf_op jit(solution)/shard_map/ppermute | solution.py:48
  181.5 16.8 %collective-permute-start.31 = (s16[2,256,512]{2,1,0:T(8,128)(2,1)S(1)}, s16[2,256,512]{2,1,0:T(8,128)(2,1)S(1)}, u32[]{:S(2)}, u32[]{:S(2)}) collective-permute-start(s16[2,256,512]{2,1,0:T(8,128)(2,1)S(1)} %copy-done.11), channel_id=1, source_target_pairs={{0,48},{1,49},{2,50},{3,51},{4,52},{5,53},{6,54},{7,55},{8,56},{9,... | collective-permute-start | bytes 1572872 | tf_op jit(solution)/shard_map/ppermute | solution.py:48
  182.5 15.8 %collective-permute-start.30 = (s16[2,256,512]{2,1,0:T(8,128)(2,1)S(1)}, s16[2,256,512]{2,1,0:T(8,128)(2,1)S(1)}, u32[]{:S(2)}, u32[]{:S(2)}) collective-permute-start(s16[2,256,512]{2,1,0:T(8,128)(2,1)S(1)} %copy-done.11), channel_id=1, source_target_pairs={{0,32},{1,33},{2,34},{3,35},{4,36},{5,37},{6,38},{7,39},{8,40},{9,... | collective-permute-start | bytes 1572872 | tf_op jit(solution)/shard_map/ppermute | solution.py:48
  184.3 26.5 %collective-permute-start.29 = (s16[2,256,512]{2,1,0:T(8,128)(2,1)S(1)}, s16[2,256,512]{2,1,0:T(8,128)(2,1)S(1)}, u32[]{:S(2)}, u32[]{:S(2)}) collective-permute-start(s16[2,256,512]{2,1,0:T(8,128)(2,1)S(1)} %copy-done.11), channel_id=1, source_target_pairs={{0,16},{1,17},{2,18},{3,19},{4,20},{5,21},{6,22},{7,23},{8,24},{9,... | collective-permute-start | bytes 1572872 | tf_op jit(solution)/shard_map/ppermute | solution.py:48
  187.1 24.5 %collective-permute-start.28 = (f32[256,512]{1,0:T(8,128)S(1)}, f32[256,512]{1,0:T(8,128)}, u32[]{:S(2)}, u32[]{:S(2)}) collective-permute-start(f32[256,512]{1,0:T(8,128)S(1)} %bitcast.82), channel_id=1, source_target_pairs={{0,8},{1,9},{2,10},{3,11},{4,12},{5,13},{6,14},{7,15},{8,0},{9,1},... | collective-permute-start | bytes 1572872 | tf_op jit(solution)/shard_map/ppermute | solution.py:48
  211.1 29.2 %collective-permute-start.32 = (s16[4,2,256,512]{3,2,1,0:T(8,128)(2,1)S(1)}, s16[4,2,256,512]{3,2,1,0:T(8,128)(2,1)}, u32[]{:S(2)}, u32[]{:S(2)}) collective-permute-start(s16[4,2,256,512]{3,2,1,0:T(8,128)(2,1)S(1)} %pad_add_fusion.own), channel_id=1, source_target_pairs={{0,8},{1,9},{2,10},{3,11},{4,12},{5,13},{6,14},{7,15},{8,0},{9,1},... | collective-permute-start | bytes 6291464 | tf_op jit(solution)/shard_map/ppermute | solution.py:48
  239.3 1.0 copy-start.9
  246.1 1.2 copy-start.1
  252.1 26.0 %all-to-all-start.2 = ((s16[8,208,512]{2,1,0:T(8,128)(2,1)}), s16[8,208,512]{2,1,0:T(8,128)(2,1)S(1)}, u32[]{:S(2)}, u32[]{:S(2)}) async-start(s16[8,208,512]{2,1,0:T(8,128)(2,1)} %copy-done.1), calls=%async_computation.2 | async-start | bytes 3407872 | tf_op jit(solution)/shard_map/all_to_all | solution.py:801
  266.1 2.2 copy-start.2
  278.1 5.6 %copy-start.10 = (s16[8,208,512]{2,1,0:T(8,128)(2,1)}, s16[8,208,512]{2,1,0:T(8,128)(2,1)S(1)}, u32[]{:S(2)}) copy-start(s16[8,208,512]{2,1,0:T(8,128)(2,1)S(1)} %all-to-all-done.2.gx) | copy-start | bytes 5111812
  278.2 5.5 %collective-permute-start.33 = (s16[8,112,512]{2,1,0:T(8,128)(2,1)S(1)}, s16[8,112,512]{2,1,0:T(8,128)(2,1)S(1)}, u32[]{:S(2)}, u32[]{:S(2)}) collective-permute-start(s16[8,112,512]{2,1,0:T(8,128)(2,1)S(1)} %slice.9), channel_id=1, source_target_pairs={{0,8},{1,9},{2,10},{3,11},{4,12},{5,13},{6,14},{7,15},{8,0},{9,1},... | collective-permute-start | bytes 2752520 | tf_op jit(solution)/shard_map/ppermute | solution.py:48

commit v7 on v6

--- a/solution.py
+++ b/solution.py
@@ -68,12 +68,28 @@
     return jnp.exp2(code * (1.0 / 128.0) - 15.0) * (32768.0 / 32766.0)
 
 
-def update_kernel(ids, slots, pat, blk, pan, mine, other, front, send, diag, gcol, tile, sem):
-    i = pl.program_id(0)
+def update_kernel(
+    ids, slots, pat, blk, pan, par, front, send, diag, gcol, tile, sem, lines, lsem
+):
+    n = pl.program_id(0)
     ch, r, c, g = ids[0], ids[1], ids[2], ids[3]
     e = (ids[8], ids[9])
-
-    @pl.when(i == 0)
+    j = lax.rem(ids[4] * 2 + n, CT)
+    turn = n % 2
+    si = [slots[ch, r * CT + i] for i in range(CT)]
+    sj = slots[ch, c * CT + j]
+
+    def leave(turn, j, act):
+        for i in range(CT):
+            act(
+                pltpu.make_async_copy(
+                    lines.at[turn, i],
+                    send.at[si[i] // QT, :, pl.ds(pl.multiple_of(j * TILE, TILE), TILE)],
+                    lsem.at[turn, i],
+                )
+            )
+
+    @pl.when(n == 0)
     def _():
         diag[...] = jnp.zeros_like(diag)
         for a in range(2):
@@ -90,38 +106,42 @@
                     copy.wait()
                     diag[a * TILE : (a + 1) * TILE, b * TILE : (b + 1) * TILE] = tile[...]
 
-    si = slots[ch, r * CT + i]
-    for n in range(CT):
-        half = mine if n < 2 else other
-        j = (ids[4] if n < 2 else 1 - ids[4]) * 2 + n % 2
-        cols = pl.ds(pl.multiple_of(j * TILE, TILE), TILE)
-        prod = lax.dot_general(
-            pan[...],
-            half[(n % 2) * TILE : (n % 2 + 1) * TILE, :],
-            (((1,), (1,)), ((), ())),
-            preferred_element_type=F32,
-        )
-        u = (blk[:, cols] - prod) * pat[ch, r * CT + i, c * CT + j].astype(F32)
+    @pl.when(n >= 2)
+    def _():
+        leave(turn, lax.rem(ids[4] * 2 + n - 2, CT), lambda copy: copy.wait())
+
+    prod = lax.dot_general(
+        pan[...], par[0], (((1,), (1,)), ((), ())), preferred_element_type=F32
+    )
+    for i in range(CT):
+        rows = slice(i * TILE, (i + 1) * TILE)
+        u = (blk[rows, :] - prod[rows, :]) * pat[ch, r * CT + i, c * CT + j].astype(F32)
         q, code = encode(u)
-        send[0, 0:TILE, cols] = q
-        send[0, TILE:, cols] = scale_rows(code)
-        sj = slots[ch, c * CT + j]
+        lines[turn, i, 0:TILE, :] = q
+        lines[turn, i, TILE:, :] = scale_rows(code)
         for b in range(2):
             at = slice(b * TILE, (b + 1) * TILE)
 
             @pl.when(sj == e[b])
             def _():
-                gcol[:, at] = u
+                gcol[rows, at] = u
                 for a in range(2):
 
-                    @pl.when(si == e[a])
+                    @pl.when(si[i] == e[a])
                     def _():
                         diag[a * TILE : (a + 1) * TILE, at] += u
 
-
-def update(ids, slots, pat, blk, pan, mine, other, front):
-    def slot(i, ids, slots, pat):
-        return slots[ids[0], ids[1] * CT + i] // QT, 0, 0
+    leave(turn, j, lambda copy: copy.start())
+
+    @pl.when(n == CT - 1)
+    def _():
+        leave(1 - turn, lax.rem(ids[4] * 2 + n - 1, CT), lambda copy: copy.wait())
+        leave(turn, j, lambda copy: copy.wait())
+
+
+def update(ids, slots, pat, blk, pan, par, front):
+    def column(n, ids, slots, pat):
+        return 0, lax.rem(ids[4] * 2 + n, CT)
 
     return pl.pallas_call(
         update_kernel,
@@ -129,27 +149,31 @@
             num_scalar_prefetch=3,
             grid=(CT,),
             in_specs=[
-                pl.BlockSpec((TILE, 1024), lambda i, *s: (i, 0)),
-                pl.BlockSpec((TILE, 1024), lambda i, *s: (i, 0)),
-                pl.BlockSpec((512, 1024), lambda i, *s: (0, 0)),
-                pl.BlockSpec((512, 1024), lambda i, *s: (0, 0)),
+                pl.BlockSpec((1024, TILE), column),
+                pl.BlockSpec((1024, 1024), lambda n, *s: (0, 0)),
+                pl.BlockSpec((1, TILE, 1024), lambda n, *s: (n, 0, 0)),
                 pl.BlockSpec(memory_space=pl.ANY),
             ],
             out_specs=[
-                pl.BlockSpec((1, TILE + CODE, 1024), slot),
-                pl.BlockSpec((PANEL, PANEL), lambda i, *s: (0, 0)),
-                pl.BlockSpec((TILE, PANEL), lambda i, *s: (i, 0)),
+                pl.BlockSpec(memory_space=pl.ANY),
+                pl.BlockSpec((PANEL, PANEL), lambda n, *s: (0, 0)),
+                pl.BlockSpec((CT * TILE, PANEL), lambda n, *s: (0, 0)),
             ],
-            scratch_shapes=[pltpu.VMEM((TILE, TILE), F32), pltpu.SemaphoreType.DMA],
+            scratch_shapes=[
+                pltpu.VMEM((TILE, TILE), F32),
+                pltpu.SemaphoreType.DMA,
+                pltpu.VMEM((2, CT, TILE + CODE, TILE), I16),
+                pltpu.SemaphoreType.DMA((2, CT)),
+            ],
         ),
         out_shape=[
             pltpu.HBM((8, TILE + CODE, 1024), I16),
             pltpu.HBM((PANEL, PANEL), F32),
             pltpu.HBM((CT * TILE, PANEL), F32),
         ],
-        compiler_params=pltpu.CompilerParams(vmem_limit_bytes=40 * MIB),
+        compiler_params=pltpu.CompilerParams(vmem_limit_bytes=48 * MIB),
         cost_estimate=pl.CostEstimate(flops=1 << 31, bytes_accessed=14 * MIB, transcendentals=0),
-    )(ids, slots, pat, blk, pan, mine, other, front)
+    )(ids, slots, pat, blk, pan, par, front)
 
 
 def strips_kernel(ids, gcol, front, *rest):
@@ -519,11 +543,18 @@
     return hi, (v - hi.astype(F32)).astype(BF16)
 
 
+def left3(v):
+    hi, lo = split(v)
+    return jnp.concatenate([hi, hi, lo], 1)
+
+
+def right3(v):
+    hi, lo = split(v)
+    return jnp.concatenate([hi, lo, hi], 1)
+
+
 def dot3(a, b):
-    def one(x, y):
-        return lax.dot_general(x, y, (((1,), (1,)), ((), ())), preferred_element_type=F32)
-
-    return one(a[0], b[0]) + (one(a[0], b[1]) + one(a[1], b[0]))
+    return lax.dot_general(a, b, (((1,), (1,)), ((), ())), preferred_element_type=F32)
 
 
 def base_kernel(ids, where, recv, front, out, tiles, codes, tsem):
@@ -595,16 +626,14 @@
 
 def final_kernel(
     ids, diag, inv, gx, goth, front, out,
-    gbuf, rows_f, lh, ll, ih, il,
+    gbuf, rows_f, left, inverse,
 ):
     t = pl.program_id(0)
     c, g, core = ids[2], ids[3], ids[4]
     col = c * QT + t
     @pl.when(t == 0)
     def _():
-        hi, lo = split(inv[...])
-        ih[...] = hi
-        il[...] = lo
+        inverse[...] = right3(inv[...])
         for s in range(8):
             scale = column_scale(gx[s, 2 * RT * STRIP :, :], 0)
             v = as_float(gx[s, 0 : RT * STRIP, :]) * scale
@@ -619,11 +648,9 @@
                 def _():
                     gbuf[p * TILE : (p + 1) * TILE, :] = diag[a * TILE : (a + 1) * TILE, :]
 
-        v = dot3(split(gbuf[...]), (ih[...], il[...]))
+        v = dot3(left3(gbuf[...]), inverse[...])
         rows_f[...] = v
-        hi, lo = split(v)
-        lh[...] = hi
-        ll[...] = lo
+        left[...] = left3(v)
 
     side = pl.multiple_of((t % RT) * STRIP, STRIP)
 
@@ -647,8 +674,8 @@
         def _():
             gbuf[0:TILE, :] = diag[a * TILE : (a + 1) * TILE, :]
 
-    right = split(dot3(split(gbuf[0:TILE, :]), (ih[...], il[...])))
-    out[...] = front[...] - dot3((lh[...], ll[...]), right)
+    right = right3(dot3(left3(gbuf[0:TILE, :]), inverse[...]))
+    out[...] = front[...] - dot3(left[...], right)
     for a in range(2):
 
         @pl.when(col == ids[8 + a])
@@ -677,10 +704,8 @@
             scratch_shapes=[
                 pltpu.VMEM((RT * TILE, PANEL), F32),
                 pltpu.VMEM((RT * TILE, PANEL), F32),
-                pltpu.VMEM((RT * TILE, PANEL), BF16),
-                pltpu.VMEM((RT * TILE, PANEL), BF16),
-                pltpu.VMEM((PANEL, PANEL), BF16),
-                pltpu.VMEM((PANEL, PANEL), BF16),
+                pltpu.VMEM((RT * TILE, 3 * PANEL), BF16),
+                pltpu.VMEM((PANEL, 3 * PANEL), BF16),
             ],
         ),
         out_shape=jax.ShapeDtypeStruct((RT * TILE, QT * TILE), F32),
@@ -772,7 +797,7 @@
     mine, theirs = fetch_partner(panel, x, core, z, yh)
     mine, theirs, ids, slots, where = lax.optimization_barrier((mine, theirs, ids, slots, where))
     send, diag, gcol = update(
-        ids, slots, child_patterns, block, panel, mine, theirs, parent_front
+        ids, slots, child_patterns, block, panel, jnp.concatenate([mine, theirs]).reshape(CT, TILE, 1024), parent_front
     )
     own = lax.all_to_all(send, ("child", "x"), split_axis=0, concat_axis=0, tiled=True)
 
@@ -780,7 +805,7 @@
     diag, gcol = lax.optimization_barrier((diag, gcol))
     parts = strips(ids, gcol, parent_front)
     parts = [parts[0]] + [shift(parts[d], dz=d) for d in range(1, 4)]
-    diag = sum_x(gathered(diag, z, dz=0).reshape(256, PANEL), x)
+    diag = gathered(diag, z, dz=0).reshape(256, PANEL)
     strip = choose_z(ids, where, parts)
     own, diag, strip = lax.optimization_barrier((own, diag, strip))
 
@@ -788,6 +813,7 @@
     send = route(ids, slots, where, own, other)
     kept, moved = pick(strip, yh), pick(strip, 1 - yh)
     moves = [shift(moved, dy=1), shift(kept, dc=1), shift(moved, dc=1, dy=1)]
+    diag, *moves = lax.optimization_barrier((sum_x(diag, x), *moves))
     strip = choose_y(ids, where, [kept] + moves)
     diag = sum_y(diag)
     send, diag, strip = lax.optimization_barrier((send, diag, strip))

time: 299 us -> 288 us (0.963)
  waiting for transfers between devices: 97.3 us -> 70.4 us
  starting transfers between devices: 102 us -> 121 us
  Pallas kernels: 80.9 us -> 76.8 us
    ppermute x30, waiting for transfers between devices: 82.7 us -> 55.7 us  [shift(): return lax.ppermute(v, AXES, pairs)]
    ppermute x30, starting transfers between devices: 73.7 us -> 99.8 us  [shift(): return lax.ppermute(v, AXES, pairs)]
    all_to_all x1, starting transfers between devices: 9.85 us -> 4.89 us  [body(): lax.all_to_all(send, ('z', 'yh'), split_axis=0, concat_axis=0, tiled=True)]
    all_to_all x1, starting transfers between devices: 8.08 us -> 4.99 us  [body(): lax.all_to_all(send, ('child', 'x'), split_axis=0, concat_axis=0, tiled=T...]
    unnamed x42 -> x44, local copies, waits for them, and re-layouts: 6.84 us -> 6 us
where the time goes in v7:
time: 288 us; the launch traced here: 287 us
  starting transfers between devices  121 us (42%)
  Pallas kernels  76.8 us (27%)
  waiting for transfers between devices  70.4 us (24%)
  local copies, waits for them, and re-layouts  11.2 us (4%)
  other arithmetic  6.95 us (2%)
    ppermute x30, starting transfers between devices, shift(): return lax.ppermute(v, AXES, pairs)  99.8 us
    ppermute x30, waiting for transfers between devices, shift(): return lax.ppermute(v, AXES, pairs)  55.7 us
    pallas_call x1, Pallas kernels, inverse_factor(): pl.pallas_call(inverse_kernel, out_shape=jax.ShapeDtypeStruct((PANEL, PAN...  26.5 us
    pallas_call x1, Pallas kernels, final(): pl.pallas_call(final_kernel, grid_spec=pltpu.PrefetchScalarGridSpec(num_s...  14.3 us
    all_to_all x1, waiting for transfers between devices, body(): lax.all_to_all(gsend, ('z', 'yh'), split_axis=0, concat_axis=0, tiled=True)  10.5 us
    pallas_call x1, Pallas kernels, update(): pl.pallas_call(update_kernel, grid_spec=pltpu.PrefetchScalarGridSpec(num_...  10.1 us
    pallas_call x1, Pallas kernels, base(): pl.pallas_call(base_kernel, grid_spec=pltpu.PrefetchScalarGridSpec(num_sc...  9.93 us
    unnamed x44, local copies, waits for them, and re-layouts  6 us
  transfers between devices with their start and end apart: 37, of which 18 were waited for; matrix products, arithmetic and copies ran while one was open for 2% of the time, Pallas kernels for 17%

profile of v7, /device:TPU:1, one launch (start us, length us, event | category | flops | bytes accessed | tf_op | source)
XLA Modules:
  0.0 286.9 jit_solution(8627807000000914391)
XLA Ops:
  0.0 2.8 dynamic-slice_bitcast_fusion
  2.8 1.3 collective-permute-start
  4.1 1.6 collective-permute-start.3
  5.8 1.6 collective-permute-start.2
  7.4 1.6 collective-permute-start.1
  9.1 1.9 fusion
  11.0 31.3 %collective-permute-start.4 = (bf16[512,1024]{1,0:T(8,128)(2,1)S(1)}, bf16[512,1024]{1,0:T(8,128)(2,1)}, u32[]{:S(2)}, u32[]{:S(2)}) collective-permute-start(bf16[512,1024]{1,0:T(8,128)(2,1)S(1)} %fusion), channel_id=1, source_target_pairs={{0,8},{1,9},{2,10},{3,11},{4,12},{5,13},{6,14},{7,15},{8,0},{9,1},... | collective-permute-start | bytes 3145736 | tf_op jit(solution)/shard_map/ppermute | solution.py:48
  42.6 0.7 select_reduce_fusion.where
  43.3 1.5 collective-permute-done.4
  44.7 1.5 pad_maximum_fusion
  46.2 10.1 %shard_map.64 = (s16[8,272,1024]{2,1,0:T(8,128)(2,1)}, f32[512,512]{1,0:T(8,128)}, f32[1024,512]{1,0:T(8,128)}) custom-call(s32[11]{0:T(128)S(1)} %stack.55.ids, s32[2,32]{1,0:T(2,128)S(1)} %select_reduce_fusion.1.slots, s32[2,32,32]{2,1,0:T(8,128)S(1)} %copy-done.8, f32[1024,1024]{1,0:T(8,128)} %bitcast.85, bf16[1024,1024]{1,0:T(8,128)(2,1)S(1)} %bitcast.83, ...), custom_call_target="tpu_custom_call" | custom-call | flops 2147483648 | bytes 14680064 | tf_op jit(solution)/shard_map/pallas_call | solution.py:146
  56.4 5.0 %all-to-all-start = ((s16[8,272,1024]{2,1,0:T(8,128)(2,1)}), s16[8,272,1024]{2,1,0:T(8,128)(2,1)}, u32[]{:S(2)}, u32[]{:S(2)}) async-start(s16[8,272,1024]{2,1,0:T(8,128)(2,1)} %get-tuple-element.39), calls=%async_computation | async-start | bytes 8912896 | tf_op jit(solution)/shard_map/all_to_all | solution.py:802
  61.4 0.8 dynamic-slice_bitcast_fusion.2
  62.2 0.6 collective-permute-start.5
  62.8 1.7 collective-permute-done.5
  64.6 1.1 bitcast_add_fusion
  65.8 1.2 collective-permute-start.8
  67.0 2.0 collective-permute-start.7
  69.0 5.7 %collective-permute-done.6 = f32[64,512]{1,0:T(8,128)S(1)} collective-permute-done((f32[64,512]{1,0:T(8,128)S(1)}, f32[64,512]{1,0:T(8,128)S(1)}, u32[]{:S(2)}, u32[]{:S(2)}) %collective-permute-start.6) | collective-permute-done | bytes 131104 | tf_op jit(solution)/shard_map/ppermute | solution.py:48
  75.0 1.2 collective-permute-start.11
  76.2 2.6 collective-permute-start.10
  79.1 1.5 shard_map.65
  80.6 0.8 copy-done.4
  81.4 2.6 collective-permute-start.12
  83.9 2.1 collective-permute-start.13
  86.6 9.1 %collective-permute-done.12.refs_1_ = s16[2,256,512]{2,1,0:T(8,128)(2,1)S(1)} collective-permute-done((s16[2,256,512]{2,1,0:T(8,128)(2,1)S(1)}, s16[2,256,512]{2,1,0:T(8,128)(2,1)S(1)}, u32[]{:S(2)}, u32[]{:S(2)}) %collective-permute-start.12) | collective-permute-done | bytes 524320 | tf_op jit(solution)/shard_map/ppermute | solution.py:48
  95.7 12.1 %collective-permute-done.13.refs_2_ = s16[2,256,512]{2,1,0:T(8,128)(2,1)S(1)} collective-permute-done((s16[2,256,512]{2,1,0:T(8,128)(2,1)S(1)}, s16[2,256,512]{2,1,0:T(8,128)(2,1)S(1)}, u32[]{:S(2)}, u32[]{:S(2)}) %collective-permute-start.13) | collective-permute-done | bytes 524320 | tf_op jit(solution)/shard_map/ppermute | solution.py:48
  108.0 0.6 copy-done.15
  108.8 2.8 shard_map.66
  111.6 2.2 all-to-all-done.own
  113.8 0.8 collective-permute-start.15
  114.7 13.0 %collective-permute-start.16 = (f32[64,512]{1,0:T(8,128)S(1)}, f32[64,512]{1,0:T(8,128)S(1)}, u32[]{:S(2)}, u32[]{:S(2)}) collective-permute-start(f32[64,512]{1,0:T(8,128)S(1)} %get-tuple-element.69), channel_id=1, source_target_pairs={{0,16},{1,17},{2,18},{3,19},{4,20},{5,21},{6,22},{7,23},{8,24},{9,... | collective-permute-start | bytes 393224 | tf_op jit(solution)/shard_map/ppermute | solution.py:48
  127.7 4.4 %collective-permute-start.18 = (f32[64,512]{1,0:T(8,128)S(1)}, f32[64,512]{1,0:T(8,128)S(1)}, u32[]{:S(2)}, u32[]{:S(2)}) collective-permute-start(f32[64,512]{1,0:T(8,128)S(1)} %get-tuple-element.70), channel_id=1, source_target_pairs={{0,32},{1,33},{2,34},{3,35},{4,36},{5,37},{6,38},{7,39},{8,40},{9,... | collective-permute-start | bytes 393224 | tf_op jit(solution)/shard_map/ppermute | solution.py:48
  132.1 1.1 dynamic-slice_bitcast_fusion.3
  133.1 1.3 collective-permute-start.20
  134.8 4.0 %collective-permute-start.21 = (s16[256,512]{1,0:T(8,128)(2,1)S(1)}, s16[256,512]{1,0:T(8,128)(2,1)S(1)}, u32[]{:S(2)}, u32[]{:S(2)}) collective-permute-start(s16[256,512]{1,0:T(8,128)(2,1)S(1)} %get-tuple-element.68), channel_id=1, source_target_pairs={{0,65},{1,64},{2,67},{3,66},{4,69},{5,68},{6,71},{7,70},{8,73},{9,... | collective-permute-start | bytes 786440 | tf_op jit(solution)/shard_map/ppermute | solution.py:48
  138.8 3.7 %collective-permute-start.19 = (s16[256,512]{1,0:T(8,128)(2,1)S(1)}, s16[256,512]{1,0:T(8,128)(2,1)S(1)}, u32[]{:S(2)}, u32[]{:S(2)}) collective-permute-start(s16[256,512]{1,0:T(8,128)(2,1)S(1)} %get-tuple-element.68), channel_id=1, source_target_pairs={{0,1},{1,0},{2,3},{3,2},{4,5},{5,4},{6,7},{7,6},{8,9},{9,8},{10,11... | collective-permute-start | bytes 786440 | tf_op jit(solution)/shard_map/ppermute | solution.py:48
  142.6 6.7 %collective-permute-done.21.both = s16[256,512]{1,0:T(8,128)(2,1)S(1)} collective-permute-done((s16[256,512]{1,0:T(8,128)(2,1)S(1)}, s16[256,512]{1,0:T(8,128)(2,1)S(1)}, u32[]{:S(2)}, u32[]{:S(2)}) %collective-permute-start.21) | collective-permute-done | bytes 262176 | tf_op jit(solution)/shard_map/ppermute | solution.py:48
  150.0 1.2 collective-permute-start.24
  151.2 2.4 collective-permute-start.23
  153.6 2.7 shard_map.68
  156.3 2.1 collective-permute-done.23
  158.4 1.1 collective-permute-done.22
  159.6 3.4 %shard_map.67 = s16[8,1552,256]{2,1,0:T(8,128)(2,1)} custom-call(s32[11]{0:T(128)S(1)} %copy-done.7, s32[2,32]{1,0:T(2,128)S(1)} %select_reduce_fusion.1.slots, s32[2,48]{1,0:T(2,128)S(1)} %copy-done.5, s16[8,272,1024]{2,1,0:T(8,128)(2,1)} %all-to-all-done.own, s16[8,272,1024]{2,1,0:T(8,128)(2,1)} %collective-permute-done.15.other), custom_call_target="tpu_custom_call" | custom-call | bytes 8388608 | tf_op jit(solution)/shard_map/pallas_call | solution.py:428
  163.0 4.9 %all-to-all-start.1 = ((s16[8,1552,256]{2,1,0:T(8,128)(2,1)}), s16[8,1552,256]{2,1,0:T(8,128)(2,1)}, u32[]{:S(2)}, u32[]{:S(2)}) async-start(s16[8,1552,256]{2,1,0:T(8,128)(2,1)} %shard_map.67), calls=%async_computation.1 | async-start | bytes 12713984 | tf_op jit(solution)/shard_map/all_to_all | solution.py:820
  168.1 2.9 collective-permute-start.26
  170.9 2.7 collective-permute-start.31
  173.7 4.1 %collective-permute-done.25 = f32[64,512]{1,0:T(8,128)S(1)} collective-permute-done((f32[64,512]{1,0:T(8,128)S(1)}, f32[64,512]{1,0:T(8,128)S(1)}, u32[]{:S(2)}, u32[]{:S(2)}) %collective-permute-start.25) | collective-permute-done | bytes 131104 | tf_op jit(solution)/shard_map/ppermute | solution.py:48
  177.8 11.9 %collective-permute-start.28 = (f32[256,512]{1,0:T(8,128)S(1)}, f32[256,512]{1,0:T(8,128)}, u32[]{:S(2)}, u32[]{:S(2)}) collective-permute-start(f32[256,512]{1,0:T(8,128)S(1)} %bitcast.86), channel_id=1, source_target_pairs={{0,8},{1,9},{2,10},{3,11},{4,12},{5,13},{6,14},{7,15},{8,0},{9,1},... | collective-permute-start | bytes 1572872 | tf_op jit(solution)/shard_map/ppermute | solution.py:48
  189.8 8.1 %collective-permute-done.29 = s16[2,256,512]{2,1,0:T(8,128)(2,1)S(1)} collective-permute-done((s16[2,256,512]{2,1,0:T(8,128)(2,1)S(1)}, s16[2,256,512]{2,1,0:T(8,128)(2,1)S(1)}, u32[]{:S(2)}, u32[]{:S(2)}) %collective-permute-start.29) | collective-permute-done | bytes 524320 | tf_op jit(solution)/shard_map/ppermute | solution.py:48
  198.1 4.1 %collective-permute-start.32 = (s16[4,2,256,512]{3,2,1,0:T(8,128)(2,1)S(1)}, s16[4,2,256,512]{3,2,1,0:T(8,128)(2,1)}, u32[]{:S(2)}, u32[]{:S(2)}) collective-permute-start(s16[4,2,256,512]{3,2,1,0:T(8,128)(2,1)S(1)} %pad_add_fusion.own), channel_id=1, source_target_pairs={{0,8},{1,9},{2,10},{3,11},{4,12},{5,13},{6,14},{7,15},{8,0},{9,1},... | collective-permute-start | bytes 6291464 | tf_op jit(solution)/shard_map/ppermute | solution.py:48
  202.2 1.2 broadcast_select_fusion.1
  203.5 26.5 %shard_map.69.inv = f32[512,512]{1,0:T(8,128)S(1)} custom-call(f32[512,512]{1,0:T(8,128)S(1)} %pad_maximum_fusion.1.a_ref.diag), custom_call_target="tpu_custom_call" | custom-call | flops 17179869184 | bytes 2097152 | tf_op jit(solution)/shard_map/pallas_call | solution.py:532
  230.0 1.0 copy-done.9
  231.0 5.7 %shard_map.70 = s16[8,208,512]{2,1,0:T(8,128)(2,1)S(1)} custom-call(s32[11]{0:T(128)S(1)} %copy-done.7, s32[2,48]{1,0:T(2,128)S(1)} %copy-done.5, s16[4,2,256,512]{3,2,1,0:T(8,128)(2,1)S(1)} %pad_add_fusion.own, s16[4,2,256,512]{3,2,1,0:T(8,128)(2,1)} %collective-permute-done.32.other), custom_call_target="tpu_custom_call" | custom-call | bytes 6291456 | tf_op jit(solution)/shard_map/pallas_call | solution.py:354
  236.7 1.2 copy-done.1
  237.9 1.9 all-to-all-done.1.recv
  239.8 5.1 %all-to-all-start.2 = ((s16[8,208,512]{2,1,0:T(8,128)(2,1)}), s16[8,208,512]{2,1,0:T(8,128)(2,1)S(1)}, u32[]{:S(2)}, u32[]{:S(2)}) async-start(s16[8,208,512]{2,1,0:T(8,128)(2,1)} %copy-done.1), calls=%async_computation.2 | async-start | bytes 3407872 | tf_op jit(solution)/shard_map/all_to_all | solution.py:827
  244.9 9.9 %shard_map.71.front = f32[768,1536]{1,0:T(8,128)S(1)} custom-call(s32[11]{0:T(128)S(1)} %copy-done.7, s32[2,48]{1,0:T(2,128)S(1)} %copy-done.5, s16[8,1552,256]{2,1,0:T(8,128)(2,1)} %all-to-all-done.1.recv, f32[768,1536]{1,0:T(8,128)} %front.5), custom_call_target="tpu_custom_call" | custom-call | bytes 20971520 | tf_op jit(solution)/shard_map/pallas_call | solution.py:608
  254.8 2.2 copy-done.2
  257.0 10.5 %all-to-all-done.2.gx = s16[8,208,512]{2,1,0:T(8,128)(2,1)S(1)} async-done(((s16[8,208,512]{2,1,0:T(8,128)(2,1)}), s16[8,208,512]{2,1,0:T(8,128)(2,1)S(1)}, u32[]{:S(2)}, u32[]{:S(2)}) %all-to-all-start.2) | async-done | bytes 1703968 | tf_op jit(solution)/shard_map/all_to_all | solution.py:827
  267.6 2.9 %collective-permute-start.33 = (s16[8,112,512]{2,1,0:T(8,128)(2,1)S(1)}, s16[8,112,512]{2,1,0:T(8,128)(2,1)S(1)}, u32[]{:S(2)}, u32[]{:S(2)}) collective-permute-start(s16[8,112,512]{2,1,0:T(8,128)(2,1)S(1)} %slice.9), channel_id=1, source_target_pairs={{0,8},{1,9},{2,10},{3,11},{4,12},{5,13},{6,14},{7,15},{8,0},{9,1},... | collective-permute-start | bytes 2752520 | tf_op jit(solution)/shard_map/ppermute | solution.py:48
  270.5 2.1 collective-permute-done.33.goth
  272.6 14.3 %shard_map.72 = f32[768,1536]{1,0:T(8,128)} custom-call(s32[11]{0:T(128)S(1)} %copy-done.7, f32[512,512]{1,0:T(8,128)S(1)} %pad_maximum_fusion.1.a_ref.diag, f32[512,512]{1,0:T(8,128)} %copy-done.9, s16[8,208,512]{2,1,0:T(8,128)(2,1)} %copy-done.10, s16[8,112,512]{2,1,0:T(8,128)(2,1)S(1)} %collective-permute-done.33.goth, f32[768,1536]{1,0:T(8,128)} %copy-done.2), custom_call_target="tpu_custom_call" | custom-call | flops 8589934592 | bytes 20971520 | tf_op jit(solution)/shard_map/pallas_call | solution.py:691
  (91 shorter events, 3.6 us)
Async XLA Ops:
  0.0 9.1 %copy-start = (bf16[1,1024,1024]{2,1,0:T(8,128)(2,1)S(1)}, bf16[1,1024,1024]{2,1,0:T(8,128)(2,1)}, u32[]{:S(2)}) copy-start(bf16[1,1024,1024]{2,1,0:T(8,128)(2,1)} %param.7) | copy-start | bytes 6291460
  2.8 6.2 %collective-permute-start = (bf16[512,1024]{1,0:T(8,128)(2,1)}, bf16[512,1024]{1,0:T(8,128)(2,1)}, u32[]{:S(2)}, u32[]{:S(2)}) collective-permute-start(bf16[512,1024]{1,0:T(8,128)(2,1)} %get-tuple-element.64), channel_id=1, source_target_pairs={{0,8},{9,1},{18,26},{27,19},{36,44},{45,37},{54,62},{63,55},{64,72... | collective-permute-start | bytes 3145736 | tf_op jit(solution)/shard_map/ppermute | solution.py:740
  4.1 4.9 %collective-permute-start.3 = (bf16[512,1024]{1,0:T(8,128)(2,1)S(1)}, bf16[512,1024]{1,0:T(8,128)(2,1)}, u32[]{:S(2)}, u32[]{:S(2)}) collective-permute-start(bf16[512,1024]{1,0:T(8,128)(2,1)S(1)} %get-tuple-element.63), channel_id=1, source_target_pairs={{0,48},{4,56},{9,49},{13,57},{18,2},{22,10},{27,3},{31,11},{36,20}... | collective-permute-start | bytes 3145736 | tf_op jit(solution)/shard_map/ppermute | solution.py:733
  5.8 3.3 %collective-permute-start.2 = (bf16[512,1024]{1,0:T(8,128)(2,1)S(1)}, bf16[512,1024]{1,0:T(8,128)(2,1)}, u32[]{:S(2)}, u32[]{:S(2)}) collective-permute-start(bf16[512,1024]{1,0:T(8,128)(2,1)S(1)} %get-tuple-element.63), channel_id=1, source_target_pairs={{0,32},{4,40},{9,33},{13,41},{18,50},{22,58},{27,51},{31,59},{36,4... | collective-permute-start | bytes 3145736 | tf_op jit(solution)/shard_map/ppermute | solution.py:733
  7.4 1.7 collective-permute-start.1
  9.0 33.3 %copy-start.20 = (s32[48]{0:T(128)S(1)}, s32[48]{0:T(128)}, u32[]{:S(2)}) copy-start(s32[48]{0:T(128)} %param.10) | copy-start | bytes 580
  9.1 33.4 %copy-start.21 = (s32[2,32]{1,0:T(2,128)S(1)}, s32[2,32]{1,0:T(2,128)}, u32[]{:S(2)}) copy-start(s32[2,32]{1,0:T(2,128)} %param.9) | copy-start | bytes 772
  11.0 33.7 %collective-permute-start.4 = (bf16[512,1024]{1,0:T(8,128)(2,1)S(1)}, bf16[512,1024]{1,0:T(8,128)(2,1)}, u32[]{:S(2)}, u32[]{:S(2)}) collective-permute-start(bf16[512,1024]{1,0:T(8,128)(2,1)S(1)} %fusion), channel_id=1, source_target_pairs={{0,8},{1,9},{2,10},{3,11},{4,12},{5,13},{6,14},{7,15},{8,0},{9,1},... | collective-permute-start | bytes 3145736 | tf_op jit(solution)/shard_map/ppermute | solution.py:48
  42.4 36.6 %copy-start.6 = (s32[11]{0:T(128)}, s32[11]{0:T(128)S(1)}, u32[]{:S(2)}) copy-start(s32[11]{0:T(128)S(1)} %stack.55.ids) | copy-start | bytes 136
  43.3 3.0 %copy-start.8 = (s32[2,32,32]{2,1,0:T(8,128)S(1)}, s32[2,32,32]{2,1,0:T(8,128)}, u32[]{:S(2)}) copy-start(s32[2,32,32]{2,1,0:T(8,128)} %pat.1) | copy-start | bytes 24580
  56.4 5.0 %copy-start.13 = (f32[512,512]{1,0:T(8,128)S(1)}, f32[512,512]{1,0:T(8,128)}, u32[]{:S(2)}) copy-start(f32[512,512]{1,0:T(8,128)} %get-tuple-element.40) | copy-start | bytes 3145732
  56.4 57.5 %all-to-all-start = ((s16[8,272,1024]{2,1,0:T(8,128)(2,1)}), s16[8,272,1024]{2,1,0:T(8,128)(2,1)}, u32[]{:S(2)}, u32[]{:S(2)}) async-start(s16[8,272,1024]{2,1,0:T(8,128)(2,1)} %get-tuple-element.39), calls=%async_computation | async-start | bytes 8912896 | tf_op jit(solution)/shard_map/all_to_all | solution.py:802
  61.4 17.7 %copy-start.3 = (f32[1024,512]{1,0:T(8,128)S(1)}, f32[1024,512]{1,0:T(8,128)}, u32[]{:S(2)}) copy-start(f32[1024,512]{1,0:T(8,128)} %get-tuple-element.43.gcol) | copy-start | bytes 6291460
  62.2 2.4 collective-permute-start.5
  65.8 8.9 %collective-permute-start.6 = (f32[64,512]{1,0:T(8,128)S(1)}, f32[64,512]{1,0:T(8,128)S(1)}, u32[]{:S(2)}, u32[]{:S(2)}) collective-permute-start(f32[64,512]{1,0:T(8,128)S(1)} %get-tuple-element.72), channel_id=1, source_target_pairs={{0,2},{1,3},{2,4},{3,5},{4,6},{5,7},{6,0},{7,1},{8,10},{9,11},{10,... | collective-permute-start | bytes 393224 | tf_op jit(solution)/shard_map/ppermute | solution.py:48
  65.8 8.9 %collective-permute-start.8 = (f32[64,512]{1,0:T(8,128)S(1)}, f32[64,512]{1,0:T(8,128)S(1)}, u32[]{:S(2)}, u32[]{:S(2)}) collective-permute-start(f32[64,512]{1,0:T(8,128)S(1)} %get-tuple-element.73), channel_id=1, source_target_pairs={{0,4},{1,5},{2,6},{3,7},{4,0},{5,1},{6,2},{7,3},{8,12},{9,13},{10,... | collective-permute-start | bytes 393224 | tf_op jit(solution)/shard_map/ppermute | solution.py:48
  67.0 7.9 %collective-permute-start.7 = (f32[64,512]{1,0:T(8,128)S(1)}, f32[64,512]{1,0:T(8,128)S(1)}, u32[]{:S(2)}, u32[]{:S(2)}) collective-permute-start(f32[64,512]{1,0:T(8,128)S(1)} %get-tuple-element.74), channel_id=1, source_target_pairs={{0,6},{1,7},{2,0},{3,1},{4,2},{5,3},{6,4},{7,5},{8,14},{9,15},{10,... | collective-permute-start | bytes 393224 | tf_op jit(solution)/shard_map/ppermute | solution.py:48
  75.0 11.6 %collective-permute-start.11 = (f32[64,512]{1,0:T(8,128)S(1)}, f32[64,512]{1,0:T(8,128)S(1)}, u32[]{:S(2)}, u32[]{:S(2)}) collective-permute-start(f32[64,512]{1,0:T(8,128)S(1)} %fusion.4), channel_id=1, source_target_pairs={{0,4},{1,5},{2,6},{3,7},{4,0},{5,1},{6,2},{7,3},{8,12},{9,13},{10,... | collective-permute-start | bytes 393224 | tf_op jit(solution)/shard_map/ppermute | solution.py:48
  76.2 10.4 %collective-permute-start.10 = (f32[64,512]{1,0:T(8,128)S(1)}, f32[64,512]{1,0:T(8,128)S(1)}, u32[]{:S(2)}, u32[]{:S(2)}) collective-permute-start(f32[64,512]{1,0:T(8,128)S(1)} %fusion.4), channel_id=1, source_target_pairs={{0,6},{1,7},{2,0},{3,1},{4,2},{5,3},{6,4},{7,5},{8,14},{9,15},{10,... | collective-permute-start | bytes 393224 | tf_op jit(solution)/shard_map/ppermute | solution.py:48
  78.7 7.4 %collective-permute-start.9 = (f32[64,512]{1,0:T(8,128)S(1)}, f32[64,512]{1,0:T(8,128)S(1)}, u32[]{:S(2)}, u32[]{:S(2)}) collective-permute-start(f32[64,512]{1,0:T(8,128)S(1)} %fusion.4), channel_id=1, source_target_pairs={{0,2},{1,3},{2,4},{3,5},{4,6},{5,7},{6,0},{7,1},{8,10},{9,11},{10,... | collective-permute-start | bytes 393224 | tf_op jit(solution)/shard_map/ppermute | solution.py:48
  80.5 0.8 copy-start.4
  81.4 14.3 %collective-permute-start.12 = (s16[2,256,512]{2,1,0:T(8,128)(2,1)S(1)}, s16[2,256,512]{2,1,0:T(8,128)(2,1)S(1)}, u32[]{:S(2)}, u32[]{:S(2)}) collective-permute-start(s16[2,256,512]{2,1,0:T(8,128)(2,1)S(1)} %get-tuple-element.45), channel_id=1, source_target_pairs={{0,2},{1,3},{2,4},{3,5},{4,6},{5,7},{6,0},{7,1},{8,10},{9,11},{10,... | collective-permute-start | bytes 1572872 | tf_op jit(solution)/shard_map/ppermute | solution.py:48
  83.9 23.9 %collective-permute-start.13 = (s16[2,256,512]{2,1,0:T(8,128)(2,1)S(1)}, s16[2,256,512]{2,1,0:T(8,128)(2,1)S(1)}, u32[]{:S(2)}, u32[]{:S(2)}) collective-permute-start(s16[2,256,512]{2,1,0:T(8,128)(2,1)S(1)} %get-tuple-element.46), channel_id=1, source_target_pairs={{0,4},{1,5},{2,6},{3,7},{4,0},{5,1},{6,2},{7,3},{8,12},{9,13},{10,... | collective-permute-start | bytes 1572872 | tf_op jit(solution)/shard_map/ppermute | solution.py:48
  86.1 21.9 %collective-permute-start.14 = (s16[2,256,512]{2,1,0:T(8,128)(2,1)S(1)}, s16[2,256,512]{2,1,0:T(8,128)(2,1)S(1)}, u32[]{:S(2)}, u32[]{:S(2)}) collective-permute-start(s16[2,256,512]{2,1,0:T(8,128)(2,1)S(1)} %get-tuple-element.47), channel_id=1, source_target_pairs={{0,6},{1,7},{2,0},{3,1},{4,2},{5,3},{6,4},{7,5},{8,14},{9,15},{10,... | collective-permute-start | bytes 1572872 | tf_op jit(solution)/shard_map/ppermute | solution.py:48
  95.7 12.3 %copy-start.14 = (s16[2,256,512]{2,1,0:T(8,128)(2,1)}, s16[2,256,512]{2,1,0:T(8,128)(2,1)S(1)}, u32[]{:S(2)}) copy-start(s16[2,256,512]{2,1,0:T(8,128)(2,1)S(1)} %collective-permute-done.12.refs_1_) | copy-start | bytes 1572868
  107.8 0.8 copy-start.15
  108.0 0.8 copy-start.16
  113.8 45.7 %collective-permute-start.15 = (s16[8,272,1024]{2,1,0:T(8,128)(2,1)}, s16[8,272,1024]{2,1,0:T(8,128)(2,1)}, u32[]{:S(2)}, u32[]{:S(2)}) collective-permute-start(s16[8,272,1024]{2,1,0:T(8,128)(2,1)} %all-to-all-done.own), channel_id=1, source_target_pairs={{0,8},{1,9},{2,10},{3,11},{4,12},{5,13},{6,14},{7,15},{8,0},{9,1},... | collective-permute-start | bytes 13369352 | tf_op jit(solution)/shard_map/ppermute | solution.py:48
  114.7 44.9 %copy-start.5 = (s32[2,48]{1,0:T(2,128)S(1)}, s32[2,48]{1,0:T(2,128)}, u32[]{:S(2)}) copy-start(s32[2,48]{1,0:T(2,128)} %select_reduce_fusion.where) | copy-start | bytes 1156
  114.7 44.9 %copy-start.7 = (s32[11]{0:T(128)S(1)}, s32[11]{0:T(128)}, u32[]{:S(2)}) copy-start(s32[11]{0:T(128)} %copy-done.6) | copy-start | bytes 136
  114.7 20.1 %collective-permute-start.16 = (f32[64,512]{1,0:T(8,128)S(1)}, f32[64,512]{1,0:T(8,128)S(1)}, u32[]{:S(2)}, u32[]{:S(2)}) collective-permute-start(f32[64,512]{1,0:T(8,128)S(1)} %get-tuple-element.69), channel_id=1, source_target_pairs={{0,16},{1,17},{2,18},{3,19},{4,20},{5,21},{6,22},{7,23},{8,24},{9,... | collective-permute-start | bytes 393224 | tf_op jit(solution)/shard_map/ppermute | solution.py:48
  127.7 11.1 %collective-permute-start.18 = (f32[64,512]{1,0:T(8,128)S(1)}, f32[64,512]{1,0:T(8,128)S(1)}, u32[]{:S(2)}, u32[]{:S(2)}) collective-permute-start(f32[64,512]{1,0:T(8,128)S(1)} %get-tuple-element.70), channel_id=1, source_target_pairs={{0,32},{1,33},{2,34},{3,35},{4,36},{5,37},{6,38},{7,39},{8,40},{9,... | collective-permute-start | bytes 393224 | tf_op jit(solution)/shard_map/ppermute | solution.py:48
  132.1 10.5 %collective-permute-start.17 = (f32[64,512]{1,0:T(8,128)S(1)}, f32[64,512]{1,0:T(8,128)S(1)}, u32[]{:S(2)}, u32[]{:S(2)}) collective-permute-start(f32[64,512]{1,0:T(8,128)S(1)} %get-tuple-element.71), channel_id=1, source_target_pairs={{0,48},{1,49},{2,50},{3,51},{4,52},{5,53},{6,54},{7,55},{8,56},{9,... | collective-permute-start | bytes 393224 | tf_op jit(solution)/shard_map/ppermute | solution.py:48
  133.1 20.4 %copy-start.12 = (s16[256,512]{1,0:T(8,128)(2,1)}, s16[256,512]{1,0:T(8,128)(2,1)S(1)}, u32[]{:S(2)}) copy-start(s16[256,512]{1,0:T(8,128)(2,1)S(1)} %get-tuple-element.67.kept) | copy-start | bytes 786436
  133.1 9.5 %collective-permute-start.20 = (s16[256,512]{1,0:T(8,128)(2,1)S(1)}, s16[256,512]{1,0:T(8,128)(2,1)S(1)}, u32[]{:S(2)}, u32[]{:S(2)}) collective-permute-start(s16[256,512]{1,0:T(8,128)(2,1)S(1)} %get-tuple-element.67.kept), channel_id=1, source_target_pairs={{0,64},{1,65},{2,66},{3,67},{4,68},{5,69},{6,70},{7,71},{8,72},{9,... | collective-permute-start | bytes 786440 | tf_op jit(solution)/shard_map/ppermute | solution.py:48
  134.8 14.6 %collective-permute-start.21 = (s16[256,512]{1,0:T(8,128)(2,1)S(1)}, s16[256,512]{1,0:T(8,128)(2,1)S(1)}, u32[]{:S(2)}, u32[]{:S(2)}) collective-permute-start(s16[256,512]{1,0:T(8,128)(2,1)S(1)} %get-tuple-element.68), channel_id=1, source_target_pairs={{0,65},{1,64},{2,67},{3,66},{4,69},{5,68},{6,71},{7,70},{8,73},{9,... | collective-permute-start | bytes 786440 | tf_op jit(solution)/shard_map/ppermute | solution.py:48
  138.8 11.1 %collective-permute-start.19 = (s16[256,512]{1,0:T(8,128)(2,1)S(1)}, s16[256,512]{1,0:T(8,128)(2,1)S(1)}, u32[]{:S(2)}, u32[]{:S(2)}) collective-permute-start(s16[256,512]{1,0:T(8,128)(2,1)S(1)} %get-tuple-element.68), channel_id=1, source_target_pairs={{0,1},{1,0},{2,3},{3,2},{4,5},{5,4},{6,7},{7,6},{8,9},{9,8},{10,11... | collective-permute-start | bytes 786440 | tf_op jit(solution)/shard_map/ppermute | solution.py:48
  142.6 11.0 %copy-start.17 = (s16[256,512]{1,0:T(8,128)(2,1)}, s16[256,512]{1,0:T(8,128)(2,1)S(1)}, u32[]{:S(2)}) copy-start(s16[256,512]{1,0:T(8,128)(2,1)S(1)} %collective-permute-done.20.across) | copy-start | bytes 786436
  149.4 4.2 %copy-start.18 = (s16[256,512]{1,0:T(8,128)(2,1)}, s16[256,512]{1,0:T(8,128)(2,1)S(1)}, u32[]{:S(2)}) copy-start(s16[256,512]{1,0:T(8,128)(2,1)S(1)} %collective-permute-done.21.both) | copy-start | bytes 786436
  150.0 3.6 %copy-start.19 = (s16[256,512]{1,0:T(8,128)(2,1)}, s16[256,512]{1,0:T(8,128)(2,1)S(1)}, u32[]{:S(2)}) copy-start(s16[256,512]{1,0:T(8,128)(2,1)S(1)} %collective-permute-done.19.beside) | copy-start | bytes 786436
  150.0 6.3 %collective-permute-start.24 = (f32[64,512]{1,0:T(8,128)S(1)}, f32[64,512]{1,0:T(8,128)S(1)}, u32[]{:S(2)}, u32[]{:S(2)}) collective-permute-start(f32[64,512]{1,0:T(8,128)S(1)} %fusion.2), channel_id=1, source_target_pairs={{0,1},{1,0},{2,3},{3,2},{4,5},{5,4},{6,7},{7,6},{8,9},{9,8},{10,11... | collective-permute-start | bytes 393224 | tf_op jit(solution)/shard_map/ppermute | solution.py:48
  151.2 7.2 %collective-permute-start.23 = (f32[64,512]{1,0:T(8,128)S(1)}, f32[64,512]{1,0:T(8,128)S(1)}, u32[]{:S(2)}, u32[]{:S(2)}) collective-permute-start(f32[64,512]{1,0:T(8,128)S(1)} %fusion.2), channel_id=1, source_target_pairs={{0,64},{1,65},{2,66},{3,67},{4,68},{5,69},{6,70},{7,71},{8,72},{9,... | collective-permute-start | bytes 393224 | tf_op jit(solution)/shard_map/ppermute | solution.py:48
  153.6 5.9 %collective-permute-start.22 = (f32[64,512]{1,0:T(8,128)S(1)}, f32[64,512]{1,0:T(8,128)S(1)}, u32[]{:S(2)}, u32[]{:S(2)}) collective-permute-start(f32[64,512]{1,0:T(8,128)S(1)} %fusion.2), channel_id=1, source_target_pairs={{0,65},{1,64},{2,67},{3,66},{4,69},{5,68},{6,71},{7,70},{8,73},{9,... | collective-permute-start | bytes 393224 | tf_op jit(solution)/shard_map/ppermute | solution.py:48
  163.0 7.9 %copy-start.11 = (s16[2,256,512]{2,1,0:T(8,128)(2,1)S(1)}, s16[2,256,512]{2,1,0:T(8,128)(2,1)}, u32[]{:S(2)}) copy-start(s16[2,256,512]{2,1,0:T(8,128)(2,1)} %shard_map.68) | copy-start | bytes 1572868
  163.0 76.8 %all-to-all-start.1 = ((s16[8,1552,256]{2,1,0:T(8,128)(2,1)}), s16[8,1552,256]{2,1,0:T(8,128)(2,1)}, u32[]{:S(2)}, u32[]{:S(2)}) async-start(s16[8,1552,256]{2,1,0:T(8,128)(2,1)} %shard_map.67), calls=%async_computation.1 | async-start | bytes 12713984 | tf_op jit(solution)/shard_map/all_to_all | solution.py:820
  168.0 9.8 %collective-permute-start.27 = (f32[64,512]{1,0:T(8,128)S(1)}, f32[64,512]{1,0:T(8,128)S(1)}, u32[]{:S(2)}, u32[]{:S(2)}) collective-permute-start(f32[64,512]{1,0:T(8,128)S(1)} %add_add_fusion), channel_id=1, source_target_pairs={{0,32},{1,33},{2,34},{3,35},{4,36},{5,37},{6,38},{7,39},{8,40},{9,... | collective-permute-start | bytes 393224 | tf_op jit(solution)/shard_map/ppermute | solution.py:48
  168.1 9.7 %collective-permute-start.26 = (f32[64,512]{1,0:T(8,128)S(1)}, f32[64,512]{1,0:T(8,128)S(1)}, u32[]{:S(2)}, u32[]{:S(2)}) collective-permute-start(f32[64,512]{1,0:T(8,128)S(1)} %add_add_fusion), channel_id=1, source_target_pairs={{0,48},{1,49},{2,50},{3,51},{4,52},{5,53},{6,54},{7,55},{8,56},{9,... | collective-permute-start | bytes 393224 | tf_op jit(solution)/shard_map/ppermute | solution.py:48
  170.9 6.8 %collective-permute-start.25 = (f32[64,512]{1,0:T(8,128)S(1)}, f32[64,512]{1,0:T(8,128)S(1)}, u32[]{:S(2)}, u32[]{:S(2)}) collective-permute-start(f32[64,512]{1,0:T(8,128)S(1)} %add_add_fusion), channel_id=1, source_target_pairs={{0,16},{1,17},{2,18},{3,19},{4,20},{5,21},{6,22},{7,23},{8,24},{9,... | collective-permute-start | bytes 393224 | tf_op jit(solution)/shard_map/ppermute | solution.py:48
  170.9 18.9 %collective-permute-start.31 = (s16[2,256,512]{2,1,0:T(8,128)(2,1)S(1)}, s16[2,256,512]{2,1,0:T(8,128)(2,1)S(1)}, u32[]{:S(2)}, u32[]{:S(2)}) collective-permute-start(s16[2,256,512]{2,1,0:T(8,128)(2,1)S(1)} %copy-done.11), channel_id=1, source_target_pairs={{0,48},{1,49},{2,50},{3,51},{4,52},{5,53},{6,54},{7,55},{8,56},{9,... | collective-permute-start | bytes 1572872 | tf_op jit(solution)/shard_map/ppermute | solution.py:48
  173.6 16.2 %collective-permute-start.30 = (s16[2,256,512]{2,1,0:T(8,128)(2,1)S(1)}, s16[2,256,512]{2,1,0:T(8,128)(2,1)S(1)}, u32[]{:S(2)}, u32[]{:S(2)}) collective-permute-start(s16[2,256,512]{2,1,0:T(8,128)(2,1)S(1)} %copy-done.11), channel_id=1, source_target_pairs={{0,32},{1,33},{2,34},{3,35},{4,36},{5,37},{6,38},{7,39},{8,40},{9,... | collective-permute-start | bytes 1572872 | tf_op jit(solution)/shard_map/ppermute | solution.py:48
  177.8 20.1 %collective-permute-start.29 = (s16[2,256,512]{2,1,0:T(8,128)(2,1)S(1)}, s16[2,256,512]{2,1,0:T(8,128)(2,1)S(1)}, u32[]{:S(2)}, u32[]{:S(2)}) collective-permute-start(s16[2,256,512]{2,1,0:T(8,128)(2,1)S(1)} %copy-done.11), channel_id=1, source_target_pairs={{0,16},{1,17},{2,18},{3,19},{4,20},{5,21},{6,22},{7,23},{8,24},{9,... | collective-permute-start | bytes 1572872 | tf_op jit(solution)/shard_map/ppermute | solution.py:48
  177.8 24.4 %collective-permute-start.28 = (f32[256,512]{1,0:T(8,128)S(1)}, f32[256,512]{1,0:T(8,128)}, u32[]{:S(2)}, u32[]{:S(2)}) collective-permute-start(f32[256,512]{1,0:T(8,128)S(1)} %bitcast.86), channel_id=1, source_target_pairs={{0,8},{1,9},{2,10},{3,11},{4,12},{5,13},{6,14},{7,15},{8,0},{9,1},... | collective-permute-start | bytes 1572872 | tf_op jit(solution)/shard_map/ppermute | solution.py:48
  198.1 32.9 %collective-permute-start.32 = (s16[4,2,256,512]{3,2,1,0:T(8,128)(2,1)S(1)}, s16[4,2,256,512]{3,2,1,0:T(8,128)(2,1)}, u32[]{:S(2)}, u32[]{:S(2)}) collective-permute-start(s16[4,2,256,512]{3,2,1,0:T(8,128)(2,1)S(1)} %pad_add_fusion.own), channel_id=1, source_target_pairs={{0,8},{1,9},{2,10},{3,11},{4,12},{5,13},{6,14},{7,15},{8,0},{9,1},... | collective-permute-start | bytes 6291464 | tf_op jit(solution)/shard_map/ppermute | solution.py:48
  230.0 1.0 copy-start.9
  236.7 1.2 copy-start.1
  239.8 27.7 %all-to-all-start.2 = ((s16[8,208,512]{2,1,0:T(8,128)(2,1)}), s16[8,208,512]{2,1,0:T(8,128)(2,1)S(1)}, u32[]{:S(2)}, u32[]{:S(2)}) async-start(s16[8,208,512]{2,1,0:T(8,128)(2,1)} %copy-done.1), calls=%async_computation.2 | async-start | bytes 3407872 | tf_op jit(solution)/shard_map/all_to_all | solution.py:827
  254.8 2.2 copy-start.2
  267.5 5.1 %copy-start.10 = (s16[8,208,512]{2,1,0:T(8,128)(2,1)}, s16[8,208,512]{2,1,0:T(8,128)(2,1)S(1)}, u32[]{:S(2)}) copy-start(s16[8,208,512]{2,1,0:T(8,128)(2,1)S(1)} %all-to-all-done.2.gx) | copy-start | bytes 5111812
  267.6 5.0 %collective-permute-start.33 = (s16[8,112,512]{2,1,0:T(8,128)(2,1)S(1)}, s16[8,112,512]{2,1,0:T(8,128)(2,1)S(1)}, u32[]{:S(2)}, u32[]{:S(2)}) collective-permute-start(s16[8,112,512]{2,1,0:T(8,128)(2,1)S(1)} %slice.9), channel_id=1, source_target_pairs={{0,8},{1,9},{2,10},{3,11},{4,12},{5,13},{6,14},{7,15},{8,0},{9,1},... | collective-permute-start | bytes 2752520 | tf_op jit(solution)/shard_map/ppermute | solution.py:48

commit v8 on v7

--- a/solution.py
+++ b/solution.py
@@ -69,7 +69,7 @@
 
 
 def update_kernel(
-    ids, slots, pat, blk, pan, par, front, send, diag, gcol, tile, sem, lines, lsem
+    ids, slots, pat, blk, pan, mine, other, front, send, diag, gcol, tile, sem, lines, lsem
 ):
     n = pl.program_id(0)
     ch, r, c, g = ids[0], ids[1], ids[2], ids[3]
@@ -110,9 +110,8 @@
     def _():
         leave(turn, lax.rem(ids[4] * 2 + n - 2, CT), lambda copy: copy.wait())
 
-    prod = lax.dot_general(
-        pan[...], par[0], (((1,), (1,)), ((), ())), preferred_element_type=F32
-    )
+    par = jnp.where(n < 2, mine[...], other[...])
+    prod = lax.dot_general(pan[...], par, (((1,), (1,)), ((), ())), preferred_element_type=F32)
     for i in range(CT):
         rows = slice(i * TILE, (i + 1) * TILE)
         u = (blk[rows, :] - prod[rows, :]) * pat[ch, r * CT + i, c * CT + j].astype(F32)
@@ -139,7 +138,7 @@
         leave(turn, j, lambda copy: copy.wait())
 
 
-def update(ids, slots, pat, blk, pan, par, front):
+def update(ids, slots, pat, blk, pan, mine, other, front):
     def column(n, ids, slots, pat):
         return 0, lax.rem(ids[4] * 2 + n, CT)
 
@@ -151,7 +150,8 @@
             in_specs=[
                 pl.BlockSpec((1024, TILE), column),
                 pl.BlockSpec((1024, 1024), lambda n, *s: (0, 0)),
-                pl.BlockSpec((1, TILE, 1024), lambda n, *s: (n, 0, 0)),
+                pl.BlockSpec((TILE, 1024), lambda n, *s: (jnp.minimum(n, 1), 0)),
+                pl.BlockSpec((TILE, 1024), lambda n, *s: (jnp.maximum(n - 2, 0), 0)),
                 pl.BlockSpec(memory_space=pl.ANY),
             ],
             out_specs=[
@@ -173,7 +173,7 @@
         ],
         compiler_params=pltpu.CompilerParams(vmem_limit_bytes=48 * MIB),
         cost_estimate=pl.CostEstimate(flops=1 << 31, bytes_accessed=14 * MIB, transcendentals=0),
-    )(ids, slots, pat, blk, pan, par, front)
+    )(ids, slots, pat, blk, pan, mine, other, front)
 
 
 def strips_kernel(ids, gcol, front, *rest):
@@ -768,7 +768,8 @@
 
 
 def sum_y(v):
-    return (v + shift(v, dc=1, dy=1)) + (shift(v, dc=1) + shift(v, dy=1))
+    v = v + shift(v, dc=1)
+    return v + shift(v, dc=1, dy=1)
 
 
 def sum_third(v, x, core):
@@ -797,7 +798,7 @@
     mine, theirs = fetch_partner(panel, x, core, z, yh)
     mine, theirs, ids, slots, where = lax.optimization_barrier((mine, theirs, ids, slots, where))
     send, diag, gcol = update(
-        ids, slots, child_patterns, block, panel, jnp.concatenate([mine, theirs]).reshape(CT, TILE, 1024), parent_front
+        ids, slots, child_patterns, block, panel, mine, theirs, parent_front
     )
     own = lax.all_to_all(send, ("child", "x"), split_axis=0, concat_axis=0, tiled=True)
 
@@ -813,12 +814,11 @@
     send = route(ids, slots, where, own, other)
     kept, moved = pick(strip, yh), pick(strip, 1 - yh)
     moves = [shift(moved, dy=1), shift(kept, dc=1), shift(moved, dc=1, dy=1)]
-    diag, *moves = lax.optimization_barrier((sum_x(diag, x), *moves))
+    diag = sum_y(sum_x(diag, x))
+    send, diag, kept, *moves = lax.optimization_barrier((send, diag, kept, *moves))
+    recv = lax.all_to_all(send, ("z", "yh"), split_axis=0, concat_axis=0, tiled=True)
+
     strip = choose_y(ids, where, [kept] + moves)
-    diag = sum_y(diag)
-    send, diag, strip = lax.optimization_barrier((send, diag, strip))
-    recv = lax.all_to_all(send, ("z", "yh"), split_axis=0, concat_axis=0, tiled=True)
-
     diag = sum_third(diag, x, core)
     line = jnp.stack([strip] + [shift(strip, dx=d) for d in range(1, 4)])
     inv = inverse_factor(diag)

time: 288 us -> 294 us (1.021)
  waiting for transfers between devices: 70.4 us -> 92.9 us
  starting transfers between devices: 121 us -> 104 us
    ppermute x30 -> x29, starting transfers between devices: 99.8 us -> 72.5 us  [shift(): return lax.ppermute(v, AXES, pairs)]
    ppermute x30 -> x29, waiting for transfers between devices: 55.7 us -> 81.5 us  [shift(): return lax.ppermute(v, AXES, pairs)]
    all_to_all x1, starting transfers between devices: 4.89 us -> 10.9 us  [body(): lax.all_to_all(send, ('z', 'yh'), split_axis=0, concat_axis=0, tiled=True)]
    all_to_all x1, starting transfers between devices: 4.99 us -> 8.08 us  [body(): lax.all_to_all(send, ('child', 'x'), split_axis=0, concat_axis=0, tiled=T...]
    unnamed x44 -> x46, local copies, waits for them, and re-layouts: 6 us -> 6.81 us
  transfers between devices with their start and end apart: 37 -> 36, of which waited for: 18 -> 18; matrix products, arithmetic and copies ran while one was open for 2% -> 2% of each run, Pallas kernels for 17% -> 18%
where the time goes in v8:
time: 294 us; the launch traced here: 293 us
  starting transfers between devices  104 us (35%)
  waiting for transfers between devices  92.9 us (32%)
  Pallas kernels  78.2 us (27%)
  local copies, waits for them, and re-layouts  12 us (4%)
  other arithmetic  5.48 us (2%)
    ppermute x29, waiting for transfers between devices, shift(): return lax.ppermute(v, AXES, pairs)  81.5 us
    ppermute x29, starting transfers between devices, shift(): return lax.ppermute(v, AXES, pairs)  72.5 us
    pallas_call x1, Pallas kernels, inverse_factor(): pl.pallas_call(inverse_kernel, out_shape=jax.ShapeDtypeStruct((PANEL, PAN...  26.5 us
    pallas_call x1, Pallas kernels, final(): pl.pallas_call(final_kernel, grid_spec=pltpu.PrefetchScalarGridSpec(num_s...  14.4 us
    all_to_all x1, waiting for transfers between devices, body(): lax.all_to_all(gsend, ('z', 'yh'), split_axis=0, concat_axis=0, tiled=True)  11.4 us
    all_to_all x1, starting transfers between devices, body(): lax.all_to_all(send, ('z', 'yh'), split_axis=0, concat_axis=0, tiled=True)  10.9 us
    pallas_call x1, Pallas kernels, update(): pl.pallas_call(update_kernel, grid_spec=pltpu.PrefetchScalarGridSpec(num_...  10.4 us
    pallas_call x1, Pallas kernels, base(): pl.pallas_call(base_kernel, grid_spec=pltpu.PrefetchScalarGridSpec(num_sc...  9.97 us
  transfers between devices with their start and end apart: 36, of which 18 were waited for; matrix products, arithmetic and copies ran while one was open for 2% of the time, Pallas kernels for 18%

profile of v8, /device:TPU:1, one launch (start us, length us, event | category | flops | bytes accessed | tf_op | source)
XLA Modules:
  0.0 293.4 jit_solution(7255971805694482877)
XLA Ops:
  0.0 2.8 dynamic-slice_bitcast_fusion
  2.8 1.3 collective-permute-start
  4.1 1.7 collective-permute-start.1
  5.8 1.6 collective-permute-start.2
  7.4 1.6 collective-permute-start.3
  9.1 1.9 fusion.mine
  11.0 23.6 %collective-permute-start.4 = (bf16[512,1024]{1,0:T(8,128)(2,1)S(1)}, bf16[512,1024]{1,0:T(8,128)(2,1)}, u32[]{:S(2)}, u32[]{:S(2)}) collective-permute-start(bf16[512,1024]{1,0:T(8,128)(2,1)S(1)} %fusion.mine), channel_id=1, source_target_pairs={{0,8},{1,9},{2,10},{3,11},{4,12},{5,13},{6,14},{7,15},{8,0},{9,1},... | collective-permute-start | bytes 3145736 | tf_op jit(solution)/shard_map/ppermute | solution.py:48
  34.9 0.7 select_reduce_fusion.where
  35.6 1.4 collective-permute-done.4.other
  37.1 10.4 %shard_map.64 = (s16[8,272,1024]{2,1,0:T(8,128)(2,1)}, f32[512,512]{1,0:T(8,128)}, f32[1024,512]{1,0:T(8,128)}) custom-call(s32[11]{0:T(128)S(1)} %stack.55.ids, s32[2,32]{1,0:T(2,128)S(1)} %select_reduce_fusion.1.slots, s32[2,32,32]{2,1,0:T(8,128)S(1)} %copy-done.10, f32[1024,1024]{1,0:T(8,128)} %bitcast.83, bf16[1024,1024]{1,0:T(8,128)(2,1)S(1)} %bitcast.82, ...), custom_call_target="tpu_custom_call" | custom-call | flops 2147483648 | bytes 14680064 | tf_op jit(solution)/shard_map/pallas_call | solution.py:145
  47.4 8.1 %all-to-all-start = ((s16[8,272,1024]{2,1,0:T(8,128)(2,1)}), s16[8,272,1024]{2,1,0:T(8,128)(2,1)}, u32[]{:S(2)}, u32[]{:S(2)}) async-start(s16[8,272,1024]{2,1,0:T(8,128)(2,1)} %get-tuple-element.38), calls=%async_computation | async-start | bytes 8912896 | tf_op jit(solution)/shard_map/all_to_all | solution.py:803
  55.5 0.8 dynamic-slice_bitcast_fusion.2
  56.8 1.7 collective-permute-done.5
  58.5 1.1 bitcast_add_fusion
  59.7 7.2 %collective-permute-start.6 = (f32[64,512]{1,0:T(8,128)S(1)}, f32[64,512]{1,0:T(8,128)S(1)}, u32[]{:S(2)}, u32[]{:S(2)}) collective-permute-start(f32[64,512]{1,0:T(8,128)S(1)} %get-tuple-element.70), channel_id=1, source_target_pairs={{0,2},{1,3},{2,4},{3,5},{4,6},{5,7},{6,0},{7,1},{8,10},{9,11},{10,... | collective-permute-start | bytes 393224 | tf_op jit(solution)/shard_map/ppermute | solution.py:48
  66.9 1.9 collective-permute-start.8
  68.8 1.2 collective-permute-done.6
  70.0 1.4 collective-permute-done.7
  71.4 2.3 collective-permute-done.8
  74.2 2.6 collective-permute-start.10
  76.8 1.1 collective-permute-start.11
  77.9 2.6 shard_map.65
  80.5 0.8 copy-done.4
  81.3 0.8 collective-permute-start.12
  82.3 2.5 collective-permute-start.14
  84.8 11.0 %collective-permute-done.12.refs_1_ = s16[2,256,512]{2,1,0:T(8,128)(2,1)S(1)} collective-permute-done((s16[2,256,512]{2,1,0:T(8,128)(2,1)S(1)}, s16[2,256,512]{2,1,0:T(8,128)(2,1)S(1)}, u32[]{:S(2)}, u32[]{:S(2)}) %collective-permute-start.12) | collective-permute-done | bytes 524320 | tf_op jit(solution)/shard_map/ppermute | solution.py:48
  95.8 10.6 %collective-permute-done.13.refs_2_ = s16[2,256,512]{2,1,0:T(8,128)(2,1)S(1)} collective-permute-done((s16[2,256,512]{2,1,0:T(8,128)(2,1)S(1)}, s16[2,256,512]{2,1,0:T(8,128)(2,1)S(1)}, u32[]{:S(2)}, u32[]{:S(2)}) %collective-permute-start.13) | collective-permute-done | bytes 524320 | tf_op jit(solution)/shard_map/ppermute | solution.py:48
  106.4 0.8 collective-permute-done.14.refs_3_
  107.2 0.7 copy-done.17
  108.0 2.8 shard_map.66
  110.8 2.1 collective-permute-start.15
  112.9 9.2 %collective-permute-start.16 = (f32[64,512]{1,0:T(8,128)S(1)}, f32[64,512]{1,0:T(8,128)S(1)}, u32[]{:S(2)}, u32[]{:S(2)}) collective-permute-start(f32[64,512]{1,0:T(8,128)S(1)} %get-tuple-element.67), channel_id=1, source_target_pairs={{0,16},{1,17},{2,18},{3,19},{4,20},{5,21},{6,22},{7,23},{8,24},{9,... | collective-permute-start | bytes 393224 | tf_op jit(solution)/shard_map/ppermute | solution.py:48
  122.1 3.3 %collective-permute-start.17 = (f32[64,512]{1,0:T(8,128)S(1)}, f32[64,512]{1,0:T(8,128)S(1)}, u32[]{:S(2)}, u32[]{:S(2)}) collective-permute-start(f32[64,512]{1,0:T(8,128)S(1)} %get-tuple-element.69), channel_id=1, source_target_pairs={{0,48},{1,49},{2,50},{3,51},{4,52},{5,53},{6,54},{7,55},{8,56},{9,... | collective-permute-start | bytes 393224 | tf_op jit(solution)/shard_map/ppermute | solution.py:48
  125.4 1.1 collective-permute-start.18
  126.5 2.7 collective-permute-done.16
  129.1 1.8 collective-permute-done.17
  131.0 2.0 collective-permute-done.18
  133.0 1.3 collective-permute-start.19
  134.2 1.1 dynamic-slice_bitcast_fusion.3
  135.3 2.0 collective-permute-start.21
  137.4 1.3 collective-permute-start.23
  138.7 1.5 collective-permute-start.20
  140.1 14.1 %collective-permute-done.20 = f32[64,512]{1,0:T(8,128)S(1)} collective-permute-done((f32[64,512]{1,0:T(8,128)S(1)}, f32[64,512]{1,0:T(8,128)S(1)}, u32[]{:S(2)}, u32[]{:S(2)}) %collective-permute-start.20) | collective-permute-done | bytes 131104 | tf_op jit(solution)/shard_map/ppermute | solution.py:48
  154.2 3.4 %shard_map.67 = s16[8,1552,256]{2,1,0:T(8,128)(2,1)} custom-call(s32[11]{0:T(128)S(1)} %copy-done.8, s32[2,32]{1,0:T(2,128)S(1)} %select_reduce_fusion.1.slots, s32[2,48]{1,0:T(2,128)S(1)} %copy-done.5, s16[8,272,1024]{2,1,0:T(8,128)(2,1)} %all-to-all-done.own, s16[8,272,1024]{2,1,0:T(8,128)(2,1)} %collective-permute-done.15.other), custom_call_target="tpu_custom_call" | custom-call | bytes 8388608 | tf_op jit(solution)/shard_map/pallas_call | solution.py:428
  158.6 10.9 %all-to-all-start.1 = ((s16[8,1552,256]{2,1,0:T(8,128)(2,1)}), s16[8,1552,256]{2,1,0:T(8,128)(2,1)}, u32[]{:S(2)}, u32[]{:S(2)}) async-start(s16[8,1552,256]{2,1,0:T(8,128)(2,1)} %shard_map.67), calls=%async_computation.1 | async-start | bytes 12713984 | tf_op jit(solution)/shard_map/all_to_all | solution.py:819
  169.5 2.7 shard_map.69
  172.7 2.2 collective-permute-start.29
  175.2 1.2 collective-permute-start.24
  176.4 1.5 collective-permute-start.25
  178.0 22.5 %collective-permute-done.24 = f32[64,512]{1,0:T(8,128)S(1)} collective-permute-done((f32[64,512]{1,0:T(8,128)S(1)}, f32[64,512]{1,0:T(8,128)S(1)}, u32[]{:S(2)}, u32[]{:S(2)}) %collective-permute-start.24) | collective-permute-done | bytes 131104 | tf_op jit(solution)/shard_map/ppermute | solution.py:48
  201.1 5.1 %collective-permute-done.26 = f32[64,512]{1,0:T(8,128)S(1)} collective-permute-done((f32[64,512]{1,0:T(8,128)S(1)}, f32[64,512]{1,0:T(8,128)S(1)}, u32[]{:S(2)}, u32[]{:S(2)}) %collective-permute-start.26) | collective-permute-done | bytes 131104 | tf_op jit(solution)/shard_map/ppermute | solution.py:48
  206.2 2.4 collective-permute-start.27
  208.6 1.3 pad_add_fusion.own
  210.4 26.5 %shard_map.68.inv = f32[512,512]{1,0:T(8,128)S(1)} custom-call(f32[512,512]{1,0:T(8,128)S(1)} %pad_maximum_fusion.a_ref.diag), custom_call_target="tpu_custom_call" | custom-call | flops 17179869184 | bytes 2097152 | tf_op jit(solution)/shard_map/pallas_call | solution.py:532
  236.9 1.0 copy-done.11
  237.8 5.6 %shard_map.70 = s16[8,208,512]{2,1,0:T(8,128)(2,1)S(1)} custom-call(s32[11]{0:T(128)S(1)} %copy-done.9, s32[2,48]{1,0:T(2,128)S(1)} %copy-done.6, s16[4,2,256,512]{3,2,1,0:T(8,128)(2,1)S(1)} %pad_add_fusion.own, s16[4,2,256,512]{3,2,1,0:T(8,128)(2,1)} %collective-permute-done.31.other), custom_call_target="tpu_custom_call" | custom-call | bytes 6291456 | tf_op jit(solution)/shard_map/pallas_call | solution.py:354
  243.5 1.2 copy-done.1
  244.7 6.6 %all-to-all-start.2 = ((s16[8,208,512]{2,1,0:T(8,128)(2,1)}), s16[8,208,512]{2,1,0:T(8,128)(2,1)S(1)}, u32[]{:S(2)}, u32[]{:S(2)}) async-start(s16[8,208,512]{2,1,0:T(8,128)(2,1)} %copy-done.1), calls=%async_computation.2 | async-start | bytes 3407872 | tf_op jit(solution)/shard_map/all_to_all | solution.py:827
  251.3 10.0 %shard_map.71.front = f32[768,1536]{1,0:T(8,128)S(1)} custom-call(s32[11]{0:T(128)S(1)} %copy-done.9, s32[2,48]{1,0:T(2,128)S(1)} %copy-done.6, s16[8,1552,256]{2,1,0:T(8,128)(2,1)} %all-to-all-done.1.recv, f32[768,1536]{1,0:T(8,128)} %front.5), custom_call_target="tpu_custom_call" | custom-call | bytes 20971520 | tf_op jit(solution)/shard_map/pallas_call | solution.py:608
  261.3 2.2 copy-done.2
  263.5 11.4 %all-to-all-done.2.gx = s16[8,208,512]{2,1,0:T(8,128)(2,1)S(1)} async-done(((s16[8,208,512]{2,1,0:T(8,128)(2,1)}), s16[8,208,512]{2,1,0:T(8,128)(2,1)S(1)}, u32[]{:S(2)}, u32[]{:S(2)}) %all-to-all-start.2) | async-done | bytes 1703968 | tf_op jit(solution)/shard_map/all_to_all | solution.py:827
  274.9 2.0 collective-permute-start.32
  276.9 2.1 collective-permute-done.32.goth
  279.0 14.4 %shard_map.72 = f32[768,1536]{1,0:T(8,128)} custom-call(s32[11]{0:T(128)S(1)} %copy-done.9, f32[512,512]{1,0:T(8,128)S(1)} %pad_maximum_fusion.a_ref.diag, f32[512,512]{1,0:T(8,128)} %copy-done.11, s16[8,208,512]{2,1,0:T(8,128)(2,1)} %copy-done.12, s16[8,112,512]{2,1,0:T(8,128)(2,1)S(1)} %collective-permute-done.32.goth, f32[768,1536]{1,0:T(8,128)} %copy-done.2), custom_call_target="tpu_custom_call" | custom-call | flops 8589934592 | bytes 20971520 | tf_op jit(solution)/shard_map/pallas_call | solution.py:691
  (91 shorter events, 4.5 us)
Async XLA Ops:
  0.0 9.1 %copy-start = (bf16[1,1024,1024]{2,1,0:T(8,128)(2,1)S(1)}, bf16[1,1024,1024]{2,1,0:T(8,128)(2,1)}, u32[]{:S(2)}) copy-start(bf16[1,1024,1024]{2,1,0:T(8,128)(2,1)} %param.7) | copy-start | bytes 6291460
  2.8 6.2 %collective-permute-start = (bf16[512,1024]{1,0:T(8,128)(2,1)}, bf16[512,1024]{1,0:T(8,128)(2,1)}, u32[]{:S(2)}, u32[]{:S(2)}) collective-permute-start(bf16[512,1024]{1,0:T(8,128)(2,1)} %get-tuple-element.62), channel_id=1, source_target_pairs={{0,8},{9,1},{18,26},{27,19},{36,44},{45,37},{54,62},{63,55},{64,72... | collective-permute-start | bytes 3145736 | tf_op jit(solution)/shard_map/ppermute | solution.py:740
  4.1 4.9 %collective-permute-start.1 = (bf16[512,1024]{1,0:T(8,128)(2,1)S(1)}, bf16[512,1024]{1,0:T(8,128)(2,1)}, u32[]{:S(2)}, u32[]{:S(2)}) collective-permute-start(bf16[512,1024]{1,0:T(8,128)(2,1)S(1)} %get-tuple-element.61), channel_id=1, source_target_pairs={{0,16},{4,24},{9,17},{13,25},{18,34},{22,42},{27,35},{31,43},{36,5... | collective-permute-start | bytes 3145736 | tf_op jit(solution)/shard_map/ppermute | solution.py:733
  5.8 3.3 %collective-permute-start.2 = (bf16[512,1024]{1,0:T(8,128)(2,1)S(1)}, bf16[512,1024]{1,0:T(8,128)(2,1)}, u32[]{:S(2)}, u32[]{:S(2)}) collective-permute-start(bf16[512,1024]{1,0:T(8,128)(2,1)S(1)} %get-tuple-element.61), channel_id=1, source_target_pairs={{0,32},{4,40},{9,33},{13,41},{18,50},{22,58},{27,51},{31,59},{36,4... | collective-permute-start | bytes 3145736 | tf_op jit(solution)/shard_map/ppermute | solution.py:733
  7.4 1.7 collective-permute-start.3
  9.0 25.6 %copy-start.21 = (s32[48]{0:T(128)S(1)}, s32[48]{0:T(128)}, u32[]{:S(2)}) copy-start(s32[48]{0:T(128)} %param.10) | copy-start | bytes 580
  9.1 25.7 %copy-start.22 = (s32[2,32]{1,0:T(2,128)S(1)}, s32[2,32]{1,0:T(2,128)}, u32[]{:S(2)}) copy-start(s32[2,32]{1,0:T(2,128)} %param.9) | copy-start | bytes 772
  9.1 28.0 %copy-start.10 = (s32[2,32,32]{2,1,0:T(8,128)S(1)}, s32[2,32,32]{2,1,0:T(8,128)}, u32[]{:S(2)}) copy-start(s32[2,32,32]{2,1,0:T(8,128)} %pat.1) | copy-start | bytes 24580
  11.0 26.0 %collective-permute-start.4 = (bf16[512,1024]{1,0:T(8,128)(2,1)S(1)}, bf16[512,1024]{1,0:T(8,128)(2,1)}, u32[]{:S(2)}, u32[]{:S(2)}) collective-permute-start(bf16[512,1024]{1,0:T(8,128)(2,1)S(1)} %fusion.mine), channel_id=1, source_target_pairs={{0,8},{1,9},{2,10},{3,11},{4,12},{5,13},{6,14},{7,15},{8,0},{9,1},... | collective-permute-start | bytes 3145736 | tf_op jit(solution)/shard_map/ppermute | solution.py:48
  34.7 43.2 %copy-start.7 = (s32[11]{0:T(128)}, s32[11]{0:T(128)S(1)}, u32[]{:S(2)}) copy-start(s32[11]{0:T(128)S(1)} %stack.55.ids) | copy-start | bytes 136
  47.4 8.1 %copy-start.14 = (f32[512,512]{1,0:T(8,128)S(1)}, f32[512,512]{1,0:T(8,128)}, u32[]{:S(2)}) copy-start(f32[512,512]{1,0:T(8,128)} %get-tuple-element.39) | copy-start | bytes 3145732
  47.4 63.3 %all-to-all-start = ((s16[8,272,1024]{2,1,0:T(8,128)(2,1)}), s16[8,272,1024]{2,1,0:T(8,128)(2,1)}, u32[]{:S(2)}, u32[]{:S(2)}) async-start(s16[8,272,1024]{2,1,0:T(8,128)(2,1)} %get-tuple-element.38), calls=%async_computation | async-start | bytes 8912896 | tf_op jit(solution)/shard_map/all_to_all | solution.py:803
  55.5 22.4 %copy-start.3 = (f32[1024,512]{1,0:T(8,128)S(1)}, f32[1024,512]{1,0:T(8,128)}, u32[]{:S(2)}) copy-start(f32[1024,512]{1,0:T(8,128)} %get-tuple-element.42.gcol) | copy-start | bytes 6291460
  56.4 2.2 collective-permute-start.5
  59.7 10.3 %collective-permute-start.6 = (f32[64,512]{1,0:T(8,128)S(1)}, f32[64,512]{1,0:T(8,128)S(1)}, u32[]{:S(2)}, u32[]{:S(2)}) collective-permute-start(f32[64,512]{1,0:T(8,128)S(1)} %get-tuple-element.70), channel_id=1, source_target_pairs={{0,2},{1,3},{2,4},{3,5},{4,6},{5,7},{6,0},{7,1},{8,10},{9,11},{10,... | collective-permute-start | bytes 393224 | tf_op jit(solution)/shard_map/ppermute | solution.py:48
  66.9 4.5 %collective-permute-start.7 = (f32[64,512]{1,0:T(8,128)S(1)}, f32[64,512]{1,0:T(8,128)S(1)}, u32[]{:S(2)}, u32[]{:S(2)}) collective-permute-start(f32[64,512]{1,0:T(8,128)S(1)} %get-tuple-element.72), channel_id=1, source_target_pairs={{0,6},{1,7},{2,0},{3,1},{4,2},{5,3},{6,4},{7,5},{8,14},{9,15},{10,... | collective-permute-start | bytes 393224 | tf_op jit(solution)/shard_map/ppermute | solution.py:48
  66.9 6.8 %collective-permute-start.8 = (f32[64,512]{1,0:T(8,128)S(1)}, f32[64,512]{1,0:T(8,128)S(1)}, u32[]{:S(2)}, u32[]{:S(2)}) collective-permute-start(f32[64,512]{1,0:T(8,128)S(1)} %get-tuple-element.71), channel_id=1, source_target_pairs={{0,4},{1,5},{2,6},{3,7},{4,0},{5,1},{6,2},{7,3},{8,12},{9,13},{10,... | collective-permute-start | bytes 393224 | tf_op jit(solution)/shard_map/ppermute | solution.py:48
  73.7 8.5 %collective-permute-start.9 = (f32[64,512]{1,0:T(8,128)S(1)}, f32[64,512]{1,0:T(8,128)S(1)}, u32[]{:S(2)}, u32[]{:S(2)}) collective-permute-start(f32[64,512]{1,0:T(8,128)S(1)} %fusion.4), channel_id=1, source_target_pairs={{0,2},{1,3},{2,4},{3,5},{4,6},{5,7},{6,0},{7,1},{8,10},{9,11},{10,... | collective-permute-start | bytes 393224 | tf_op jit(solution)/shard_map/ppermute | solution.py:48
  74.2 10.5 %collective-permute-start.10 = (f32[64,512]{1,0:T(8,128)S(1)}, f32[64,512]{1,0:T(8,128)S(1)}, u32[]{:S(2)}, u32[]{:S(2)}) collective-permute-start(f32[64,512]{1,0:T(8,128)S(1)} %fusion.4), channel_id=1, source_target_pairs={{0,6},{1,7},{2,0},{3,1},{4,2},{5,3},{6,4},{7,5},{8,14},{9,15},{10,... | collective-permute-start | bytes 393224 | tf_op jit(solution)/shard_map/ppermute | solution.py:48
  76.8 8.0 %collective-permute-start.11 = (f32[64,512]{1,0:T(8,128)S(1)}, f32[64,512]{1,0:T(8,128)S(1)}, u32[]{:S(2)}, u32[]{:S(2)}) collective-permute-start(f32[64,512]{1,0:T(8,128)S(1)} %fusion.4), channel_id=1, source_target_pairs={{0,4},{1,5},{2,6},{3,7},{4,0},{5,1},{6,2},{7,3},{8,12},{9,13},{10,... | collective-permute-start | bytes 393224 | tf_op jit(solution)/shard_map/ppermute | solution.py:48
  80.5 0.8 copy-start.4
  81.3 14.4 %collective-permute-start.12 = (s16[2,256,512]{2,1,0:T(8,128)(2,1)S(1)}, s16[2,256,512]{2,1,0:T(8,128)(2,1)S(1)}, u32[]{:S(2)}, u32[]{:S(2)}) collective-permute-start(s16[2,256,512]{2,1,0:T(8,128)(2,1)S(1)} %get-tuple-element.44), channel_id=1, source_target_pairs={{0,2},{1,3},{2,4},{3,5},{4,6},{5,7},{6,0},{7,1},{8,10},{9,11},{10,... | collective-permute-start | bytes 1572872 | tf_op jit(solution)/shard_map/ppermute | solution.py:48
  82.2 24.3 %collective-permute-start.13 = (s16[2,256,512]{2,1,0:T(8,128)(2,1)S(1)}, s16[2,256,512]{2,1,0:T(8,128)(2,1)S(1)}, u32[]{:S(2)}, u32[]{:S(2)}) collective-permute-start(s16[2,256,512]{2,1,0:T(8,128)(2,1)S(1)} %get-tuple-element.45), channel_id=1, source_target_pairs={{0,4},{1,5},{2,6},{3,7},{4,0},{5,1},{6,2},{7,3},{8,12},{9,13},{10,... | collective-permute-start | bytes 1572872 | tf_op jit(solution)/shard_map/ppermute | solution.py:48
  82.3 24.9 %collective-permute-start.14 = (s16[2,256,512]{2,1,0:T(8,128)(2,1)S(1)}, s16[2,256,512]{2,1,0:T(8,128)(2,1)S(1)}, u32[]{:S(2)}, u32[]{:S(2)}) collective-permute-start(s16[2,256,512]{2,1,0:T(8,128)(2,1)S(1)} %get-tuple-element.46), channel_id=1, source_target_pairs={{0,6},{1,7},{2,0},{3,1},{4,2},{5,3},{6,4},{7,5},{8,14},{9,15},{10,... | collective-permute-start | bytes 1572872 | tf_op jit(solution)/shard_map/ppermute | solution.py:48
  95.8 11.4 %copy-start.15 = (s16[2,256,512]{2,1,0:T(8,128)(2,1)}, s16[2,256,512]{2,1,0:T(8,128)(2,1)S(1)}, u32[]{:S(2)}) copy-start(s16[2,256,512]{2,1,0:T(8,128)(2,1)S(1)} %collective-permute-done.12.refs_1_) | copy-start | bytes 1572868
  106.4 0.8 copy-start.16
  107.2 0.8 copy-start.17
  110.7 43.5 %copy-start.5 = (s32[2,48]{1,0:T(2,128)S(1)}, s32[2,48]{1,0:T(2,128)}, u32[]{:S(2)}) copy-start(s32[2,48]{1,0:T(2,128)} %select_reduce_fusion.where) | copy-start | bytes 1156
  110.7 43.5 %copy-start.8 = (s32[11]{0:T(128)S(1)}, s32[11]{0:T(128)}, u32[]{:S(2)}) copy-start(s32[11]{0:T(128)} %copy-done.7) | copy-start | bytes 136
  110.8 43.5 %collective-permute-start.15 = (s16[8,272,1024]{2,1,0:T(8,128)(2,1)}, s16[8,272,1024]{2,1,0:T(8,128)(2,1)}, u32[]{:S(2)}, u32[]{:S(2)}) collective-permute-start(s16[8,272,1024]{2,1,0:T(8,128)(2,1)} %all-to-all-done.own), channel_id=1, source_target_pairs={{0,8},{1,9},{2,10},{3,11},{4,12},{5,13},{6,14},{7,15},{8,0},{9,1},... | collective-permute-start | bytes 13369352 | tf_op jit(solution)/shard_map/ppermute | solution.py:48
  112.9 16.3 %collective-permute-start.16 = (f32[64,512]{1,0:T(8,128)S(1)}, f32[64,512]{1,0:T(8,128)S(1)}, u32[]{:S(2)}, u32[]{:S(2)}) collective-permute-start(f32[64,512]{1,0:T(8,128)S(1)} %get-tuple-element.67), channel_id=1, source_target_pairs={{0,16},{1,17},{2,18},{3,19},{4,20},{5,21},{6,22},{7,23},{8,24},{9,... | collective-permute-start | bytes 393224 | tf_op jit(solution)/shard_map/ppermute | solution.py:48
  122.1 8.9 %collective-permute-start.17 = (f32[64,512]{1,0:T(8,128)S(1)}, f32[64,512]{1,0:T(8,128)S(1)}, u32[]{:S(2)}, u32[]{:S(2)}) collective-permute-start(f32[64,512]{1,0:T(8,128)S(1)} %get-tuple-element.69), channel_id=1, source_target_pairs={{0,48},{1,49},{2,50},{3,51},{4,52},{5,53},{6,54},{7,55},{8,56},{9,... | collective-permute-start | bytes 393224 | tf_op jit(solution)/shard_map/ppermute | solution.py:48
  125.4 7.6 %collective-permute-start.18 = (f32[64,512]{1,0:T(8,128)S(1)}, f32[64,512]{1,0:T(8,128)S(1)}, u32[]{:S(2)}, u32[]{:S(2)}) collective-permute-start(f32[64,512]{1,0:T(8,128)S(1)} %get-tuple-element.68), channel_id=1, source_target_pairs={{0,32},{1,33},{2,34},{3,35},{4,36},{5,37},{6,38},{7,39},{8,40},{9,... | collective-permute-start | bytes 393224 | tf_op jit(solution)/shard_map/ppermute | solution.py:48
  133.0 5.7 %collective-permute-start.19 = (f32[64,512]{1,0:T(8,128)S(1)}, f32[64,512]{1,0:T(8,128)S(1)}, u32[]{:S(2)}, u32[]{:S(2)}) collective-permute-start(f32[64,512]{1,0:T(8,128)S(1)} %fusion.2), channel_id=1, source_target_pairs={{0,64},{1,65},{2,66},{3,67},{4,68},{5,69},{6,70},{7,71},{8,72},{9,... | collective-permute-start | bytes 393224 | tf_op jit(solution)/shard_map/ppermute | solution.py:48
  135.3 22.3 %copy-start.13 = (s16[256,512]{1,0:T(8,128)(2,1)}, s16[256,512]{1,0:T(8,128)(2,1)S(1)}, u32[]{:S(2)}) copy-start(s16[256,512]{1,0:T(8,128)(2,1)S(1)} %get-tuple-element.52.kept) | copy-start | bytes 786436
  135.3 22.3 %collective-permute-start.21 = (s16[256,512]{1,0:T(8,128)(2,1)S(1)}, s16[256,512]{1,0:T(8,128)(2,1)S(1)}, u32[]{:S(2)}, u32[]{:S(2)}) collective-permute-start(s16[256,512]{1,0:T(8,128)(2,1)S(1)} %get-tuple-element.65), channel_id=1, source_target_pairs={{0,1},{1,0},{2,3},{3,2},{4,5},{5,4},{6,7},{7,6},{8,9},{9,8},{10,11... | collective-permute-start | bytes 786440 | tf_op jit(solution)/shard_map/ppermute | solution.py:48
  137.4 20.3 %collective-permute-start.22 = (s16[256,512]{1,0:T(8,128)(2,1)S(1)}, s16[256,512]{1,0:T(8,128)(2,1)S(1)}, u32[]{:S(2)}, u32[]{:S(2)}) collective-permute-start(s16[256,512]{1,0:T(8,128)(2,1)S(1)} %get-tuple-element.52.kept), channel_id=1, source_target_pairs={{0,64},{1,65},{2,66},{3,67},{4,68},{5,69},{6,70},{7,71},{8,72},{9,... | collective-permute-start | bytes 786440 | tf_op jit(solution)/shard_map/ppermute | solution.py:48
  137.4 20.3 %collective-permute-start.23 = (s16[256,512]{1,0:T(8,128)(2,1)S(1)}, s16[256,512]{1,0:T(8,128)(2,1)S(1)}, u32[]{:S(2)}, u32[]{:S(2)}) collective-permute-start(s16[256,512]{1,0:T(8,128)(2,1)S(1)} %get-tuple-element.65), channel_id=1, source_target_pairs={{0,65},{1,64},{2,67},{3,66},{4,69},{5,68},{6,71},{7,70},{8,73},{9,... | collective-permute-start | bytes 786440 | tf_op jit(solution)/shard_map/ppermute | solution.py:48
  138.7 15.5 %collective-permute-start.20 = (f32[64,512]{1,0:T(8,128)S(1)}, f32[64,512]{1,0:T(8,128)S(1)}, u32[]{:S(2)}, u32[]{:S(2)}) collective-permute-start(f32[64,512]{1,0:T(8,128)S(1)} %add.225), channel_id=1, source_target_pairs={{0,65},{1,64},{2,67},{3,66},{4,69},{5,68},{6,71},{7,70},{8,73},{9,... | collective-permute-start | bytes 393224 | tf_op jit(solution)/shard_map/ppermute | solution.py:48
  157.7 0.7 copy-start.18
  157.7 0.8 copy-start.19
  157.7 0.9 copy-start.20
  158.6 86.1 %all-to-all-start.1 = ((s16[8,1552,256]{2,1,0:T(8,128)(2,1)}), s16[8,1552,256]{2,1,0:T(8,128)(2,1)}, u32[]{:S(2)}, u32[]{:S(2)}) async-start(s16[8,1552,256]{2,1,0:T(8,128)(2,1)} %shard_map.67), calls=%async_computation.1 | async-start | bytes 12713984 | tf_op jit(solution)/shard_map/all_to_all | solution.py:819
  172.2 36.4 %collective-permute-start.28 = (s16[2,256,512]{2,1,0:T(8,128)(2,1)}, s16[2,256,512]{2,1,0:T(8,128)(2,1)S(1)}, u32[]{:S(2)}, u32[]{:S(2)}) collective-permute-start(s16[2,256,512]{2,1,0:T(8,128)(2,1)} %shard_map.69), channel_id=1, source_target_pairs={{0,16},{1,17},{2,18},{3,19},{4,20},{5,21},{6,22},{7,23},{8,24},{9,... | collective-permute-start | bytes 1572872 | tf_op jit(solution)/shard_map/ppermute | solution.py:48
  172.7 35.9 %collective-permute-start.29 = (s16[2,256,512]{2,1,0:T(8,128)(2,1)}, s16[2,256,512]{2,1,0:T(8,128)(2,1)S(1)}, u32[]{:S(2)}, u32[]{:S(2)}) collective-permute-start(s16[2,256,512]{2,1,0:T(8,128)(2,1)} %shard_map.69), channel_id=1, source_target_pairs={{0,32},{1,33},{2,34},{3,35},{4,36},{5,37},{6,38},{7,39},{8,40},{9,... | collective-permute-start | bytes 1572872 | tf_op jit(solution)/shard_map/ppermute | solution.py:48
  175.0 33.6 %collective-permute-start.30 = (s16[2,256,512]{2,1,0:T(8,128)(2,1)}, s16[2,256,512]{2,1,0:T(8,128)(2,1)S(1)}, u32[]{:S(2)}, u32[]{:S(2)}) collective-permute-start(s16[2,256,512]{2,1,0:T(8,128)(2,1)} %shard_map.69), channel_id=1, source_target_pairs={{0,48},{1,49},{2,50},{3,51},{4,52},{5,53},{6,54},{7,55},{8,56},{9,... | collective-permute-start | bytes 1572872 | tf_op jit(solution)/shard_map/ppermute | solution.py:48
  175.2 25.3 %collective-permute-start.24 = (f32[64,512]{1,0:T(8,128)S(1)}, f32[64,512]{1,0:T(8,128)S(1)}, u32[]{:S(2)}, u32[]{:S(2)}) collective-permute-start(f32[64,512]{1,0:T(8,128)S(1)} %add.226), channel_id=1, source_target_pairs={{0,16},{1,17},{2,18},{3,19},{4,20},{5,21},{6,22},{7,23},{8,24},{9,... | collective-permute-start | bytes 393224 | tf_op jit(solution)/shard_map/ppermute | solution.py:48
  176.4 24.7 %collective-permute-start.25 = (f32[64,512]{1,0:T(8,128)S(1)}, f32[64,512]{1,0:T(8,128)S(1)}, u32[]{:S(2)}, u32[]{:S(2)}) collective-permute-start(f32[64,512]{1,0:T(8,128)S(1)} %add.226), channel_id=1, source_target_pairs={{0,48},{1,49},{2,50},{3,51},{4,52},{5,53},{6,54},{7,55},{8,56},{9,... | collective-permute-start | bytes 393224 | tf_op jit(solution)/shard_map/ppermute | solution.py:48
  200.5 5.7 %collective-permute-start.26 = (f32[64,512]{1,0:T(8,128)S(1)}, f32[64,512]{1,0:T(8,128)S(1)}, u32[]{:S(2)}, u32[]{:S(2)}) collective-permute-start(f32[64,512]{1,0:T(8,128)S(1)} %add.226), channel_id=1, source_target_pairs={{0,32},{1,33},{2,34},{3,35},{4,36},{5,37},{6,38},{7,39},{8,40},{9,... | collective-permute-start | bytes 393224 | tf_op jit(solution)/shard_map/ppermute | solution.py:48
  206.2 3.9 %collective-permute-start.27 = (f32[256,512]{1,0:T(8,128)S(1)}, f32[256,512]{1,0:T(8,128)S(1)}, u32[]{:S(2)}, u32[]{:S(2)}) collective-permute-start(f32[256,512]{1,0:T(8,128)S(1)} %bitcast.84), channel_id=1, source_target_pairs={{0,8},{1,9},{2,10},{3,11},{4,12},{5,13},{6,14},{7,15},{8,0},{9,1},... | collective-permute-start | bytes 1572872 | tf_op jit(solution)/shard_map/ppermute | solution.py:48
  209.9 28.0 %collective-permute-start.31 = (s16[4,2,256,512]{3,2,1,0:T(8,128)(2,1)S(1)}, s16[4,2,256,512]{3,2,1,0:T(8,128)(2,1)}, u32[]{:S(2)}, u32[]{:S(2)}) collective-permute-start(s16[4,2,256,512]{3,2,1,0:T(8,128)(2,1)S(1)} %pad_add_fusion.own), channel_id=1, source_target_pairs={{0,8},{1,9},{2,10},{3,11},{4,12},{5,13},{6,14},{7,15},{8,0},{9,1},... | collective-permute-start | bytes 6291464 | tf_op jit(solution)/shard_map/ppermute | solution.py:48
  210.4 27.5 %copy-start.6 = (s32[2,48]{1,0:T(2,128)S(1)}, s32[2,48]{1,0:T(2,128)}, u32[]{:S(2)}) copy-start(s32[2,48]{1,0:T(2,128)} %select_reduce_fusion.where) | copy-start | bytes 1156
  210.4 27.5 %copy-start.9 = (s32[11]{0:T(128)S(1)}, s32[11]{0:T(128)}, u32[]{:S(2)}) copy-start(s32[11]{0:T(128)} %copy-done.7) | copy-start | bytes 136
  236.9 1.0 copy-start.11
  243.5 1.2 copy-start.1
  244.7 30.2 %all-to-all-start.2 = ((s16[8,208,512]{2,1,0:T(8,128)(2,1)}), s16[8,208,512]{2,1,0:T(8,128)(2,1)S(1)}, u32[]{:S(2)}, u32[]{:S(2)}) async-start(s16[8,208,512]{2,1,0:T(8,128)(2,1)} %copy-done.1), calls=%async_computation.2 | async-start | bytes 3407872 | tf_op jit(solution)/shard_map/all_to_all | solution.py:827
  261.3 2.2 copy-start.2
  274.9 4.2 %copy-start.12 = (s16[8,208,512]{2,1,0:T(8,128)(2,1)}, s16[8,208,512]{2,1,0:T(8,128)(2,1)S(1)}, u32[]{:S(2)}) copy-start(s16[8,208,512]{2,1,0:T(8,128)(2,1)S(1)} %all-to-all-done.2.gx) | copy-start | bytes 5111812
  274.9 4.1 %collective-permute-start.32 = (s16[8,112,512]{2,1,0:T(8,128)(2,1)S(1)}, s16[8,112,512]{2,1,0:T(8,128)(2,1)S(1)}, u32[]{:S(2)}, u32[]{:S(2)}) collective-permute-start(s16[8,112,512]{2,1,0:T(8,128)(2,1)S(1)} %slice.9), channel_id=1, source_target_pairs={{0,8},{1,9},{2,10},{3,11},{4,12},{5,13},{6,14},{7,15},{8,0},{9,1},... | collective-permute-start | bytes 2752520 | tf_op jit(solution)/shard_map/ppermute | solution.py:48

commit v9 on v8

--- a/solution.py
+++ b/solution.py
@@ -768,12 +768,10 @@
 
 
 def sum_y(v):
-    v = v + shift(v, dc=1)
-    return v + shift(v, dc=1, dy=1)
-
-
-def sum_third(v, x, core):
-    v = gathered(v, x, dx=0).reshape(256, PANEL)
+    return (v + shift(v, dc=1, dy=1)) + (shift(v, dc=1) + shift(v, dy=1))
+
+
+def join_cores(v, core):
     other = shift(v, dk=1)
     return jnp.concatenate([jnp.where(core == 0, v, other), jnp.where(core == 0, other, v)])
 
@@ -814,12 +812,15 @@
     send = route(ids, slots, where, own, other)
     kept, moved = pick(strip, yh), pick(strip, 1 - yh)
     moves = [shift(moved, dy=1), shift(kept, dc=1), shift(moved, dc=1, dy=1)]
-    diag = sum_y(sum_x(diag, x))
+    diag, *moves = lax.optimization_barrier((sum_x(diag, x), *moves))
+    diag = sum_y(diag)
     send, diag, kept, *moves = lax.optimization_barrier((send, diag, kept, *moves))
     recv = lax.all_to_all(send, ("z", "yh"), split_axis=0, concat_axis=0, tiled=True)
 
+    diag = gathered(diag, x, dx=0).reshape(256, PANEL)
+    diag, kept, *moves = lax.optimization_barrier((diag, kept, *moves))
     strip = choose_y(ids, where, [kept] + moves)
-    diag = sum_third(diag, x, core)
+    diag = join_cores(diag, core)
     line = jnp.stack([strip] + [shift(strip, dx=d) for d in range(1, 4)])
     inv = inverse_factor(diag)
     gsend = compose(ids, where, line, shift(line, dk=1))

time: 294 us -> 291 us (0.990)
  waiting for transfers between devices: 92.9 us -> 85.3 us
  starting transfers between devices: 104 us -> 111 us
    ppermute x29 -> x30, waiting for transfers between devices: 81.5 us -> 73.3 us  [shift(): return lax.ppermute(v, AXES, pairs)]
    ppermute x29 -> x30, starting transfers between devices: 72.5 us -> 79.1 us  [shift(): return lax.ppermute(v, AXES, pairs)]
  transfers between devices with their start and end apart: 36 -> 37, of which waited for: 18 -> 23; matrix products, arithmetic and copies ran while one was open for 2% -> 2% of each run, Pallas kernels for 18% -> 17%
where the time goes in v9:
time: 291 us; the launch traced here: 290 us
  starting transfers between devices  111 us (38%)
  waiting for transfers between devices  85.3 us (29%)
  Pallas kernels  76.5 us (26%)
  local copies, waits for them, and re-layouts  11.3 us (4%)
  other arithmetic  5.45 us (2%)
    ppermute x30, starting transfers between devices, shift(): return lax.ppermute(v, AXES, pairs)  79.1 us
    ppermute x30, waiting for transfers between devices, shift(): return lax.ppermute(v, AXES, pairs)  73.3 us
    pallas_call x1, Pallas kernels, inverse_factor(): pl.pallas_call(inverse_kernel, out_shape=jax.ShapeDtypeStruct((PANEL, PAN...  26.5 us
    pallas_call x1, Pallas kernels, final(): pl.pallas_call(final_kernel, grid_spec=pltpu.PrefetchScalarGridSpec(num_s...  14.3 us
    all_to_all x1, waiting for transfers between devices, body(): lax.all_to_all(gsend, ('z', 'yh'), split_axis=0, concat_axis=0, tiled=True)  12 us
    all_to_all x1, starting transfers between devices, body(): lax.all_to_all(send, ('z', 'yh'), split_axis=0, concat_axis=0, tiled=True)  11.2 us
    pallas_call x1, Pallas kernels, update(): pl.pallas_call(update_kernel, grid_spec=pltpu.PrefetchScalarGridSpec(num_...  10.4 us
    pallas_call x1, Pallas kernels, base(): pl.pallas_call(base_kernel, grid_spec=pltpu.PrefetchScalarGridSpec(num_sc...  9.62 us
  transfers between devices with their start and end apart: 37, of which 23 were waited for; matrix products, arithmetic and copies ran while one was open for 2% of the time, Pallas kernels for 17%

profile of v9, /device:TPU:1, one launch (start us, length us, event | category | flops | bytes accessed | tf_op | source)
XLA Modules:
  0.0 290.1 jit_solution(3994905293086734877)
XLA Ops:
  0.0 2.8 dynamic-slice_bitcast_fusion
  2.8 1.3 collective-permute-start
  4.1 1.7 collective-permute-start.1
  5.8 1.6 collective-permute-start.2
  7.4 1.6 collective-permute-start.3
  9.1 1.9 fusion.mine
  11.0 23.6 %collective-permute-start.4 = (bf16[512,1024]{1,0:T(8,128)(2,1)S(1)}, bf16[512,1024]{1,0:T(8,128)(2,1)}, u32[]{:S(2)}, u32[]{:S(2)}) collective-permute-start(bf16[512,1024]{1,0:T(8,128)(2,1)S(1)} %fusion.mine), channel_id=1, source_target_pairs={{0,8},{1,9},{2,10},{3,11},{4,12},{5,13},{6,14},{7,15},{8,0},{9,1},... | collective-permute-start | bytes 3145736 | tf_op jit(solution)/shard_map/ppermute | solution.py:48
  35.6 1.5 collective-permute-done.4.other
  37.1 10.4 %shard_map.64 = (s16[8,272,1024]{2,1,0:T(8,128)(2,1)}, f32[512,512]{1,0:T(8,128)}, f32[1024,512]{1,0:T(8,128)}) custom-call(s32[11]{0:T(128)S(1)} %stack.55.ids, s32[2,32]{1,0:T(2,128)S(1)} %select_reduce_fusion.1.slots, s32[2,32,32]{2,1,0:T(8,128)S(1)} %copy-done.10, f32[1024,1024]{1,0:T(8,128)} %bitcast.81, bf16[1024,1024]{1,0:T(8,128)(2,1)S(1)} %bitcast.80, ...), custom_call_target="tpu_custom_call" | custom-call | flops 2147483648 | bytes 14680064 | tf_op jit(solution)/shard_map/pallas_call | solution.py:145
  47.5 8.1 %all-to-all-start = ((s16[8,272,1024]{2,1,0:T(8,128)(2,1)}), s16[8,272,1024]{2,1,0:T(8,128)(2,1)}, u32[]{:S(2)}, u32[]{:S(2)}) async-start(s16[8,272,1024]{2,1,0:T(8,128)(2,1)} %get-tuple-element.47), calls=%async_computation | async-start | bytes 8912896 | tf_op jit(solution)/shard_map/all_to_all | solution.py:801
  56.8 1.7 collective-permute-done.5
  58.6 1.1 bitcast_add_fusion
  59.7 6.2 %collective-permute-start.6 = (f32[64,512]{1,0:T(8,128)S(1)}, f32[64,512]{1,0:T(8,128)S(1)}, u32[]{:S(2)}, u32[]{:S(2)}) collective-permute-start(f32[64,512]{1,0:T(8,128)S(1)} %get-tuple-element.88), channel_id=1, source_target_pairs={{0,2},{1,3},{2,4},{3,5},{4,6},{5,7},{6,0},{7,1},{8,10},{9,11},{10,... | collective-permute-start | bytes 393224 | tf_op jit(solution)/shard_map/ppermute | solution.py:48
  66.4 1.4 collective-permute-start.8
  67.8 2.2 collective-permute-done.6
  70.4 3.2 %collective-permute-done.8 = f32[64,512]{1,0:T(8,128)S(1)} collective-permute-done((f32[64,512]{1,0:T(8,128)S(1)}, f32[64,512]{1,0:T(8,128)S(1)}, u32[]{:S(2)}, u32[]{:S(2)}) %collective-permute-start.8) | collective-permute-done | bytes 131104 | tf_op jit(solution)/shard_map/ppermute | solution.py:48
  73.6 1.0 collective-permute-start.9
  74.6 1.8 collective-permute-start.10
  76.9 1.5 shard_map.65
  80.1 1.9 collective-permute-start.13
  82.0 1.9 collective-permute-start.14
  84.0 10.3 %collective-permute-done.12.refs_1_ = s16[2,256,512]{2,1,0:T(8,128)(2,1)S(1)} collective-permute-done((s16[2,256,512]{2,1,0:T(8,128)(2,1)S(1)}, s16[2,256,512]{2,1,0:T(8,128)(2,1)S(1)}, u32[]{:S(2)}, u32[]{:S(2)}) %collective-permute-start.12) | collective-permute-done | bytes 524320 | tf_op jit(solution)/shard_map/ppermute | solution.py:48
  94.3 11.1 %collective-permute-done.13.refs_2_ = s16[2,256,512]{2,1,0:T(8,128)(2,1)S(1)} collective-permute-done((s16[2,256,512]{2,1,0:T(8,128)(2,1)S(1)}, s16[2,256,512]{2,1,0:T(8,128)(2,1)S(1)}, u32[]{:S(2)}, u32[]{:S(2)}) %collective-permute-start.13) | collective-permute-done | bytes 524320 | tf_op jit(solution)/shard_map/ppermute | solution.py:48
  106.3 2.8 shard_map.66
  109.1 1.9 collective-permute-start.15
  111.0 11.1 %collective-permute-start.16 = (f32[64,512]{1,0:T(8,128)S(1)}, f32[64,512]{1,0:T(8,128)S(1)}, u32[]{:S(2)}, u32[]{:S(2)}) collective-permute-start(f32[64,512]{1,0:T(8,128)S(1)} %get-tuple-element.85), channel_id=1, source_target_pairs={{0,16},{1,17},{2,18},{3,19},{4,20},{5,21},{6,22},{7,23},{8,24},{9,... | collective-permute-start | bytes 393224 | tf_op jit(solution)/shard_map/ppermute | solution.py:48
  122.1 3.3 %collective-permute-start.17 = (f32[64,512]{1,0:T(8,128)S(1)}, f32[64,512]{1,0:T(8,128)S(1)}, u32[]{:S(2)}, u32[]{:S(2)}) collective-permute-start(f32[64,512]{1,0:T(8,128)S(1)} %get-tuple-element.87), channel_id=1, source_target_pairs={{0,48},{1,49},{2,50},{3,51},{4,52},{5,53},{6,54},{7,55},{8,56},{9,... | collective-permute-start | bytes 393224 | tf_op jit(solution)/shard_map/ppermute | solution.py:48
  125.4 1.1 collective-permute-start.18
  126.5 1.1 dynamic-slice_bitcast_fusion.3
  127.5 1.8 collective-permute-start.19
  129.4 1.0 collective-permute-start.20
  131.0 1.7 collective-permute-start.21
  133.0 3.5 %collective-permute-done.19.beside = s16[256,512]{1,0:T(8,128)(2,1)S(1)} collective-permute-done((s16[256,512]{1,0:T(8,128)(2,1)S(1)}, s16[256,512]{1,0:T(8,128)(2,1)S(1)}, u32[]{:S(2)}, u32[]{:S(2)}) %collective-permute-start.19) | collective-permute-done | bytes 262176 | tf_op jit(solution)/shard_map/ppermute | solution.py:48
  136.4 5.0 %collective-permute-done.20.across = s16[256,512]{1,0:T(8,128)(2,1)S(1)} collective-permute-done((s16[256,512]{1,0:T(8,128)(2,1)S(1)}, s16[256,512]{1,0:T(8,128)(2,1)S(1)}, u32[]{:S(2)}, u32[]{:S(2)}) %collective-permute-start.20) | collective-permute-done | bytes 262176 | tf_op jit(solution)/shard_map/ppermute | solution.py:48
  141.4 1.6 collective-permute-done.21.both
  143.0 1.7 collective-permute-start.22
  144.7 2.1 collective-permute-start.24
  146.8 1.9 collective-permute-done.22
  149.0 3.5 %collective-permute-done.24 = f32[64,512]{1,0:T(8,128)S(1)} collective-permute-done((f32[64,512]{1,0:T(8,128)S(1)}, f32[64,512]{1,0:T(8,128)S(1)}, u32[]{:S(2)}, u32[]{:S(2)}) %collective-permute-start.24) | collective-permute-done | bytes 131104 | tf_op jit(solution)/shard_map/ppermute | solution.py:48
  152.5 3.3 %shard_map.67 = s16[8,1552,256]{2,1,0:T(8,128)(2,1)} custom-call(s32[11]{0:T(128)S(1)} %copy-done.8, s32[2,32]{1,0:T(2,128)S(1)} %select_reduce_fusion.1.slots, s32[2,48]{1,0:T(2,128)S(1)} %copy-done.5, s16[8,272,1024]{2,1,0:T(8,128)(2,1)} %all-to-all-done.own, s16[8,272,1024]{2,1,0:T(8,128)(2,1)} %collective-permute-done.15.other), custom_call_target="tpu_custom_call" | custom-call | bytes 8388608 | tf_op jit(solution)/shard_map/pallas_call | solution.py:428
  155.8 11.2 %all-to-all-start.1 = ((s16[8,1552,256]{2,1,0:T(8,128)(2,1)}), s16[8,1552,256]{2,1,0:T(8,128)(2,1)}, u32[]{:S(2)}, u32[]{:S(2)}) async-start(s16[8,1552,256]{2,1,0:T(8,128)(2,1)} %shard_map.67), calls=%async_computation.1 | async-start | bytes 12713984 | tf_op jit(solution)/shard_map/all_to_all | solution.py:818
  167.9 1.8 collective-permute-start.26
  170.4 1.6 collective-permute-done.25
  173.0 2.4 collective-permute-done.27
  175.4 2.7 shard_map.69
  178.9 1.6 collective-permute-start.30
  180.5 1.7 collective-permute-start.31
  182.2 2.7 collective-permute-start.28
  185.0 5.1 %collective-permute-done.29 = s16[2,256,512]{2,1,0:T(8,128)(2,1)S(1)} collective-permute-done((s16[2,256,512]{2,1,0:T(8,128)(2,1)}, s16[2,256,512]{2,1,0:T(8,128)(2,1)S(1)}, u32[]{:S(2)}, u32[]{:S(2)}) %collective-permute-start.29) | collective-permute-done | bytes 524320 | tf_op jit(solution)/shard_map/ppermute | solution.py:48
  190.1 10.9 %collective-permute-done.30 = s16[2,256,512]{2,1,0:T(8,128)(2,1)S(1)} collective-permute-done((s16[2,256,512]{2,1,0:T(8,128)(2,1)}, s16[2,256,512]{2,1,0:T(8,128)(2,1)S(1)}, u32[]{:S(2)}, u32[]{:S(2)}) %collective-permute-start.30) | collective-permute-done | bytes 524320 | tf_op jit(solution)/shard_map/ppermute | solution.py:48
  201.0 3.3 %collective-permute-done.31 = s16[2,256,512]{2,1,0:T(8,128)(2,1)S(1)} collective-permute-done((s16[2,256,512]{2,1,0:T(8,128)(2,1)}, s16[2,256,512]{2,1,0:T(8,128)(2,1)S(1)}, u32[]{:S(2)}, u32[]{:S(2)}) %collective-permute-start.31) | collective-permute-done | bytes 524320 | tf_op jit(solution)/shard_map/ppermute | solution.py:48
  204.4 1.2 pad_add_fusion.own
  205.6 1.5 collective-permute-start.32
  207.4 26.5 %shard_map.68.inv = f32[512,512]{1,0:T(8,128)S(1)} custom-call(f32[512,512]{1,0:T(8,128)S(1)} %pad_maximum_fusion.a_ref.diag), custom_call_target="tpu_custom_call" | custom-call | flops 17179869184 | bytes 2097152 | tf_op jit(solution)/shard_map/pallas_call | solution.py:532
  233.9 1.0 copy-done.11
  234.8 5.6 %shard_map.70 = s16[8,208,512]{2,1,0:T(8,128)(2,1)S(1)} custom-call(s32[11]{0:T(128)S(1)} %copy-done.9, s32[2,48]{1,0:T(2,128)S(1)} %copy-done.6, s16[4,2,256,512]{3,2,1,0:T(8,128)(2,1)S(1)} %pad_add_fusion.own, s16[4,2,256,512]{3,2,1,0:T(8,128)(2,1)} %collective-permute-done.32.other), custom_call_target="tpu_custom_call" | custom-call | bytes 6291456 | tf_op jit(solution)/shard_map/pallas_call | solution.py:354
  240.4 1.2 copy-done.1
  241.6 6.5 %all-to-all-start.2 = ((s16[8,208,512]{2,1,0:T(8,128)(2,1)}), s16[8,208,512]{2,1,0:T(8,128)(2,1)S(1)}, u32[]{:S(2)}, u32[]{:S(2)}) async-start(s16[8,208,512]{2,1,0:T(8,128)(2,1)} %copy-done.1), calls=%async_computation.2 | async-start | bytes 3407872 | tf_op jit(solution)/shard_map/all_to_all | solution.py:828
  248.1 9.6 %shard_map.71.front = f32[768,1536]{1,0:T(8,128)S(1)} custom-call(s32[11]{0:T(128)S(1)} %copy-done.9, s32[2,48]{1,0:T(2,128)S(1)} %copy-done.6, s16[8,1552,256]{2,1,0:T(8,128)(2,1)} %all-to-all-done.1.recv, f32[768,1536]{1,0:T(8,128)} %front.5), custom_call_target="tpu_custom_call" | custom-call | bytes 20971520 | tf_op jit(solution)/shard_map/pallas_call | solution.py:608
  257.8 2.2 copy-done.2
  259.9 12.0 %all-to-all-done.2.gx = s16[8,208,512]{2,1,0:T(8,128)(2,1)S(1)} async-done(((s16[8,208,512]{2,1,0:T(8,128)(2,1)}), s16[8,208,512]{2,1,0:T(8,128)(2,1)S(1)}, u32[]{:S(2)}, u32[]{:S(2)}) %all-to-all-start.2) | async-done | bytes 1703968 | tf_op jit(solution)/shard_map/all_to_all | solution.py:828
  272.0 1.7 collective-permute-start.33
  273.7 2.1 collective-permute-done.33.goth
  275.8 14.3 %shard_map.72 = f32[768,1536]{1,0:T(8,128)} custom-call(s32[11]{0:T(128)S(1)} %copy-done.9, f32[512,512]{1,0:T(8,128)S(1)} %pad_maximum_fusion.a_ref.diag, f32[512,512]{1,0:T(8,128)} %copy-done.11, s16[8,208,512]{2,1,0:T(8,128)(2,1)} %copy-done.12, s16[8,112,512]{2,1,0:T(8,128)(2,1)S(1)} %collective-permute-done.33.goth, f32[768,1536]{1,0:T(8,128)} %copy-done.2), custom_call_target="tpu_custom_call" | custom-call | flops 8589934592 | bytes 20971520 | tf_op jit(solution)/shard_map/pallas_call | solution.py:691
  (92 shorter events, 11.4 us)
Async XLA Ops:
  0.0 9.1 %copy-start = (bf16[1,1024,1024]{2,1,0:T(8,128)(2,1)S(1)}, bf16[1,1024,1024]{2,1,0:T(8,128)(2,1)}, u32[]{:S(2)}) copy-start(bf16[1,1024,1024]{2,1,0:T(8,128)(2,1)} %param.7) | copy-start | bytes 6291460
  2.8 6.2 %collective-permute-start = (bf16[512,1024]{1,0:T(8,128)(2,1)}, bf16[512,1024]{1,0:T(8,128)(2,1)}, u32[]{:S(2)}, u32[]{:S(2)}) collective-permute-start(bf16[512,1024]{1,0:T(8,128)(2,1)} %get-tuple-element.80), channel_id=1, source_target_pairs={{0,8},{9,1},{18,26},{27,19},{36,44},{45,37},{54,62},{63,55},{64,72... | collective-permute-start | bytes 3145736 | tf_op jit(solution)/shard_map/ppermute | solution.py:740
  4.1 5.0 %collective-permute-start.1 = (bf16[512,1024]{1,0:T(8,128)(2,1)S(1)}, bf16[512,1024]{1,0:T(8,128)(2,1)}, u32[]{:S(2)}, u32[]{:S(2)}) collective-permute-start(bf16[512,1024]{1,0:T(8,128)(2,1)S(1)} %get-tuple-element.79), channel_id=1, source_target_pairs={{0,16},{4,24},{9,17},{13,25},{18,34},{22,42},{27,35},{31,43},{36,5... | collective-permute-start | bytes 3145736 | tf_op jit(solution)/shard_map/ppermute | solution.py:733
  5.8 3.3 %collective-permute-start.2 = (bf16[512,1024]{1,0:T(8,128)(2,1)S(1)}, bf16[512,1024]{1,0:T(8,128)(2,1)}, u32[]{:S(2)}, u32[]{:S(2)}) collective-permute-start(bf16[512,1024]{1,0:T(8,128)(2,1)S(1)} %get-tuple-element.79), channel_id=1, source_target_pairs={{0,32},{4,40},{9,33},{13,41},{18,50},{22,58},{27,51},{31,59},{36,4... | collective-permute-start | bytes 3145736 | tf_op jit(solution)/shard_map/ppermute | solution.py:733
  7.4 1.7 collective-permute-start.3
  9.1 25.6 %copy-start.21 = (s32[48]{0:T(128)S(1)}, s32[48]{0:T(128)}, u32[]{:S(2)}) copy-start(s32[48]{0:T(128)} %param.10) | copy-start | bytes 580
  9.1 25.7 %copy-start.22 = (s32[2,32]{1,0:T(2,128)S(1)}, s32[2,32]{1,0:T(2,128)}, u32[]{:S(2)}) copy-start(s32[2,32]{1,0:T(2,128)} %param.9) | copy-start | bytes 772
  9.1 28.0 %copy-start.10 = (s32[2,32,32]{2,1,0:T(8,128)S(1)}, s32[2,32,32]{2,1,0:T(8,128)}, u32[]{:S(2)}) copy-start(s32[2,32,32]{2,1,0:T(8,128)} %pat.1) | copy-start | bytes 24580
  11.0 26.0 %collective-permute-start.4 = (bf16[512,1024]{1,0:T(8,128)(2,1)S(1)}, bf16[512,1024]{1,0:T(8,128)(2,1)}, u32[]{:S(2)}, u32[]{:S(2)}) collective-permute-start(bf16[512,1024]{1,0:T(8,128)(2,1)S(1)} %fusion.mine), channel_id=1, source_target_pairs={{0,8},{1,9},{2,10},{3,11},{4,12},{5,13},{6,14},{7,15},{8,0},{9,1},... | collective-permute-start | bytes 3145736 | tf_op jit(solution)/shard_map/ppermute | solution.py:48
  34.7 42.2 %copy-start.7 = (s32[11]{0:T(128)}, s32[11]{0:T(128)S(1)}, u32[]{:S(2)}) copy-start(s32[11]{0:T(128)S(1)} %stack.55.ids) | copy-start | bytes 136
  47.4 8.1 %copy-start.14 = (f32[512,512]{1,0:T(8,128)S(1)}, f32[512,512]{1,0:T(8,128)}, u32[]{:S(2)}) copy-start(f32[512,512]{1,0:T(8,128)} %get-tuple-element.48) | copy-start | bytes 3145732
  47.5 61.7 %all-to-all-start = ((s16[8,272,1024]{2,1,0:T(8,128)(2,1)}), s16[8,272,1024]{2,1,0:T(8,128)(2,1)}, u32[]{:S(2)}, u32[]{:S(2)}) async-start(s16[8,272,1024]{2,1,0:T(8,128)(2,1)} %get-tuple-element.47), calls=%async_computation | async-start | bytes 8912896 | tf_op jit(solution)/shard_map/all_to_all | solution.py:801
  55.5 21.4 %copy-start.3 = (f32[1024,512]{1,0:T(8,128)S(1)}, f32[1024,512]{1,0:T(8,128)}, u32[]{:S(2)}) copy-start(f32[1024,512]{1,0:T(8,128)} %get-tuple-element.51.gcol) | copy-start | bytes 6291460
  56.4 2.2 collective-permute-start.5
  59.7 10.3 %collective-permute-start.6 = (f32[64,512]{1,0:T(8,128)S(1)}, f32[64,512]{1,0:T(8,128)S(1)}, u32[]{:S(2)}, u32[]{:S(2)}) collective-permute-start(f32[64,512]{1,0:T(8,128)S(1)} %get-tuple-element.88), channel_id=1, source_target_pairs={{0,2},{1,3},{2,4},{3,5},{4,6},{5,7},{6,0},{7,1},{8,10},{9,11},{10,... | collective-permute-start | bytes 393224 | tf_op jit(solution)/shard_map/ppermute | solution.py:48
  65.9 4.5 %collective-permute-start.7 = (f32[64,512]{1,0:T(8,128)S(1)}, f32[64,512]{1,0:T(8,128)S(1)}, u32[]{:S(2)}, u32[]{:S(2)}) collective-permute-start(f32[64,512]{1,0:T(8,128)S(1)} %get-tuple-element.90), channel_id=1, source_target_pairs={{0,6},{1,7},{2,0},{3,1},{4,2},{5,3},{6,4},{7,5},{8,14},{9,15},{10,... | collective-permute-start | bytes 393224 | tf_op jit(solution)/shard_map/ppermute | solution.py:48
  66.4 7.2 %collective-permute-start.8 = (f32[64,512]{1,0:T(8,128)S(1)}, f32[64,512]{1,0:T(8,128)S(1)}, u32[]{:S(2)}, u32[]{:S(2)}) collective-permute-start(f32[64,512]{1,0:T(8,128)S(1)} %get-tuple-element.89), channel_id=1, source_target_pairs={{0,4},{1,5},{2,6},{3,7},{4,0},{5,1},{6,2},{7,3},{8,12},{9,13},{10,... | collective-permute-start | bytes 393224 | tf_op jit(solution)/shard_map/ppermute | solution.py:48
  73.6 8.4 %collective-permute-start.9 = (f32[64,512]{1,0:T(8,128)S(1)}, f32[64,512]{1,0:T(8,128)S(1)}, u32[]{:S(2)}, u32[]{:S(2)}) collective-permute-start(f32[64,512]{1,0:T(8,128)S(1)} %fusion.4), channel_id=1, source_target_pairs={{0,2},{1,3},{2,4},{3,5},{4,6},{5,7},{6,0},{7,1},{8,10},{9,11},{10,... | collective-permute-start | bytes 393224 | tf_op jit(solution)/shard_map/ppermute | solution.py:48
  74.6 9.3 %collective-permute-start.10 = (f32[64,512]{1,0:T(8,128)S(1)}, f32[64,512]{1,0:T(8,128)S(1)}, u32[]{:S(2)}, u32[]{:S(2)}) collective-permute-start(f32[64,512]{1,0:T(8,128)S(1)} %fusion.4), channel_id=1, source_target_pairs={{0,6},{1,7},{2,0},{3,1},{4,2},{5,3},{6,4},{7,5},{8,14},{9,15},{10,... | collective-permute-start | bytes 393224 | tf_op jit(solution)/shard_map/ppermute | solution.py:48
  76.4 7.6 %collective-permute-start.11 = (f32[64,512]{1,0:T(8,128)S(1)}, f32[64,512]{1,0:T(8,128)S(1)}, u32[]{:S(2)}, u32[]{:S(2)}) collective-permute-start(f32[64,512]{1,0:T(8,128)S(1)} %fusion.4), channel_id=1, source_target_pairs={{0,4},{1,5},{2,6},{3,7},{4,0},{5,1},{6,2},{7,3},{8,12},{9,13},{10,... | collective-permute-start | bytes 393224 | tf_op jit(solution)/shard_map/ppermute | solution.py:48
  78.4 0.8 copy-start.4
  79.2 15.0 %collective-permute-start.12 = (s16[2,256,512]{2,1,0:T(8,128)(2,1)S(1)}, s16[2,256,512]{2,1,0:T(8,128)(2,1)S(1)}, u32[]{:S(2)}, u32[]{:S(2)}) collective-permute-start(s16[2,256,512]{2,1,0:T(8,128)(2,1)S(1)} %get-tuple-element.53), channel_id=1, source_target_pairs={{0,2},{1,3},{2,4},{3,5},{4,6},{5,7},{6,0},{7,1},{8,10},{9,11},{10,... | collective-permute-start | bytes 1572872 | tf_op jit(solution)/shard_map/ppermute | solution.py:48
  80.1 25.3 %collective-permute-start.13 = (s16[2,256,512]{2,1,0:T(8,128)(2,1)S(1)}, s16[2,256,512]{2,1,0:T(8,128)(2,1)S(1)}, u32[]{:S(2)}, u32[]{:S(2)}) collective-permute-start(s16[2,256,512]{2,1,0:T(8,128)(2,1)S(1)} %get-tuple-element.54), channel_id=1, source_target_pairs={{0,4},{1,5},{2,6},{3,7},{4,0},{5,1},{6,2},{7,3},{8,12},{9,13},{10,... | collective-permute-start | bytes 1572872 | tf_op jit(solution)/shard_map/ppermute | solution.py:48
  82.0 23.3 %collective-permute-start.14 = (s16[2,256,512]{2,1,0:T(8,128)(2,1)S(1)}, s16[2,256,512]{2,1,0:T(8,128)(2,1)S(1)}, u32[]{:S(2)}, u32[]{:S(2)}) collective-permute-start(s16[2,256,512]{2,1,0:T(8,128)(2,1)S(1)} %get-tuple-element.55), channel_id=1, source_target_pairs={{0,6},{1,7},{2,0},{3,1},{4,2},{5,3},{6,4},{7,5},{8,14},{9,15},{10,... | collective-permute-start | bytes 1572872 | tf_op jit(solution)/shard_map/ppermute | solution.py:48
  94.3 11.1 %copy-start.15 = (s16[2,256,512]{2,1,0:T(8,128)(2,1)}, s16[2,256,512]{2,1,0:T(8,128)(2,1)S(1)}, u32[]{:S(2)}) copy-start(s16[2,256,512]{2,1,0:T(8,128)(2,1)S(1)} %collective-permute-done.12.refs_1_) | copy-start | bytes 1572868
  105.3 0.8 copy-start.16
  105.3 1.0 copy-start.17
  109.1 43.4 %copy-start.5 = (s32[2,48]{1,0:T(2,128)S(1)}, s32[2,48]{1,0:T(2,128)}, u32[]{:S(2)}) copy-start(s32[2,48]{1,0:T(2,128)} %select_reduce_fusion.where) | copy-start | bytes 1156
  109.1 43.4 %copy-start.8 = (s32[11]{0:T(128)S(1)}, s32[11]{0:T(128)}, u32[]{:S(2)}) copy-start(s32[11]{0:T(128)} %copy-done.7) | copy-start | bytes 136
  109.1 43.3 %collective-permute-start.15 = (s16[8,272,1024]{2,1,0:T(8,128)(2,1)}, s16[8,272,1024]{2,1,0:T(8,128)(2,1)}, u32[]{:S(2)}, u32[]{:S(2)}) collective-permute-start(s16[8,272,1024]{2,1,0:T(8,128)(2,1)} %all-to-all-done.own), channel_id=1, source_target_pairs={{0,8},{1,9},{2,10},{3,11},{4,12},{5,13},{6,14},{7,15},{8,0},{9,1},... | collective-permute-start | bytes 13369352 | tf_op jit(solution)/shard_map/ppermute | solution.py:48
  111.0 18.4 %collective-permute-start.16 = (f32[64,512]{1,0:T(8,128)S(1)}, f32[64,512]{1,0:T(8,128)S(1)}, u32[]{:S(2)}, u32[]{:S(2)}) collective-permute-start(f32[64,512]{1,0:T(8,128)S(1)} %get-tuple-element.85), channel_id=1, source_target_pairs={{0,16},{1,17},{2,18},{3,19},{4,20},{5,21},{6,22},{7,23},{8,24},{9,... | collective-permute-start | bytes 393224 | tf_op jit(solution)/shard_map/ppermute | solution.py:48
  122.1 8.9 %collective-permute-start.17 = (f32[64,512]{1,0:T(8,128)S(1)}, f32[64,512]{1,0:T(8,128)S(1)}, u32[]{:S(2)}, u32[]{:S(2)}) collective-permute-start(f32[64,512]{1,0:T(8,128)S(1)} %get-tuple-element.87), channel_id=1, source_target_pairs={{0,48},{1,49},{2,50},{3,51},{4,52},{5,53},{6,54},{7,55},{8,56},{9,... | collective-permute-start | bytes 393224 | tf_op jit(solution)/shard_map/ppermute | solution.py:48
  125.4 7.6 %collective-permute-start.18 = (f32[64,512]{1,0:T(8,128)S(1)}, f32[64,512]{1,0:T(8,128)S(1)}, u32[]{:S(2)}, u32[]{:S(2)}) collective-permute-start(f32[64,512]{1,0:T(8,128)S(1)} %get-tuple-element.86), channel_id=1, source_target_pairs={{0,32},{1,33},{2,34},{3,35},{4,36},{5,37},{6,38},{7,39},{8,40},{9,... | collective-permute-start | bytes 393224 | tf_op jit(solution)/shard_map/ppermute | solution.py:48
  127.5 28.2 %copy-start.13 = (s16[256,512]{1,0:T(8,128)(2,1)}, s16[256,512]{1,0:T(8,128)(2,1)S(1)}, u32[]{:S(2)}) copy-start(s16[256,512]{1,0:T(8,128)(2,1)S(1)} %get-tuple-element.70.kept) | copy-start | bytes 786436
  127.5 8.9 %collective-permute-start.19 = (s16[256,512]{1,0:T(8,128)(2,1)S(1)}, s16[256,512]{1,0:T(8,128)(2,1)S(1)}, u32[]{:S(2)}, u32[]{:S(2)}) collective-permute-start(s16[256,512]{1,0:T(8,128)(2,1)S(1)} %get-tuple-element.84), channel_id=1, source_target_pairs={{0,1},{1,0},{2,3},{3,2},{4,5},{5,4},{6,7},{7,6},{8,9},{9,8},{10,11... | collective-permute-start | bytes 786440 | tf_op jit(solution)/shard_map/ppermute | solution.py:48
  129.4 12.0 %collective-permute-start.20 = (s16[256,512]{1,0:T(8,128)(2,1)S(1)}, s16[256,512]{1,0:T(8,128)(2,1)S(1)}, u32[]{:S(2)}, u32[]{:S(2)}) collective-permute-start(s16[256,512]{1,0:T(8,128)(2,1)S(1)} %get-tuple-element.70.kept), channel_id=1, source_target_pairs={{0,64},{1,65},{2,66},{3,67},{4,68},{5,69},{6,70},{7,71},{8,72},{9,... | collective-permute-start | bytes 786440 | tf_op jit(solution)/shard_map/ppermute | solution.py:48
  131.0 12.0 %collective-permute-start.21 = (s16[256,512]{1,0:T(8,128)(2,1)S(1)}, s16[256,512]{1,0:T(8,128)(2,1)S(1)}, u32[]{:S(2)}, u32[]{:S(2)}) collective-permute-start(s16[256,512]{1,0:T(8,128)(2,1)S(1)} %get-tuple-element.84), channel_id=1, source_target_pairs={{0,65},{1,64},{2,67},{3,66},{4,69},{5,68},{6,71},{7,70},{8,73},{9,... | collective-permute-start | bytes 786440 | tf_op jit(solution)/shard_map/ppermute | solution.py:48
  136.4 19.3 %copy-start.18 = (s16[256,512]{1,0:T(8,128)(2,1)}, s16[256,512]{1,0:T(8,128)(2,1)S(1)}, u32[]{:S(2)}) copy-start(s16[256,512]{1,0:T(8,128)(2,1)S(1)} %collective-permute-done.19.beside) | copy-start | bytes 786436
  141.4 14.4 %copy-start.19 = (s16[256,512]{1,0:T(8,128)(2,1)}, s16[256,512]{1,0:T(8,128)(2,1)S(1)}, u32[]{:S(2)}) copy-start(s16[256,512]{1,0:T(8,128)(2,1)S(1)} %collective-permute-done.20.across) | copy-start | bytes 786436
  143.0 12.8 %copy-start.20 = (s16[256,512]{1,0:T(8,128)(2,1)}, s16[256,512]{1,0:T(8,128)(2,1)S(1)}, u32[]{:S(2)}) copy-start(s16[256,512]{1,0:T(8,128)(2,1)S(1)} %collective-permute-done.21.both) | copy-start | bytes 786436
  143.0 5.8 %collective-permute-start.22 = (f32[64,512]{1,0:T(8,128)S(1)}, f32[64,512]{1,0:T(8,128)S(1)}, u32[]{:S(2)}, u32[]{:S(2)}) collective-permute-start(f32[64,512]{1,0:T(8,128)S(1)} %fusion.2), channel_id=1, source_target_pairs={{0,65},{1,64},{2,67},{3,66},{4,69},{5,68},{6,71},{7,70},{8,73},{9,... | collective-permute-start | bytes 393224 | tf_op jit(solution)/shard_map/ppermute | solution.py:48
  144.7 4.2 %collective-permute-start.23 = (f32[64,512]{1,0:T(8,128)S(1)}, f32[64,512]{1,0:T(8,128)S(1)}, u32[]{:S(2)}, u32[]{:S(2)}) collective-permute-start(f32[64,512]{1,0:T(8,128)S(1)} %fusion.2), channel_id=1, source_target_pairs={{0,64},{1,65},{2,66},{3,67},{4,68},{5,69},{6,70},{7,71},{8,72},{9,... | collective-permute-start | bytes 393224 | tf_op jit(solution)/shard_map/ppermute | solution.py:48
  144.7 7.7 %collective-permute-start.24 = (f32[64,512]{1,0:T(8,128)S(1)}, f32[64,512]{1,0:T(8,128)S(1)}, u32[]{:S(2)}, u32[]{:S(2)}) collective-permute-start(f32[64,512]{1,0:T(8,128)S(1)} %fusion.2), channel_id=1, source_target_pairs={{0,1},{1,0},{2,3},{3,2},{4,5},{5,4},{6,7},{7,6},{8,9},{9,8},{10,11... | collective-permute-start | bytes 393224 | tf_op jit(solution)/shard_map/ppermute | solution.py:48
  155.8 85.8 %all-to-all-start.1 = ((s16[8,1552,256]{2,1,0:T(8,128)(2,1)}), s16[8,1552,256]{2,1,0:T(8,128)(2,1)}, u32[]{:S(2)}, u32[]{:S(2)}) async-start(s16[8,1552,256]{2,1,0:T(8,128)(2,1)} %shard_map.67), calls=%async_computation.1 | async-start | bytes 12713984 | tf_op jit(solution)/shard_map/all_to_all | solution.py:818
  167.0 5.0 %collective-permute-start.25 = (f32[64,512]{1,0:T(8,128)S(1)}, f32[64,512]{1,0:T(8,128)S(1)}, u32[]{:S(2)}, u32[]{:S(2)}) collective-permute-start(f32[64,512]{1,0:T(8,128)S(1)} %add_add_fusion), channel_id=1, source_target_pairs={{0,16},{1,17},{2,18},{3,19},{4,20},{5,21},{6,22},{7,23},{8,24},{9,... | collective-permute-start | bytes 393224 | tf_op jit(solution)/shard_map/ppermute | solution.py:48
  167.9 5.1 %collective-permute-start.26 = (f32[64,512]{1,0:T(8,128)S(1)}, f32[64,512]{1,0:T(8,128)S(1)}, u32[]{:S(2)}, u32[]{:S(2)}) collective-permute-start(f32[64,512]{1,0:T(8,128)S(1)} %add_add_fusion), channel_id=1, source_target_pairs={{0,48},{1,49},{2,50},{3,51},{4,52},{5,53},{6,54},{7,55},{8,56},{9,... | collective-permute-start | bytes 393224 | tf_op jit(solution)/shard_map/ppermute | solution.py:48
  169.7 5.8 %collective-permute-start.27 = (f32[64,512]{1,0:T(8,128)S(1)}, f32[64,512]{1,0:T(8,128)S(1)}, u32[]{:S(2)}, u32[]{:S(2)}) collective-permute-start(f32[64,512]{1,0:T(8,128)S(1)} %add_add_fusion), channel_id=1, source_target_pairs={{0,32},{1,33},{2,34},{3,35},{4,36},{5,37},{6,38},{7,39},{8,40},{9,... | collective-permute-start | bytes 393224 | tf_op jit(solution)/shard_map/ppermute | solution.py:48
  178.1 12.0 %collective-permute-start.29 = (s16[2,256,512]{2,1,0:T(8,128)(2,1)}, s16[2,256,512]{2,1,0:T(8,128)(2,1)S(1)}, u32[]{:S(2)}, u32[]{:S(2)}) collective-permute-start(s16[2,256,512]{2,1,0:T(8,128)(2,1)} %shard_map.69), channel_id=1, source_target_pairs={{0,16},{1,17},{2,18},{3,19},{4,20},{5,21},{6,22},{7,23},{8,24},{9,... | collective-permute-start | bytes 1572872 | tf_op jit(solution)/shard_map/ppermute | solution.py:48
  178.9 22.1 %collective-permute-start.30 = (s16[2,256,512]{2,1,0:T(8,128)(2,1)}, s16[2,256,512]{2,1,0:T(8,128)(2,1)S(1)}, u32[]{:S(2)}, u32[]{:S(2)}) collective-permute-start(s16[2,256,512]{2,1,0:T(8,128)(2,1)} %shard_map.69), channel_id=1, source_target_pairs={{0,32},{1,33},{2,34},{3,35},{4,36},{5,37},{6,38},{7,39},{8,40},{9,... | collective-permute-start | bytes 1572872 | tf_op jit(solution)/shard_map/ppermute | solution.py:48
  180.5 23.8 %collective-permute-start.31 = (s16[2,256,512]{2,1,0:T(8,128)(2,1)}, s16[2,256,512]{2,1,0:T(8,128)(2,1)S(1)}, u32[]{:S(2)}, u32[]{:S(2)}) collective-permute-start(s16[2,256,512]{2,1,0:T(8,128)(2,1)} %shard_map.69), channel_id=1, source_target_pairs={{0,48},{1,49},{2,50},{3,51},{4,52},{5,53},{6,54},{7,55},{8,56},{9,... | collective-permute-start | bytes 1572872 | tf_op jit(solution)/shard_map/ppermute | solution.py:48
  182.2 24.9 %collective-permute-start.28 = (f32[256,512]{1,0:T(8,128)S(1)}, f32[256,512]{1,0:T(8,128)S(1)}, u32[]{:S(2)}, u32[]{:S(2)}) collective-permute-start(f32[256,512]{1,0:T(8,128)S(1)} %bitcast.82), channel_id=1, source_target_pairs={{0,8},{1,9},{2,10},{3,11},{4,12},{5,13},{6,14},{7,15},{8,0},{9,1},... | collective-permute-start | bytes 1572872 | tf_op jit(solution)/shard_map/ppermute | solution.py:48
  205.6 29.2 %collective-permute-start.32 = (s16[4,2,256,512]{3,2,1,0:T(8,128)(2,1)S(1)}, s16[4,2,256,512]{3,2,1,0:T(8,128)(2,1)}, u32[]{:S(2)}, u32[]{:S(2)}) collective-permute-start(s16[4,2,256,512]{3,2,1,0:T(8,128)(2,1)S(1)} %pad_add_fusion.own), channel_id=1, source_target_pairs={{0,8},{1,9},{2,10},{3,11},{4,12},{5,13},{6,14},{7,15},{8,0},{9,1},... | collective-permute-start | bytes 6291464 | tf_op jit(solution)/shard_map/ppermute | solution.py:48
  207.3 27.5 %copy-start.6 = (s32[2,48]{1,0:T(2,128)S(1)}, s32[2,48]{1,0:T(2,128)}, u32[]{:S(2)}) copy-start(s32[2,48]{1,0:T(2,128)} %select_reduce_fusion.where) | copy-start | bytes 1156
  207.4 27.5 %copy-start.9 = (s32[11]{0:T(128)S(1)}, s32[11]{0:T(128)}, u32[]{:S(2)}) copy-start(s32[11]{0:T(128)} %copy-done.7) | copy-start | bytes 136
  233.8 1.0 copy-start.11
  240.4 1.2 copy-start.1
  241.6 30.3 %all-to-all-start.2 = ((s16[8,208,512]{2,1,0:T(8,128)(2,1)}), s16[8,208,512]{2,1,0:T(8,128)(2,1)S(1)}, u32[]{:S(2)}, u32[]{:S(2)}) async-start(s16[8,208,512]{2,1,0:T(8,128)(2,1)} %copy-done.1), calls=%async_computation.2 | async-start | bytes 3407872 | tf_op jit(solution)/shard_map/all_to_all | solution.py:828
  257.7 2.2 copy-start.2
  271.9 3.9 %copy-start.12 = (s16[8,208,512]{2,1,0:T(8,128)(2,1)}, s16[8,208,512]{2,1,0:T(8,128)(2,1)S(1)}, u32[]{:S(2)}) copy-start(s16[8,208,512]{2,1,0:T(8,128)(2,1)S(1)} %all-to-all-done.2.gx) | copy-start | bytes 5111812
  272.0 3.8 %collective-permute-start.33 = (s16[8,112,512]{2,1,0:T(8,128)(2,1)S(1)}, s16[8,112,512]{2,1,0:T(8,128)(2,1)S(1)}, u32[]{:S(2)}, u32[]{:S(2)}) collective-permute-start(s16[8,112,512]{2,1,0:T(8,128)(2,1)S(1)} %slice.9), channel_id=1, source_target_pairs={{0,8},{1,9},{2,10},{3,11},{4,12},{5,13},{6,14},{7,15},{8,0},{9,1},... | collective-permute-start | bytes 2752520 | tf_op jit(solution)/shard_map/ppermute | solution.py:48

commit v10 on v9

--- a/solution.py
+++ b/solution.py
@@ -821,8 +821,10 @@
     diag, kept, *moves = lax.optimization_barrier((diag, kept, *moves))
     strip = choose_y(ids, where, [kept] + moves)
     diag = join_cores(diag, core)
-    line = jnp.stack([strip] + [shift(strip, dx=d) for d in range(1, 4)])
     inv = inverse_factor(diag)
+    line = [strip] + [shift(strip, dx=d) for d in range(1, 4)]
+    inv, *line = lax.optimization_barrier((inv, *line))
+    line = jnp.stack(line)
     gsend = compose(ids, where, line, shift(line, dk=1))
     recv, inv, gsend = lax.optimization_barrier((recv, inv, gsend))
     gx = lax.all_to_all(gsend, ("z", "yh"), split_axis=0, concat_axis=0, tiled=True)

time: 291 us -> 290 us (level)
    all_to_all x1, waiting for transfers between devices: 0.01 us -> 23.3 us  [body(): lax.all_to_all(send, ('z', 'yh'), split_axis=0, concat_axis=0, tiled=True)]
    ppermute x30, waiting for transfers between devices: 73.3 us -> 52.7 us  [shift(): return lax.ppermute(v, AXES, pairs)]
  transfers between devices with their start and end apart: 37 -> 37, of which waited for: 23 -> 19; matrix products, arithmetic and copies ran while one was open for 2% -> 2% of each run, Pallas kernels for 17% -> 17%
where the time goes in v10:
time: 290 us; the launch traced here: 289 us
  starting transfers between devices  111 us (38%)
  waiting for transfers between devices  85.8 us (30%)
  Pallas kernels  77 us (27%)
  local copies, waits for them, and re-layouts  10.2 us (4%)
  other arithmetic  4.33 us (1%)
    ppermute x30, starting transfers between devices, shift(): return lax.ppermute(v, AXES, pairs)  80.5 us
    ppermute x30, waiting for transfers between devices, shift(): return lax.ppermute(v, AXES, pairs)  52.7 us
    pallas_call x1, Pallas kernels, inverse_factor(): pl.pallas_call(inverse_kernel, out_shape=jax.ShapeDtypeStruct((PANEL, PAN...  26.5 us
    all_to_all x1, waiting for transfers between devices, body(): lax.all_to_all(send, ('z', 'yh'), split_axis=0, concat_axis=0, tiled=True)  23.3 us
    pallas_call x1, Pallas kernels, final(): pl.pallas_call(final_kernel, grid_spec=pltpu.PrefetchScalarGridSpec(num_s...  14.3 us
    all_to_all x1, starting transfers between devices, body(): lax.all_to_all(send, ('z', 'yh'), split_axis=0, concat_axis=0, tiled=True)  11 us
    pallas_call x1, Pallas kernels, update(): pl.pallas_call(update_kernel, grid_spec=pltpu.PrefetchScalarGridSpec(num_...  10.4 us
    pallas_call x1, Pallas kernels, base(): pl.pallas_call(base_kernel, grid_spec=pltpu.PrefetchScalarGridSpec(num_sc...  9.98 us
  transfers between devices with their start and end apart: 37, of which 19 were waited for; matrix products, arithmetic and copies ran while one was open for 2% of the time, Pallas kernels for 17%

profile of v10, /device:TPU:1, one launch (start us, length us, event | category | flops | bytes accessed | tf_op | source)
XLA Modules:
  0.0 288.8 jit_solution(11897498273004501020)
XLA Ops:
  0.0 2.8 dynamic-slice_bitcast_fusion
  2.8 1.3 collective-permute-start
  4.1 1.7 collective-permute-start.1
  5.8 1.6 collective-permute-start.2
  7.4 1.6 collective-permute-start.3
  9.1 1.9 fusion.mine
  11.0 23.6 %collective-permute-start.4 = (bf16[512,1024]{1,0:T(8,128)(2,1)S(1)}, bf16[512,1024]{1,0:T(8,128)(2,1)}, u32[]{:S(2)}, u32[]{:S(2)}) collective-permute-start(bf16[512,1024]{1,0:T(8,128)(2,1)S(1)} %fusion.mine), channel_id=1, source_target_pairs={{0,8},{1,9},{2,10},{3,11},{4,12},{5,13},{6,14},{7,15},{8,0},{9,1},... | collective-permute-start | bytes 3145736 | tf_op jit(solution)/shard_map/ppermute | solution.py:48
  35.6 1.5 collective-permute-done.4.other
  37.1 10.4 %shard_map.64 = (s16[8,272,1024]{2,1,0:T(8,128)(2,1)}, f32[512,512]{1,0:T(8,128)}, f32[1024,512]{1,0:T(8,128)}) custom-call(s32[11]{0:T(128)S(1)} %stack.55.ids, s32[2,32]{1,0:T(2,128)S(1)} %select_reduce_fusion.1.slots, s32[2,32,32]{2,1,0:T(8,128)S(1)} %copy-done.9, f32[1024,1024]{1,0:T(8,128)} %bitcast.81, bf16[1024,1024]{1,0:T(8,128)(2,1)S(1)} %bitcast.80, ...), custom_call_target="tpu_custom_call" | custom-call | flops 2147483648 | bytes 14680064 | tf_op jit(solution)/shard_map/pallas_call | solution.py:145
  47.5 8.1 %all-to-all-start = ((s16[8,272,1024]{2,1,0:T(8,128)(2,1)}), s16[8,272,1024]{2,1,0:T(8,128)(2,1)}, u32[]{:S(2)}, u32[]{:S(2)}) async-start(s16[8,272,1024]{2,1,0:T(8,128)(2,1)} %get-tuple-element.52), calls=%async_computation | async-start | bytes 8912896 | tf_op jit(solution)/shard_map/all_to_all | solution.py:801
  55.5 0.8 dynamic-slice_bitcast_fusion.2
  56.8 1.7 collective-permute-done.5
  58.6 1.1 bitcast_add_fusion
  59.7 6.2 %collective-permute-start.6 = (f32[64,512]{1,0:T(8,128)S(1)}, f32[64,512]{1,0:T(8,128)S(1)}, u32[]{:S(2)}, u32[]{:S(2)}) collective-permute-start(f32[64,512]{1,0:T(8,128)S(1)} %get-tuple-element.98), channel_id=1, source_target_pairs={{0,2},{1,3},{2,4},{3,5},{4,6},{5,7},{6,0},{7,1},{8,10},{9,11},{10,... | collective-permute-start | bytes 393224 | tf_op jit(solution)/shard_map/ppermute | solution.py:48
  66.4 1.4 collective-permute-start.8
  67.8 2.2 collective-permute-done.6
  70.4 3.2 %collective-permute-done.8 = f32[64,512]{1,0:T(8,128)S(1)} collective-permute-done((f32[64,512]{1,0:T(8,128)S(1)}, f32[64,512]{1,0:T(8,128)S(1)}, u32[]{:S(2)}, u32[]{:S(2)}) %collective-permute-start.8) | collective-permute-done | bytes 131104 | tf_op jit(solution)/shard_map/ppermute | solution.py:48
  73.6 1.0 collective-permute-start.9
  74.6 1.8 collective-permute-start.10
  76.9 1.5 shard_map.65
  78.4 0.8 copy-done.3
  79.2 0.9 collective-permute-start.12
  80.1 1.9 collective-permute-start.13
  82.0 1.9 collective-permute-start.14
  84.0 10.3 %collective-permute-done.12.refs_1_ = s16[2,256,512]{2,1,0:T(8,128)(2,1)S(1)} collective-permute-done((s16[2,256,512]{2,1,0:T(8,128)(2,1)S(1)}, s16[2,256,512]{2,1,0:T(8,128)(2,1)S(1)}, u32[]{:S(2)}, u32[]{:S(2)}) %collective-permute-start.12) | collective-permute-done | bytes 524320 | tf_op jit(solution)/shard_map/ppermute | solution.py:48
  94.3 11.1 %collective-permute-done.13.refs_2_ = s16[2,256,512]{2,1,0:T(8,128)(2,1)S(1)} collective-permute-done((s16[2,256,512]{2,1,0:T(8,128)(2,1)S(1)}, s16[2,256,512]{2,1,0:T(8,128)(2,1)S(1)}, u32[]{:S(2)}, u32[]{:S(2)}) %collective-permute-start.13) | collective-permute-done | bytes 524320 | tf_op jit(solution)/shard_map/ppermute | solution.py:48
  105.4 0.8 copy-done.16
  106.3 2.8 shard_map.66
  109.1 1.9 collective-permute-start.15
  111.0 11.1 %collective-permute-start.16 = (f32[64,512]{1,0:T(8,128)S(1)}, f32[64,512]{1,0:T(8,128)S(1)}, u32[]{:S(2)}, u32[]{:S(2)}) collective-permute-start(f32[64,512]{1,0:T(8,128)S(1)} %get-tuple-element.95), channel_id=1, source_target_pairs={{0,16},{1,17},{2,18},{3,19},{4,20},{5,21},{6,22},{7,23},{8,24},{9,... | collective-permute-start | bytes 393224 | tf_op jit(solution)/shard_map/ppermute | solution.py:48
  122.1 3.3 %collective-permute-start.17 = (f32[64,512]{1,0:T(8,128)S(1)}, f32[64,512]{1,0:T(8,128)S(1)}, u32[]{:S(2)}, u32[]{:S(2)}) collective-permute-start(f32[64,512]{1,0:T(8,128)S(1)} %get-tuple-element.97), channel_id=1, source_target_pairs={{0,48},{1,49},{2,50},{3,51},{4,52},{5,53},{6,54},{7,55},{8,56},{9,... | collective-permute-start | bytes 393224 | tf_op jit(solution)/shard_map/ppermute | solution.py:48
  125.4 1.1 collective-permute-start.18
  126.5 1.1 dynamic-slice_bitcast_fusion.3
  127.5 1.8 collective-permute-start.19
  129.4 1.0 collective-permute-start.20
  131.0 1.7 collective-permute-start.21
  133.0 3.5 %collective-permute-done.19.beside = s16[256,512]{1,0:T(8,128)(2,1)S(1)} collective-permute-done((s16[256,512]{1,0:T(8,128)(2,1)S(1)}, s16[256,512]{1,0:T(8,128)(2,1)S(1)}, u32[]{:S(2)}, u32[]{:S(2)}) %collective-permute-start.19) | collective-permute-done | bytes 262176 | tf_op jit(solution)/shard_map/ppermute | solution.py:48
  136.4 5.0 %collective-permute-done.20.across = s16[256,512]{1,0:T(8,128)(2,1)S(1)} collective-permute-done((s16[256,512]{1,0:T(8,128)(2,1)S(1)}, s16[256,512]{1,0:T(8,128)(2,1)S(1)}, u32[]{:S(2)}, u32[]{:S(2)}) %collective-permute-start.20) | collective-permute-done | bytes 262176 | tf_op jit(solution)/shard_map/ppermute | solution.py:48
  141.4 1.6 collective-permute-done.21.both
  143.0 1.7 collective-permute-start.22
  144.7 2.1 collective-permute-start.24
  146.8 1.9 collective-permute-done.22
  149.0 3.5 %collective-permute-done.24 = f32[64,512]{1,0:T(8,128)S(1)} collective-permute-done((f32[64,512]{1,0:T(8,128)S(1)}, f32[64,512]{1,0:T(8,128)S(1)}, u32[]{:S(2)}, u32[]{:S(2)}) %collective-permute-start.24) | collective-permute-done | bytes 131104 | tf_op jit(solution)/shard_map/ppermute | solution.py:48
  152.5 3.4 %shard_map.67 = s16[8,1552,256]{2,1,0:T(8,128)(2,1)} custom-call(s32[11]{0:T(128)S(1)} %copy-done.7, s32[2,32]{1,0:T(2,128)S(1)} %select_reduce_fusion.1.slots, s32[2,48]{1,0:T(2,128)S(1)} %copy-done.4, s16[8,272,1024]{2,1,0:T(8,128)(2,1)} %all-to-all-done.own, s16[8,272,1024]{2,1,0:T(8,128)(2,1)} %collective-permute-done.15.other), custom_call_target="tpu_custom_call" | custom-call | bytes 8388608 | tf_op jit(solution)/shard_map/pallas_call | solution.py:428
  156.0 0.9 collective-permute-start.25
  156.9 1.8 collective-permute-start.26
  159.2 11.0 %all-to-all-start.1 = ((s16[8,1552,256]{2,1,0:T(8,128)(2,1)}), s16[8,1552,256]{2,1,0:T(8,128)(2,1)}, u32[]{:S(2)}, u32[]{:S(2)}) async-start(s16[8,1552,256]{2,1,0:T(8,128)(2,1)} %shard_map.67), calls=%async_computation.1 | async-start | bytes 12713984 | tf_op jit(solution)/shard_map/all_to_all | solution.py:818
  170.4 2.8 collective-permute-start.28
  173.2 2.7 shard_map.69
  176.0 2.4 collective-permute-start.30
  178.3 1.8 collective-permute-start.31
  180.4 26.5 %shard_map.68.inv = f32[512,512]{1,0:T(8,128)S(1)} custom-call(f32[512,512]{1,0:T(8,128)S(1)} %pad_maximum_fusion.a_ref.diag), custom_call_target="tpu_custom_call" | custom-call | flops 17179869184 | bytes 2097152 | tf_op jit(solution)/shard_map/pallas_call | solution.py:532
  206.9 1.0 copy-done.10
  208.0 0.9 collective-permute-start.32
  209.0 3.8 %collective-permute-done.32.other = s16[4,2,256,512]{3,2,1,0:T(8,128)(2,1)S(1)} collective-permute-done((s16[4,2,256,512]{3,2,1,0:T(8,128)(2,1)S(1)}, s16[4,2,256,512]{3,2,1,0:T(8,128)(2,1)S(1)}, u32[]{:S(2)}, u32[]{:S(2)}) %collective-permute-start.32) | collective-permute-done | bytes 2097184 | tf_op jit(solution)/shard_map/ppermute | solution.py:48
  212.8 5.6 %shard_map.70 = s16[8,208,512]{2,1,0:T(8,128)(2,1)} custom-call(s32[11]{0:T(128)S(1)} %copy-done.8, s32[2,48]{1,0:T(2,128)S(1)} %copy-done.5, s16[4,2,256,512]{3,2,1,0:T(8,128)(2,1)S(1)} %pad_add_fusion.own, s16[4,2,256,512]{3,2,1,0:T(8,128)(2,1)S(1)} %collective-permute-done.32.other), custom_call_target="tpu_custom_call" | custom-call | bytes 6291456 | tf_op jit(solution)/shard_map/pallas_call | solution.py:354
  218.3 23.3 %all-to-all-done.1.recv = s16[8,1552,256]{2,1,0:T(8,128)(2,1)} async-done(((s16[8,1552,256]{2,1,0:T(8,128)(2,1)}), s16[8,1552,256]{2,1,0:T(8,128)(2,1)}, u32[]{:S(2)}, u32[]{:S(2)}) %all-to-all-start.1) | async-done | bytes 6357024 | tf_op jit(solution)/shard_map/all_to_all | solution.py:818
  241.6 5.2 %all-to-all-start.2 = ((s16[8,208,512]{2,1,0:T(8,128)(2,1)}), s16[8,208,512]{2,1,0:T(8,128)(2,1)S(1)}, u32[]{:S(2)}, u32[]{:S(2)}) async-start(s16[8,208,512]{2,1,0:T(8,128)(2,1)} %shard_map.70), calls=%async_computation.2 | async-start | bytes 3407872 | tf_op jit(solution)/shard_map/all_to_all | solution.py:830
  246.9 10.0 %shard_map.71.front = f32[768,1536]{1,0:T(8,128)S(1)} custom-call(s32[11]{0:T(128)S(1)} %copy-done.8, s32[2,48]{1,0:T(2,128)S(1)} %copy-done.5, s16[8,1552,256]{2,1,0:T(8,128)(2,1)} %all-to-all-done.1.recv, f32[768,1536]{1,0:T(8,128)} %front.5), custom_call_target="tpu_custom_call" | custom-call | bytes 20971520 | tf_op jit(solution)/shard_map/pallas_call | solution.py:608
  256.9 2.2 copy-done.1
  259.0 9.8 %all-to-all-done.2.gx = s16[8,208,512]{2,1,0:T(8,128)(2,1)S(1)} async-done(((s16[8,208,512]{2,1,0:T(8,128)(2,1)}), s16[8,208,512]{2,1,0:T(8,128)(2,1)S(1)}, u32[]{:S(2)}, u32[]{:S(2)}) %all-to-all-start.2) | async-done | bytes 1703968 | tf_op jit(solution)/shard_map/all_to_all | solution.py:830
  268.9 3.5 %collective-permute-start.33 = (s16[8,112,512]{2,1,0:T(8,128)(2,1)S(1)}, s16[8,112,512]{2,1,0:T(8,128)(2,1)S(1)}, u32[]{:S(2)}, u32[]{:S(2)}) collective-permute-start(s16[8,112,512]{2,1,0:T(8,128)(2,1)S(1)} %slice.9), channel_id=1, source_target_pairs={{0,8},{1,9},{2,10},{3,11},{4,12},{5,13},{6,14},{7,15},{8,0},{9,1},... | collective-permute-start | bytes 2752520 | tf_op jit(solution)/shard_map/ppermute | solution.py:48
  272.4 2.1 collective-permute-done.33.goth
  274.5 14.3 %shard_map.72 = f32[768,1536]{1,0:T(8,128)} custom-call(s32[11]{0:T(128)S(1)} %copy-done.8, f32[512,512]{1,0:T(8,128)S(1)} %pad_maximum_fusion.a_ref.diag, f32[512,512]{1,0:T(8,128)} %copy-done.10, s16[8,208,512]{2,1,0:T(8,128)(2,1)} %copy-done.11, s16[8,112,512]{2,1,0:T(8,128)(2,1)S(1)} %collective-permute-done.33.goth, f32[768,1536]{1,0:T(8,128)} %copy-done.1), custom_call_target="tpu_custom_call" | custom-call | flops 8589934592 | bytes 20971520 | tf_op jit(solution)/shard_map/pallas_call | solution.py:691
  (92 shorter events, 5.5 us)
Async XLA Ops:
  0.0 9.1 %copy-start = (bf16[1,1024,1024]{2,1,0:T(8,128)(2,1)S(1)}, bf16[1,1024,1024]{2,1,0:T(8,128)(2,1)}, u32[]{:S(2)}) copy-start(bf16[1,1024,1024]{2,1,0:T(8,128)(2,1)} %param.7) | copy-start | bytes 6291460
  2.8 6.2 %collective-permute-start = (bf16[512,1024]{1,0:T(8,128)(2,1)}, bf16[512,1024]{1,0:T(8,128)(2,1)}, u32[]{:S(2)}, u32[]{:S(2)}) collective-permute-start(bf16[512,1024]{1,0:T(8,128)(2,1)} %get-tuple-element.90), channel_id=1, source_target_pairs={{0,8},{9,1},{18,26},{27,19},{36,44},{45,37},{54,62},{63,55},{64,72... | collective-permute-start | bytes 3145736 | tf_op jit(solution)/shard_map/ppermute | solution.py:740
  4.1 5.0 %collective-permute-start.1 = (bf16[512,1024]{1,0:T(8,128)(2,1)S(1)}, bf16[512,1024]{1,0:T(8,128)(2,1)}, u32[]{:S(2)}, u32[]{:S(2)}) collective-permute-start(bf16[512,1024]{1,0:T(8,128)(2,1)S(1)} %get-tuple-element.89), channel_id=1, source_target_pairs={{0,16},{4,24},{9,17},{13,25},{18,34},{22,42},{27,35},{31,43},{36,5... | collective-permute-start | bytes 3145736 | tf_op jit(solution)/shard_map/ppermute | solution.py:733
  5.8 3.3 %collective-permute-start.2 = (bf16[512,1024]{1,0:T(8,128)(2,1)S(1)}, bf16[512,1024]{1,0:T(8,128)(2,1)}, u32[]{:S(2)}, u32[]{:S(2)}) collective-permute-start(bf16[512,1024]{1,0:T(8,128)(2,1)S(1)} %get-tuple-element.89), channel_id=1, source_target_pairs={{0,32},{4,40},{9,33},{13,41},{18,50},{22,58},{27,51},{31,59},{36,4... | collective-permute-start | bytes 3145736 | tf_op jit(solution)/shard_map/ppermute | solution.py:733
  7.4 1.7 collective-permute-start.3
  9.1 25.6 %copy-start.21 = (s32[48]{0:T(128)S(1)}, s32[48]{0:T(128)}, u32[]{:S(2)}) copy-start(s32[48]{0:T(128)} %param.10) | copy-start | bytes 580
  9.1 25.7 %copy-start.22 = (s32[2,32]{1,0:T(2,128)S(1)}, s32[2,32]{1,0:T(2,128)}, u32[]{:S(2)}) copy-start(s32[2,32]{1,0:T(2,128)} %param.9) | copy-start | bytes 772
  9.1 28.0 %copy-start.9 = (s32[2,32,32]{2,1,0:T(8,128)S(1)}, s32[2,32,32]{2,1,0:T(8,128)}, u32[]{:S(2)}) copy-start(s32[2,32,32]{2,1,0:T(8,128)} %pat.1) | copy-start | bytes 24580
  11.0 26.0 %collective-permute-start.4 = (bf16[512,1024]{1,0:T(8,128)(2,1)S(1)}, bf16[512,1024]{1,0:T(8,128)(2,1)}, u32[]{:S(2)}, u32[]{:S(2)}) collective-permute-start(bf16[512,1024]{1,0:T(8,128)(2,1)S(1)} %fusion.mine), channel_id=1, source_target_pairs={{0,8},{1,9},{2,10},{3,11},{4,12},{5,13},{6,14},{7,15},{8,0},{9,1},... | collective-permute-start | bytes 3145736 | tf_op jit(solution)/shard_map/ppermute | solution.py:48
  34.7 42.2 %copy-start.6 = (s32[11]{0:T(128)}, s32[11]{0:T(128)S(1)}, u32[]{:S(2)}) copy-start(s32[11]{0:T(128)S(1)} %stack.55.ids) | copy-start | bytes 136
  47.4 8.1 %copy-start.14 = (f32[512,512]{1,0:T(8,128)S(1)}, f32[512,512]{1,0:T(8,128)}, u32[]{:S(2)}) copy-start(f32[512,512]{1,0:T(8,128)} %get-tuple-element.53) | copy-start | bytes 3145732
  47.5 61.7 %all-to-all-start = ((s16[8,272,1024]{2,1,0:T(8,128)(2,1)}), s16[8,272,1024]{2,1,0:T(8,128)(2,1)}, u32[]{:S(2)}, u32[]{:S(2)}) async-start(s16[8,272,1024]{2,1,0:T(8,128)(2,1)} %get-tuple-element.52), calls=%async_computation | async-start | bytes 8912896 | tf_op jit(solution)/shard_map/all_to_all | solution.py:801
  55.5 21.4 %copy-start.2 = (f32[1024,512]{1,0:T(8,128)S(1)}, f32[1024,512]{1,0:T(8,128)}, u32[]{:S(2)}) copy-start(f32[1024,512]{1,0:T(8,128)} %get-tuple-element.56.gcol) | copy-start | bytes 6291460
  56.4 2.2 collective-permute-start.5
  59.7 10.3 %collective-permute-start.6 = (f32[64,512]{1,0:T(8,128)S(1)}, f32[64,512]{1,0:T(8,128)S(1)}, u32[]{:S(2)}, u32[]{:S(2)}) collective-permute-start(f32[64,512]{1,0:T(8,128)S(1)} %get-tuple-element.98), channel_id=1, source_target_pairs={{0,2},{1,3},{2,4},{3,5},{4,6},{5,7},{6,0},{7,1},{8,10},{9,11},{10,... | collective-permute-start | bytes 393224 | tf_op jit(solution)/shard_map/ppermute | solution.py:48
  65.9 4.5 %collective-permute-start.7 = (f32[64,512]{1,0:T(8,128)S(1)}, f32[64,512]{1,0:T(8,128)S(1)}, u32[]{:S(2)}, u32[]{:S(2)}) collective-permute-start(f32[64,512]{1,0:T(8,128)S(1)} %get-tuple-element.100), channel_id=1, source_target_pairs={{0,6},{1,7},{2,0},{3,1},{4,2},{5,3},{6,4},{7,5},{8,14},{9,15},{10,... | collective-permute-start | bytes 393224 | tf_op jit(solution)/shard_map/ppermute | solution.py:48
  66.4 7.2 %collective-permute-start.8 = (f32[64,512]{1,0:T(8,128)S(1)}, f32[64,512]{1,0:T(8,128)S(1)}, u32[]{:S(2)}, u32[]{:S(2)}) collective-permute-start(f32[64,512]{1,0:T(8,128)S(1)} %get-tuple-element.99), channel_id=1, source_target_pairs={{0,4},{1,5},{2,6},{3,7},{4,0},{5,1},{6,2},{7,3},{8,12},{9,13},{10,... | collective-permute-start | bytes 393224 | tf_op jit(solution)/shard_map/ppermute | solution.py:48
  73.6 8.4 %collective-permute-start.9 = (f32[64,512]{1,0:T(8,128)S(1)}, f32[64,512]{1,0:T(8,128)S(1)}, u32[]{:S(2)}, u32[]{:S(2)}) collective-permute-start(f32[64,512]{1,0:T(8,128)S(1)} %fusion.4), channel_id=1, source_target_pairs={{0,2},{1,3},{2,4},{3,5},{4,6},{5,7},{6,0},{7,1},{8,10},{9,11},{10,... | collective-permute-start | bytes 393224 | tf_op jit(solution)/shard_map/ppermute | solution.py:48
  74.6 9.3 %collective-permute-start.10 = (f32[64,512]{1,0:T(8,128)S(1)}, f32[64,512]{1,0:T(8,128)S(1)}, u32[]{:S(2)}, u32[]{:S(2)}) collective-permute-start(f32[64,512]{1,0:T(8,128)S(1)} %fusion.4), channel_id=1, source_target_pairs={{0,6},{1,7},{2,0},{3,1},{4,2},{5,3},{6,4},{7,5},{8,14},{9,15},{10,... | collective-permute-start | bytes 393224 | tf_op jit(solution)/shard_map/ppermute | solution.py:48
  76.4 7.6 %collective-permute-start.11 = (f32[64,512]{1,0:T(8,128)S(1)}, f32[64,512]{1,0:T(8,128)S(1)}, u32[]{:S(2)}, u32[]{:S(2)}) collective-permute-start(f32[64,512]{1,0:T(8,128)S(1)} %fusion.4), channel_id=1, source_target_pairs={{0,4},{1,5},{2,6},{3,7},{4,0},{5,1},{6,2},{7,3},{8,12},{9,13},{10,... | collective-permute-start | bytes 393224 | tf_op jit(solution)/shard_map/ppermute | solution.py:48
  78.4 0.8 copy-start.3
  79.2 15.0 %collective-permute-start.12 = (s16[2,256,512]{2,1,0:T(8,128)(2,1)S(1)}, s16[2,256,512]{2,1,0:T(8,128)(2,1)S(1)}, u32[]{:S(2)}, u32[]{:S(2)}) collective-permute-start(s16[2,256,512]{2,1,0:T(8,128)(2,1)S(1)} %get-tuple-element.58), channel_id=1, source_target_pairs={{0,2},{1,3},{2,4},{3,5},{4,6},{5,7},{6,0},{7,1},{8,10},{9,11},{10,... | collective-permute-start | bytes 1572872 | tf_op jit(solution)/shard_map/ppermute | solution.py:48
  80.1 25.3 %collective-permute-start.13 = (s16[2,256,512]{2,1,0:T(8,128)(2,1)S(1)}, s16[2,256,512]{2,1,0:T(8,128)(2,1)S(1)}, u32[]{:S(2)}, u32[]{:S(2)}) collective-permute-start(s16[2,256,512]{2,1,0:T(8,128)(2,1)S(1)} %get-tuple-element.59), channel_id=1, source_target_pairs={{0,4},{1,5},{2,6},{3,7},{4,0},{5,1},{6,2},{7,3},{8,12},{9,13},{10,... | collective-permute-start | bytes 1572872 | tf_op jit(solution)/shard_map/ppermute | solution.py:48
  82.0 23.3 %collective-permute-start.14 = (s16[2,256,512]{2,1,0:T(8,128)(2,1)S(1)}, s16[2,256,512]{2,1,0:T(8,128)(2,1)S(1)}, u32[]{:S(2)}, u32[]{:S(2)}) collective-permute-start(s16[2,256,512]{2,1,0:T(8,128)(2,1)S(1)} %get-tuple-element.60), channel_id=1, source_target_pairs={{0,6},{1,7},{2,0},{3,1},{4,2},{5,3},{6,4},{7,5},{8,14},{9,15},{10,... | collective-permute-start | bytes 1572872 | tf_op jit(solution)/shard_map/ppermute | solution.py:48
  94.3 11.1 %copy-start.15 = (s16[2,256,512]{2,1,0:T(8,128)(2,1)}, s16[2,256,512]{2,1,0:T(8,128)(2,1)S(1)}, u32[]{:S(2)}) copy-start(s16[2,256,512]{2,1,0:T(8,128)(2,1)S(1)} %collective-permute-done.12.refs_1_) | copy-start | bytes 1572868
  105.3 0.8 copy-start.16
  105.3 1.0 copy-start.17
  109.1 43.4 %copy-start.4 = (s32[2,48]{1,0:T(2,128)S(1)}, s32[2,48]{1,0:T(2,128)}, u32[]{:S(2)}) copy-start(s32[2,48]{1,0:T(2,128)} %select_reduce_fusion.where) | copy-start | bytes 1156
  109.1 43.4 %copy-start.7 = (s32[11]{0:T(128)S(1)}, s32[11]{0:T(128)}, u32[]{:S(2)}) copy-start(s32[11]{0:T(128)} %copy-done.6) | copy-start | bytes 136
  109.1 43.3 %collective-permute-start.15 = (s16[8,272,1024]{2,1,0:T(8,128)(2,1)}, s16[8,272,1024]{2,1,0:T(8,128)(2,1)}, u32[]{:S(2)}, u32[]{:S(2)}) collective-permute-start(s16[8,272,1024]{2,1,0:T(8,128)(2,1)} %all-to-all-done.own), channel_id=1, source_target_pairs={{0,8},{1,9},{2,10},{3,11},{4,12},{5,13},{6,14},{7,15},{8,0},{9,1},... | collective-permute-start | bytes 13369352 | tf_op jit(solution)/shard_map/ppermute | solution.py:48
  111.0 18.4 %collective-permute-start.16 = (f32[64,512]{1,0:T(8,128)S(1)}, f32[64,512]{1,0:T(8,128)S(1)}, u32[]{:S(2)}, u32[]{:S(2)}) collective-permute-start(f32[64,512]{1,0:T(8,128)S(1)} %get-tuple-element.95), channel_id=1, source_target_pairs={{0,16},{1,17},{2,18},{3,19},{4,20},{5,21},{6,22},{7,23},{8,24},{9,... | collective-permute-start | bytes 393224 | tf_op jit(solution)/shard_map/ppermute | solution.py:48
  122.1 8.9 %collective-permute-start.17 = (f32[64,512]{1,0:T(8,128)S(1)}, f32[64,512]{1,0:T(8,128)S(1)}, u32[]{:S(2)}, u32[]{:S(2)}) collective-permute-start(f32[64,512]{1,0:T(8,128)S(1)} %get-tuple-element.97), channel_id=1, source_target_pairs={{0,48},{1,49},{2,50},{3,51},{4,52},{5,53},{6,54},{7,55},{8,56},{9,... | collective-permute-start | bytes 393224 | tf_op jit(solution)/shard_map/ppermute | solution.py:48
  125.4 7.6 %collective-permute-start.18 = (f32[64,512]{1,0:T(8,128)S(1)}, f32[64,512]{1,0:T(8,128)S(1)}, u32[]{:S(2)}, u32[]{:S(2)}) collective-permute-start(f32[64,512]{1,0:T(8,128)S(1)} %get-tuple-element.96), channel_id=1, source_target_pairs={{0,32},{1,33},{2,34},{3,35},{4,36},{5,37},{6,38},{7,39},{8,40},{9,... | collective-permute-start | bytes 393224 | tf_op jit(solution)/shard_map/ppermute | solution.py:48
  127.5 28.4 %copy-start.13 = (s16[256,512]{1,0:T(8,128)(2,1)}, s16[256,512]{1,0:T(8,128)(2,1)S(1)}, u32[]{:S(2)}) copy-start(s16[256,512]{1,0:T(8,128)(2,1)S(1)} %get-tuple-element.75.kept) | copy-start | bytes 786436
  127.5 8.9 %collective-permute-start.19 = (s16[256,512]{1,0:T(8,128)(2,1)S(1)}, s16[256,512]{1,0:T(8,128)(2,1)S(1)}, u32[]{:S(2)}, u32[]{:S(2)}) collective-permute-start(s16[256,512]{1,0:T(8,128)(2,1)S(1)} %get-tuple-element.94), channel_id=1, source_target_pairs={{0,1},{1,0},{2,3},{3,2},{4,5},{5,4},{6,7},{7,6},{8,9},{9,8},{10,11... | collective-permute-start | bytes 786440 | tf_op jit(solution)/shard_map/ppermute | solution.py:48
  129.4 12.0 %collective-permute-start.20 = (s16[256,512]{1,0:T(8,128)(2,1)S(1)}, s16[256,512]{1,0:T(8,128)(2,1)S(1)}, u32[]{:S(2)}, u32[]{:S(2)}) collective-permute-start(s16[256,512]{1,0:T(8,128)(2,1)S(1)} %get-tuple-element.75.kept), channel_id=1, source_target_pairs={{0,64},{1,65},{2,66},{3,67},{4,68},{5,69},{6,70},{7,71},{8,72},{9,... | collective-permute-start | bytes 786440 | tf_op jit(solution)/shard_map/ppermute | solution.py:48
  131.0 12.0 %collective-permute-start.21 = (s16[256,512]{1,0:T(8,128)(2,1)S(1)}, s16[256,512]{1,0:T(8,128)(2,1)S(1)}, u32[]{:S(2)}, u32[]{:S(2)}) collective-permute-start(s16[256,512]{1,0:T(8,128)(2,1)S(1)} %get-tuple-element.94), channel_id=1, source_target_pairs={{0,65},{1,64},{2,67},{3,66},{4,69},{5,68},{6,71},{7,70},{8,73},{9,... | collective-permute-start | bytes 786440 | tf_op jit(solution)/shard_map/ppermute | solution.py:48
  136.4 19.5 %copy-start.18 = (s16[256,512]{1,0:T(8,128)(2,1)}, s16[256,512]{1,0:T(8,128)(2,1)S(1)}, u32[]{:S(2)}) copy-start(s16[256,512]{1,0:T(8,128)(2,1)S(1)} %collective-permute-done.19.beside) | copy-start | bytes 786436
  141.4 14.5 %copy-start.19 = (s16[256,512]{1,0:T(8,128)(2,1)}, s16[256,512]{1,0:T(8,128)(2,1)S(1)}, u32[]{:S(2)}) copy-start(s16[256,512]{1,0:T(8,128)(2,1)S(1)} %collective-permute-done.20.across) | copy-start | bytes 786436
  143.0 13.0 %copy-start.20 = (s16[256,512]{1,0:T(8,128)(2,1)}, s16[256,512]{1,0:T(8,128)(2,1)S(1)}, u32[]{:S(2)}) copy-start(s16[256,512]{1,0:T(8,128)(2,1)S(1)} %collective-permute-done.21.both) | copy-start | bytes 786436
  143.0 5.8 %collective-permute-start.22 = (f32[64,512]{1,0:T(8,128)S(1)}, f32[64,512]{1,0:T(8,128)S(1)}, u32[]{:S(2)}, u32[]{:S(2)}) collective-permute-start(f32[64,512]{1,0:T(8,128)S(1)} %fusion.2), channel_id=1, source_target_pairs={{0,65},{1,64},{2,67},{3,66},{4,69},{5,68},{6,71},{7,70},{8,73},{9,... | collective-permute-start | bytes 393224 | tf_op jit(solution)/shard_map/ppermute | solution.py:48
  144.7 4.2 %collective-permute-start.23 = (f32[64,512]{1,0:T(8,128)S(1)}, f32[64,512]{1,0:T(8,128)S(1)}, u32[]{:S(2)}, u32[]{:S(2)}) collective-permute-start(f32[64,512]{1,0:T(8,128)S(1)} %fusion.2), channel_id=1, source_target_pairs={{0,64},{1,65},{2,66},{3,67},{4,68},{5,69},{6,70},{7,71},{8,72},{9,... | collective-permute-start | bytes 393224 | tf_op jit(solution)/shard_map/ppermute | solution.py:48
  144.7 7.7 %collective-permute-start.24 = (f32[64,512]{1,0:T(8,128)S(1)}, f32[64,512]{1,0:T(8,128)S(1)}, u32[]{:S(2)}, u32[]{:S(2)}) collective-permute-start(f32[64,512]{1,0:T(8,128)S(1)} %fusion.2), channel_id=1, source_target_pairs={{0,1},{1,0},{2,3},{3,2},{4,5},{5,4},{6,7},{7,6},{8,9},{9,8},{10,11... | collective-permute-start | bytes 393224 | tf_op jit(solution)/shard_map/ppermute | solution.py:48
  156.0 14.3 %collective-permute-start.25 = (f32[64,512]{1,0:T(8,128)S(1)}, f32[64,512]{1,0:T(8,128)S(1)}, u32[]{:S(2)}, u32[]{:S(2)}) collective-permute-start(f32[64,512]{1,0:T(8,128)S(1)} %add_add_fusion), channel_id=1, source_target_pairs={{0,16},{1,17},{2,18},{3,19},{4,20},{5,21},{6,22},{7,23},{8,24},{9,... | collective-permute-start | bytes 393224 | tf_op jit(solution)/shard_map/ppermute | solution.py:48
  156.9 13.4 %collective-permute-start.26 = (f32[64,512]{1,0:T(8,128)S(1)}, f32[64,512]{1,0:T(8,128)S(1)}, u32[]{:S(2)}, u32[]{:S(2)}) collective-permute-start(f32[64,512]{1,0:T(8,128)S(1)} %add_add_fusion), channel_id=1, source_target_pairs={{0,48},{1,49},{2,50},{3,51},{4,52},{5,53},{6,54},{7,55},{8,56},{9,... | collective-permute-start | bytes 393224 | tf_op jit(solution)/shard_map/ppermute | solution.py:48
  158.7 11.6 %collective-permute-start.27 = (f32[64,512]{1,0:T(8,128)S(1)}, f32[64,512]{1,0:T(8,128)S(1)}, u32[]{:S(2)}, u32[]{:S(2)}) collective-permute-start(f32[64,512]{1,0:T(8,128)S(1)} %add_add_fusion), channel_id=1, source_target_pairs={{0,32},{1,33},{2,34},{3,35},{4,36},{5,37},{6,38},{7,39},{8,40},{9,... | collective-permute-start | bytes 393224 | tf_op jit(solution)/shard_map/ppermute | solution.py:48
  159.2 82.4 %all-to-all-start.1 = ((s16[8,1552,256]{2,1,0:T(8,128)(2,1)}), s16[8,1552,256]{2,1,0:T(8,128)(2,1)}, u32[]{:S(2)}, u32[]{:S(2)}) async-start(s16[8,1552,256]{2,1,0:T(8,128)(2,1)} %shard_map.67), calls=%async_computation.1 | async-start | bytes 12713984 | tf_op jit(solution)/shard_map/all_to_all | solution.py:818
  170.4 9.8 %collective-permute-start.28 = (f32[256,512]{1,0:T(8,128)S(1)}, f32[256,512]{1,0:T(8,128)S(1)}, u32[]{:S(2)}, u32[]{:S(2)}) collective-permute-start(f32[256,512]{1,0:T(8,128)S(1)} %bitcast.82), channel_id=1, source_target_pairs={{0,8},{1,9},{2,10},{3,11},{4,12},{5,13},{6,14},{7,15},{8,0},{9,1},... | collective-permute-start | bytes 1572872 | tf_op jit(solution)/shard_map/ppermute | solution.py:48
  175.9 32.0 %collective-permute-start.29 = (s16[2,256,512]{2,1,0:T(8,128)(2,1)}, s16[2,256,512]{2,1,0:T(8,128)(2,1)S(1)}, u32[]{:S(2)}, u32[]{:S(2)}) collective-permute-start(s16[2,256,512]{2,1,0:T(8,128)(2,1)} %shard_map.69), channel_id=1, source_target_pairs={{0,16},{1,17},{2,18},{3,19},{4,20},{5,21},{6,22},{7,23},{8,24},{9,... | collective-permute-start | bytes 1572872 | tf_op jit(solution)/shard_map/ppermute | solution.py:48
  176.0 31.9 %collective-permute-start.30 = (s16[2,256,512]{2,1,0:T(8,128)(2,1)}, s16[2,256,512]{2,1,0:T(8,128)(2,1)S(1)}, u32[]{:S(2)}, u32[]{:S(2)}) collective-permute-start(s16[2,256,512]{2,1,0:T(8,128)(2,1)} %shard_map.69), channel_id=1, source_target_pairs={{0,32},{1,33},{2,34},{3,35},{4,36},{5,37},{6,38},{7,39},{8,40},{9,... | collective-permute-start | bytes 1572872 | tf_op jit(solution)/shard_map/ppermute | solution.py:48
  178.3 29.5 %collective-permute-start.31 = (s16[2,256,512]{2,1,0:T(8,128)(2,1)}, s16[2,256,512]{2,1,0:T(8,128)(2,1)S(1)}, u32[]{:S(2)}, u32[]{:S(2)}) collective-permute-start(s16[2,256,512]{2,1,0:T(8,128)(2,1)} %shard_map.69), channel_id=1, source_target_pairs={{0,48},{1,49},{2,50},{3,51},{4,52},{5,53},{6,54},{7,55},{8,56},{9,... | collective-permute-start | bytes 1572872 | tf_op jit(solution)/shard_map/ppermute | solution.py:48
  180.4 27.5 %copy-start.12 = (s16[2,256,512]{2,1,0:T(8,128)(2,1)S(1)}, s16[2,256,512]{2,1,0:T(8,128)(2,1)}, u32[]{:S(2)}) copy-start(s16[2,256,512]{2,1,0:T(8,128)(2,1)} %shard_map.69) | copy-start | bytes 1572868
  206.9 1.0 copy-start.10
  207.9 4.9 %copy-start.5 = (s32[2,48]{1,0:T(2,128)S(1)}, s32[2,48]{1,0:T(2,128)}, u32[]{:S(2)}) copy-start(s32[2,48]{1,0:T(2,128)} %select_reduce_fusion.where) | copy-start | bytes 1156
  207.9 4.9 %copy-start.8 = (s32[11]{0:T(128)S(1)}, s32[11]{0:T(128)}, u32[]{:S(2)}) copy-start(s32[11]{0:T(128)} %copy-done.6) | copy-start | bytes 136
  208.0 4.7 %collective-permute-start.32 = (s16[4,2,256,512]{3,2,1,0:T(8,128)(2,1)S(1)}, s16[4,2,256,512]{3,2,1,0:T(8,128)(2,1)S(1)}, u32[]{:S(2)}, u32[]{:S(2)}) collective-permute-start(s16[4,2,256,512]{3,2,1,0:T(8,128)(2,1)S(1)} %pad_add_fusion.own), channel_id=1, source_target_pairs={{0,8},{1,9},{2,10},{3,11},{4,12},{5,13},{6,14},{7,15},{8,0},{9,1},... | collective-permute-start | bytes 6291464 | tf_op jit(solution)/shard_map/ppermute | solution.py:48
  241.6 27.2 %all-to-all-start.2 = ((s16[8,208,512]{2,1,0:T(8,128)(2,1)}), s16[8,208,512]{2,1,0:T(8,128)(2,1)S(1)}, u32[]{:S(2)}, u32[]{:S(2)}) async-start(s16[8,208,512]{2,1,0:T(8,128)(2,1)} %shard_map.70), calls=%async_computation.2 | async-start | bytes 3407872 | tf_op jit(solution)/shard_map/all_to_all | solution.py:830
  256.9 2.2 copy-start.1
  268.8 5.7 %copy-start.11 = (s16[8,208,512]{2,1,0:T(8,128)(2,1)}, s16[8,208,512]{2,1,0:T(8,128)(2,1)S(1)}, u32[]{:S(2)}) copy-start(s16[8,208,512]{2,1,0:T(8,128)(2,1)S(1)} %all-to-all-done.2.gx) | copy-start | bytes 5111812
  268.9 5.6 %collective-permute-start.33 = (s16[8,112,512]{2,1,0:T(8,128)(2,1)S(1)}, s16[8,112,512]{2,1,0:T(8,128)(2,1)S(1)}, u32[]{:S(2)}, u32[]{:S(2)}) collective-permute-start(s16[8,112,512]{2,1,0:T(8,128)(2,1)S(1)} %slice.9), channel_id=1, source_target_pairs={{0,8},{1,9},{2,10},{3,11},{4,12},{5,13},{6,14},{7,15},{8,0},{9,1},... | collective-permute-start | bytes 2752520 | tf_op jit(solution)/shard_map/ppermute | solution.py:48

commit v11 on v8

--- a/solution.py
+++ b/solution.py
@@ -768,8 +768,7 @@
 
 
 def sum_y(v):
-    v = v + shift(v, dc=1)
-    return v + shift(v, dc=1, dy=1)
+    return (v + shift(v, dc=1, dy=1)) + (shift(v, dc=1) + shift(v, dy=1))
 
 
 def sum_third(v, x, core):
@@ -814,11 +813,12 @@
     send = route(ids, slots, where, own, other)
     kept, moved = pick(strip, yh), pick(strip, 1 - yh)
     moves = [shift(moved, dy=1), shift(kept, dc=1), shift(moved, dc=1, dy=1)]
-    diag = sum_y(sum_x(diag, x))
-    send, diag, kept, *moves = lax.optimization_barrier((send, diag, kept, *moves))
+    diag, *moves = lax.optimization_barrier((sum_x(diag, x), *moves))
+    strip = choose_y(ids, where, [kept] + moves)
+    diag = sum_y(diag)
+    send, diag, strip = lax.optimization_barrier((send, diag, strip))
     recv = lax.all_to_all(send, ("z", "yh"), split_axis=0, concat_axis=0, tiled=True)
 
-    strip = choose_y(ids, where, [kept] + moves)
     diag = sum_third(diag, x, core)
     line = jnp.stack([strip] + [shift(strip, dx=d) for d in range(1, 4)])
     inv = inverse_factor(diag)

time: 294 us -> 287 us (0.976)
  waiting for transfers between devices: 92.9 us -> 71 us
  starting transfers between devices: 104 us -> 121 us
    ppermute x29 -> x30, starting transfers between devices: 72.5 us -> 99.9 us  [shift(): return lax.ppermute(v, AXES, pairs)]
    ppermute x29 -> x30, waiting for transfers between devices: 81.5 us -> 54.8 us  [shift(): return lax.ppermute(v, AXES, pairs)]
    all_to_all x1, starting transfers between devices: 10.9 us -> 4.89 us  [body(): lax.all_to_all(send, ('z', 'yh'), split_axis=0, concat_axis=0, tiled=True)]
    all_to_all x1, starting transfers between devices: 8.08 us -> 5.06 us  [body(): lax.all_to_all(send, ('child', 'x'), split_axis=0, concat_axis=0, tiled=T...]
    unnamed x46 -> x44, local copies, waits for them, and re-layouts: 6.81 us -> 5.96 us
  transfers between devices with their start and end apart: 36 -> 37, of which waited for: 18 -> 18; matrix products, arithmetic and copies ran while one was open for 2% -> 2% of each run, Pallas kernels for 18% -> 17%
where the time goes in v11:
time: 287 us; the launch traced here: 286 us
  starting transfers between devices  121 us (42%)
  Pallas kernels  76.9 us (27%)
  waiting for transfers between devices  71 us (25%)
  local copies, waits for them, and re-layouts  11.1 us (4%)
  other arithmetic  5.48 us (2%)
    ppermute x30, starting transfers between devices, shift(): return lax.ppermute(v, AXES, pairs)  99.9 us
    ppermute x30, waiting for transfers between devices, shift(): return lax.ppermute(v, AXES, pairs)  54.8 us
    pallas_call x1, Pallas kernels, inverse_factor(): pl.pallas_call(inverse_kernel, out_shape=jax.ShapeDtypeStruct((PANEL, PAN...  26.5 us
    pallas_call x1, Pallas kernels, final(): pl.pallas_call(final_kernel, grid_spec=pltpu.PrefetchScalarGridSpec(num_s...  14.3 us
    all_to_all x1, waiting for transfers between devices, body(): lax.all_to_all(gsend, ('z', 'yh'), split_axis=0, concat_axis=0, tiled=True)  10.9 us
    pallas_call x1, Pallas kernels, update(): pl.pallas_call(update_kernel, grid_spec=pltpu.PrefetchScalarGridSpec(num_...  10.4 us
    pallas_call x1, Pallas kernels, base(): pl.pallas_call(base_kernel, grid_spec=pltpu.PrefetchScalarGridSpec(num_sc...  9.51 us
    unnamed x44, local copies, waits for them, and re-layouts  5.96 us
  transfers between devices with their start and end apart: 37, of which 18 were waited for; matrix products, arithmetic and copies ran while one was open for 2% of the time, Pallas kernels for 17%

profile of v11, /device:TPU:1, one launch (start us, length us, event | category | flops | bytes accessed | tf_op | source)
XLA Modules:
  0.0 285.9 jit_solution(4661151284302530175)
XLA Ops:
  0.0 2.8 dynamic-slice_bitcast_fusion
  2.8 1.3 collective-permute-start
  4.1 1.6 collective-permute-start.3
  5.8 1.6 collective-permute-start.2
  7.4 1.6 collective-permute-start.1
  9.1 1.9 fusion.mine
  11.0 31.3 %collective-permute-start.4 = (bf16[512,1024]{1,0:T(8,128)(2,1)S(1)}, bf16[512,1024]{1,0:T(8,128)(2,1)}, u32[]{:S(2)}, u32[]{:S(2)}) collective-permute-start(bf16[512,1024]{1,0:T(8,128)(2,1)S(1)} %fusion.mine), channel_id=1, source_target_pairs={{0,8},{1,9},{2,10},{3,11},{4,12},{5,13},{6,14},{7,15},{8,0},{9,1},... | collective-permute-start | bytes 3145736 | tf_op jit(solution)/shard_map/ppermute | solution.py:48
  42.6 0.7 select_reduce_fusion.where
  43.3 1.5 collective-permute-done.4.other
  44.7 10.4 %shard_map.64 = (s16[8,272,1024]{2,1,0:T(8,128)(2,1)}, f32[512,512]{1,0:T(8,128)}, f32[1024,512]{1,0:T(8,128)}) custom-call(s32[11]{0:T(128)S(1)} %stack.55.ids, s32[2,32]{1,0:T(2,128)S(1)} %select_reduce_fusion.1.slots, s32[2,32,32]{2,1,0:T(8,128)S(1)} %copy-done.8, f32[1024,1024]{1,0:T(8,128)} %bitcast.83, bf16[1024,1024]{1,0:T(8,128)(2,1)S(1)} %bitcast.82, ...), custom_call_target="tpu_custom_call" | custom-call | flops 2147483648 | bytes 14680064 | tf_op jit(solution)/shard_map/pallas_call | solution.py:145
  55.1 5.1 %all-to-all-start = ((s16[8,272,1024]{2,1,0:T(8,128)(2,1)}), s16[8,272,1024]{2,1,0:T(8,128)(2,1)}, u32[]{:S(2)}, u32[]{:S(2)}) async-start(s16[8,272,1024]{2,1,0:T(8,128)(2,1)} %get-tuple-element.39), calls=%async_computation | async-start | bytes 8912896 | tf_op jit(solution)/shard_map/all_to_all | solution.py:802
  60.2 0.8 dynamic-slice_bitcast_fusion.2
  61.7 1.7 collective-permute-done.5
  63.4 1.1 bitcast_add_fusion
  64.7 1.1 collective-permute-start.8
  65.8 2.0 collective-permute-start.7
  67.8 5.8 %collective-permute-done.6 = f32[64,512]{1,0:T(8,128)S(1)} collective-permute-done((f32[64,512]{1,0:T(8,128)S(1)}, f32[64,512]{1,0:T(8,128)S(1)}, u32[]{:S(2)}, u32[]{:S(2)}) %collective-permute-start.6) | collective-permute-done | bytes 131104 | tf_op jit(solution)/shard_map/ppermute | solution.py:48
  73.8 1.1 collective-permute-start.11
  74.9 2.5 collective-permute-start.10
  77.9 1.5 shard_map.65
  79.4 0.8 copy-done.4
  80.2 2.6 collective-permute-start.12
  82.8 0.8 collective-permute-start.13
  83.7 1.7 collective-permute-start.14
  85.4 9.8 %collective-permute-done.12.refs_1_ = s16[2,256,512]{2,1,0:T(8,128)(2,1)S(1)} collective-permute-done((s16[2,256,512]{2,1,0:T(8,128)(2,1)S(1)}, s16[2,256,512]{2,1,0:T(8,128)(2,1)S(1)}, u32[]{:S(2)}, u32[]{:S(2)}) %collective-permute-start.12) | collective-permute-done | bytes 524320 | tf_op jit(solution)/shard_map/ppermute | solution.py:48
  95.3 10.0 %collective-permute-done.13.refs_2_ = s16[2,256,512]{2,1,0:T(8,128)(2,1)S(1)} collective-permute-done((s16[2,256,512]{2,1,0:T(8,128)(2,1)S(1)}, s16[2,256,512]{2,1,0:T(8,128)(2,1)S(1)}, u32[]{:S(2)}, u32[]{:S(2)}) %collective-permute-start.13) | collective-permute-done | bytes 524320 | tf_op jit(solution)/shard_map/ppermute | solution.py:48
  105.3 0.9 collective-permute-done.14.refs_3_
  106.2 0.8 copy-done.16
  106.9 2.8 shard_map.66
  109.7 2.9 %all-to-all-done.own = s16[8,272,1024]{2,1,0:T(8,128)(2,1)} async-done(((s16[8,272,1024]{2,1,0:T(8,128)(2,1)}), s16[8,272,1024]{2,1,0:T(8,128)(2,1)}, u32[]{:S(2)}, u32[]{:S(2)}) %all-to-all-start) | async-done | bytes 4456480 | tf_op jit(solution)/shard_map/all_to_all | solution.py:802
  112.7 0.8 collective-permute-start.15
  113.5 13.0 %collective-permute-start.16 = (f32[64,512]{1,0:T(8,128)S(1)}, f32[64,512]{1,0:T(8,128)S(1)}, u32[]{:S(2)}, u32[]{:S(2)}) collective-permute-start(f32[64,512]{1,0:T(8,128)S(1)} %get-tuple-element.69), channel_id=1, source_target_pairs={{0,16},{1,17},{2,18},{3,19},{4,20},{5,21},{6,22},{7,23},{8,24},{9,... | collective-permute-start | bytes 393224 | tf_op jit(solution)/shard_map/ppermute | solution.py:48
  126.5 4.4 %collective-permute-start.18 = (f32[64,512]{1,0:T(8,128)S(1)}, f32[64,512]{1,0:T(8,128)S(1)}, u32[]{:S(2)}, u32[]{:S(2)}) collective-permute-start(f32[64,512]{1,0:T(8,128)S(1)} %get-tuple-element.70), channel_id=1, source_target_pairs={{0,32},{1,33},{2,34},{3,35},{4,36},{5,37},{6,38},{7,39},{8,40},{9,... | collective-permute-start | bytes 393224 | tf_op jit(solution)/shard_map/ppermute | solution.py:48
  130.9 1.1 dynamic-slice_bitcast_fusion.3
  132.0 1.3 collective-permute-start.20
  133.6 4.1 %collective-permute-start.21 = (s16[256,512]{1,0:T(8,128)(2,1)S(1)}, s16[256,512]{1,0:T(8,128)(2,1)S(1)}, u32[]{:S(2)}, u32[]{:S(2)}) collective-permute-start(s16[256,512]{1,0:T(8,128)(2,1)S(1)} %get-tuple-element.68), channel_id=1, source_target_pairs={{0,65},{1,64},{2,67},{3,66},{4,69},{5,68},{6,71},{7,70},{8,73},{9,... | collective-permute-start | bytes 786440 | tf_op jit(solution)/shard_map/ppermute | solution.py:48
  137.6 3.8 %collective-permute-start.19 = (s16[256,512]{1,0:T(8,128)(2,1)S(1)}, s16[256,512]{1,0:T(8,128)(2,1)S(1)}, u32[]{:S(2)}, u32[]{:S(2)}) collective-permute-start(s16[256,512]{1,0:T(8,128)(2,1)S(1)} %get-tuple-element.68), channel_id=1, source_target_pairs={{0,1},{1,0},{2,3},{3,2},{4,5},{5,4},{6,7},{7,6},{8,9},{9,8},{10,11... | collective-permute-start | bytes 786440 | tf_op jit(solution)/shard_map/ppermute | solution.py:48
  141.5 6.7 %collective-permute-done.21.both = s16[256,512]{1,0:T(8,128)(2,1)S(1)} collective-permute-done((s16[256,512]{1,0:T(8,128)(2,1)S(1)}, s16[256,512]{1,0:T(8,128)(2,1)S(1)}, u32[]{:S(2)}, u32[]{:S(2)}) %collective-permute-start.21) | collective-permute-done | bytes 262176 | tf_op jit(solution)/shard_map/ppermute | solution.py:48
  148.8 1.2 collective-permute-start.24
  150.0 2.4 collective-permute-start.23
  152.4 2.7 shard_map.68
  155.1 2.1 collective-permute-done.23
  157.2 1.1 collective-permute-done.22
  158.4 3.6 %shard_map.67 = s16[8,1552,256]{2,1,0:T(8,128)(2,1)} custom-call(s32[11]{0:T(128)S(1)} %copy-done.7, s32[2,32]{1,0:T(2,128)S(1)} %select_reduce_fusion.1.slots, s32[2,48]{1,0:T(2,128)S(1)} %copy-done.5, s16[8,272,1024]{2,1,0:T(8,128)(2,1)} %all-to-all-done.own, s16[8,272,1024]{2,1,0:T(8,128)(2,1)} %collective-permute-done.15.other), custom_call_target="tpu_custom_call" | custom-call | bytes 8388608 | tf_op jit(solution)/shard_map/pallas_call | solution.py:428
  162.0 4.9 %all-to-all-start.1 = ((s16[8,1552,256]{2,1,0:T(8,128)(2,1)}), s16[8,1552,256]{2,1,0:T(8,128)(2,1)}, u32[]{:S(2)}, u32[]{:S(2)}) async-start(s16[8,1552,256]{2,1,0:T(8,128)(2,1)} %shard_map.67), calls=%async_computation.1 | async-start | bytes 12713984 | tf_op jit(solution)/shard_map/all_to_all | solution.py:820
  167.4 2.1 collective-permute-start.26
  169.5 2.7 collective-permute-start.31
  172.2 4.1 %collective-permute-done.25 = f32[64,512]{1,0:T(8,128)S(1)} collective-permute-done((f32[64,512]{1,0:T(8,128)S(1)}, f32[64,512]{1,0:T(8,128)S(1)}, u32[]{:S(2)}, u32[]{:S(2)}) %collective-permute-start.25) | collective-permute-done | bytes 131104 | tf_op jit(solution)/shard_map/ppermute | solution.py:48
  176.4 12.5 %collective-permute-start.28 = (f32[256,512]{1,0:T(8,128)S(1)}, f32[256,512]{1,0:T(8,128)}, u32[]{:S(2)}, u32[]{:S(2)}) collective-permute-start(f32[256,512]{1,0:T(8,128)S(1)} %bitcast.84), channel_id=1, source_target_pairs={{0,8},{1,9},{2,10},{3,11},{4,12},{5,13},{6,14},{7,15},{8,0},{9,1},... | collective-permute-start | bytes 1572872 | tf_op jit(solution)/shard_map/ppermute | solution.py:48
  188.9 7.8 %collective-permute-done.29 = s16[2,256,512]{2,1,0:T(8,128)(2,1)S(1)} collective-permute-done((s16[2,256,512]{2,1,0:T(8,128)(2,1)S(1)}, s16[2,256,512]{2,1,0:T(8,128)(2,1)S(1)}, u32[]{:S(2)}, u32[]{:S(2)}) %collective-permute-start.29) | collective-permute-done | bytes 524320 | tf_op jit(solution)/shard_map/ppermute | solution.py:48
  196.9 4.3 %collective-permute-start.32 = (s16[4,2,256,512]{3,2,1,0:T(8,128)(2,1)S(1)}, s16[4,2,256,512]{3,2,1,0:T(8,128)(2,1)}, u32[]{:S(2)}, u32[]{:S(2)}) collective-permute-start(s16[4,2,256,512]{3,2,1,0:T(8,128)(2,1)S(1)} %pad_add_fusion.own), channel_id=1, source_target_pairs={{0,8},{1,9},{2,10},{3,11},{4,12},{5,13},{6,14},{7,15},{8,0},{9,1},... | collective-permute-start | bytes 6291464 | tf_op jit(solution)/shard_map/ppermute | solution.py:48
  201.2 1.2 broadcast_select_fusion.1
  202.4 26.5 %shard_map.69.inv = f32[512,512]{1,0:T(8,128)S(1)} custom-call(f32[512,512]{1,0:T(8,128)S(1)} %pad_maximum_fusion.a_ref.diag), custom_call_target="tpu_custom_call" | custom-call | flops 17179869184 | bytes 2097152 | tf_op jit(solution)/shard_map/pallas_call | solution.py:532
  228.9 1.0 copy-done.9
  229.9 5.8 %shard_map.70 = s16[8,208,512]{2,1,0:T(8,128)(2,1)S(1)} custom-call(s32[11]{0:T(128)S(1)} %copy-done.7, s32[2,48]{1,0:T(2,128)S(1)} %copy-done.5, s16[4,2,256,512]{3,2,1,0:T(8,128)(2,1)S(1)} %pad_add_fusion.own, s16[4,2,256,512]{3,2,1,0:T(8,128)(2,1)} %collective-permute-done.32.other), custom_call_target="tpu_custom_call" | custom-call | bytes 6291456 | tf_op jit(solution)/shard_map/pallas_call | solution.py:354
  235.7 1.2 copy-done.1
  236.9 2.3 all-to-all-done.1.recv
  239.2 4.8 %all-to-all-start.2 = ((s16[8,208,512]{2,1,0:T(8,128)(2,1)}), s16[8,208,512]{2,1,0:T(8,128)(2,1)S(1)}, u32[]{:S(2)}, u32[]{:S(2)}) async-start(s16[8,208,512]{2,1,0:T(8,128)(2,1)} %copy-done.1), calls=%async_computation.2 | async-start | bytes 3407872 | tf_op jit(solution)/shard_map/all_to_all | solution.py:827
  243.9 9.5 %shard_map.71.front = f32[768,1536]{1,0:T(8,128)S(1)} custom-call(s32[11]{0:T(128)S(1)} %copy-done.7, s32[2,48]{1,0:T(2,128)S(1)} %copy-done.5, s16[8,1552,256]{2,1,0:T(8,128)(2,1)} %all-to-all-done.1.recv, f32[768,1536]{1,0:T(8,128)} %front.5), custom_call_target="tpu_custom_call" | custom-call | bytes 20971520 | tf_op jit(solution)/shard_map/pallas_call | solution.py:608
  253.5 2.2 copy-done.2
  255.6 10.9 %all-to-all-done.2.gx = s16[8,208,512]{2,1,0:T(8,128)(2,1)S(1)} async-done(((s16[8,208,512]{2,1,0:T(8,128)(2,1)}), s16[8,208,512]{2,1,0:T(8,128)(2,1)S(1)}, u32[]{:S(2)}, u32[]{:S(2)}) %all-to-all-start.2) | async-done | bytes 1703968 | tf_op jit(solution)/shard_map/all_to_all | solution.py:827
  266.6 2.9 %collective-permute-start.33 = (s16[8,112,512]{2,1,0:T(8,128)(2,1)S(1)}, s16[8,112,512]{2,1,0:T(8,128)(2,1)S(1)}, u32[]{:S(2)}, u32[]{:S(2)}) collective-permute-start(s16[8,112,512]{2,1,0:T(8,128)(2,1)S(1)} %slice.9), channel_id=1, source_target_pairs={{0,8},{1,9},{2,10},{3,11},{4,12},{5,13},{6,14},{7,15},{8,0},{9,1},... | collective-permute-start | bytes 2752520 | tf_op jit(solution)/shard_map/ppermute | solution.py:48
  269.5 2.1 collective-permute-done.33.goth
  271.6 14.3 %shard_map.72 = f32[768,1536]{1,0:T(8,128)} custom-call(s32[11]{0:T(128)S(1)} %copy-done.7, f32[512,512]{1,0:T(8,128)S(1)} %pad_maximum_fusion.a_ref.diag, f32[512,512]{1,0:T(8,128)} %copy-done.9, s16[8,208,512]{2,1,0:T(8,128)(2,1)} %copy-done.10, s16[8,112,512]{2,1,0:T(8,128)(2,1)S(1)} %collective-permute-done.33.goth, f32[768,1536]{1,0:T(8,128)} %copy-done.2), custom_call_target="tpu_custom_call" | custom-call | flops 8589934592 | bytes 20971520 | tf_op jit(solution)/shard_map/pallas_call | solution.py:691
  (90 shorter events, 3.9 us)
Async XLA Ops:
  0.0 9.1 %copy-start = (bf16[1,1024,1024]{2,1,0:T(8,128)(2,1)S(1)}, bf16[1,1024,1024]{2,1,0:T(8,128)(2,1)}, u32[]{:S(2)}) copy-start(bf16[1,1024,1024]{2,1,0:T(8,128)(2,1)} %param.7) | copy-start | bytes 6291460
  2.8 6.2 %collective-permute-start = (bf16[512,1024]{1,0:T(8,128)(2,1)}, bf16[512,1024]{1,0:T(8,128)(2,1)}, u32[]{:S(2)}, u32[]{:S(2)}) collective-permute-start(bf16[512,1024]{1,0:T(8,128)(2,1)} %get-tuple-element.64), channel_id=1, source_target_pairs={{0,8},{9,1},{18,26},{27,19},{36,44},{45,37},{54,62},{63,55},{64,72... | collective-permute-start | bytes 3145736 | tf_op jit(solution)/shard_map/ppermute | solution.py:740
  4.1 4.9 %collective-permute-start.3 = (bf16[512,1024]{1,0:T(8,128)(2,1)S(1)}, bf16[512,1024]{1,0:T(8,128)(2,1)}, u32[]{:S(2)}, u32[]{:S(2)}) collective-permute-start(bf16[512,1024]{1,0:T(8,128)(2,1)S(1)} %get-tuple-element.63), channel_id=1, source_target_pairs={{0,48},{4,56},{9,49},{13,57},{18,2},{22,10},{27,3},{31,11},{36,20}... | collective-permute-start | bytes 3145736 | tf_op jit(solution)/shard_map/ppermute | solution.py:733
  5.8 3.3 %collective-permute-start.2 = (bf16[512,1024]{1,0:T(8,128)(2,1)S(1)}, bf16[512,1024]{1,0:T(8,128)(2,1)}, u32[]{:S(2)}, u32[]{:S(2)}) collective-permute-start(bf16[512,1024]{1,0:T(8,128)(2,1)S(1)} %get-tuple-element.63), channel_id=1, source_target_pairs={{0,32},{4,40},{9,33},{13,41},{18,50},{22,58},{27,51},{31,59},{36,4... | collective-permute-start | bytes 3145736 | tf_op jit(solution)/shard_map/ppermute | solution.py:733
  7.4 1.7 collective-permute-start.1
  9.0 33.3 %copy-start.20 = (s32[48]{0:T(128)S(1)}, s32[48]{0:T(128)}, u32[]{:S(2)}) copy-start(s32[48]{0:T(128)} %param.10) | copy-start | bytes 580
  9.1 33.4 %copy-start.21 = (s32[2,32]{1,0:T(2,128)S(1)}, s32[2,32]{1,0:T(2,128)}, u32[]{:S(2)}) copy-start(s32[2,32]{1,0:T(2,128)} %param.9) | copy-start | bytes 772
  9.1 35.7 %copy-start.8 = (s32[2,32,32]{2,1,0:T(8,128)S(1)}, s32[2,32,32]{2,1,0:T(8,128)}, u32[]{:S(2)}) copy-start(s32[2,32,32]{2,1,0:T(8,128)} %pat.1) | copy-start | bytes 24580
  11.0 33.7 %collective-permute-start.4 = (bf16[512,1024]{1,0:T(8,128)(2,1)S(1)}, bf16[512,1024]{1,0:T(8,128)(2,1)}, u32[]{:S(2)}, u32[]{:S(2)}) collective-permute-start(bf16[512,1024]{1,0:T(8,128)(2,1)S(1)} %fusion.mine), channel_id=1, source_target_pairs={{0,8},{1,9},{2,10},{3,11},{4,12},{5,13},{6,14},{7,15},{8,0},{9,1},... | collective-permute-start | bytes 3145736 | tf_op jit(solution)/shard_map/ppermute | solution.py:48
  42.4 35.5 %copy-start.6 = (s32[11]{0:T(128)}, s32[11]{0:T(128)S(1)}, u32[]{:S(2)}) copy-start(s32[11]{0:T(128)S(1)} %stack.55.ids) | copy-start | bytes 136
  55.1 5.1 %copy-start.13 = (f32[512,512]{1,0:T(8,128)S(1)}, f32[512,512]{1,0:T(8,128)}, u32[]{:S(2)}) copy-start(f32[512,512]{1,0:T(8,128)} %get-tuple-element.40) | copy-start | bytes 3145732
  55.1 57.5 %all-to-all-start = ((s16[8,272,1024]{2,1,0:T(8,128)(2,1)}), s16[8,272,1024]{2,1,0:T(8,128)(2,1)}, u32[]{:S(2)}, u32[]{:S(2)}) async-start(s16[8,272,1024]{2,1,0:T(8,128)(2,1)} %get-tuple-element.39), calls=%async_computation | async-start | bytes 8912896 | tf_op jit(solution)/shard_map/all_to_all | solution.py:802
  60.2 17.7 %copy-start.3 = (f32[1024,512]{1,0:T(8,128)S(1)}, f32[1024,512]{1,0:T(8,128)}, u32[]{:S(2)}) copy-start(f32[1024,512]{1,0:T(8,128)} %get-tuple-element.43.gcol) | copy-start | bytes 6291460
  61.0 2.4 collective-permute-start.5
  64.6 9.0 %collective-permute-start.6 = (f32[64,512]{1,0:T(8,128)S(1)}, f32[64,512]{1,0:T(8,128)S(1)}, u32[]{:S(2)}, u32[]{:S(2)}) collective-permute-start(f32[64,512]{1,0:T(8,128)S(1)} %get-tuple-element.72), channel_id=1, source_target_pairs={{0,2},{1,3},{2,4},{3,5},{4,6},{5,7},{6,0},{7,1},{8,10},{9,11},{10,... | collective-permute-start | bytes 393224 | tf_op jit(solution)/shard_map/ppermute | solution.py:48
  64.7 8.9 %collective-permute-start.8 = (f32[64,512]{1,0:T(8,128)S(1)}, f32[64,512]{1,0:T(8,128)S(1)}, u32[]{:S(2)}, u32[]{:S(2)}) collective-permute-start(f32[64,512]{1,0:T(8,128)S(1)} %get-tuple-element.73), channel_id=1, source_target_pairs={{0,4},{1,5},{2,6},{3,7},{4,0},{5,1},{6,2},{7,3},{8,12},{9,13},{10,... | collective-permute-start | bytes 393224 | tf_op jit(solution)/shard_map/ppermute | solution.py:48
  65.8 8.0 %collective-permute-start.7 = (f32[64,512]{1,0:T(8,128)S(1)}, f32[64,512]{1,0:T(8,128)S(1)}, u32[]{:S(2)}, u32[]{:S(2)}) collective-permute-start(f32[64,512]{1,0:T(8,128)S(1)} %get-tuple-element.74), channel_id=1, source_target_pairs={{0,6},{1,7},{2,0},{3,1},{4,2},{5,3},{6,4},{7,5},{8,14},{9,15},{10,... | collective-permute-start | bytes 393224 | tf_op jit(solution)/shard_map/ppermute | solution.py:48
  73.8 11.6 %collective-permute-start.11 = (f32[64,512]{1,0:T(8,128)S(1)}, f32[64,512]{1,0:T(8,128)S(1)}, u32[]{:S(2)}, u32[]{:S(2)}) collective-permute-start(f32[64,512]{1,0:T(8,128)S(1)} %fusion.4), channel_id=1, source_target_pairs={{0,4},{1,5},{2,6},{3,7},{4,0},{5,1},{6,2},{7,3},{8,12},{9,13},{10,... | collective-permute-start | bytes 393224 | tf_op jit(solution)/shard_map/ppermute | solution.py:48
  74.9 10.4 %collective-permute-start.10 = (f32[64,512]{1,0:T(8,128)S(1)}, f32[64,512]{1,0:T(8,128)S(1)}, u32[]{:S(2)}, u32[]{:S(2)}) collective-permute-start(f32[64,512]{1,0:T(8,128)S(1)} %fusion.4), channel_id=1, source_target_pairs={{0,6},{1,7},{2,0},{3,1},{4,2},{5,3},{6,4},{7,5},{8,14},{9,15},{10,... | collective-permute-start | bytes 393224 | tf_op jit(solution)/shard_map/ppermute | solution.py:48
  77.4 6.3 %collective-permute-start.9 = (f32[64,512]{1,0:T(8,128)S(1)}, f32[64,512]{1,0:T(8,128)S(1)}, u32[]{:S(2)}, u32[]{:S(2)}) collective-permute-start(f32[64,512]{1,0:T(8,128)S(1)} %fusion.4), channel_id=1, source_target_pairs={{0,2},{1,3},{2,4},{3,5},{4,6},{5,7},{6,0},{7,1},{8,10},{9,11},{10,... | collective-permute-start | bytes 393224 | tf_op jit(solution)/shard_map/ppermute | solution.py:48
  79.4 0.8 copy-start.4
  80.2 15.1 %collective-permute-start.12 = (s16[2,256,512]{2,1,0:T(8,128)(2,1)S(1)}, s16[2,256,512]{2,1,0:T(8,128)(2,1)S(1)}, u32[]{:S(2)}, u32[]{:S(2)}) collective-permute-start(s16[2,256,512]{2,1,0:T(8,128)(2,1)S(1)} %get-tuple-element.45), channel_id=1, source_target_pairs={{0,2},{1,3},{2,4},{3,5},{4,6},{5,7},{6,0},{7,1},{8,10},{9,11},{10,... | collective-permute-start | bytes 1572872 | tf_op jit(solution)/shard_map/ppermute | solution.py:48
  82.8 22.5 %collective-permute-start.13 = (s16[2,256,512]{2,1,0:T(8,128)(2,1)S(1)}, s16[2,256,512]{2,1,0:T(8,128)(2,1)S(1)}, u32[]{:S(2)}, u32[]{:S(2)}) collective-permute-start(s16[2,256,512]{2,1,0:T(8,128)(2,1)S(1)} %get-tuple-element.46), channel_id=1, source_target_pairs={{0,4},{1,5},{2,6},{3,7},{4,0},{5,1},{6,2},{7,3},{8,12},{9,13},{10,... | collective-permute-start | bytes 1572872 | tf_op jit(solution)/shard_map/ppermute | solution.py:48
  83.7 22.5 %collective-permute-start.14 = (s16[2,256,512]{2,1,0:T(8,128)(2,1)S(1)}, s16[2,256,512]{2,1,0:T(8,128)(2,1)S(1)}, u32[]{:S(2)}, u32[]{:S(2)}) collective-permute-start(s16[2,256,512]{2,1,0:T(8,128)(2,1)S(1)} %get-tuple-element.47), channel_id=1, source_target_pairs={{0,6},{1,7},{2,0},{3,1},{4,2},{5,3},{6,4},{7,5},{8,14},{9,15},{10,... | collective-permute-start | bytes 1572872 | tf_op jit(solution)/shard_map/ppermute | solution.py:48
  95.3 10.9 %copy-start.14 = (s16[2,256,512]{2,1,0:T(8,128)(2,1)}, s16[2,256,512]{2,1,0:T(8,128)(2,1)S(1)}, u32[]{:S(2)}) copy-start(s16[2,256,512]{2,1,0:T(8,128)(2,1)S(1)} %collective-permute-done.12.refs_1_) | copy-start | bytes 1572868
  105.3 0.9 copy-start.15
  106.1 0.8 copy-start.16
  112.7 45.7 %collective-permute-start.15 = (s16[8,272,1024]{2,1,0:T(8,128)(2,1)}, s16[8,272,1024]{2,1,0:T(8,128)(2,1)}, u32[]{:S(2)}, u32[]{:S(2)}) collective-permute-start(s16[8,272,1024]{2,1,0:T(8,128)(2,1)} %all-to-all-done.own), channel_id=1, source_target_pairs={{0,8},{1,9},{2,10},{3,11},{4,12},{5,13},{6,14},{7,15},{8,0},{9,1},... | collective-permute-start | bytes 13369352 | tf_op jit(solution)/shard_map/ppermute | solution.py:48
  113.5 44.9 %copy-start.5 = (s32[2,48]{1,0:T(2,128)S(1)}, s32[2,48]{1,0:T(2,128)}, u32[]{:S(2)}) copy-start(s32[2,48]{1,0:T(2,128)} %select_reduce_fusion.where) | copy-start | bytes 1156
  113.5 44.9 %copy-start.7 = (s32[11]{0:T(128)S(1)}, s32[11]{0:T(128)}, u32[]{:S(2)}) copy-start(s32[11]{0:T(128)} %copy-done.6) | copy-start | bytes 136
  113.5 20.1 %collective-permute-start.16 = (f32[64,512]{1,0:T(8,128)S(1)}, f32[64,512]{1,0:T(8,128)S(1)}, u32[]{:S(2)}, u32[]{:S(2)}) collective-permute-start(f32[64,512]{1,0:T(8,128)S(1)} %get-tuple-element.69), channel_id=1, source_target_pairs={{0,16},{1,17},{2,18},{3,19},{4,20},{5,21},{6,22},{7,23},{8,24},{9,... | collective-permute-start | bytes 393224 | tf_op jit(solution)/shard_map/ppermute | solution.py:48
  126.5 11.1 %collective-permute-start.18 = (f32[64,512]{1,0:T(8,128)S(1)}, f32[64,512]{1,0:T(8,128)S(1)}, u32[]{:S(2)}, u32[]{:S(2)}) collective-permute-start(f32[64,512]{1,0:T(8,128)S(1)} %get-tuple-element.70), channel_id=1, source_target_pairs={{0,32},{1,33},{2,34},{3,35},{4,36},{5,37},{6,38},{7,39},{8,40},{9,... | collective-permute-start | bytes 393224 | tf_op jit(solution)/shard_map/ppermute | solution.py:48
  130.9 10.5 %collective-permute-start.17 = (f32[64,512]{1,0:T(8,128)S(1)}, f32[64,512]{1,0:T(8,128)S(1)}, u32[]{:S(2)}, u32[]{:S(2)}) collective-permute-start(f32[64,512]{1,0:T(8,128)S(1)} %get-tuple-element.71), channel_id=1, source_target_pairs={{0,48},{1,49},{2,50},{3,51},{4,52},{5,53},{6,54},{7,55},{8,56},{9,... | collective-permute-start | bytes 393224 | tf_op jit(solution)/shard_map/ppermute | solution.py:48
  131.9 20.5 %copy-start.12 = (s16[256,512]{1,0:T(8,128)(2,1)}, s16[256,512]{1,0:T(8,128)(2,1)S(1)}, u32[]{:S(2)}) copy-start(s16[256,512]{1,0:T(8,128)(2,1)S(1)} %get-tuple-element.67.kept) | copy-start | bytes 786436
  132.0 9.5 %collective-permute-start.20 = (s16[256,512]{1,0:T(8,128)(2,1)S(1)}, s16[256,512]{1,0:T(8,128)(2,1)S(1)}, u32[]{:S(2)}, u32[]{:S(2)}) collective-permute-start(s16[256,512]{1,0:T(8,128)(2,1)S(1)} %get-tuple-element.67.kept), channel_id=1, source_target_pairs={{0,64},{1,65},{2,66},{3,67},{4,68},{5,69},{6,70},{7,71},{8,72},{9,... | collective-permute-start | bytes 786440 | tf_op jit(solution)/shard_map/ppermute | solution.py:48
  133.6 14.6 %collective-permute-start.21 = (s16[256,512]{1,0:T(8,128)(2,1)S(1)}, s16[256,512]{1,0:T(8,128)(2,1)S(1)}, u32[]{:S(2)}, u32[]{:S(2)}) collective-permute-start(s16[256,512]{1,0:T(8,128)(2,1)S(1)} %get-tuple-element.68), channel_id=1, source_target_pairs={{0,65},{1,64},{2,67},{3,66},{4,69},{5,68},{6,71},{7,70},{8,73},{9,... | collective-permute-start | bytes 786440 | tf_op jit(solution)/shard_map/ppermute | solution.py:48
  137.6 11.1 %collective-permute-start.19 = (s16[256,512]{1,0:T(8,128)(2,1)S(1)}, s16[256,512]{1,0:T(8,128)(2,1)S(1)}, u32[]{:S(2)}, u32[]{:S(2)}) collective-permute-start(s16[256,512]{1,0:T(8,128)(2,1)S(1)} %get-tuple-element.68), channel_id=1, source_target_pairs={{0,1},{1,0},{2,3},{3,2},{4,5},{5,4},{6,7},{7,6},{8,9},{9,8},{10,11... | collective-permute-start | bytes 786440 | tf_op jit(solution)/shard_map/ppermute | solution.py:48
  141.5 11.0 %copy-start.17 = (s16[256,512]{1,0:T(8,128)(2,1)}, s16[256,512]{1,0:T(8,128)(2,1)S(1)}, u32[]{:S(2)}) copy-start(s16[256,512]{1,0:T(8,128)(2,1)S(1)} %collective-permute-done.20.across) | copy-start | bytes 786436
  148.2 4.2 %copy-start.18 = (s16[256,512]{1,0:T(8,128)(2,1)}, s16[256,512]{1,0:T(8,128)(2,1)S(1)}, u32[]{:S(2)}) copy-start(s16[256,512]{1,0:T(8,128)(2,1)S(1)} %collective-permute-done.21.both) | copy-start | bytes 786436
  148.8 3.6 %copy-start.19 = (s16[256,512]{1,0:T(8,128)(2,1)}, s16[256,512]{1,0:T(8,128)(2,1)S(1)}, u32[]{:S(2)}) copy-start(s16[256,512]{1,0:T(8,128)(2,1)S(1)} %collective-permute-done.19.beside) | copy-start | bytes 786436
  148.8 6.3 %collective-permute-start.24 = (f32[64,512]{1,0:T(8,128)S(1)}, f32[64,512]{1,0:T(8,128)S(1)}, u32[]{:S(2)}, u32[]{:S(2)}) collective-permute-start(f32[64,512]{1,0:T(8,128)S(1)} %fusion.2), channel_id=1, source_target_pairs={{0,1},{1,0},{2,3},{3,2},{4,5},{5,4},{6,7},{7,6},{8,9},{9,8},{10,11... | collective-permute-start | bytes 393224 | tf_op jit(solution)/shard_map/ppermute | solution.py:48
  150.0 7.2 %collective-permute-start.23 = (f32[64,512]{1,0:T(8,128)S(1)}, f32[64,512]{1,0:T(8,128)S(1)}, u32[]{:S(2)}, u32[]{:S(2)}) collective-permute-start(f32[64,512]{1,0:T(8,128)S(1)} %fusion.2), channel_id=1, source_target_pairs={{0,64},{1,65},{2,66},{3,67},{4,68},{5,69},{6,70},{7,71},{8,72},{9,... | collective-permute-start | bytes 393224 | tf_op jit(solution)/shard_map/ppermute | solution.py:48
  152.4 5.9 %collective-permute-start.22 = (f32[64,512]{1,0:T(8,128)S(1)}, f32[64,512]{1,0:T(8,128)S(1)}, u32[]{:S(2)}, u32[]{:S(2)}) collective-permute-start(f32[64,512]{1,0:T(8,128)S(1)} %fusion.2), channel_id=1, source_target_pairs={{0,65},{1,64},{2,67},{3,66},{4,69},{5,68},{6,71},{7,70},{8,73},{9,... | collective-permute-start | bytes 393224 | tf_op jit(solution)/shard_map/ppermute | solution.py:48
  162.0 7.4 %copy-start.11 = (s16[2,256,512]{2,1,0:T(8,128)(2,1)S(1)}, s16[2,256,512]{2,1,0:T(8,128)(2,1)}, u32[]{:S(2)}) copy-start(s16[2,256,512]{2,1,0:T(8,128)(2,1)} %shard_map.68) | copy-start | bytes 1572868
  162.0 77.1 %all-to-all-start.1 = ((s16[8,1552,256]{2,1,0:T(8,128)(2,1)}), s16[8,1552,256]{2,1,0:T(8,128)(2,1)}, u32[]{:S(2)}, u32[]{:S(2)}) async-start(s16[8,1552,256]{2,1,0:T(8,128)(2,1)} %shard_map.67), calls=%async_computation.1 | async-start | bytes 12713984 | tf_op jit(solution)/shard_map/all_to_all | solution.py:820
  167.0 9.3 %collective-permute-start.27 = (f32[64,512]{1,0:T(8,128)S(1)}, f32[64,512]{1,0:T(8,128)S(1)}, u32[]{:S(2)}, u32[]{:S(2)}) collective-permute-start(f32[64,512]{1,0:T(8,128)S(1)} %add_add_fusion), channel_id=1, source_target_pairs={{0,32},{1,33},{2,34},{3,35},{4,36},{5,37},{6,38},{7,39},{8,40},{9,... | collective-permute-start | bytes 393224 | tf_op jit(solution)/shard_map/ppermute | solution.py:48
  167.4 8.9 %collective-permute-start.26 = (f32[64,512]{1,0:T(8,128)S(1)}, f32[64,512]{1,0:T(8,128)S(1)}, u32[]{:S(2)}, u32[]{:S(2)}) collective-permute-start(f32[64,512]{1,0:T(8,128)S(1)} %add_add_fusion), channel_id=1, source_target_pairs={{0,48},{1,49},{2,50},{3,51},{4,52},{5,53},{6,54},{7,55},{8,56},{9,... | collective-permute-start | bytes 393224 | tf_op jit(solution)/shard_map/ppermute | solution.py:48
  169.5 6.8 %collective-permute-start.25 = (f32[64,512]{1,0:T(8,128)S(1)}, f32[64,512]{1,0:T(8,128)S(1)}, u32[]{:S(2)}, u32[]{:S(2)}) collective-permute-start(f32[64,512]{1,0:T(8,128)S(1)} %add_add_fusion), channel_id=1, source_target_pairs={{0,16},{1,17},{2,18},{3,19},{4,20},{5,21},{6,22},{7,23},{8,24},{9,... | collective-permute-start | bytes 393224 | tf_op jit(solution)/shard_map/ppermute | solution.py:48
  169.5 19.4 %collective-permute-start.31 = (s16[2,256,512]{2,1,0:T(8,128)(2,1)S(1)}, s16[2,256,512]{2,1,0:T(8,128)(2,1)S(1)}, u32[]{:S(2)}, u32[]{:S(2)}) collective-permute-start(s16[2,256,512]{2,1,0:T(8,128)(2,1)S(1)} %copy-done.11), channel_id=1, source_target_pairs={{0,48},{1,49},{2,50},{3,51},{4,52},{5,53},{6,54},{7,55},{8,56},{9,... | collective-permute-start | bytes 1572872 | tf_op jit(solution)/shard_map/ppermute | solution.py:48
  172.2 16.7 %collective-permute-start.30 = (s16[2,256,512]{2,1,0:T(8,128)(2,1)S(1)}, s16[2,256,512]{2,1,0:T(8,128)(2,1)S(1)}, u32[]{:S(2)}, u32[]{:S(2)}) collective-permute-start(s16[2,256,512]{2,1,0:T(8,128)(2,1)S(1)} %copy-done.11), channel_id=1, source_target_pairs={{0,32},{1,33},{2,34},{3,35},{4,36},{5,37},{6,38},{7,39},{8,40},{9,... | collective-permute-start | bytes 1572872 | tf_op jit(solution)/shard_map/ppermute | solution.py:48
  176.3 20.4 %collective-permute-start.29 = (s16[2,256,512]{2,1,0:T(8,128)(2,1)S(1)}, s16[2,256,512]{2,1,0:T(8,128)(2,1)S(1)}, u32[]{:S(2)}, u32[]{:S(2)}) collective-permute-start(s16[2,256,512]{2,1,0:T(8,128)(2,1)S(1)} %copy-done.11), channel_id=1, source_target_pairs={{0,16},{1,17},{2,18},{3,19},{4,20},{5,21},{6,22},{7,23},{8,24},{9,... | collective-permute-start | bytes 1572872 | tf_op jit(solution)/shard_map/ppermute | solution.py:48
  176.4 24.8 %collective-permute-start.28 = (f32[256,512]{1,0:T(8,128)S(1)}, f32[256,512]{1,0:T(8,128)}, u32[]{:S(2)}, u32[]{:S(2)}) collective-permute-start(f32[256,512]{1,0:T(8,128)S(1)} %bitcast.84), channel_id=1, source_target_pairs={{0,8},{1,9},{2,10},{3,11},{4,12},{5,13},{6,14},{7,15},{8,0},{9,1},... | collective-permute-start | bytes 1572872 | tf_op jit(solution)/shard_map/ppermute | solution.py:48
  196.9 33.0 %collective-permute-start.32 = (s16[4,2,256,512]{3,2,1,0:T(8,128)(2,1)S(1)}, s16[4,2,256,512]{3,2,1,0:T(8,128)(2,1)}, u32[]{:S(2)}, u32[]{:S(2)}) collective-permute-start(s16[4,2,256,512]{3,2,1,0:T(8,128)(2,1)S(1)} %pad_add_fusion.own), channel_id=1, source_target_pairs={{0,8},{1,9},{2,10},{3,11},{4,12},{5,13},{6,14},{7,15},{8,0},{9,1},... | collective-permute-start | bytes 6291464 | tf_op jit(solution)/shard_map/ppermute | solution.py:48
  228.9 1.0 copy-start.9
  235.7 1.2 copy-start.1
  239.2 27.4 %all-to-all-start.2 = ((s16[8,208,512]{2,1,0:T(8,128)(2,1)}), s16[8,208,512]{2,1,0:T(8,128)(2,1)S(1)}, u32[]{:S(2)}, u32[]{:S(2)}) async-start(s16[8,208,512]{2,1,0:T(8,128)(2,1)} %copy-done.1), calls=%async_computation.2 | async-start | bytes 3407872 | tf_op jit(solution)/shard_map/all_to_all | solution.py:827
  253.4 2.2 copy-start.2
  266.5 5.1 %copy-start.10 = (s16[8,208,512]{2,1,0:T(8,128)(2,1)}, s16[8,208,512]{2,1,0:T(8,128)(2,1)S(1)}, u32[]{:S(2)}) copy-start(s16[8,208,512]{2,1,0:T(8,128)(2,1)S(1)} %all-to-all-done.2.gx) | copy-start | bytes 5111812
  266.6 5.0 %collective-permute-start.33 = (s16[8,112,512]{2,1,0:T(8,128)(2,1)S(1)}, s16[8,112,512]{2,1,0:T(8,128)(2,1)S(1)}, u32[]{:S(2)}, u32[]{:S(2)}) collective-permute-start(s16[8,112,512]{2,1,0:T(8,128)(2,1)S(1)} %slice.9), channel_id=1, source_target_pairs={{0,8},{1,9},{2,10},{3,11},{4,12},{5,13},{6,14},{7,15},{8,0},{9,1},... | collective-permute-start | bytes 2752520 | tf_op jit(solution)/shard_map/ppermute | solution.py:48
